TPU v7x, 256 devices: a whole 4x4x8 slice. The times are simulated.
256 devices in a mesh: seq: 32 (over z_lo, y, x), dp: 8 (over z_hi, core).
Axes of the slice: x: 4, y: 4, z: 8 (z_hi: 4, z_lo: 2; z = z_hi * 2 + z_lo), core: 2. Of those that a mesh axis runs over, the one named last changes fastest.
Arguments:
- frames: bfloat16 [8, 4096, 1024], P('dp', 'seq'), may hold values from -6 to 6
- cotangent: bfloat16 [8, 4096, 1024], P('dp', 'seq'), may hold values from -6 to 6
- lengths: int32 [8], P('dp'), may hold values from 2048 to 4096, as said below
- w_qkv: bfloat16 [1024, 1536], replicated
- w_out: bfloat16 [512, 1024], replicated, may hold values from -1.5 to 1.5
- w_up: bfloat16 [1024, 2048], replicated, may hold values from -0.1875 to 0.1875
- w_down: bfloat16 [1024, 1024], replicated, may hold values from -0.1875 to 0.1875
- conv_kernel: float32 [31, 1024], replicated, may hold values from -1 to 1
Outputs:
- layer_out: bfloat16 [8, 4096, 1024], P('dp', 'seq')
- d_frames: bfloat16 [8, 4096, 1024], P('dp', 'seq')
- g_qkv: float32 [1024, 1536], P('dp', 'seq')
- g_out: float32 [512, 1024], P('dp', 'seq')
- g_up: float32 [1024, 2048], P('dp', 'seq')
- g_down: float32 [1024, 1024], P('dp', 'seq')
- g_kernel: float32 [31, 1024], P(None, 'seq')
Inputs may be any that keep to these rules, and one draw needn't show every extreme that they name: `lengths`: some recording has all 4096 frames valid and another has 2048.
All inputs are finite; a program needn't handle non-finite values.
Results may differ from a plain program's by a relative error of at most 0.04.
The roundings to bfloat16 on the way count: a program that leaves them out, or rounds other values in their place, can miss the bound.
Values may be sent and summed in bfloat16 or wider, within the bound.
No kernel may reach another device: no remote copies, remote signals or barrier semaphores. Data moves between devices by JAX's collectives and lax.ppermute only.
A program may use at most 128 MiB of HBM per device.

v0:
```python
import jax
import jax.numpy as jnp
from jax import lax
from jax.sharding import PartitionSpec as P

HEAD = 64
BAND = 512


EPSILON = 1e-05
NEG_LARGE = -1e30
HALF_ROOT = 0.7071067811865476
NORMAL_PEAK = 0.3989422804014327


def from_behind(array, axis, by):
    devices = lax.axis_size(axis)
    pairs = [(i, i + by) for i in range(devices) if 0 <= i + by < devices]
    return lax.ppermute(array, axis, pairs)


def with_halo(array, sides, width):
    for axis, dim in sides:
        devices, length = (lax.axis_size(axis), array.shape[dim])
        up = [(i, (i + 1) % devices) for i in range(devices - 1)]
        down = [(j, i) for i, j in up]
        last = lax.slice_in_dim(array, length - width, length, axis=dim)
        first = lax.slice_in_dim(array, 0, width, axis=dim)
        before = lax.ppermute(last, axis, up)
        after = lax.ppermute(first, axis, down)
        array = jnp.concatenate([before, array, after], axis=dim)
    return array


def normalize(values):
    row_mean = jnp.mean(values, axis=-1, keepdims=True)
    centred = values - row_mean
    inverse = lax.rsqrt(jnp.mean(centred * centred, axis=-1, keepdims=True) + EPSILON)
    return (centred * inverse, inverse)


def norm_back(gradient, unit_rows, inverse):
    return inverse * (
        gradient
        - jnp.mean(gradient, axis=-1, keepdims=True)
        - unit_rows * jnp.mean(gradient * unit_rows, axis=-1, keepdims=True)
    )


def gelu_slope(upper):
    return (
        0.5 * (1.0 + lax.erf(upper * HALF_ROOT))
        + upper * jnp.exp(-0.5 * upper * upper) * NORMAL_PEAK
    )


def band_forward(query_rows, window, query_pos, key_pos, length, head_count):
    slice_rows, inner_width = query_rows.shape
    query_heads = query_rows.reshape(slice_rows, head_count, HEAD)
    key_heads = window[:, :inner_width].reshape(-1, head_count, HEAD)
    value_heads = window[:, inner_width:].reshape(-1, head_count, HEAD)
    scores = jnp.einsum(
        "shd,whd->hsw", query_heads, key_heads, preferred_element_type=jnp.float32
    ) * HEAD ** (-0.5)
    allowed = (
        (jnp.abs(query_pos[:, None] - key_pos[None, :]) <= BAND)
        & (key_pos[None, :] >= 0)
        & (key_pos[None, :] < length)
    )
    scores = jnp.where(allowed[None], scores, NEG_LARGE)
    row_max = jnp.max(scores, axis=-1, keepdims=True)
    weights = jnp.where(allowed[None], jnp.exp(scores - row_max), 0.0)
    row_total = jnp.maximum(jnp.sum(weights, axis=-1, keepdims=True), 1.0)
    soft_weights = (weights / row_total).astype(jnp.bfloat16)
    context = jnp.einsum(
        "hsw,whd->shd", soft_weights, value_heads, preferred_element_type=jnp.float32
    )
    return (soft_weights, context.reshape(slice_rows, inner_width).astype(jnp.bfloat16))


def band_backward(query_rows, window, soft_weights, d_context, head_count):
    slice_rows, inner_width = query_rows.shape
    query_heads = query_rows.reshape(slice_rows, head_count, HEAD)
    key_heads = window[:, :inner_width].reshape(-1, head_count, HEAD)
    value_heads = window[:, inner_width:].reshape(-1, head_count, HEAD)
    d_heads = d_context.reshape(slice_rows, head_count, HEAD)
    d_soft = jnp.einsum("shd,whd->hsw", d_heads, value_heads, preferred_element_type=jnp.float32)
    weights_f = soft_weights.astype(jnp.float32)
    row_dot = jnp.sum(weights_f * d_soft, axis=-1, keepdims=True)
    d_scores = (weights_f * (d_soft - row_dot) * HEAD ** (-0.5)).astype(jnp.bfloat16)
    d_query = jnp.einsum(
        "hsw,whd->shd", d_scores, key_heads, preferred_element_type=jnp.float32
    ).reshape(slice_rows, inner_width)
    d_key = jnp.einsum(
        "hsw,shd->whd", d_scores, query_heads, preferred_element_type=jnp.float32
    ).reshape(-1, inner_width)
    d_value = jnp.einsum(
        "hsw,shd->whd", soft_weights, d_heads, preferred_element_type=jnp.float32
    ).reshape(-1, inner_width)
    return (d_query, jnp.concatenate([d_key, d_value], axis=1))


def local(frames, cotangent, lengths, w_qkv, w_out, w_up, w_down, conv_kernel):
    record_count, slice_rows, model_width = frames.shape
    inner_width = w_out.shape[0]
    half_width = w_down.shape[0]
    tap_count = conv_kernel.shape[0]
    margin = tap_count // 2
    head_count = inner_width // HEAD
    reach_slices = (BAND + slice_rows - 1) // slice_rows
    first_frame = lax.axis_index("seq") * slice_rows
    query_pos = first_frame + jnp.arange(slice_rows, dtype=jnp.int32)
    key_pos = (
        first_frame
        - reach_slices * slice_rows
        + jnp.arange((2 * reach_slices + 1) * slice_rows, dtype=jnp.int32)
    )
    unit_rows, unit_inv = normalize(frames.astype(jnp.float32))
    normed = unit_rows.astype(jnp.bfloat16)
    joined_rows = jnp.einsum(
        "rsd,de->rse", normed, w_qkv, preferred_element_type=jnp.float32
    ).astype(jnp.bfloat16)
    query_rows = joined_rows[..., :inner_width]
    keyval = joined_rows[..., inner_width:]
    before_list = []
    after_list = []
    for distance in range(1, reach_slices + 1):
        before_list.append(from_behind(keyval, "seq", distance))
        after_list.append(from_behind(keyval, "seq", -distance))
    window = jnp.concatenate(before_list[::-1] + [keyval] + after_list, axis=1)

    def attend_one(query_block, window_block, length):
        return band_forward(query_block, window_block, query_pos, key_pos, length, head_count)

    soft_weights, context = jax.vmap(attend_one)(query_rows, window, lengths)
    upper = jnp.einsum("rsd,dh->rsh", normed, w_up, preferred_element_type=jnp.float32)
    hidden = jax.nn.gelu(upper, approximate=False).astype(jnp.bfloat16)
    resid_half = hidden[..., :half_width]
    gate_unit, gate_inv = normalize(hidden[..., half_width:].astype(jnp.float32))
    valid_rows = (query_pos[None, :] < lengths[:, None])[..., None]
    gating = jnp.where(valid_rows, gate_unit, 0.0).astype(jnp.bfloat16)
    gating_ext = with_halo(gating, (("seq", 1),), margin)
    gating_f = gating_ext.astype(jnp.float32)
    conv_out = jnp.zeros((record_count, slice_rows, half_width), jnp.float32)
    for offset in range(tap_count):
        conv_out = conv_out + conv_kernel[offset] * gating_f[:, offset : offset + slice_rows]
    gated_rows = (resid_half.astype(jnp.float32) * conv_out).astype(jnp.bfloat16)
    layer_out = (
        frames.astype(jnp.float32)
        + jnp.einsum("rsi,id->rsd", context, w_out, preferred_element_type=jnp.float32)
        + jnp.einsum("rsh,hd->rsd", gated_rows, w_down, preferred_element_type=jnp.float32)
    ).astype(jnp.bfloat16)
    g_down = jnp.einsum("rsh,rsd->hd", gated_rows, cotangent, preferred_element_type=jnp.float32)
    d_gated = jnp.einsum(
        "rsd,hd->rsh", cotangent, w_down, preferred_element_type=jnp.float32
    ).astype(jnp.bfloat16)
    d_resid = d_gated.astype(jnp.float32) * conv_out
    d_conv = (d_gated.astype(jnp.float32) * resid_half.astype(jnp.float32)).astype(jnp.bfloat16)
    d_conv_f = d_conv.astype(jnp.float32)
    g_kernel = jnp.stack(
        [
            jnp.sum(gating_f[:, offset : offset + slice_rows] * d_conv_f, axis=(0, 1))
            for offset in range(tap_count)
        ]
    )
    d_conv_ext = with_halo(d_conv, (("seq", 1),), margin).astype(jnp.float32)
    d_gating = jnp.zeros((record_count, slice_rows, half_width), jnp.float32)
    for offset in range(tap_count):
        d_gating = (
            d_gating
            + conv_kernel[offset]
            * d_conv_ext[:, 2 * margin - offset : 2 * margin - offset + slice_rows]
        )
    d_gate_half = norm_back(jnp.where(valid_rows, d_gating, 0.0), gate_unit, gate_inv)
    d_upper = (jnp.concatenate([d_resid, d_gate_half], axis=-1) * gelu_slope(upper)).astype(
        jnp.bfloat16
    )
    g_up = jnp.einsum("rsd,rsh->dh", normed, d_upper, preferred_element_type=jnp.float32)
    d_normed = jnp.einsum("rsh,dh->rsd", d_upper, w_up, preferred_element_type=jnp.float32)
    g_out = jnp.einsum("rsi,rsd->id", context, cotangent, preferred_element_type=jnp.float32)
    d_context = jnp.einsum(
        "rsd,id->rsi", cotangent, w_out, preferred_element_type=jnp.float32
    ).astype(jnp.bfloat16)

    def back_one(query_block, window_block, soft_block, d_context_block):
        return band_backward(query_block, window_block, soft_block, d_context_block, head_count)

    d_query, d_window = jax.vmap(back_one)(query_rows, window, soft_weights, d_context)
    slot_list = [
        d_window[:, slot * slice_rows : (slot + 1) * slice_rows]
        for slot in range(2 * reach_slices + 1)
    ]
    d_keyval = slot_list[reach_slices]
    for distance in range(1, reach_slices + 1):
        d_keyval = d_keyval + from_behind(slot_list[reach_slices - distance], "seq", -distance)
        d_keyval = d_keyval + from_behind(slot_list[reach_slices + distance], "seq", distance)
    d_joined = jnp.concatenate([d_query, d_keyval], axis=-1).astype(jnp.bfloat16)
    g_qkv = jnp.einsum("rsd,rse->de", normed, d_joined, preferred_element_type=jnp.float32)
    d_normed = d_normed + jnp.einsum(
        "rse,de->rsd", d_joined, w_qkv, preferred_element_type=jnp.float32
    )
    d_frames = (cotangent.astype(jnp.float32) + norm_back(d_normed, unit_rows, unit_inv)).astype(
        jnp.bfloat16
    )
    g_kernel = lax.psum(g_kernel, "dp")
    g_qkv, g_out, g_up, g_down, g_kernel = (
        lax.psum_scatter(g_qkv, "seq", scatter_dimension=1, tiled=True),
        lax.psum_scatter(g_out, "seq", scatter_dimension=1, tiled=True),
        lax.psum_scatter(g_up, "seq", scatter_dimension=1, tiled=True),
        lax.psum_scatter(g_down, "seq", scatter_dimension=1, tiled=True),
        lax.psum_scatter(g_kernel, "seq", scatter_dimension=1, tiled=True),
    )
    g_qkv, g_out, g_up, g_down = (
        lax.psum_scatter(g_qkv, "dp", scatter_dimension=0, tiled=True),
        lax.psum_scatter(g_out, "dp", scatter_dimension=0, tiled=True),
        lax.psum_scatter(g_up, "dp", scatter_dimension=0, tiled=True),
        lax.psum_scatter(g_down, "dp", scatter_dimension=0, tiled=True),
    )
    return (layer_out, d_frames, g_qkv, g_out, g_up, g_down, g_kernel)


def solution(mesh):
    return jax.shard_map(
        local,
        mesh=mesh,
        in_specs=(P("dp", "seq", None), P("dp", "seq", None), P("dp"), P(), P(), P(), P(), P()),
        out_specs=(
            P("dp", "seq", None),
            P("dp", "seq", None),
            P("dp", "seq"),
            P("dp", "seq"),
            P("dp", "seq"),
            P("dp", "seq"),
            P(None, "seq"),
        ),
        check_vma=False,
    )
```

profile of v0, /device:TPU:8, one launch (start us, length us, event | category | flops | bytes accessed | tf_op | source)
XLA Modules:
  0.0 1132.3 jit_solution(12946580593896139767)
XLA Ops:
  12.8 4.1 collective-permute-start.7
  18.8 3.2 collective-permute-start.2
  22.0 5.4 collective-permute-start.1
  27.4 3.5 collective-permute-start
  32.6 4.0 fusion.165
  37.8 4.6 collective-permute-done
  48.3 6.0 collective-permute-start.4
  55.2 5.2 collective-permute-done.3
  61.4 2.5 collective-permute-done.4
  72.4 6.1 fusion.176
  79.2 2.9 divide_convert_fusion
  86.5 3.6 fusion.137
  91.0 3.2 collective-permute-start.8
  94.2 4.9 collective-permute-start.9
  100.7 3.4 fusion.89
  104.4 2.8 multiply_bitcast_fusion
  108.0 2.7 fusion.141
  114.9 4.3 fusion.178
  119.2 8.1 fusion.8
  131.9 6.3 collective-permute-start.12
  140.2 3.4 collective-permute-start.14
  143.6 4.0 collective-permute-start.15
  147.6 4.2 collective-permute-start.16
  151.8 24.1 %collective-permute-done.12 = f32[1,128,1024]{1,2,0:T(8,128)} collective-permute-done((f32[1,128,1024]{1,2,0:T(8,128)S(1)}, f32[1,128,1024]{1,2,0:T(8,128)}, u32[]{:S(2)}, u32[]{:S(2)}) %collective-permute-start.12) | collective-permute-done | bytes 524320 | tf_op jit(solution)/shard_map/ppermute | solution.py:19
  175.9 7.3 collective-permute-start.17
  183.3 8.4 collective-permute-start.19
  193.6 7.6 fusion.16
  203.5 3.8 collective-permute-done.19
  207.3 2.5 fusion.147
  210.5 3.8 fusion.148
  217.7 6.3 collective-permute-start.11
  224.0 6.2 fusion.88
  230.2 5.6 stack.127
  238.9 4.9 fusion.168
  245.3 4.6 fusion.162
  250.0 30.4 %reduce-scatter.18.cloned.1.call-done = f32[512,32]{0,1:T(8,128)} async-done(((f32[512,1024]{0,1:T(8,128)}), f32[512,32]{0,1:T(8,128)}) %reduce-scatter.18.cloned.1.call-update) | async-done | bytes 65552 | tf_op jit(solution)/shard_map/reduce_scatter | solution.py:208
  282.2 3.1 convolution_bitcast_fusion
  285.3 164.4 %reduce-scatter.24.cloned.1.call-done = f32[1024,32]{0,1:T(8,128)} async-done(((f32[1024,1024]{0,1:T(8,128)}), f32[1024,32]{0,1:T(8,128)}) %reduce-scatter.24.cloned.1.call-update) | async-done | bytes 131088 | tf_op jit(solution)/shard_map/reduce_scatter | solution.py:210
  449.8 4.7 fusion.177
  454.5 171.3 %reduce-scatter.14.cloned.1.call-done = f32[1024,48]{0,1:T(8,128)} async-done(((f32[1024,1536]{0,1:T(8,128)}), f32[1024,48]{0,1:T(8,128)}) %reduce-scatter.14.cloned.1.call-update) | async-done | bytes 196624 | tf_op jit(solution)/shard_map/reduce_scatter | solution.py:207
  628.3 159.2 %reduce-scatter.30.cloned.1.call-done = f32[32,31]{1,0:T(8,128)} async-done(((f32[1024,31]{1,0:T(8,128)}), f32[32,31]{1,0:T(8,128)}) %reduce-scatter.30.cloned.1.call-update) | async-done | bytes 3984
  788.3 28.1 %psum.8 = f32[31,32]{1,0:T(8,128)} all-reduce(f32[31,32]{1,0:T(8,128)S(1)} %copy.34), channel_id=1, replica_groups=mesh['seq'=32,'dp'=8] {'dp'}, use_global_device_ids=true, to_apply=%region_50.51 | all-reduce | flops 992 | bytes 7936 | tf_op jit(solution)/shard_map/psum | solution.py:205
  816.4 3.2 fusion.45
  819.6 148.1 %reduce-scatter.20.cloned.1.call-done = f32[1024,64]{0,1:T(8,128)} async-done(((f32[1024,2048]{0,1:T(8,128)}), f32[1024,64]{0,1:T(8,128)}) %reduce-scatter.20.cloned.1.call-update) | async-done | bytes 262160 | tf_op jit(solution)/shard_map/reduce_scatter | solution.py:209
  971.0 40.6 %reduce-scatter.28.cloned.1.call-done = f32[64,32]{1,0:T(8,128)} async-done(((f32[512,32]{1,0:T(8,128)}), f32[64,32]{1,0:T(8,128)}) %reduce-scatter.28.cloned.1.call-update) | async-done | bytes 8208
  1013.0 36.6 %reduce-scatter.26.cloned.1.call-done = f32[128,32]{0,1:T(8,128)} async-done(((f32[1024,32]{0,1:T(8,128)}), f32[128,32]{0,1:T(8,128)}) %reduce-scatter.26.cloned.1.call-update) | async-done | bytes 16400 | tf_op jit(solution)/shard_map/reduce_scatter | solution.py:217
  1049.6 38.0 %reduce-scatter.16.cloned.1.call-done = f32[128,48]{0,1:T(8,128)} async-done(((f32[1024,48]{0,1:T(8,128)}), f32[128,48]{0,1:T(8,128)}) %reduce-scatter.16.cloned.1.call-update) | async-done | bytes 24592 | tf_op jit(solution)/shard_map/reduce_scatter | solution.py:214
  1087.5 38.3 %reduce-scatter.22.cloned.1.call-done = f32[128,64]{0,1:T(8,128)} async-done(((f32[1024,64]{0,1:T(8,128)}), f32[128,64]{0,1:T(8,128)}) %reduce-scatter.22.cloned.1.call-update) | async-done | bytes 32784 | tf_op jit(solution)/shard_map/reduce_scatter | solution.py:216
  (213 shorter events, 67.2 us)
Async XLA Ops:
  7.2 273.3 %reduce-scatter.18.cloned.1.call-start = ((), (), s32[]{:S(2)}) async-start(), calls=%async_computation.11 | async-start | bytes 2162688 | tf_op jit(solution)/shard_map/reduce_scatter | solution.py:208
  8.5 24.1 %copy-start.48 = (f32[128]{0:T(128)}, f32[128]{0:T(128)S(1)}, u32[]{:S(2)}) copy-start(f32[128]{0:T(128)S(1)} %broadcast_multiply_fusion.5) | copy-start | bytes 1540
  8.5 24.1 %copy-start.2 = (bf16[1,128,1024]{2,1,0:T(8,128)(2,1)S(1)}, bf16[1,128,1024]{2,1,0:T(8,128)(2,1)}, u32[]{:S(2)}) copy-start(bf16[1,128,1024]{2,1,0:T(8,128)(2,1)} %param.8) | copy-start | bytes 786436
  9.7 26.8 %copy-start.51 = (f32[128]{0:T(128)}, f32[128]{0:T(128)S(1)}, u32[]{:S(2)}) copy-start(f32[128]{0:T(128)S(1)} %add_rsqrt_fusion.1) | copy-start | bytes 1540
  12.8 52.2 %collective-permute-start.7 = (bf16[1,128,1024]{2,1,0:T(8,128)(2,1)}, bf16[1,128,1024]{2,1,0:T(8,128)(2,1)}, u32[]{:S(2)}, u32[]{:S(2)}) collective-permute-start(bf16[1,128,1024]{2,1,0:T(8,128)(2,1)} %slice.512), channel_id=1, source_target_pairs={{32,0},{40,8},{48,16},{56,24},{64,32},{72,40},{80,48},{88,56},{96,... | collective-permute-start | bytes 786440 | tf_op jit(solution)/shard_map/ppermute | solution.py:19
  16.9 47.1 %collective-permute-start.6 = (bf16[1,128,1024]{2,1,0:T(8,128)(2,1)}, bf16[1,128,1024]{2,1,0:T(8,128)(2,1)}, u32[]{:S(2)}, u32[]{:S(2)}) collective-permute-start(bf16[1,128,1024]{2,1,0:T(8,128)(2,1)} %slice.512), channel_id=1, source_target_pairs={{24,0},{32,8},{40,16},{48,24},{56,32},{64,40},{72,48},{80,56},{88,... | collective-permute-start | bytes 786440 | tf_op jit(solution)/shard_map/ppermute | solution.py:19
  18.8 29.5 %collective-permute-start.2 = (bf16[1,128,1024]{2,1,0:T(8,128)(2,1)}, bf16[1,128,1024]{2,1,0:T(8,128)(2,1)}, u32[]{:S(2)}, u32[]{:S(2)}) collective-permute-start(bf16[1,128,1024]{2,1,0:T(8,128)(2,1)} %slice.512), channel_id=1, source_target_pairs={{0,16},{8,24},{16,32},{24,40},{32,48},{40,56},{48,64},{56,72},{64,... | collective-permute-start | bytes 786440 | tf_op jit(solution)/shard_map/ppermute | solution.py:19
  22.0 23.3 %collective-permute-start.1 = (bf16[1,128,1024]{2,1,0:T(8,128)(2,1)}, bf16[1,128,1024]{2,1,0:T(8,128)(2,1)}, u32[]{:S(2)}, u32[]{:S(2)}) collective-permute-start(bf16[1,128,1024]{2,1,0:T(8,128)(2,1)} %slice.512), channel_id=1, source_target_pairs={{0,24},{8,32},{16,40},{24,48},{32,56},{40,64},{48,72},{56,80},{64,... | collective-permute-start | bytes 786440 | tf_op jit(solution)/shard_map/ppermute | solution.py:19
  27.4 15.0 %collective-permute-start = (bf16[1,128,1024]{2,1,0:T(8,128)(2,1)}, bf16[1,128,1024]{2,1,0:T(8,128)(2,1)}, u32[]{:S(2)}, u32[]{:S(2)}) collective-permute-start(bf16[1,128,1024]{2,1,0:T(8,128)(2,1)} %slice.512), channel_id=1, source_target_pairs={{0,32},{8,40},{16,48},{24,56},{32,64},{40,72},{48,80},{56,88},{64,... | collective-permute-start | bytes 786440 | tf_op jit(solution)/shard_map/ppermute | solution.py:19
  42.4 18.0 %collective-permute-start.3 = (bf16[1,128,1024]{2,1,0:T(8,128)(2,1)}, bf16[1,128,1024]{2,1,0:T(8,128)(2,1)S(1)}, u32[]{:S(2)}, u32[]{:S(2)}) collective-permute-start(bf16[1,128,1024]{2,1,0:T(8,128)(2,1)} %slice.512), channel_id=1, source_target_pairs={{0,8},{8,16},{16,24},{24,32},{32,40},{40,48},{48,56},{56,64},{64,7... | collective-permute-start | bytes 786440 | tf_op jit(solution)/shard_map/ppermute | solution.py:19
  45.4 18.6 %collective-permute-start.5 = (bf16[1,128,1024]{2,1,0:T(8,128)(2,1)}, bf16[1,128,1024]{2,1,0:T(8,128)(2,1)S(1)}, u32[]{:S(2)}, u32[]{:S(2)}) collective-permute-start(bf16[1,128,1024]{2,1,0:T(8,128)(2,1)} %slice.512), channel_id=1, source_target_pairs={{16,0},{24,8},{32,16},{40,24},{48,32},{56,40},{64,48},{72,56},{80,... | collective-permute-start | bytes 786440 | tf_op jit(solution)/shard_map/ppermute | solution.py:19
  48.3 15.7 %collective-permute-start.4 = (bf16[1,128,1024]{2,1,0:T(8,128)(2,1)}, bf16[1,128,1024]{2,1,0:T(8,128)(2,1)S(1)}, u32[]{:S(2)}, u32[]{:S(2)}) collective-permute-start(bf16[1,128,1024]{2,1,0:T(8,128)(2,1)} %slice.512), channel_id=1, source_target_pairs={{8,0},{16,8},{24,16},{32,24},{40,32},{48,40},{56,48},{64,56},{72,6... | collective-permute-start | bytes 786440 | tf_op jit(solution)/shard_map/ppermute | solution.py:19
  86.4 363.3 %reduce-scatter.24.cloned.1.call-start = ((), (), s32[]{:S(2)}) async-start(), calls=%async_computation.14 | async-start | bytes 4325376 | tf_op jit(solution)/shard_map/reduce_scatter | solution.py:210
  86.4 12.7 %copy-start.20 = (f32[31,1024]{1,0:T(8,128)S(1)}, f32[31,1024]{1,0:T(8,128)}, u32[]{:S(2)}) copy-start(f32[31,1024]{1,0:T(8,128)} %param.15) | copy-start | bytes 380932
  86.5 14.2 %copy-start.13 = (bf16[1,128,1024]{2,1,0:T(8,128)(2,1)S(1)}, bf16[1,128,1024]{2,1,0:T(8,128)(2,1)}, u32[]{:S(2)}) copy-start(bf16[1,128,1024]{2,1,0:T(8,128)(2,1)} %param.9) | copy-start | bytes 786436
  86.5 14.2 %copy-start.17 = (bf16[1024,1024]{1,0:T(8,128)(2,1)S(1)}, bf16[1024,1024]{1,0:T(8,128)(2,1)}, u32[]{:S(2)}) copy-start(bf16[1024,1024]{1,0:T(8,128)(2,1)} %param.14) | copy-start | bytes 6291460
  90.1 17.1 %copy-start.5 = (bf16[1,128,2048]{2,1,0:T(8,128)(2,1)}, bf16[1,128,2048]{2,1,0:T(8,128)(2,1)S(1)}, u32[]{:S(2)}) copy-start(bf16[1,128,2048]{2,1,0:T(8,128)(2,1)S(1)} %fusion.137) | copy-start | bytes 1572868
  91.0 8.5 collective-permute-start.8
  94.2 6.3 collective-permute-start.9
  99.3 4.9 copy-start.21
  99.3 4.8 copy-start.22
  99.3 4.8 copy-start.23
  99.3 4.8 copy-start.24
  110.8 515.0 %reduce-scatter.14.cloned.1.call-start = ((), (), s32[]{:S(2)}) async-start(), calls=%async_computation.9 | async-start | bytes 6488064 | tf_op jit(solution)/shard_map/reduce_scatter | solution.py:207
  131.9 44.0 %collective-permute-start.12 = (f32[1,128,1024]{1,2,0:T(8,128)S(1)}, f32[1,128,1024]{1,2,0:T(8,128)}, u32[]{:S(2)}, u32[]{:S(2)}) collective-permute-start(f32[1,128,1024]{1,2,0:T(8,128)S(1)} %get-tuple-element.44), channel_id=1, source_target_pairs={{8,0},{16,8},{24,16},{32,24},{40,32},{48,40},{56,48},{64,56},{72,6... | collective-permute-start | bytes 1572872 | tf_op jit(solution)/shard_map/ppermute | solution.py:19
  138.3 45.0 %collective-permute-start.13 = (f32[1,128,1024]{1,2,0:T(8,128)S(1)}, f32[1,128,1024]{1,2,0:T(8,128)}, u32[]{:S(2)}, u32[]{:S(2)}) collective-permute-start(f32[1,128,1024]{1,2,0:T(8,128)S(1)} %get-tuple-element.45), channel_id=1, source_target_pairs={{0,8},{8,16},{16,24},{24,32},{32,40},{40,48},{48,56},{56,64},{64,7... | collective-permute-start | bytes 1572872 | tf_op jit(solution)/shard_map/ppermute | solution.py:19
  140.2 51.5 %collective-permute-start.14 = (f32[1,128,1024]{1,2,0:T(8,128)S(1)}, f32[1,128,1024]{1,2,0:T(8,128)}, u32[]{:S(2)}, u32[]{:S(2)}) collective-permute-start(f32[1,128,1024]{1,2,0:T(8,128)S(1)} %get-tuple-element.46), channel_id=1, source_target_pairs={{16,0},{24,8},{32,16},{40,24},{48,32},{56,40},{64,48},{72,56},{80,... | collective-permute-start | bytes 1572872 | tf_op jit(solution)/shard_map/ppermute | solution.py:19
  143.6 57.6 %collective-permute-start.15 = (f32[1,128,1024]{1,2,0:T(8,128)}, f32[1,128,1024]{1,2,0:T(8,128)}, u32[]{:S(2)}, u32[]{:S(2)}) collective-permute-start(f32[1,128,1024]{1,2,0:T(8,128)} %get-tuple-element.47), channel_id=1, source_target_pairs={{0,16},{8,24},{16,32},{24,40},{32,48},{40,56},{48,64},{56,72},{64,... | collective-permute-start | bytes 1572872 | tf_op jit(solution)/shard_map/ppermute | solution.py:19
  147.6 53.6 %collective-permute-start.16 = (f32[1,128,1024]{1,2,0:T(8,128)}, f32[1,128,1024]{1,2,0:T(8,128)}, u32[]{:S(2)}, u32[]{:S(2)}) collective-permute-start(f32[1,128,1024]{1,2,0:T(8,128)} %get-tuple-element.48), channel_id=1, source_target_pairs={{24,0},{32,8},{40,16},{48,24},{56,32},{64,40},{72,48},{80,56},{88,... | collective-permute-start | bytes 1572872 | tf_op jit(solution)/shard_map/ppermute | solution.py:19
  175.9 27.6 %collective-permute-start.17 = (f32[1,128,1024]{1,2,0:T(8,128)}, f32[1,128,1024]{1,2,0:T(8,128)}, u32[]{:S(2)}, u32[]{:S(2)}) collective-permute-start(f32[1,128,1024]{1,2,0:T(8,128)} %get-tuple-element.49), channel_id=1, source_target_pairs={{0,24},{8,32},{16,40},{24,48},{32,56},{40,64},{48,72},{56,80},{64,... | collective-permute-start | bytes 1572872 | tf_op jit(solution)/shard_map/ppermute | solution.py:19
  183.3 24.0 %collective-permute-start.19 = (f32[1,128,1024]{1,2,0:T(8,128)}, f32[1,128,1024]{1,2,0:T(8,128)}, u32[]{:S(2)}, u32[]{:S(2)}) collective-permute-start(f32[1,128,1024]{1,2,0:T(8,128)} %get-tuple-element.50), channel_id=1, source_target_pairs={{0,32},{8,40},{16,48},{24,56},{32,64},{40,72},{48,80},{56,88},{64,... | collective-permute-start | bytes 1572872 | tf_op jit(solution)/shard_map/ppermute | solution.py:19
  191.7 15.6 %collective-permute-start.18 = (f32[1,128,1024]{1,2,0:T(8,128)}, f32[1,128,1024]{1,2,0:T(8,128)}, u32[]{:S(2)}, u32[]{:S(2)}) collective-permute-start(f32[1,128,1024]{1,2,0:T(8,128)} %get-tuple-element.51), channel_id=1, source_target_pairs={{32,0},{40,8},{48,16},{56,24},{64,32},{72,40},{80,48},{88,56},{96,... | collective-permute-start | bytes 1572872 | tf_op jit(solution)/shard_map/ppermute | solution.py:19
  201.2 9.3 copy-start.18
  201.2 9.3 copy-start.49
  201.2 9.3 copy-start.52
  214.3 573.1 %reduce-scatter.30.cloned.1.call-start = ((), (), s32[]{:S(2)}) async-start(), calls=%async_computation.17 | async-start | bytes 540672
  215.8 22.0 %collective-permute-start.10 = (bf16[1,15,1024]{2,1,0:T(8,128)(2,1)}, bf16[1,15,1024]{2,1,0:T(8,128)(2,1)}, u32[]{:S(2)}, u32[]{:S(2)}) collective-permute-start(bf16[1,15,1024]{2,1,0:T(8,128)(2,1)} %get-tuple-element.54), channel_id=1, source_target_pairs={{0,8},{8,16},{16,24},{24,32},{32,40},{40,48},{48,56},{56,64},{64,7... | collective-permute-start | bytes 92168 | tf_op jit(solution)/shard_map/ppermute | solution.py:29
  217.7 20.0 %collective-permute-start.11 = (bf16[1,15,1024]{2,1,0:T(8,128)(2,1)}, bf16[1,15,1024]{2,1,0:T(8,128)(2,1)}, u32[]{:S(2)}, u32[]{:S(2)}) collective-permute-start(bf16[1,15,1024]{2,1,0:T(8,128)(2,1)} %get-tuple-element.55), channel_id=1, source_target_pairs={{8,0},{16,8},{24,16},{32,24},{40,32},{48,40},{56,48},{64,56},{72,6... | collective-permute-start | bytes 92168 | tf_op jit(solution)/shard_map/ppermute | solution.py:30
  237.7 730.0 %reduce-scatter.20.cloned.1.call-start = ((), (), s32[]{:S(2)}) async-start(), calls=%async_computation.12 | async-start | bytes 8650752 | tf_op jit(solution)/shard_map/reduce_scatter | solution.py:209
  238.8 5.0 copy-start.6
  238.8 5.0 copy-start.55
  238.8 5.0 copy-start.57
  238.8 5.2 copy-start.9
  238.9 5.2 copy-start.16
  249.9 761.6 %reduce-scatter.28.cloned.1.call-start = ((), (), s32[]{:S(2)}) async-start(), calls=%async_computation.16 | async-start | bytes 294912
  282.1 767.4 %reduce-scatter.26.cloned.1.call-start = ((), (), s32[]{:S(2)}) async-start(), calls=%async_computation.15 | async-start | bytes 147456 | tf_op jit(solution)/shard_map/reduce_scatter | solution.py:217
  449.8 637.8 %reduce-scatter.16.cloned.1.call-start = ((), (), s32[]{:S(2)}) async-start(), calls=%async_computation.10 | async-start | bytes 221184 | tf_op jit(solution)/shard_map/reduce_scatter | solution.py:214
  625.8 500.0 %reduce-scatter.22.cloned.1.call-start = ((), (), s32[]{:S(2)}) async-start(), calls=%async_computation.13 | async-start | bytes 294912 | tf_op jit(solution)/shard_map/reduce_scatter | solution.py:216
  (41 other events, 150.4 us)
Sparse Core Ops, SparseCore 0:
  86.5 193.8 reduce-scatter.17
  283.1 166.5 reduce-scatter.23
  452.5 173.2 reduce-scatter.13
  628.3 159.1 reduce-scatter.29
  789.9 177.7 reduce-scatter.19
  970.0 41.4 reduce-scatter.27
  1014.8 34.7 reduce-scatter.25
  1052.6 34.8 reduce-scatter.15
  1090.8 34.9 reduce-scatter.21
where the time goes:
time: 1130 us
  waiting for transfers between devices  871 us (77%)
  starting transfers between devices  82.1 us (7%)
  matrix products  67.1 us (6%)
  other arithmetic  34.9 us (3%)
  local copies, waits for them, and re-layouts  33.9 us (3%)
  blocking collectives  28.1 us (2%)
  between operations  15.7 us (1%)
    unnamed x11, waiting for transfers between devices  200 us
    reduce_scatter x1, waiting for transfers between devices, local(): lax.psum_scatter(g_qkv, 'seq', scatter_dimension=1, tiled=True)  171 us
    reduce_scatter x1, waiting for transfers between devices, local(): lax.psum_scatter(g_down, 'seq', scatter_dimension=1, tiled=True)  164 us
    reduce_scatter x1, waiting for transfers between devices, local(): lax.psum_scatter(g_up, 'seq', scatter_dimension=1, tiled=True)  148 us
    ppermute x16, starting transfers between devices, from_behind(): return lax.ppermute(array, axis, pairs)  65.4 us
    ppermute x16, waiting for transfers between devices, from_behind(): return lax.ppermute(array, axis, pairs)  42.6 us
    reduce_scatter x1, waiting for transfers between devices, local(): lax.psum_scatter(g_up, 'dp', scatter_dimension=0, tiled=True)  38.3 us
    reduce_scatter x1, waiting for transfers between devices, local(): lax.psum_scatter(g_qkv, 'dp', scatter_dimension=0, tiled=True)  38 us
  transfers between devices with their start and end apart: 29, of which 16 were waited for; matrix products, arithmetic and copies ran while one was open for 9% of the time, Pallas kernels for 0%

commit v1 on v0

v1 whole, which is shorter than its diff:
```python
import jax
import jax.numpy as jnp
from jax import lax
from jax.experimental import pallas as pl
from jax.experimental.pallas import tpu as pltpu
from jax.sharding import PartitionSpec as P

HEAD = 64
BAND = 512
ROWS = 128
GROUP = 4
WINDOW = 2 * BAND + ROWS
MARGIN = 15
TAPS = 31

EPSILON = 1e-05
NEG_LARGE = -1e30
HALF_ROOT = 0.7071067811865476
NORMAL_PEAK = 0.3989422804014327

BF16 = jnp.bfloat16
F32 = jnp.float32
VMEM_LIMIT = 50 * 2**20

X_GROUPS = [[4 * g + x for x in range(4)] for g in range(8)]
Z_GROUPS = [[0, 2, 4, 6], [1, 3, 5, 7]]


def call(body, outs, scratch=(), scalars=0):
    def run(*args):
        specs = [pl.BlockSpec(memory_space=pltpu.SMEM)] * scalars
        specs += [pl.BlockSpec(memory_space=pltpu.VMEM)] * (len(args) - scalars)
        return pl.pallas_call(
            body,
            out_shape=[jax.ShapeDtypeStruct(shape, dtype) for shape, dtype in outs],
            in_specs=specs,
            out_specs=[pl.BlockSpec(memory_space=pltpu.VMEM)] * len(outs),
            scratch_shapes=list(scratch),
            compiler_params=pltpu.CompilerParams(vmem_limit_bytes=VMEM_LIMIT),
        )(*args)

    return run


def dot(left, right, left_dim=1, right_dim=0):
    return lax.dot_general(
        left, right, (((left_dim,), (right_dim,)), ((), ())), preferred_element_type=F32
    )


def normalize(values):
    centred = values - jnp.mean(values, axis=-1, keepdims=True)
    inverse = lax.rsqrt(jnp.mean(centred * centred, axis=-1, keepdims=True) + EPSILON)
    return (centred * inverse, inverse)


def norm_back(gradient, unit_rows, inverse):
    return inverse * (
        gradient
        - jnp.mean(gradient, axis=-1, keepdims=True)
        - unit_rows * jnp.mean(gradient * unit_rows, axis=-1, keepdims=True)
    )


def project_kernel(frames, cotangent, w_qkv, w_out, normed, cot_t, kv, qd):
    unit_rows, _ = normalize(frames[...].astype(F32))
    unit = unit_rows.astype(BF16)
    normed[...] = unit
    joined = dot(unit, w_qkv[...]).astype(BF16)
    d_context = dot(cotangent[...], w_out[...], 1, 1).astype(BF16)
    for pair in range(4):
        lanes = slice(128 * pair, 128 * pair + 128)
        kv[pair, :, :128] = joined[:, 512 + 128 * pair : 640 + 128 * pair]
        kv[pair, :, 128:] = joined[:, 1024 + 128 * pair : 1152 + 128 * pair]
        qd[pair, :, :128] = joined[:, lanes]
        qd[pair, :, 128:] = d_context[:, lanes]
    cot_t[...] = cotangent[...].T


def gate_kernel(
    place, normed, cotangent, w_up, w_down, resid, d_gated, gating, d_conv, unit, inverse, slope, top, bottom
):
    first_frame, length = place[0], place[1]
    upper = dot(normed[...], w_up[...])
    phi = 0.5 * (1.0 + lax.erf(upper * HALF_ROOT))
    slope[...] = phi + upper * jnp.exp(-0.5 * upper * upper) * NORMAL_PEAK
    hidden = (upper * phi).astype(BF16)
    gate_unit, gate_inv = normalize(hidden[:, 1024:].astype(F32))
    unit[...] = gate_unit
    inverse[...] = jnp.broadcast_to(gate_inv, inverse.shape)
    rows = first_frame + lax.broadcasted_iota(jnp.int32, (ROWS, 1024), 0)
    masked = jnp.where(rows < length, gate_unit, 0.0).astype(BF16)
    gating[...] = masked
    resid[...] = hidden[:, :1024]
    back = dot(cotangent[...], w_down[...], 1, 1).astype(BF16)
    d_gated[...] = back
    conv_back = (back.astype(F32) * hidden[:, :1024].astype(F32)).astype(BF16)
    d_conv[...] = conv_back
    top[:, :1024] = masked[:16]
    top[:, 1024:] = conv_back[:16]
    bottom[:, :1024] = masked[112:]
    bottom[:, 1024:] = conv_back[112:]


def conv_kernel_body(
    place, resid, d_gated, gating, d_conv, unit, inverse, slope, before, after, taps,
    gated, d_upper, d_upper_t, g_taps, gate_ext, conv_ext, conv_out, d_gating
):
    first_frame, length = place[0], place[1]
    gate_ext[:16] = before[:, :1024].astype(F32)
    gate_ext[16:144] = gating[...].astype(F32)
    gate_ext[144:] = after[:, :1024].astype(F32)
    conv_ext[:16] = before[:, 1024:].astype(F32)
    conv_ext[16:144] = d_conv[...].astype(F32)
    conv_ext[144:] = after[:, 1024:].astype(F32)
    g_taps[...] = jnp.zeros_like(g_taps)

    def chunk(index, _):
        lanes = pl.ds(pl.multiple_of(index * 128, 128), 128)
        own = conv_ext[16:144, lanes]
        forward = jnp.zeros((ROWS, 128), F32)
        for shift in range(8):
            moved = gate_ext[pl.ds(shift, 152), lanes]
            for step in range(4):
                offset = 8 * step + shift
                if 1 <= offset <= TAPS:
                    part = moved[8 * step : 8 * step + ROWS]
                    forward = forward + taps[offset - 1 : offset, lanes] * part
                    g_taps[offset - 1 : offset, lanes] = jnp.sum(part * own, axis=0, keepdims=True)
        conv_out[:, lanes] = forward
        backward = jnp.zeros((ROWS, 128), F32)
        for shift in range(8):
            moved = conv_ext[pl.ds(shift, 152), lanes]
            for step in range(4):
                offset = 8 * step + shift
                if 1 <= offset <= TAPS:
                    part = moved[8 * step : 8 * step + ROWS]
                    backward = backward + taps[TAPS - offset : TAPS - offset + 1, lanes] * part
        d_gating[:, lanes] = backward
        return 0

    lax.fori_loop(0, 8, chunk, 0)
    conv = conv_out[...]
    gated[...] = (resid[...].astype(F32) * conv).astype(BF16)
    rows = first_frame + lax.broadcasted_iota(jnp.int32, (ROWS, 1024), 0)
    d_gate = jnp.where(rows < length, d_gating[...], 0.0)
    d_gate = norm_back(d_gate, unit[...], inverse[:, :1])
    left = (d_gated[...].astype(F32) * conv * slope[:, :1024]).astype(BF16)
    right = (d_gate * slope[:, 1024:]).astype(BF16)
    d_upper[:, :1024] = left
    d_upper[:, 1024:] = right
    d_upper_t[:1024] = left.T
    d_upper_t[1024:] = right.T


def own_columns(array, core, width):
    parts = [
        array[:, pl.ds(pl.multiple_of(2 * width * z + width * core, width), width)] for z in range(4)
    ]
    return jnp.concatenate(parts, axis=1)


def gate_grads_kernel(
    place, normed, normed_far, gated, gated_far, d_upper_t, d_upper_far, cot_t, cot_far, taps, taps_far, out
):
    core = place[2]
    unit = jnp.concatenate([own_columns(normed, core, 128), own_columns(normed_far, core, 128)], axis=0)
    half = jnp.concatenate([own_columns(gated, core, 128), own_columns(gated_far, core, 128)], axis=0)
    up = dot(jnp.concatenate([d_upper_t[...], d_upper_far[...]], axis=1), unit)
    out[:, :64, :] = up.astype(BF16).reshape(32, 64, 512)
    down = dot(jnp.concatenate([cot_t[...], cot_far[...]], axis=1), half)
    out[:, 64:96, :] = down.astype(BF16).reshape(32, 32, 512)
    total = taps[...] + taps_far[...]
    wide = jnp.concatenate([total, jnp.zeros((96, 1024), F32)], axis=0).T.reshape(32, 32, 128)
    packed = wide[:, :16, :] + pltpu.roll(wide[:, 16:, :], 32, 2)
    packed = packed.astype(BF16)
    for z in range(4):
        out[:, 96:, 128 * z : 128 * z + 128] = packed


def attend_kernel(
    place, qd, kv, before, after, context_dq, d_before, d_after, d_own,
    key, value, key_t, value_t, scores, weights, d_scores, d_key, d_value
):
    group_first, length = place[3], place[1]
    for part, ref in enumerate((before, kv, after)):
        for piece in range(GROUP):
            start = 512 * part + ROWS * piece
            key_block = ref[piece, :, :128]
            value_block = ref[piece, :, 128:]
            key[start : start + ROWS] = key_block
            value[start : start + ROWS] = value_block
            key_t[:, start : start + ROWS] = key_block.T
            value_t[:, start : start + ROWS] = value_block.T
    d_key[...] = jnp.zeros_like(d_key)
    d_value[...] = jnp.zeros_like(d_value)
    lane = lax.broadcasted_iota(jnp.int32, (ROWS, 128), 1)
    first_head = lane < HEAD
    query_index = lax.broadcasted_iota(jnp.int32, (1, 256), 1)
    query_index = jnp.where(query_index < ROWS, query_index, query_index - ROWS)
    chunks = WINDOW // 128
    for block in range(GROUP):
        base = ROWS * block
        low = jnp.maximum(query_index, 512 - group_first - base)
        high = jnp.minimum(query_index + 1024, length - group_first + 511 - base)
        query = qd[block, :, :128].astype(F32) * 0.125
        d_context = qd[block, :, 128:].astype(F32)
        zero = jnp.zeros_like(query)
        query_pair = jnp.concatenate(
            [jnp.where(first_head, query, zero), jnp.where(first_head, zero, query)], axis=0
        ).astype(BF16)
        d_pair = jnp.concatenate(
            [jnp.where(first_head, d_context, zero), jnp.where(first_head, zero, d_context)], axis=0
        ).astype(BF16)

        def allowed_of(index):
            position = 128 * index + lax.broadcasted_iota(jnp.int32, (128, 256), 0)
            return (position >= low) & (position <= high)

        peak = jnp.full((128, 256), NEG_LARGE, F32)
        for index in range(chunks):
            part = dot(key[base + 128 * index : base + 128 * index + 128], query_pair, 1, 1)
            part = jnp.where(allowed_of(index), part, NEG_LARGE)
            scores[128 * index : 128 * index + 128] = part
            peak = jnp.maximum(peak, part)
        peak = jnp.max(peak, axis=0, keepdims=True)
        total = jnp.zeros((128, 256), F32)
        for index in range(chunks):
            part = scores[128 * index : 128 * index + 128]
            part = jnp.where(allowed_of(index), jnp.exp(part - peak), 0.0)
            scores[128 * index : 128 * index + 128] = part
            total = total + part
        scale = 1.0 / jnp.maximum(jnp.sum(total, axis=0, keepdims=True), 1.0)
        for index in range(chunks):
            part = scores[128 * index : 128 * index + 128] * scale
            weights[128 * index : 128 * index + 128] = part.astype(BF16)
        wide = dot(value_t[:, base : base + WINDOW], weights[...])
        context_t = jnp.concatenate([wide[:HEAD, :128], wide[HEAD:, 128:]], axis=0)
        context_dq[block, :, :128] = context_t.T.astype(BF16)
        product = context_t * d_context.T
        row_dot = jnp.concatenate(
            [
                jnp.sum(product[:HEAD], axis=0, keepdims=True),
                jnp.sum(product[HEAD:], axis=0, keepdims=True),
            ],
            axis=1,
        )
        for index in range(chunks):
            part = dot(value[base + 128 * index : base + 128 * index + 128], d_pair, 1, 1)
            part = weights[128 * index : 128 * index + 128].astype(F32) * (part - row_dot)
            d_scores[128 * index : 128 * index + 128] = part.astype(BF16)
        wide = dot(key_t[:, base : base + WINDOW], d_scores[...])
        d_query_t = jnp.concatenate([wide[:HEAD, :128], wide[HEAD:, 128:]], axis=0)
        context_dq[block, :, 128:] = (d_query_t.T * 0.125).astype(BF16)
        d_key[base : base + WINDOW] += dot(d_scores[...], query_pair)
        d_value[base : base + WINDOW] += dot(weights[...], d_pair)
    for piece in range(GROUP):
        for part, ref in enumerate((d_before, d_own, d_after)):
            start = 512 * part + ROWS * piece
            ref[piece, :, :128] = d_key[start : start + ROWS].astype(ref.dtype)
            ref[piece, :, 128:] = d_value[start : start + ROWS].astype(ref.dtype)


def join_kernel(own, from_before, from_after, out):
    out[...] = (own[...] + from_before[...].astype(F32) + from_after[...].astype(F32)).astype(BF16)


def gather_kernel(context_dq, d_kv, joined, joined_t, context):
    for pair in range(4):
        lanes = slice(128 * pair, 128 * pair + 128)
        context[:, lanes] = context_dq[pair, :, :128]
        joined[:, lanes] = context_dq[pair, :, 128:]
        joined[:, 512 + 128 * pair : 640 + 128 * pair] = d_kv[pair, :, :128]
        joined[:, 1024 + 128 * pair : 1152 + 128 * pair] = d_kv[pair, :, 128:]
    joined_t[...] = joined[...].T


def attention_grads_kernel(
    place, normed, normed_far, context, context_far, joined_t, joined_far, cot_t, cot_far, out
):
    core = place[2]
    unit = jnp.concatenate([own_columns(normed, core, 128), own_columns(normed_far, core, 128)], axis=0)
    grad = dot(jnp.concatenate([joined_t[...], joined_far[...]], axis=1), unit)
    out[:, :48, :] = grad.astype(BF16).reshape(32, 48, 512)
    both = jnp.concatenate([context[...], context_far[...]], axis=0).astype(F32)
    lane = lax.broadcasted_iota(jnp.int32, (2 * ROWS, 128), 1)
    keep = (lane < HEAD) == (core == 0)
    parts = []
    for z in range(4):
        block = both[:, 128 * z : 128 * z + 128]
        parts.append(jnp.where(keep, block, pltpu.roll(block, HEAD, 1)))
    doubled = jnp.concatenate(parts, axis=1).astype(BF16)
    grad = dot(jnp.concatenate([cot_t[...], cot_far[...]], axis=1), doubled).reshape(32, 32, 512)
    lane = lax.broadcasted_iota(jnp.int32, (32, 16, 512), 2)
    out[:, 48:, :] = jnp.where((lane & 127) < HEAD, grad[:, :16], grad[:, 16:]).astype(BF16)


def rows_kernel(
    frames, cotangent, context, gated, d_upper, joined, w_qkv, w_out, w_up, w_down, layer_out, d_frames
):
    values = frames[...].astype(F32)
    out = values + dot(context[...], w_out[...]) + dot(gated[...], w_down[...])
    layer_out[...] = out.astype(BF16)
    unit_rows, inverse = normalize(values)
    d_normed = dot(d_upper[...], w_up[...], 1, 1) + dot(joined[...], w_qkv[...], 1, 1)
    d_frames[...] = (cotangent[...].astype(F32) + norm_back(d_normed, unit_rows, inverse)).astype(BF16)


def chunk_sum_kernel(parts, out):
    total = parts[0].astype(F32)
    for index in range(1, parts.shape[0]):
        total = total + parts[index].astype(F32)
    for z in range(4):
        out[z] = total[:, 128 * z : 128 * z + 128].astype(BF16)


def gate_final_kernel(parts, g_up, g_down, g_taps):
    total = parts[0].astype(F32)
    for index in range(1, 4):
        total = total + parts[index].astype(F32)
    turned = total.T
    g_up[...] = turned[:, :64]
    g_down[...] = turned[:, 64:96]
    g_taps[...] = jnp.concatenate([turned[:TAPS, 96:], turned[32 : 32 + TAPS, 96:]], axis=1)


def attention_final_kernel(parts, g_qkv, g_out):
    total = parts[0].astype(F32)
    for index in range(1, 4):
        total = total + parts[index].astype(F32)
    turned = total.T
    g_qkv[...] = turned[:, :48]
    g_out[...] = jnp.concatenate([turned[:HEAD, 48:], turned[HEAD:, 48:]], axis=1)


def shift(array, by):
    return lax.ppermute(array, "seq", [(i, i + by) for i in range(32) if 0 <= i + by < 32])


def other_core(array):
    return lax.ppermute(array, "dp", [(i, i ^ 1) for i in range(8)])


def swap_x(array):
    return lax.all_to_all(array, "seq", 0, 0, axis_index_groups=X_GROUPS)


def local(frames, cotangent, lengths, w_qkv, w_out, w_up, w_down, conv_kernel):
    frames, cotangent = frames[0], cotangent[0]
    seq_index = lax.axis_index("seq")
    core = lax.axis_index("dp") % 2
    place = jnp.stack(
        [seq_index * ROWS, lengths[0], core, (seq_index // GROUP) * (GROUP * ROWS)]
    ).astype(jnp.int32)

    normed, cot_t, kv, qd = call(
        project_kernel,
        [((ROWS, 1024), BF16), ((1024, ROWS), BF16), ((4, ROWS, 256), BF16), ((4, ROWS, 256), BF16)],
    )(frames, cotangent, w_qkv, w_out)
    kv = swap_x(kv)
    qd = swap_x(qd)
    kv_before, kv_after = shift(kv, 4), shift(kv, -4)
    normed_far, cot_far = other_core(normed), other_core(cot_t)

    wide = ((ROWS, 1024), BF16)
    resid, d_gated, gating, d_conv, unit, inverse, slope, top, bottom = call(
        gate_kernel,
        [wide, wide, wide, wide, ((ROWS, 1024), F32), ((ROWS, 128), F32), ((ROWS, 2048), F32),
         ((16, 2048), BF16), ((16, 2048), BF16)],
        scalars=1,
    )(place, normed, cotangent, w_up, w_down)
    before, after = shift(bottom, 1), shift(top, -1)
    gated, d_upper, d_upper_t, g_taps = call(
        conv_kernel_body,
        [wide, ((ROWS, 2048), BF16), ((2048, ROWS), BF16), ((32, 1024), F32)],
        [pltpu.VMEM((160, 1024), F32), pltpu.VMEM((160, 1024), F32),
         pltpu.VMEM((ROWS, 1024), F32), pltpu.VMEM((ROWS, 1024), F32)],
        scalars=1,
    )(place, resid, d_gated, gating, d_conv, unit, inverse, slope, before, after, conv_kernel)
    (gate_grads,) = call(gate_grads_kernel, [((32, 112, 512), BF16)], scalars=1)(
        place, normed, normed_far, gated, other_core(gated), d_upper_t, other_core(d_upper_t),
        cot_t, cot_far, g_taps, other_core(g_taps),
    )
    gate_grads = lax.all_to_all(gate_grads, "seq", 0, 0)

    quad = (4, ROWS, 256)
    context_dq, d_before, d_after, d_own = call(
        attend_kernel,
        [(quad, BF16), (quad, BF16), (quad, BF16), (quad, F32)],
        [pltpu.VMEM((1536, 128), BF16), pltpu.VMEM((1536, 128), BF16),
         pltpu.VMEM((128, 1536), BF16), pltpu.VMEM((128, 1536), BF16),
         pltpu.VMEM((WINDOW, 256), F32), pltpu.VMEM((WINDOW, 256), BF16), pltpu.VMEM((WINDOW, 256), BF16),
         pltpu.VMEM((1536, 128), F32), pltpu.VMEM((1536, 128), F32)],
        scalars=1,
    )(place, qd, kv, kv_before, kv_after)
    context_dq = swap_x(context_dq)
    (d_kv,) = call(join_kernel, [(quad, BF16)])(d_own, shift(d_after, 4), shift(d_before, -4))
    d_kv = swap_x(d_kv)
    joined, joined_t, context = call(
        gather_kernel, [((ROWS, 1536), BF16), ((1536, ROWS), BF16), ((ROWS, 512), BF16)]
    )(context_dq, d_kv)
    (attention_grads,) = call(attention_grads_kernel, [((32, 64, 512), BF16)], scalars=1)(
        place, normed, normed_far, context, other_core(context), joined_t, other_core(joined_t), cot_t, cot_far
    )
    attention_grads = lax.all_to_all(attention_grads, "seq", 0, 0)
    layer_out, d_frames = call(rows_kernel, [wide, wide])(
        frames, cotangent, context, gated, d_upper, joined, w_qkv, w_out, w_up, w_down
    )
    (gate_grads,) = call(chunk_sum_kernel, [((4, 112, 128), BF16)])(gate_grads)
    gate_grads = lax.all_to_all(gate_grads, "dp", 0, 0, axis_index_groups=Z_GROUPS)
    g_up, g_down, g_kernel = call(
        gate_final_kernel, [((128, 64), F32), ((128, 32), F32), ((TAPS, 32), F32)]
    )(gate_grads)
    (attention_grads,) = call(chunk_sum_kernel, [((4, 64, 128), BF16)])(attention_grads)
    attention_grads = lax.all_to_all(attention_grads, "dp", 0, 0, axis_index_groups=Z_GROUPS)
    g_qkv, g_out = call(attention_final_kernel, [((128, 48), F32), ((64, 32), F32)])(attention_grads)
    return (layer_out[None], d_frames[None], g_qkv, g_out, g_up, g_down, g_kernel)


def solution(mesh):
    return jax.shard_map(
        local,
        mesh=mesh,
        in_specs=(P("dp", "seq", None), P("dp", "seq", None), P("dp"), P(), P(), P(), P(), P()),
        out_specs=(
            P("dp", "seq", None),
            P("dp", "seq", None),
            P("dp", "seq"),
            P("dp", "seq"),
            P("dp", "seq"),
            P("dp", "seq"),
            P(None, "seq"),
        ),
        check_vma=False,
    )
```

time: 1130 us -> 214 us (0.19)
  the two profiles are of different devices: /device:TPU:8 before, /device:TPU:4 now
where the time goes in v1:
time: 214 us; the launch traced here: 213 us
  waiting for transfers between devices  78.6 us (37%)
  starting transfers between devices  61.5 us (29%)
  Pallas kernels  44.1 us (21%)
  blocking collectives  17.9 us (8%)
  local copies, waits for them, and re-layouts  9.76 us (5%)
    all_to_all x1, waiting for transfers between devices, local(): gate_grads = lax.all_to_all(gate_grads, 'seq', 0, 0)  48.9 us
    pallas_call x13, Pallas kernels, run(): pl.pallas_call(body, out_shape=[jax.ShapeDtypeStruct(shape, dtype) for sh...  44.1 us
    all_to_all x2, blocking collectives, swap_x(): return lax.all_to_all(array, 'seq', 0, 0, axis_index_groups=X_GROUPS)  17.9 us
    ppermute x6, starting transfers between devices, shift(): lax.ppermute(array, 'seq', [(i, i + by) for i in range(32) if 0 <= i + by...  16.4 us
    ppermute x6, waiting for transfers between devices, shift(): lax.ppermute(array, 'seq', [(i, i + by) for i in range(32) if 0 <= i + by...  15.1 us
    all_to_all x2, starting transfers between devices, swap_x(): return lax.all_to_all(array, 'seq', 0, 0, axis_index_groups=X_GROUPS)  12.5 us
    all_to_all x1, starting transfers between devices, local(): attention_grads = lax.all_to_all(attention_grads, 'seq', 0, 0)  11.1 us
    unnamed x34, local copies, waits for them, and re-layouts  9.76 us
  transfers between devices with their start and end apart: 19, of which 11 were waited for; matrix products, arithmetic and copies ran while one was open for 1% of the time, Pallas kernels for 14%

profile of v1, /device:TPU:4, one launch (start us, length us, event | category | flops | bytes accessed | tf_op | source)
XLA Modules:
  0.0 213.4 jit_solution(14512701841075900656)
XLA Ops:
  0.6 1.2 copy-done
  1.9 0.9 copy-done.2
  2.8 0.9 copy-done.5
  3.8 3.7 %shard_map.135 = (bf16[128,1024]{1,0:T(8,128)(2,1)S(1)}, bf16[1024,128]{1,0:T(8,128)(2,1)S(1)}, bf16[4,128,256]{2,1,0:T(8,128)(2,1)S(1)}, bf16[4,128,256]{2,1,0:T(8,128)(2,1)}) custom-call(bf16[128,1024]{1,0:T(8,128)(2,1)S(1)} %bitcast.10, bf16[128,1024]{1,0:T(8,128)(2,1)S(1)} %bitcast.7, bf16[1024,1536]{1,0:T(8,128)(2,1)} %w_qkv.3, ...), custom_call_target="tpu_custom_call" | custom-call | tf_op jit(solution)/shard_map/pallas_call | solution.py:33
  7.4 8.6 %all_to_all.40.kv = bf16[4,128,256]{2,1,0:T(8,128)(2,1)S(1)} all-to-all(bf16[4,128,256]{2,1,0:T(8,128)(2,1)S(1)} %get-tuple-element.39), channel_id=1, replica_groups={{0,8,16,24},{32,40,48,56},{64,72,80,88},{96,104,112,120},{128,136,144,1..., dimensions={0} | all-to-all | bytes 524288 | tf_op jit(solution)/shard_map/all_to_all | solution.py:345
  16.0 1.3 collective-permute-start.1
  17.3 4.6 %collective-permute-start = (bf16[4,128,256]{2,1,0:T(8,128)(2,1)S(1)}, bf16[4,128,256]{2,1,0:T(8,128)(2,1)S(1)}, u32[]{:S(2)}, u32[]{:S(2)}) collective-permute-start(bf16[4,128,256]{2,1,0:T(8,128)(2,1)S(1)} %all_to_all.40.kv), channel_id=1, source_target_pairs={{0,32},{8,40},{16,48},{24,56},{32,64},{40,72},{48,80},{56,88},{64,... | collective-permute-start | bytes 786440 | tf_op jit(solution)/shard_map/ppermute | solution.py:337
  21.9 6.1 %all-to-all-start = ((bf16[4,128,256]{2,1,0:T(8,128)(2,1)}), bf16[4,128,256]{2,1,0:T(8,128)(2,1)S(1)}, u32[]{:S(2)}, u32[]{:S(2)}) async-start(bf16[4,128,256]{2,1,0:T(8,128)(2,1)} %get-tuple-element.38), calls=%async_computation | async-start | bytes 524288 | tf_op jit(solution)/shard_map/all_to_all | solution.py:345
  28.7 3.0 %all-to-all-done.qd = bf16[4,128,256]{2,1,0:T(8,128)(2,1)S(1)} async-done(((bf16[4,128,256]{2,1,0:T(8,128)(2,1)}), bf16[4,128,256]{2,1,0:T(8,128)(2,1)S(1)}, u32[]{:S(2)}, u32[]{:S(2)}) %all-to-all-start) | async-done | bytes 262176 | tf_op jit(solution)/shard_map/all_to_all | solution.py:345
  31.7 7.7 %shard_map.136 = (bf16[4,128,256]{2,1,0:T(8,128)(2,1)}, bf16[4,128,256]{2,1,0:T(8,128)(2,1)S(1)}, bf16[4,128,256]{2,1,0:T(8,128)(2,1)S(1)}, f32[4,128,256]{2,1,0:T(8,128)S(1)}) custom-call(s32[4]{0:T(128)S(1)} %pad_add_fusion.place, bf16[4,128,256]{2,1,0:T(8,128)(2,1)S(1)} %all-to-all-done.qd, bf16[4,128,256]{2,1,0:T(8,128)(2,1)S(1)} %all_to_all.40.kv, ...), custom_call_target="tpu_custom_call" | custom-call | tf_op jit(solution)/shard_map/pallas_call | solution.py:33
  39.4 3.4 %collective-permute-start.2 = (bf16[4,128,256]{2,1,0:T(8,128)(2,1)S(1)}, bf16[4,128,256]{2,1,0:T(8,128)(2,1)S(1)}, u32[]{:S(2)}, u32[]{:S(2)}) collective-permute-start(bf16[4,128,256]{2,1,0:T(8,128)(2,1)S(1)} %get-tuple-element.42), channel_id=1, source_target_pairs={{0,32},{8,40},{16,48},{24,56},{32,64},{40,72},{48,80},{56,88},{64,... | collective-permute-start | bytes 786440 | tf_op jit(solution)/shard_map/ppermute | solution.py:337
  42.9 1.3 collective-permute-start.3
  44.2 6.4 %all-to-all-start.2 = ((bf16[4,128,256]{2,1,0:T(8,128)(2,1)}), bf16[4,128,256]{2,1,0:T(8,128)(2,1)S(1)}, u32[]{:S(2)}, u32[]{:S(2)}) async-start(bf16[4,128,256]{2,1,0:T(8,128)(2,1)} %get-tuple-element.40), calls=%async_computation.2 | async-start | bytes 524288 | tf_op jit(solution)/shard_map/all_to_all | solution.py:345
  50.6 0.6 collective-permute-done.3.from_after
  51.2 3.0 %all-to-all-done.2.context_dq = bf16[4,128,256]{2,1,0:T(8,128)(2,1)S(1)} async-done(((bf16[4,128,256]{2,1,0:T(8,128)(2,1)}), bf16[4,128,256]{2,1,0:T(8,128)(2,1)S(1)}, u32[]{:S(2)}, u32[]{:S(2)}) %all-to-all-start.2) | async-done | bytes 262176 | tf_op jit(solution)/shard_map/all_to_all | solution.py:345
  54.3 9.3 %all_to_all.41.d_kv = bf16[4,128,256]{2,1,0:T(8,128)(2,1)S(1)} all-to-all(bf16[4,128,256]{2,1,0:T(8,128)(2,1)S(1)} %shard_map.137), channel_id=1, replica_groups={{0,8,16,24},{32,40,48,56},{64,72,80,88},{96,104,112,120},{128,136,144,1..., dimensions={0} | all-to-all | bytes 524288 | tf_op jit(solution)/shard_map/all_to_all | solution.py:345
  63.8 0.8 copy-done.11
  64.5 0.5 collective-permute-start.9
  65.0 0.5 collective-permute-start.7
  65.5 1.1 collective-permute-done.9.cot_far
  66.6 0.4 collective-permute-done.6.normed_far
  67.2 2.8 %shard_map.142 = bf16[32,64,512]{2,1,0:T(8,128)(2,1)} custom-call(s32[4]{0:T(128)S(1)} %pad_add_fusion.place, bf16[128,1024]{1,0:T(8,128)(2,1)S(1)} %get-tuple-element.45.normed, bf16[128,1024]{1,0:T(8,128)(2,1)S(1)} %collective-permute-done.6.normed_far, bf16[128,512]{1,0:T(8,128)(2,1)S(1)} %get-tuple-element.44.context, ...), custom_call_target="tpu_custom_call" | custom-call | tf_op jit(solution)/shard_map/pallas_call | solution.py:33
  70.0 11.1 %all-to-all-start.4 = ((bf16[32,64,512]{2,1,0:T(8,128)(2,1)}), bf16[32,64,512]{2,1,0:T(8,128)(2,1)S(1)}, u32[]{:S(2)}, u32[]{:S(2)}) async-start(bf16[32,64,512]{2,1,0:T(8,128)(2,1)} %shard_map.142), calls=%async_computation.4 | async-start | bytes 4194304 | tf_op jit(solution)/shard_map/all_to_all | solution.py:405
  81.1 4.7 %shard_map.139 = (bf16[128,1024]{1,0:T(8,128)(2,1)S(1)}, bf16[128,1024]{1,0:T(8,128)(2,1)S(1)}, bf16[128,1024]{1,0:T(8,128)(2,1)S(1)}, bf16[128,1024]{1,0:T(8,12...) custom-call(s32[4]{0:T(128)S(1)} %pad_add_fusion.place, ...), custom_call_target="tpu_custom_call" | custom-call | tf_op jit(solution)/shard_map/pallas_call | solution.py:33
  85.7 1.0 copy-done.4
  86.7 3.1 %collective-permute-start.4 = (bf16[16,2048]{1,0:T(8,128)(2,1)S(1)}, bf16[16,2048]{1,0:T(8,128)(2,1)S(1)}, u32[]{:S(2)}, u32[]{:S(2)}) collective-permute-start(bf16[16,2048]{1,0:T(8,128)(2,1)S(1)} %get-tuple-element.53), channel_id=1, source_target_pairs={{0,8},{8,16},{16,24},{24,32},{32,40},{40,48},{48,56},{56,64},{64,7... | collective-permute-start | bytes 196616 | tf_op jit(solution)/shard_map/ppermute | solution.py:337
  89.8 2.8 %collective-permute-start.5 = (bf16[16,2048]{1,0:T(8,128)(2,1)S(1)}, bf16[16,2048]{1,0:T(8,128)(2,1)S(1)}, u32[]{:S(2)}, u32[]{:S(2)}) collective-permute-start(bf16[16,2048]{1,0:T(8,128)(2,1)S(1)} %get-tuple-element.54), channel_id=1, source_target_pairs={{8,0},{16,8},{24,16},{32,24},{40,32},{48,40},{56,48},{64,56},{72,6... | collective-permute-start | bytes 196616 | tf_op jit(solution)/shard_map/ppermute | solution.py:337
  92.6 13.4 %collective-permute-done.4.before = bf16[16,2048]{1,0:T(8,128)(2,1)S(1)} collective-permute-done((bf16[16,2048]{1,0:T(8,128)(2,1)S(1)}, bf16[16,2048]{1,0:T(8,128)(2,1)S(1)}, u32[]{:S(2)}, u32[]{:S(2)}) %collective-permute-start.4) | collective-permute-done | bytes 65568 | tf_op jit(solution)/shard_map/ppermute | solution.py:337
  106.0 1.1 collective-permute-done.5.after
  107.1 9.6 %shard_map.140 = (bf16[128,1024]{1,0:T(8,128)(2,1)S(1)}, bf16[128,2048]{1,0:T(8,128)(2,1)S(1)}, bf16[2048,128]{1,0:T(8,128)(2,1)S(1)}, f32[32,1024]{1,0:T(8,128)S(1)}) custom-call(s32[4]{0:T(128)S(1)} %pad_add_fusion.place, bf16[128,1024]{1,0:T(8,128)(2,1)S(1)} %get-tuple-element.46.resid, bf16[128,1024]{1,0:T(8,128)(2,1)S(1)} %get-tuple-element.47.d_gated, ...), custom_call_target="tpu_custom_call" | custom-call | tf_op jit(solution)/shard_map/pallas_call | solution.py:33
  116.7 0.8 copy-done.9
  117.5 0.5 collective-permute-start.10
  118.0 2.0 collective-permute-done.12.taps_far
  120.0 3.4 %shard_map.145 = bf16[32,112,512]{2,1,0:T(8,128)(2,1)} custom-call(s32[4]{0:T(128)S(1)} %pad_add_fusion.place, bf16[128,1024]{1,0:T(8,128)(2,1)S(1)} %get-tuple-element.45.normed, bf16[128,1024]{1,0:T(8,128)(2,1)S(1)} %collective-permute-done.6.normed_far, bf16[128,1024]{1,0:T(8,128)(2,1)S(1)} %get-tuple-element.55.gated, ...), custom_call_target="tpu_custom_call" | custom-call | tf_op jit(solution)/shard_map/pallas_call | solution.py:33
  123.3 0.7 copy-done.7
  124.0 8.3 %all-to-all-start.6 = ((bf16[32,112,512]{2,1,0:T(8,128)(2,1)}), bf16[32,112,512]{2,1,0:T(8,128)(2,1)}, u32[]{:S(2)}, u32[]{:S(2)}) async-start(bf16[32,112,512]{2,1,0:T(8,128)(2,1)} %shard_map.145), calls=%async_computation.6 | async-start | bytes 7340032 | tf_op jit(solution)/shard_map/all_to_all | solution.py:384
  132.6 0.6 copy-done.13
  133.2 48.9 %all-to-all-done.6.parts = bf16[32,112,512]{2,1,0:T(8,128)(2,1)} async-done(((bf16[32,112,512]{2,1,0:T(8,128)(2,1)}), bf16[32,112,512]{2,1,0:T(8,128)(2,1)}, u32[]{:S(2)}, u32[]{:S(2)}) %all-to-all-start.6) | async-done | bytes 3670048 | tf_op jit(solution)/shard_map/all_to_all | solution.py:384
  182.1 8.5 %all-to-all-start.5 = ((bf16[4,64,128]{2,1,0:T(8,128)(2,1)}), bf16[4,64,128]{2,1,0:T(8,128)(2,1)S(1)}, u32[]{:S(2)}, u32[]{:S(2)}) async-start(bf16[4,64,128]{2,1,0:T(8,128)(2,1)} %copy-done.13), calls=%async_computation.5 | async-start | bytes 131072 | tf_op jit(solution)/shard_map/all_to_all | solution.py:415
  190.6 3.2 %shard_map.146 = bf16[4,112,128]{2,1,0:T(8,128)(2,1)} custom-call(bf16[32,112,512]{2,1,0:T(8,128)(2,1)} %all-to-all-done.6.parts), custom_call_target="tpu_custom_call" | custom-call | tf_op jit(solution)/shard_map/pallas_call | solution.py:33
  193.7 5.0 %all-to-all-done.5.parts = bf16[4,64,128]{2,1,0:T(8,128)(2,1)S(1)} async-done(((bf16[4,64,128]{2,1,0:T(8,128)(2,1)}), bf16[4,64,128]{2,1,0:T(8,128)(2,1)S(1)}, u32[]{:S(2)}, u32[]{:S(2)}) %all-to-all-start.5) | async-done | bytes 65568 | tf_op jit(solution)/shard_map/all_to_all | solution.py:415
  198.8 3.3 %all-to-all-start.7 = ((bf16[4,112,128]{2,1,0:T(8,128)(2,1)}), bf16[4,112,128]{2,1,0:T(8,128)(2,1)S(1)}, u32[]{:S(2)}, u32[]{:S(2)}) async-start(bf16[4,112,128]{2,1,0:T(8,128)(2,1)} %shard_map.146), calls=%async_computation.7 | async-start | bytes 229376 | tf_op jit(solution)/shard_map/all_to_all | solution.py:410
  202.1 7.6 %shard_map.141 = (bf16[128,1024]{1,0:T(8,128)(2,1)}, bf16[128,1024]{1,0:T(8,128)(2,1)}) custom-call(bf16[128,1024]{1,0:T(8,128)(2,1)S(1)} %bitcast.11, bf16[128,1024]{1,0:T(8,128)(2,1)S(1)} %bitcast.9, bf16[128,512]{1,0:T(8,128)(2,1)S(1)} %get-tuple-element.44.context, bf16[128,1024]{1,0:T(8,128)(2,1)S(1)} %copy-done.8, bf16[128,2048]{1,0:T(8,128)(2,1)S(1)} %copy-done.10, ...), custom_call_target="tpu_custom_call" | custom-call | tf_op jit(solution)/shard_map/pallas_call | solution.py:33
  209.9 0.7 copy.15
  210.6 0.7 copy.16
  211.3 0.8 shard_map.147
  212.0 0.7 copy.17
  212.7 0.7 copy.18
  (40 shorter events, 1.1 us)
Async XLA Ops:
  0.6 1.2 copy-start
  1.9 0.9 copy-start.2
  2.8 0.9 copy-start.5
  16.0 15.7 %collective-permute-start.1 = (bf16[4,128,256]{2,1,0:T(8,128)(2,1)S(1)}, bf16[4,128,256]{2,1,0:T(8,128)(2,1)S(1)}, u32[]{:S(2)}, u32[]{:S(2)}) collective-permute-start(bf16[4,128,256]{2,1,0:T(8,128)(2,1)S(1)} %all_to_all.40.kv), channel_id=1, source_target_pairs={{32,0},{40,8},{48,16},{56,24},{64,32},{72,40},{80,48},{88,56},{96,... | collective-permute-start | bytes 786440 | tf_op jit(solution)/shard_map/ppermute | solution.py:337
  17.3 14.4 %collective-permute-start = (bf16[4,128,256]{2,1,0:T(8,128)(2,1)S(1)}, bf16[4,128,256]{2,1,0:T(8,128)(2,1)S(1)}, u32[]{:S(2)}, u32[]{:S(2)}) collective-permute-start(bf16[4,128,256]{2,1,0:T(8,128)(2,1)S(1)} %all_to_all.40.kv), channel_id=1, source_target_pairs={{0,32},{8,40},{16,48},{24,56},{32,64},{40,72},{48,80},{56,88},{64,... | collective-permute-start | bytes 786440 | tf_op jit(solution)/shard_map/ppermute | solution.py:337
  21.9 9.8 %all-to-all-start = ((bf16[4,128,256]{2,1,0:T(8,128)(2,1)}), bf16[4,128,256]{2,1,0:T(8,128)(2,1)S(1)}, u32[]{:S(2)}, u32[]{:S(2)}) async-start(bf16[4,128,256]{2,1,0:T(8,128)(2,1)} %get-tuple-element.38), calls=%async_computation | async-start | bytes 524288 | tf_op jit(solution)/shard_map/all_to_all | solution.py:345
  39.4 11.1 %collective-permute-start.2 = (bf16[4,128,256]{2,1,0:T(8,128)(2,1)S(1)}, bf16[4,128,256]{2,1,0:T(8,128)(2,1)S(1)}, u32[]{:S(2)}, u32[]{:S(2)}) collective-permute-start(bf16[4,128,256]{2,1,0:T(8,128)(2,1)S(1)} %get-tuple-element.42), channel_id=1, source_target_pairs={{0,32},{8,40},{16,48},{24,56},{32,64},{40,72},{48,80},{56,88},{64,... | collective-permute-start | bytes 786440 | tf_op jit(solution)/shard_map/ppermute | solution.py:337
  42.9 8.3 %collective-permute-start.3 = (bf16[4,128,256]{2,1,0:T(8,128)(2,1)S(1)}, bf16[4,128,256]{2,1,0:T(8,128)(2,1)S(1)}, u32[]{:S(2)}, u32[]{:S(2)}) collective-permute-start(bf16[4,128,256]{2,1,0:T(8,128)(2,1)S(1)} %get-tuple-element.43), channel_id=1, source_target_pairs={{32,0},{40,8},{48,16},{56,24},{64,32},{72,40},{80,48},{88,56},{96,... | collective-permute-start | bytes 786440 | tf_op jit(solution)/shard_map/ppermute | solution.py:337
  44.2 10.1 %all-to-all-start.2 = ((bf16[4,128,256]{2,1,0:T(8,128)(2,1)}), bf16[4,128,256]{2,1,0:T(8,128)(2,1)S(1)}, u32[]{:S(2)}, u32[]{:S(2)}) async-start(bf16[4,128,256]{2,1,0:T(8,128)(2,1)} %get-tuple-element.40), calls=%async_computation.2 | async-start | bytes 524288 | tf_op jit(solution)/shard_map/all_to_all | solution.py:345
  63.8 0.8 copy-start.11
  64.5 2.7 %collective-permute-start.8 = (bf16[1536,128]{1,0:T(8,128)(2,1)S(1)}, bf16[1536,128]{1,0:T(8,128)(2,1)S(1)}, u32[]{:S(2)}, u32[]{:S(2)}) collective-permute-start(bf16[1536,128]{1,0:T(8,128)(2,1)S(1)} %get-tuple-element.60.joined_t), channel_id=1, source_target_pairs={{0,1},{1,0},{2,3},{3,2},{4,5},{5,4},{6,7},{7,6},{8,9},{9,8},{10,11... | collective-permute-start | bytes 1179656 | tf_op jit(solution)/shard_map/ppermute | solution.py:341
  64.5 2.1 collective-permute-start.9
  65.0 2.0 collective-permute-start.6
  65.0 2.1 %collective-permute-start.7 = (bf16[128,512]{1,0:T(8,128)(2,1)S(1)}, bf16[128,512]{1,0:T(8,128)(2,1)S(1)}, u32[]{:S(2)}, u32[]{:S(2)}) collective-permute-start(bf16[128,512]{1,0:T(8,128)(2,1)S(1)} %get-tuple-element.44.context), channel_id=1, source_target_pairs={{0,1},{1,0},{2,3},{3,2},{4,5},{5,4},{6,7},{7,6},{8,9},{9,8},{10,11... | collective-permute-start | bytes 393224 | tf_op jit(solution)/shard_map/ppermute | solution.py:341
  70.0 11.1 %copy-start.3 = (bf16[1,128,1024]{2,1,0:T(8,128)(2,1)S(1)}, bf16[1,128,1024]{2,1,0:T(8,128)(2,1)}, u32[]{:S(2)}) copy-start(bf16[1,128,1024]{2,1,0:T(8,128)(2,1)} %param.9) | copy-start | bytes 786436
  70.0 54.1 %all-to-all-start.4 = ((bf16[32,64,512]{2,1,0:T(8,128)(2,1)}), bf16[32,64,512]{2,1,0:T(8,128)(2,1)S(1)}, u32[]{:S(2)}, u32[]{:S(2)}) async-start(bf16[32,64,512]{2,1,0:T(8,128)(2,1)} %shard_map.142), calls=%async_computation.4 | async-start | bytes 4194304 | tf_op jit(solution)/shard_map/all_to_all | solution.py:405
  81.1 26.0 %copy-start.14 = (f32[31,1024]{1,0:T(8,128)S(1)}, f32[31,1024]{1,0:T(8,128)}, u32[]{:S(2)}) copy-start(f32[31,1024]{1,0:T(8,128)} %taps.1) | copy-start | bytes 380932
  85.7 1.0 copy-start.4
  86.7 19.3 %collective-permute-start.4 = (bf16[16,2048]{1,0:T(8,128)(2,1)S(1)}, bf16[16,2048]{1,0:T(8,128)(2,1)S(1)}, u32[]{:S(2)}, u32[]{:S(2)}) collective-permute-start(bf16[16,2048]{1,0:T(8,128)(2,1)S(1)} %get-tuple-element.53), channel_id=1, source_target_pairs={{0,8},{8,16},{16,24},{24,32},{32,40},{40,48},{48,56},{56,64},{64,7... | collective-permute-start | bytes 196616 | tf_op jit(solution)/shard_map/ppermute | solution.py:337
  89.8 17.3 %collective-permute-start.5 = (bf16[16,2048]{1,0:T(8,128)(2,1)S(1)}, bf16[16,2048]{1,0:T(8,128)(2,1)S(1)}, u32[]{:S(2)}, u32[]{:S(2)}) collective-permute-start(bf16[16,2048]{1,0:T(8,128)(2,1)S(1)} %get-tuple-element.54), channel_id=1, source_target_pairs={{8,0},{16,8},{24,16},{32,24},{40,32},{48,40},{56,48},{64,56},{72,6... | collective-permute-start | bytes 196616 | tf_op jit(solution)/shard_map/ppermute | solution.py:337
  116.6 0.8 copy-start.9
  117.5 2.5 %collective-permute-start.11 = (bf16[2048,128]{1,0:T(8,128)(2,1)S(1)}, bf16[2048,128]{1,0:T(8,128)(2,1)S(1)}, u32[]{:S(2)}, u32[]{:S(2)}) collective-permute-start(bf16[2048,128]{1,0:T(8,128)(2,1)S(1)} %get-tuple-element.64.d_upper_t), channel_id=1, source_target_pairs={{0,1},{1,0},{2,3},{3,2},{4,5},{5,4},{6,7},{7,6},{8,9},{9,8},{10,11... | collective-permute-start | bytes 1572872 | tf_op jit(solution)/shard_map/ppermute | solution.py:341
  117.5 2.5 %collective-permute-start.10 = (bf16[128,1024]{1,0:T(8,128)(2,1)S(1)}, bf16[128,1024]{1,0:T(8,128)(2,1)S(1)}, u32[]{:S(2)}, u32[]{:S(2)}) collective-permute-start(bf16[128,1024]{1,0:T(8,128)(2,1)S(1)} %get-tuple-element.55.gated), channel_id=1, source_target_pairs={{0,1},{1,0},{2,3},{3,2},{4,5},{5,4},{6,7},{7,6},{8,9},{9,8},{10,11... | collective-permute-start | bytes 786440 | tf_op jit(solution)/shard_map/ppermute | solution.py:341
  118.0 2.0 collective-permute-start.12
  123.3 0.7 copy-start.7
  124.0 58.1 %all-to-all-start.6 = ((bf16[32,112,512]{2,1,0:T(8,128)(2,1)}), bf16[32,112,512]{2,1,0:T(8,128)(2,1)}, u32[]{:S(2)}, u32[]{:S(2)}) async-start(bf16[32,112,512]{2,1,0:T(8,128)(2,1)} %shard_map.145), calls=%async_computation.6 | async-start | bytes 7340032 | tf_op jit(solution)/shard_map/all_to_all | solution.py:384
  132.3 69.8 %copy-start.1 = (bf16[512,1024]{1,0:T(8,128)(2,1)S(1)}, bf16[512,1024]{1,0:T(8,128)(2,1)}, u32[]{:S(2)}) copy-start(bf16[512,1024]{1,0:T(8,128)(2,1)} %w_out.3) | copy-start | bytes 3145732
  132.6 0.6 copy-start.13
  133.2 68.9 %copy-start.6 = (bf16[1,128,1024]{2,1,0:T(8,128)(2,1)S(1)}, bf16[1,128,1024]{2,1,0:T(8,128)(2,1)}, u32[]{:S(2)}) copy-start(bf16[1,128,1024]{2,1,0:T(8,128)(2,1)} %param.8) | copy-start | bytes 786436
  133.2 68.9 %copy-start.8 = (bf16[128,1024]{1,0:T(8,128)(2,1)S(1)}, bf16[128,1024]{1,0:T(8,128)(2,1)}, u32[]{:S(2)}) copy-start(bf16[128,1024]{1,0:T(8,128)(2,1)} %copy-done.7) | copy-start | bytes 786436
  133.2 68.9 %copy-start.10 = (bf16[128,2048]{1,0:T(8,128)(2,1)S(1)}, bf16[128,2048]{1,0:T(8,128)(2,1)}, u32[]{:S(2)}) copy-start(bf16[128,2048]{1,0:T(8,128)(2,1)} %copy-done.9) | copy-start | bytes 1572868
  133.2 68.9 %copy-start.12 = (bf16[128,1536]{1,0:T(8,128)(2,1)S(1)}, bf16[128,1536]{1,0:T(8,128)(2,1)}, u32[]{:S(2)}) copy-start(bf16[128,1536]{1,0:T(8,128)(2,1)} %copy-done.11) | copy-start | bytes 1179652
  182.1 16.7 %all-to-all-start.5 = ((bf16[4,64,128]{2,1,0:T(8,128)(2,1)}), bf16[4,64,128]{2,1,0:T(8,128)(2,1)S(1)}, u32[]{:S(2)}, u32[]{:S(2)}) async-start(bf16[4,64,128]{2,1,0:T(8,128)(2,1)} %copy-done.13), calls=%async_computation.5 | async-start | bytes 131072 | tf_op jit(solution)/shard_map/all_to_all | solution.py:415
  198.8 12.5 %all-to-all-start.7 = ((bf16[4,112,128]{2,1,0:T(8,128)(2,1)}), bf16[4,112,128]{2,1,0:T(8,128)(2,1)S(1)}, u32[]{:S(2)}, u32[]{:S(2)}) async-start(bf16[4,112,128]{2,1,0:T(8,128)(2,1)} %shard_map.146), calls=%async_computation.7 | async-start | bytes 229376 | tf_op jit(solution)/shard_map/all_to_all | solution.py:410

commit v2 on v1

v2 whole, which is shorter than its diff:
```python
import jax
import jax.numpy as jnp
from jax import lax
from jax.experimental import pallas as pl
from jax.experimental.pallas import tpu as pltpu
from jax.sharding import PartitionSpec as P

HEAD = 64
BAND = 512
ROWS = 128
GROUP = 4
WINDOW = 2 * BAND + ROWS
MARGIN = 15
TAPS = 31

EPSILON = 1e-05
NEG_LARGE = -1e30
HALF_ROOT = 0.7071067811865476
NORMAL_PEAK = 0.3989422804014327

BF16 = jnp.bfloat16
F32 = jnp.float32
HBM = pltpu.HBM
VMEM_LIMIT = 24 * 2**20

ROW_GROUPS = [[4 * m + x for m in range(8)] for x in range(4)]


def call(body, outs, scratch=(), scalars=0):
    def run(*args):
        specs = [pl.BlockSpec(memory_space=pltpu.SMEM)] * scalars
        specs += [pl.BlockSpec(memory_space=pltpu.VMEM)] * (len(args) - scalars)
        return pl.pallas_call(
            body,
            out_shape=[
                HBM(*out[:2]) if len(out) > 2 else jax.ShapeDtypeStruct(*out) for out in outs
            ],
            in_specs=specs,
            out_specs=[pl.BlockSpec(memory_space=pltpu.VMEM)] * len(outs),
            scratch_shapes=list(scratch),
            compiler_params=pltpu.CompilerParams(vmem_limit_bytes=VMEM_LIMIT),
        )(*args)

    return run


def dot(left, right, left_dim=1, right_dim=0):
    return lax.dot_general(
        left, right, (((left_dim,), (right_dim,)), ((), ())), preferred_element_type=F32
    )


def normalize(values):
    centred = values - jnp.mean(values, axis=-1, keepdims=True)
    inverse = lax.rsqrt(jnp.mean(centred * centred, axis=-1, keepdims=True) + EPSILON)
    return (centred * inverse, inverse)


def norm_back(gradient, unit_rows, inverse):
    return inverse * (
        gradient
        - jnp.mean(gradient, axis=-1, keepdims=True)
        - unit_rows * jnp.mean(gradient * unit_rows, axis=-1, keepdims=True)
    )


def slot(place, turn):
    return (place[4] + 4 - turn) & 3


def span(index, size):
    return pl.ds(pl.multiple_of(index * size, size), size)


def project_kernel(place, frames_0, frames_1, frames_2, frames_3, w_qkv, normed, query, kv):
    x = place[4]
    for turn, ref in enumerate((frames_0, frames_1, frames_2, frames_3)):
        unit_rows, _ = normalize(ref[...].astype(F32))
        normed[span(slot(place, turn), ROWS), :] = unit_rows.astype(BF16)
    weight = jnp.concatenate([w_qkv[:, span(x + 4 * part, 128)] for part in range(3)], axis=1)
    joined = dot(normed[...], weight).astype(BF16)
    query[...] = joined[:, :128].reshape(4, ROWS, 128)
    kv[...] = joined[:, 128:].reshape(4, ROWS, 256)


def gate_kernel(
    place, frames, cotangent, w_up, w_down,
    resid, d_gated, gating, d_conv, unit, inverse, slope, top, bottom
):
    first_frame, length = place[0], place[1]
    unit_rows, _ = normalize(frames[...].astype(F32))
    upper = dot(unit_rows.astype(BF16), w_up[...])
    phi = 0.5 * (1.0 + lax.erf(upper * HALF_ROOT))
    slope[...] = phi + upper * jnp.exp(-0.5 * upper * upper) * NORMAL_PEAK
    hidden = (upper * phi).astype(BF16)
    gate_unit, gate_inv = normalize(hidden[:, 1024:].astype(F32))
    unit[...] = gate_unit
    inverse[...] = jnp.broadcast_to(gate_inv, inverse.shape)
    rows = first_frame + lax.broadcasted_iota(jnp.int32, (ROWS, 1024), 0)
    masked = jnp.where(rows < length, gate_unit, 0.0).astype(BF16)
    gating[...] = masked
    resid[...] = hidden[:, :1024]
    back = dot(cotangent[...], w_down[...], 1, 1).astype(BF16)
    d_gated[...] = back
    conv_back = (back.astype(F32) * hidden[:, :1024].astype(F32)).astype(BF16)
    d_conv[...] = conv_back
    top[:, :1024] = masked[:16]
    top[:, 1024:] = conv_back[:16]
    bottom[:, :1024] = masked[112:]
    bottom[:, 1024:] = conv_back[112:]


def conv_inner_kernel(gating, d_conv, taps, conv_out, d_gating, g_taps, gate_ext, conv_ext):
    for ext, ref in ((gate_ext, gating), (conv_ext, d_conv)):
        ext[:16] = jnp.zeros((16, 1024), F32)
        ext[16:144] = ref[...].astype(F32)
        ext[144:] = jnp.zeros((16, 1024), F32)
    g_taps[...] = jnp.zeros_like(g_taps)

    def chunk(index, _):
        lanes = pl.ds(pl.multiple_of(index * 128, 128), 128)
        own = conv_ext[16:144, lanes]
        forward = jnp.zeros((ROWS, 128), F32)
        for shift in range(8):
            moved = gate_ext[pl.ds(shift, 152), lanes]
            for step in range(4):
                offset = 8 * step + shift
                if 1 <= offset <= TAPS:
                    part = moved[8 * step : 8 * step + ROWS]
                    forward = forward + taps[offset - 1 : offset, lanes] * part
                    g_taps[offset - 1 : offset, lanes] = jnp.sum(part * own, axis=0, keepdims=True)
        conv_out[:, lanes] = forward
        backward = jnp.zeros((ROWS, 128), F32)
        for shift in range(8):
            moved = conv_ext[pl.ds(shift, 152), lanes]
            for step in range(4):
                offset = 8 * step + shift
                if 1 <= offset <= TAPS:
                    part = moved[8 * step : 8 * step + ROWS]
                    backward = backward + taps[TAPS - offset : TAPS - offset + 1, lanes] * part
        d_gating[:, lanes] = backward
        return 0

    lax.fori_loop(0, 8, chunk, 0)


def conv_outer_kernel(
    place, conv_in, d_gating_in, g_taps_in, d_conv, resid, d_gated, unit, inverse, slope, before, after, taps,
    d_upper, out_0, out_1, out_2, out_3, conv_out, d_gating, before_ext, after_ext, g_taps, d_upper_t, g_taps_t
):
    first_frame, length = place[0], place[1]
    conv_out[...] = conv_in[...]
    d_gating[...] = d_gating_in[...]
    g_taps[...] = g_taps_in[...]
    before_ext[:16] = before[...].astype(F32)
    before_ext[16:] = jnp.zeros((16, 2048), F32)
    after_ext[:16] = jnp.zeros((16, 2048), F32)
    after_ext[16:] = after[...].astype(F32)

    def chunk(index, _):
        lanes = pl.ds(pl.multiple_of(index * 128, 128), 128)
        far = pl.ds(pl.multiple_of(index * 128 + 1024, 128), 128)
        for ext, first, skip in ((before_ext, 0, 0), (after_ext, 112, 16)):
            own = d_conv[first : first + 16, lanes].astype(F32)
            forward = conv_out[first : first + 16, lanes]
            backward = d_gating[first : first + 16, lanes]
            for step in range(1, 16):
                offset = step + skip
                part = ext[pl.ds(step, 16), lanes]
                forward = forward + taps[offset - 1 : offset, lanes] * part
                g_taps[offset - 1 : offset, lanes] += jnp.sum(part * own, axis=0, keepdims=True)
                part = ext[pl.ds(step, 16), far]
                backward = backward + taps[TAPS - offset : TAPS - offset + 1, lanes] * part
            conv_out[first : first + 16, lanes] = forward
            d_gating[first : first + 16, lanes] = backward
        return 0

    lax.fori_loop(0, 8, chunk, 0)
    conv = conv_out[...]
    gated = (resid[...].astype(F32) * conv).astype(BF16)
    rows = first_frame + lax.broadcasted_iota(jnp.int32, (ROWS, 1024), 0)
    d_gate = jnp.where(rows < length, d_gating[...], 0.0)
    d_gate = norm_back(d_gate, unit[...], inverse[:, :1])
    left = (d_gated[...].astype(F32) * conv * slope[:, :1024]).astype(BF16)
    right = (d_gate * slope[:, 1024:]).astype(BF16)
    d_upper[:, :1024] = left
    d_upper[:, 1024:] = right
    d_upper_t[:1024] = left.T
    d_upper_t[1024:] = right.T
    turned = jnp.concatenate([g_taps[...], jnp.zeros((96, 1024), F32)], axis=0).T.reshape(32, 32, 128)
    g_taps_t[...] = (turned[:, :16, :] + pltpu.roll(turned[:, 16:, :], 32, 2)).astype(BF16)
    for turn, ref in enumerate((out_0, out_1, out_2, out_3)):
        x = (place[4] + turn) & 3
        for m in range(8):
            ref[64 * m : 64 * m + 64] = d_upper_t[span(4 * m + x, 64), :]
            ref[512 + 16 * m : 528 + 16 * m] = g_taps_t[4 * m + x]
            ref[640 + 128 * m : 768 + 128 * m] = gated[:, 128 * m : 128 * m + 128]


def own_columns(array, core, width):
    parts = [
        array[:, pl.ds(pl.multiple_of(2 * width * z + width * core, width), width)] for z in range(4)
    ]
    return jnp.concatenate(parts, axis=1)


def gate_grads_kernel(
    place, normed, cot_0, cot_1, cot_2, cot_3, gate_0, gate_1, gate_2, gate_3,
    keep, send, cot_own, d_upper_t, gated, cot_t
):
    x, core = place[4], place[2]
    gates = (gate_0, gate_1, gate_2, gate_3)
    g_taps = gate_0[512:640].astype(F32)
    for ref in gates[1:]:
        g_taps = g_taps + ref[512:640].astype(F32)
    g_taps = g_taps.astype(BF16).reshape(8, 16, 128)
    for turn, (gate, cot) in enumerate(zip(gates, (cot_0, cot_1, cot_2, cot_3))):
        here = span(slot(place, turn), 128)
        d_upper_t[:, here] = gate[:512]
        for block in range(8):
            gated[here, 128 * block : 128 * block + 128] = gate[640 + 128 * block : 768 + 128 * block]
        cot_t[:, here] = cot[...].T
    for m in range(8):
        cot_own[32 * m : 32 * m + 32] = cot_t[span(4 * m + x, 32), :]
    for parity, out in ((core, keep), (1 - core, send)):
        grad = dot(d_upper_t[...], own_columns(normed, parity, 128))
        out[:, :64, :] = grad.astype(BF16).reshape(8, 64, 512)
        grad = dot(cot_own[...], own_columns(gated, parity, 128))
        out[:, 64:96, :] = grad.astype(BF16).reshape(8, 32, 512)
        for z in range(4):
            out[:, 96:, 128 * z : 128 * z + 128] = g_taps


def attention_grads_kernel(
    place, normed, cot_own, near_0, near_1, near_2, near_3, far_0, far_1, far_2, far_3,
    keep, send, context_own, joined_own, joined_t, context, rows_t
):
    x, core = place[4], place[2]
    nears, fars = (near_0, near_1, near_2, near_3), (far_0, far_1, far_2, far_3)
    for turn, (near, far) in enumerate(zip(nears, fars)):
        pair = slot(place, turn)
        for block in range(GROUP):
            tokens = slice(128 * block, 128 * block + 128)
            context[tokens, span(pair, 128)] = near[block, :, :128]
            joined_t[span(pair, 128), tokens] = near[block, :, 128:]
            joined_t[span(pair + 4, 128), tokens] = far[block, :, :128]
            joined_t[span(pair + 8, 128), tokens] = far[block, :, 128:]
    for m in range(8):
        rows_t[48 * m : 48 * m + 48] = joined_t[span(4 * m + x, 48), :]
    context_own[...] = context[span(x, ROWS), :]
    joined_own[...] = joined_t[:, span(x, ROWS)]
    lane = lax.broadcasted_iota(jnp.int32, (512, 128), 1)
    blocks, swapped = [], []
    for z in range(4):
        block = context[:, 128 * z : 128 * z + 128].astype(F32)
        blocks.append(block)
        swapped.append(pltpu.roll(block, HEAD, 1))
    lane_out = lax.broadcasted_iota(jnp.int32, (8, 16, 512), 2)
    for parity, out in ((core, keep), (1 - core, send)):
        grad = dot(rows_t[...], own_columns(normed, parity, 128))
        out[:, :48, :] = grad.astype(BF16).reshape(8, 48, 512)
        mine = (lane < HEAD) == (parity == 0)
        doubled = jnp.concatenate(
            [jnp.where(mine, block, other) for block, other in zip(blocks, swapped)], axis=1
        ).astype(BF16)
        grad = dot(cot_own[...], doubled).reshape(8, 32, 512)
        out[:, 48:, :] = jnp.where((lane_out & 127) < HEAD, grad[:, :16], grad[:, 16:]).astype(BF16)


def attend_kernel(
    place, queries, kv, before, after, cot_0, cot_1, cot_2, cot_3, w_out, context_dq, d_before, d_after, d_own,
    d_contexts, key, value, key_t, value_t, scores, weights, d_scores, d_key, d_value
):
    group_first, length = place[3], place[1]
    w_pair = w_out[span(place[4], 128), :]
    for turn, ref in enumerate((cot_0, cot_1, cot_2, cot_3)):
        d_contexts[slot(place, turn)] = dot(ref[...], w_pair, 1, 1).astype(BF16)
    for part, ref in enumerate((before, kv, after)):
        for piece in range(GROUP):
            start = 512 * part + ROWS * piece
            key_block = ref[piece, :, :128]
            value_block = ref[piece, :, 128:]
            key[start : start + ROWS] = key_block
            value[start : start + ROWS] = value_block
            key_t[:, start : start + ROWS] = key_block.T
            value_t[:, start : start + ROWS] = value_block.T
    d_key[...] = jnp.zeros_like(d_key)
    d_value[...] = jnp.zeros_like(d_value)
    lane = lax.broadcasted_iota(jnp.int32, (ROWS, 128), 1)
    first_head = lane < HEAD
    query_index = lax.broadcasted_iota(jnp.int32, (1, 256), 1)
    query_index = jnp.where(query_index < ROWS, query_index, query_index - ROWS)
    chunks = WINDOW // 128
    for block in range(GROUP):
        base = ROWS * block
        low = jnp.maximum(query_index, 512 - group_first - base)
        high = jnp.minimum(query_index + 1024, length - group_first + 511 - base)
        query = queries[block].astype(F32) * 0.125
        d_context = d_contexts[block].astype(F32)
        zero = jnp.zeros_like(query)
        query_pair = jnp.concatenate(
            [jnp.where(first_head, query, zero), jnp.where(first_head, zero, query)], axis=0
        ).astype(BF16)
        d_pair = jnp.concatenate(
            [jnp.where(first_head, d_context, zero), jnp.where(first_head, zero, d_context)], axis=0
        ).astype(BF16)

        def allowed_of(index):
            position = 128 * index + lax.broadcasted_iota(jnp.int32, (128, 256), 0)
            return (position >= low) & (position <= high)

        peak = jnp.full((128, 256), NEG_LARGE, F32)
        for index in range(chunks):
            part = dot(key[base + 128 * index : base + 128 * index + 128], query_pair, 1, 1)
            part = jnp.where(allowed_of(index), part, NEG_LARGE)
            scores[128 * index : 128 * index + 128] = part
            peak = jnp.maximum(peak, part)
        peak = jnp.max(peak, axis=0, keepdims=True)
        total = jnp.zeros((128, 256), F32)
        for index in range(chunks):
            part = scores[128 * index : 128 * index + 128]
            part = jnp.where(allowed_of(index), jnp.exp(part - peak), 0.0)
            scores[128 * index : 128 * index + 128] = part
            total = total + part
        scale = 1.0 / jnp.maximum(jnp.sum(total, axis=0, keepdims=True), 1.0)
        for index in range(chunks):
            part = scores[128 * index : 128 * index + 128] * scale
            weights[128 * index : 128 * index + 128] = part.astype(BF16)
        wide = dot(value_t[:, base : base + WINDOW], weights[...])
        context_t = jnp.concatenate([wide[:HEAD, :128], wide[HEAD:, 128:]], axis=0)
        context_dq[block, :, :128] = context_t.T.astype(BF16)
        product = context_t * d_context.T
        row_dot = jnp.concatenate(
            [
                jnp.sum(product[:HEAD], axis=0, keepdims=True),
                jnp.sum(product[HEAD:], axis=0, keepdims=True),
            ],
            axis=1,
        )
        for index in range(chunks):
            part = dot(value[base + 128 * index : base + 128 * index + 128], d_pair, 1, 1)
            part = weights[128 * index : 128 * index + 128].astype(F32) * (part - row_dot)
            d_scores[128 * index : 128 * index + 128] = part.astype(BF16)
        wide = dot(key_t[:, base : base + WINDOW], d_scores[...])
        d_query_t = jnp.concatenate([wide[:HEAD, :128], wide[HEAD:, 128:]], axis=0)
        context_dq[block, :, 128:] = (d_query_t * 0.125).astype(BF16)
        d_key[base : base + WINDOW] += dot(d_scores[...], query_pair)
        d_value[base : base + WINDOW] += dot(weights[...], d_pair)
    for piece in range(GROUP):
        for part, ref in enumerate((d_before, d_own, d_after)):
            start = 512 * part + ROWS * piece
            ref[piece, :, :128] = d_key[start : start + ROWS].astype(ref.dtype)
            ref[piece, :, 128:] = d_value[start : start + ROWS].astype(ref.dtype)


def join_kernel(own, from_before, from_after, out):
    for piece in range(GROUP):
        total = own[piece] + from_before[piece].astype(F32) + from_after[piece].astype(F32)
        total = total.astype(BF16)
        out[piece, :, :128] = total[:, :128].T
        out[piece, :, 128:] = total[:, 128:].T


def rows_kernel(
    frames, cotangent, context, gate, d_upper, joined_t, w_qkv, w_out, w_up, w_down, layer_out, d_frames
):
    gated = jnp.concatenate([gate[640 + 128 * m : 768 + 128 * m] for m in range(8)], axis=1)
    values = frames[...].astype(F32)
    out = values + dot(context[...], w_out[...]) + dot(gated, w_down[...])
    layer_out[...] = out.astype(BF16)
    unit_rows, inverse = normalize(values)
    d_normed = dot(d_upper[...], w_up[...], 1, 1) + dot(joined_t[...].T, w_qkv[...], 1, 1)
    d_frames[...] = (cotangent[...].astype(F32) + norm_back(d_normed, unit_rows, inverse)).astype(BF16)


def add_kernel(near, far, out):
    out[...] = (near[...].astype(F32) + far[...].astype(F32)).astype(BF16)


def chunk_sum_kernel(place, gate_parts, attention_parts, out_0, out_1, out_2, out_3, total):
    for parts, start in ((gate_parts, 0), (attention_parts, 112)):
        for first in range(0, parts.shape[1], 16):
            rows = slice(first, first + 16)
            acc = parts[0, rows, :].astype(F32)
            for source in range(1, 8):
                acc = acc + parts[source, rows, :].astype(F32)
            for z in range(4):
                total[z, start + first : start + first + 16, :] = acc[:, 128 * z : 128 * z + 128].astype(BF16)
    for turn, ref in enumerate((out_0, out_1, out_2, out_3)):
        ref[...] = total[(place[5] + turn) & 3]


def final_kernel(place, part_0, part_1, part_2, part_3, g_qkv_t, g_out_t, g_up_t, g_down_t, g_taps, ordered):
    for turn, ref in enumerate((part_0, part_1, part_2, part_3)):
        ordered[(place[5] + 4 - turn) & 3] = ref[...].astype(F32)
    total = (ordered[0] + ordered[1]) + (ordered[2] + ordered[3])
    g_up_t[...] = total[:64]
    g_down_t[...] = total[64:96]
    turned = total[96:112].T
    g_taps[...] = jnp.concatenate([turned[:TAPS], turned[32 : 32 + TAPS]], axis=1)
    g_qkv_t[...] = total[112:160]
    g_out_t[:16] = total[160:, :HEAD]
    g_out_t[16:] = total[160:, HEAD:]


def shift(array, by):
    return lax.ppermute(array, "seq", [(i, i + by) for i in range(32) if 0 <= i + by < 32])


def other_core(array):
    return lax.ppermute(array, "dp", [(i, i ^ 1) for i in range(8)])


def swap_rows(array):
    return lax.all_to_all(array, "seq", 0, 0, axis_index_groups=ROW_GROUPS)


def turn_x(pieces):
    return [pieces[0]] + [
        lax.ppermute(pieces[by], "seq", [(i, i // 4 * 4 + (i + by) % 4) for i in range(32)])
        for by in range(1, 4)
    ]


def turn_z(pieces):
    return [pieces[0]] + [
        lax.ppermute(pieces[by], "dp", [(i, (i + 2 * by) % 8) for i in range(8)]) for by in range(1, 4)
    ]


def local(frames, cotangent, lengths, w_qkv, w_out, w_up, w_down, conv_kernel):
    frames, cotangent = frames[0], cotangent[0]
    seq_index = lax.axis_index("seq")
    dp_index = lax.axis_index("dp")
    place = jnp.stack(
        [seq_index * ROWS, lengths[0], dp_index & 1, (seq_index >> 2) * (GROUP * ROWS), seq_index & 3, dp_index >> 1]
    ).astype(jnp.int32)

    wide = ((ROWS, 1024), BF16)
    wide_f = ((ROWS, 1024), F32)
    quad = ((4, ROWS, 256), BF16)
    frames_x = turn_x([frames] * 4)
    resid, d_gated, gating, d_conv, unit, inverse, slope, top, bottom = call(
        gate_kernel,
        [wide + (HBM,), wide + (HBM,), wide, wide, wide_f + (HBM,), ((ROWS, 128), F32, HBM),
         ((ROWS, 2048), F32, HBM), ((16, 2048), BF16), ((16, 2048), BF16)],
        scalars=1,
    )(place, frames, cotangent, w_up, w_down)
    before, after = shift(bottom, 1), shift(top, -1)
    gating, d_conv, cot_later = lax.optimization_barrier((gating, d_conv, cotangent))
    cot_x = turn_x([cot_later] * 4)
    conv_in, d_gating_in, g_taps_in = call(
        conv_inner_kernel,
        [wide_f, wide_f, ((32, 1024), F32)],
        [pltpu.VMEM((160, 1024), F32), pltpu.VMEM((160, 1024), F32)],
    )(gating, d_conv, conv_kernel)
    normed, query, kv = call(
        project_kernel, [((512, 1024), BF16), ((4, ROWS, 128), BF16), quad], scalars=1
    )(place, *frames_x, w_qkv)
    conv_in, normed, kv = lax.optimization_barrier((conv_in, normed, kv))
    kv_before, kv_after = shift(kv, 4), shift(kv, -4)
    gate = ((1664, 128), BF16)
    d_upper, *gate_x = call(
        conv_outer_kernel,
        [((ROWS, 2048), BF16, HBM), gate, gate, gate, gate],
        [pltpu.VMEM((ROWS, 1024), F32), pltpu.VMEM((ROWS, 1024), F32),
         pltpu.VMEM((32, 2048), F32), pltpu.VMEM((32, 2048), F32),
         pltpu.VMEM((32, 1024), F32), pltpu.VMEM((2048, ROWS), BF16), pltpu.VMEM((32, 16, 128), BF16)],
        scalars=1,
    )(place, conv_in, d_gating_in, g_taps_in, d_conv, resid, d_gated, unit, inverse, slope, before, after, conv_kernel)
    query, d_upper, *gate_x = lax.optimization_barrier((query, d_upper, *gate_x))
    gate_x = turn_x(gate_x)
    near, d_before, d_after, d_own = call(
        attend_kernel,
        [quad, quad, quad, ((4, ROWS, 256), F32)],
        [pltpu.VMEM((4, ROWS, 128), BF16),
         pltpu.VMEM((1536, 128), BF16), pltpu.VMEM((1536, 128), BF16),
         pltpu.VMEM((128, 1536), BF16), pltpu.VMEM((128, 1536), BF16),
         pltpu.VMEM((WINDOW, 256), F32), pltpu.VMEM((WINDOW, 256), BF16), pltpu.VMEM((WINDOW, 256), BF16),
         pltpu.VMEM((1536, 128), F32), pltpu.VMEM((1536, 128), F32)],
        scalars=1,
    )(place, query, kv, kv_before, kv_after, *cot_x, w_out)
    from_before, from_after = shift(d_after, 4), shift(d_before, -4)
    near_x = turn_x([near] * 4)
    keep, send, cot_own = call(
        gate_grads_kernel,
        [((8, 112, 512), BF16), ((8, 112, 512), BF16), ((256, 512), BF16)],
        [pltpu.VMEM((512, 512), BF16), pltpu.VMEM((512, 1024), BF16), pltpu.VMEM((1024, 512), BF16)],
        scalars=1,
    )(place, normed, *cot_x, *gate_x)
    (far,) = call(join_kernel, [quad])(d_own, from_before, from_after)
    far_x = turn_x([far] * 4)
    (gate_parts,) = call(add_kernel, [((8, 112, 512), BF16)])(keep, other_core(send))
    gate_parts = swap_rows(gate_parts)
    keep, send, context, joined_t = call(
        attention_grads_kernel,
        [((8, 64, 512), BF16), ((8, 64, 512), BF16), ((ROWS, 512), BF16), ((1536, ROWS), BF16)],
        [pltpu.VMEM((1536, 512), BF16), pltpu.VMEM((512, 512), BF16), pltpu.VMEM((384, 512), BF16)],
        scalars=1,
    )(place, normed, cot_own, *near_x, *far_x)
    (attention_parts,) = call(add_kernel, [((8, 64, 512), BF16)])(keep, other_core(send))
    attention_parts = swap_rows(attention_parts)
    layer_out, d_frames = call(rows_kernel, [wide, wide])(
        frames, cotangent, context, gate_x[0], d_upper, joined_t, w_qkv, w_out, w_up, w_down
    )
    parts = call(
        chunk_sum_kernel, [((176, 128), BF16)] * 4, [pltpu.VMEM((4, 176, 128), BF16)], scalars=1
    )(place, gate_parts, attention_parts)
    g_qkv, g_out, g_up, g_down, g_kernel = call(
        final_kernel,
        [((48, 128), F32), ((32, HEAD), F32), ((64, 128), F32), ((32, 128), F32), ((TAPS, 32), F32)],
        [pltpu.VMEM((4, 176, 128), F32)],
        scalars=1,
    )(place, *turn_z(parts))
    return (layer_out[None], d_frames[None], g_qkv.T, g_out.T, g_up.T, g_down.T, g_kernel)


def solution(mesh):
    return jax.shard_map(
        local,
        mesh=mesh,
        in_specs=(P("dp", "seq", None), P("dp", "seq", None), P("dp"), P(), P(), P(), P(), P()),
        out_specs=(
            P("dp", "seq", None),
            P("dp", "seq", None),
            P("dp", "seq"),
            P("dp", "seq"),
            P("dp", "seq"),
            P("dp", "seq"),
            P(None, "seq"),
        ),
        check_vma=False,
    )
```

time: 214 us -> 169 us (0.79)
  the two profiles are of different devices: /device:TPU:4 before, /device:TPU:8 now
where the time goes in v2:
time: 169 us; the launch traced here: 167 us
  starting transfers between devices  58.7 us (35%)
  Pallas kernels  37.4 us (22%)
  waiting for transfers between devices  34.4 us (20%)
  blocking collectives  18.1 us (11%)
  local copies, waits for them, and re-layouts  16.6 us (10%)
    pallas_call x13, Pallas kernels, run(): pl.pallas_call(body, out_shape=[HBM(*out[:2]) if len(out) > 2 else jax.Sh...  37.4 us
    ppermute x6, starting transfers between devices, shift(): lax.ppermute(array, 'seq', [(i, i + by) for i in range(32) if 0 <= i + by...  20.9 us
    ppermute x15, starting transfers between devices, turn_x(): lax.ppermute(pieces[by], 'seq', [(i, i // 4 * 4 + (i + by) % 4) for i in...  19.7 us
    all_to_all x1, blocking collectives, swap_rows(): return lax.all_to_all(array, 'seq', 0, 0, axis_index_groups=ROW_GROUPS)  18.1 us
    ppermute x15, waiting for transfers between devices, turn_x(): lax.ppermute(pieces[by], 'seq', [(i, i // 4 * 4 + (i + by) % 4) for i in...  16.8 us
    unnamed x52, local copies, waits for them, and re-layouts  16.5 us
    ppermute x6, waiting for transfers between devices, shift(): lax.ppermute(array, 'seq', [(i, i + by) for i in range(32) if 0 <= i + by...  10.6 us
    ppermute x3, starting transfers between devices, turn_z(): lax.ppermute(pieces[by], 'dp', [(i, (i + 2 * by) % 8) for i in range(8)])  10.5 us
  transfers between devices with their start and end apart: 27, of which 8 were waited for; matrix products, arithmetic and copies ran while one was open for 0% of the time, Pallas kernels for 15%

profile of v2, /device:TPU:8, one launch (start us, length us, event | category | flops | bytes accessed | tf_op | source)
XLA Modules:
  0.0 166.8 jit_solution(4278387219760376731)
XLA Ops:
  0.6 1.6 collective-permute-start
  2.2 2.7 %collective-permute-start.1 = (bf16[128,1024]{1,0:T(8,128)(2,1)}, bf16[128,1024]{1,0:T(8,128)(2,1)}, u32[]{:S(2)}, u32[]{:S(2)}) collective-permute-start(bf16[128,1024]{1,0:T(8,128)(2,1)} %bitcast.21), channel_id=1, source_target_pairs={{0,16},{8,24},{16,0},{24,8},{32,48},{40,56},{48,32},{56,40},{64,80... | collective-permute-start | bytes 786440 | tf_op jit(solution)/shard_map/ppermute | solution.py:420
  4.9 1.4 collective-permute-start.2
  7.1 2.2 %copy-done = bf16[1024,2048]{1,0:T(8,128)(2,1)S(1)} copy-done((bf16[1024,2048]{1,0:T(8,128)(2,1)S(1)}, bf16[1024,2048]{1,0:T(8,128)(2,1)}, u32[]{:S(2)}) %copy-start) | copy-done | bytes 4194328
  9.3 1.6 copy-done.3
  10.9 0.9 copy-done.7
  12.8 3.4 %shard_map.135 = (bf16[128,1024]{1,0:T(8,128)(2,1)}, bf16[128,1024]{1,0:T(8,128)(2,1)}, bf16[128,1024]{1,0:T(8,128)(2,1)S(1)}, bf16[128,1024]{1,0:T(8,128)(2,1)S...) custom-call(s32[6]{0:T(128)S(1)} %stack.23.place, ...), custom_call_target="tpu_custom_call" | custom-call | tf_op jit(solution)/shard_map/pallas_call | solution.py:33
  16.3 2.6 %collective-permute-start.6 = (bf16[16,2048]{1,0:T(8,128)(2,1)S(1)}, bf16[16,2048]{1,0:T(8,128)(2,1)S(1)}, u32[]{:S(2)}, u32[]{:S(2)}) collective-permute-start(bf16[16,2048]{1,0:T(8,128)(2,1)S(1)} %get-tuple-element.79), channel_id=1, source_target_pairs={{0,8},{8,16},{16,24},{24,32},{32,40},{40,48},{48,56},{56,64},{64,7... | collective-permute-start | bytes 196616 | tf_op jit(solution)/shard_map/ppermute | solution.py:407
  18.9 5.4 %collective-permute-start.7 = (bf16[16,2048]{1,0:T(8,128)(2,1)S(1)}, bf16[16,2048]{1,0:T(8,128)(2,1)S(1)}, u32[]{:S(2)}, u32[]{:S(2)}) collective-permute-start(bf16[16,2048]{1,0:T(8,128)(2,1)S(1)} %get-tuple-element.80), channel_id=1, source_target_pairs={{8,0},{16,8},{24,16},{32,24},{40,32},{48,40},{56,48},{64,56},{72,6... | collective-permute-start | bytes 196616 | tf_op jit(solution)/shard_map/ppermute | solution.py:407
  24.4 7.8 %shard_map.136 = (f32[128,1024]{1,0:T(8,128)S(1)}, f32[128,1024]{1,0:T(8,128)S(1)}, f32[32,1024]{1,0:T(8,128)S(1)}) custom-call(bf16[128,1024]{1,0:T(8,128)(2,1)S(1)} %get-tuple-element.63.gating, bf16[128,1024]{1,0:T(8,128)(2,1)S(1)} %get-tuple-element.64.d_conv, f32[31,1024]{1,0:T(8,128)S(1)} %copy-done.19), custom_call_target="tpu_custom_call" | custom-call | tf_op jit(solution)/shard_map/pallas_call | solution.py:33
  32.3 1.6 collective-permute-start.4
  33.9 1.7 %collective-permute-start.5 = (bf16[128,1024]{1,0:T(8,128)(2,1)S(1)}, bf16[128,1024]{1,0:T(8,128)(2,1)S(1)}, u32[]{:S(2)}, u32[]{:S(2)}) collective-permute-start(bf16[128,1024]{1,0:T(8,128)(2,1)S(1)} %bitcast.16), channel_id=1, source_target_pairs={{0,24},{8,0},{16,8},{24,16},{32,56},{40,32},{48,40},{56,48},{64,88... | collective-permute-start | bytes 786440 | tf_op jit(solution)/shard_map/ppermute | solution.py:420
  35.6 2.4 %shard_map.137 = (bf16[512,1024]{1,0:T(8,128)(2,1)S(1)}, bf16[4,128,128]{2,1,0:T(8,128)(2,1)S(1)}, bf16[4,128,256]{2,1,0:T(8,128)(2,1)S(1)}) custom-call(s32[6]{0:T(128)S(1)} %stack.23.place, bf16[128,1024]{1,0:T(8,128)(2,1)S(1)} %bitcast.24, bf16[128,1024]{1,0:T(8,128)(2,1)} %collective-permute-done.frames_1, ...), custom_call_target="tpu_custom_call" | custom-call | tf_op jit(solution)/shard_map/pallas_call | solution.py:33
  38.1 3.5 %collective-permute-start.11 = (bf16[4,128,256]{2,1,0:T(8,128)(2,1)S(1)}, bf16[4,128,256]{2,1,0:T(8,128)(2,1)S(1)}, u32[]{:S(2)}, u32[]{:S(2)}) collective-permute-start(bf16[4,128,256]{2,1,0:T(8,128)(2,1)S(1)} %get-tuple-element.92.kv), channel_id=1, source_target_pairs={{0,32},{8,40},{16,48},{24,56},{32,64},{40,72},{48,80},{56,88},{64,... | collective-permute-start | bytes 786440 | tf_op jit(solution)/shard_map/ppermute | solution.py:407
  41.6 2.5 %collective-permute-start.12 = (bf16[4,128,256]{2,1,0:T(8,128)(2,1)S(1)}, bf16[4,128,256]{2,1,0:T(8,128)(2,1)S(1)}, u32[]{:S(2)}, u32[]{:S(2)}) collective-permute-start(bf16[4,128,256]{2,1,0:T(8,128)(2,1)S(1)} %get-tuple-element.92.kv), channel_id=1, source_target_pairs={{32,0},{40,8},{48,16},{56,24},{64,32},{72,40},{80,48},{88,56},{96,... | collective-permute-start | bytes 786440 | tf_op jit(solution)/shard_map/ppermute | solution.py:407
  44.2 3.3 %shard_map.138 = (bf16[128,2048]{1,0:T(8,128)(2,1)}, bf16[1664,128]{1,0:T(8,128)(2,1)S(1)}, bf16[1664,128]{1,0:T(8,128)(2,1)S(1)}, bf16[1664,128]{1,0:T(8,128)(2,1)S(1)}, bf16[1664,128]{1,0:T(8,128)(2,1)S(1)}) custom-call(s32[6]{0:T(128)S(1)} %stack.23.place, f32[128,1024]{1,0:T(8,128)S(1)} %get-tuple-element.71.conv_in, ...), custom_call_target="tpu_custom_call" | custom-call | tf_op jit(solution)/shard_map/pallas_call | solution.py:33
  47.6 2.3 %collective-permute-done.12.after = bf16[4,128,256]{2,1,0:T(8,128)(2,1)S(1)} collective-permute-done((bf16[4,128,256]{2,1,0:T(8,128)(2,1)S(1)}, bf16[4,128,256]{2,1,0:T(8,128)(2,1)S(1)}, u32[]{:S(2)}, u32[]{:S(2)}) %collective-permute-start.12) | collective-permute-done | bytes 262176 | tf_op jit(solution)/shard_map/ppermute | solution.py:407
  49.8 7.2 %shard_map.140 = (bf16[4,128,256]{2,1,0:T(8,128)(2,1)S(1)}, bf16[4,128,256]{2,1,0:T(8,128)(2,1)S(1)}, bf16[4,128,256]{2,1,0:T(8,128)(2,1)S(1)}, f32[4,128,256]{2,1,0:T(8,128)S(1)}) custom-call(s32[6]{0:T(128)S(1)} %stack.23.place, bf16[4,128,128]{2,1,0:T(8,128)(2,1)S(1)} %get-tuple-element.91.queries, bf16[4,128,256]{2,1,0:T(8,128)(2,1)S(1)} %get-tuple-element.92.kv, ...), custom_call_target="tpu_custom_call" | custom-call | tf_op jit(solution)/shard_map/pallas_call | solution.py:33
  57.0 4.9 %collective-permute-start.16 = (bf16[4,128,256]{2,1,0:T(8,128)(2,1)S(1)}, bf16[4,128,256]{2,1,0:T(8,128)(2,1)S(1)}, u32[]{:S(2)}, u32[]{:S(2)}) collective-permute-start(bf16[4,128,256]{2,1,0:T(8,128)(2,1)S(1)} %get-tuple-element.95), channel_id=1, source_target_pairs={{0,32},{8,40},{16,48},{24,56},{32,64},{40,72},{48,80},{56,88},{64,... | collective-permute-start | bytes 786440 | tf_op jit(solution)/shard_map/ppermute | solution.py:407
  62.8 2.2 %collective-permute-start.9 = (bf16[1664,128]{1,0:T(8,128)(2,1)S(1)}, bf16[1664,128]{1,0:T(8,128)(2,1)S(1)}, u32[]{:S(2)}, u32[]{:S(2)}) collective-permute-start(bf16[1664,128]{1,0:T(8,128)(2,1)S(1)} %get-tuple-element.88), channel_id=1, source_target_pairs={{0,16},{8,24},{16,0},{24,8},{32,48},{40,56},{48,32},{56,40},{64,80... | collective-permute-start | bytes 1277960 | tf_op jit(solution)/shard_map/ppermute | solution.py:420
  65.0 2.5 %collective-permute-start.10 = (bf16[1664,128]{1,0:T(8,128)(2,1)S(1)}, bf16[1664,128]{1,0:T(8,128)(2,1)S(1)}, u32[]{:S(2)}, u32[]{:S(2)}) collective-permute-start(bf16[1664,128]{1,0:T(8,128)(2,1)S(1)} %get-tuple-element.89), channel_id=1, source_target_pairs={{0,24},{8,0},{16,8},{24,16},{32,56},{40,32},{48,40},{56,48},{64,88... | collective-permute-start | bytes 1277960 | tf_op jit(solution)/shard_map/ppermute | solution.py:420
  67.5 1.9 %collective-permute-start.17 = (bf16[4,128,256]{2,1,0:T(8,128)(2,1)S(1)}, bf16[4,128,256]{2,1,0:T(8,128)(2,1)S(1)}, u32[]{:S(2)}, u32[]{:S(2)}) collective-permute-start(bf16[4,128,256]{2,1,0:T(8,128)(2,1)S(1)} %get-tuple-element.96), channel_id=1, source_target_pairs={{32,0},{40,8},{48,16},{56,24},{64,32},{72,40},{80,48},{88,56},{96,... | collective-permute-start | bytes 786440 | tf_op jit(solution)/shard_map/ppermute | solution.py:407
  69.5 8.3 %collective-permute-done.17.from_after = bf16[4,128,256]{2,1,0:T(8,128)(2,1)S(1)} collective-permute-done((bf16[4,128,256]{2,1,0:T(8,128)(2,1)S(1)}, bf16[4,128,256]{2,1,0:T(8,128)(2,1)S(1)}, u32[]{:S(2)}, u32[]{:S(2)}) %collective-permute-start.17) | collective-permute-done | bytes 262176 | tf_op jit(solution)/shard_map/ppermute | solution.py:407
  78.7 8.4 %collective-permute-done.8.gate_1 = bf16[1664,128]{1,0:T(8,128)(2,1)S(1)} collective-permute-done((bf16[1664,128]{1,0:T(8,128)(2,1)S(1)}, bf16[1664,128]{1,0:T(8,128)(2,1)S(1)}, u32[]{:S(2)}, u32[]{:S(2)}) %collective-permute-start.8) | collective-permute-done | bytes 426016 | tf_op jit(solution)/shard_map/ppermute | solution.py:420
  87.1 2.0 %collective-permute-start.18 = (bf16[4,128,256]{2,1,0:T(8,128)(2,1)S(1)}, bf16[4,128,256]{2,1,0:T(8,128)(2,1)S(1)}, u32[]{:S(2)}, u32[]{:S(2)}) collective-permute-start(bf16[4,128,256]{2,1,0:T(8,128)(2,1)S(1)} %shard_map.141.far_0), channel_id=1, source_target_pairs={{0,8},{8,16},{16,24},{24,0},{32,40},{40,48},{48,56},{56,32},{64,72... | collective-permute-start | bytes 786440 | tf_op jit(solution)/shard_map/ppermute | solution.py:420
  89.1 2.2 %collective-permute-start.19 = (bf16[4,128,256]{2,1,0:T(8,128)(2,1)S(1)}, bf16[4,128,256]{2,1,0:T(8,128)(2,1)S(1)}, u32[]{:S(2)}, u32[]{:S(2)}) collective-permute-start(bf16[4,128,256]{2,1,0:T(8,128)(2,1)S(1)} %shard_map.141.far_0), channel_id=1, source_target_pairs={{0,16},{8,24},{16,0},{24,8},{32,48},{40,56},{48,32},{56,40},{64,80... | collective-permute-start | bytes 786440 | tf_op jit(solution)/shard_map/ppermute | solution.py:420
  91.3 5.3 %collective-permute-done.13.near_1 = bf16[4,128,256]{2,1,0:T(8,128)(2,1)S(1)} collective-permute-done((bf16[4,128,256]{2,1,0:T(8,128)(2,1)S(1)}, bf16[4,128,256]{2,1,0:T(8,128)(2,1)S(1)}, u32[]{:S(2)}, u32[]{:S(2)}) %collective-permute-start.13) | collective-permute-done | bytes 262176 | tf_op jit(solution)/shard_map/ppermute | solution.py:420
  96.6 3.1 %shard_map.139 = (bf16[8,112,512]{2,1,0:T(8,128)(2,1)S(1)}, bf16[8,112,512]{2,1,0:T(8,128)(2,1)}, bf16[256,512]{1,0:T(8,128)(2,1)S(1)}) custom-call(s32[6]{0:T(128)S(1)} %stack.23.place, bf16[512,1024]{1,0:T(8,128)(2,1)S(1)} %get-tuple-element.68.normed, bf16[128,1024]{1,0:T(8,128)(2,1)S(1)} %bitcast.18, bf16[128,1024]{1,0:T(8,128)(2,1)S(1)} %collective-permute-done.3.cot_1, ...), custom_call_target="tpu_custom_call" | custom-call | tf_op jit(solution)/shard_map/pallas_call | solution.py:33
  99.7 0.9 copy-done.16
  100.7 2.3 %collective-permute-done.18.far_1 = bf16[4,128,256]{2,1,0:T(8,128)(2,1)S(1)} collective-permute-done((bf16[4,128,256]{2,1,0:T(8,128)(2,1)S(1)}, bf16[4,128,256]{2,1,0:T(8,128)(2,1)S(1)}, u32[]{:S(2)}, u32[]{:S(2)}) %collective-permute-start.18) | collective-permute-done | bytes 262176 | tf_op jit(solution)/shard_map/ppermute | solution.py:420
  103.7 2.0 %shard_map.142 = (bf16[8,64,512]{2,1,0:T(8,128)(2,1)S(1)}, bf16[8,64,512]{2,1,0:T(8,128)(2,1)S(1)}, bf16[128,512]{1,0:T(8,128)(2,1)S(1)}, bf16[1536,128]{1,0:T(8,128)(2,1)S(1)}) custom-call(s32[6]{0:T(128)S(1)} %stack.23.place, bf16[512,1024]{1,0:T(8,128)(2,1)S(1)} %get-tuple-element.68.normed, bf16[256,512]{1,0:T(8,128)(2,1)S(1)} %get-tuple-element.90.cot_own, ...), custom_call_target="tpu_custom_call" | custom-call | tf_op jit(solution)/shard_map/pallas_call | solution.py:33
  106.9 2.1 %collective-permute-done.22.far = bf16[8,64,512]{2,1,0:T(8,128)(2,1)S(1)} collective-permute-done((bf16[8,64,512]{2,1,0:T(8,128)(2,1)S(1)}, bf16[8,64,512]{2,1,0:T(8,128)(2,1)S(1)}, u32[]{:S(2)}, u32[]{:S(2)}) %collective-permute-start.22) | collective-permute-done | bytes 524320 | tf_op jit(solution)/shard_map/ppermute | solution.py:411
  110.0 7.2 %all-to-all-start.1 = ((bf16[8,64,512]{2,1,0:T(8,128)(2,1)}), bf16[8,64,512]{2,1,0:T(8,128)(2,1)}, u32[]{:S(2)}, u32[]{:S(2)}) async-start(bf16[8,64,512]{2,1,0:T(8,128)(2,1)} %copy-done.12), calls=%async_computation.1 | async-start | bytes 1048576 | tf_op jit(solution)/shard_map/all_to_all | solution.py:415
  117.2 1.2 copy-done.17
  118.3 1.4 shard_map.144
  119.7 1.0 copy-done.9
  120.7 4.9 %all-to-all-done.1.attention_parts = bf16[8,64,512]{2,1,0:T(8,128)(2,1)} async-done(((bf16[8,64,512]{2,1,0:T(8,128)(2,1)}), bf16[8,64,512]{2,1,0:T(8,128)(2,1)}, u32[]{:S(2)}, u32[]{:S(2)}) %all-to-all-start.1) | async-done | bytes 524320 | tf_op jit(solution)/shard_map/all_to_all | solution.py:415
  125.6 18.1 %all_to_all.10.gate_parts = bf16[8,112,512]{2,1,0:T(8,128)(2,1)S(1)} all-to-all(bf16[8,112,512]{2,1,0:T(8,128)(2,1)} %copy-done.9), channel_id=1, replica_groups={{0,32,64,96,128,160,192,224},{8,40,72,104,136,168,200,232},{16,48,80,11..., dimensions={0} | all-to-all | bytes 1835008 | tf_op jit(solution)/shard_map/all_to_all | solution.py:415
  143.7 1.2 shard_map.146
  144.9 3.3 %collective-permute-start.23 = (bf16[176,128]{1,0:T(8,128)(2,1)S(1)}, bf16[176,128]{1,0:T(8,128)(2,1)S(1)}, u32[]{:S(2)}, u32[]{:S(2)}) collective-permute-start(bf16[176,128]{1,0:T(8,128)(2,1)S(1)} %get-tuple-element.107), channel_id=1, source_target_pairs={{0,2},{1,3},{2,4},{3,5},{4,6},{5,7},{6,0},{7,1},{8,10},{9,11},{10,... | collective-permute-start | bytes 135176 | tf_op jit(solution)/shard_map/ppermute | solution.py:427
  148.3 4.5 %collective-permute-start.24 = (bf16[176,128]{1,0:T(8,128)(2,1)S(1)}, bf16[176,128]{1,0:T(8,128)(2,1)S(1)}, u32[]{:S(2)}, u32[]{:S(2)}) collective-permute-start(bf16[176,128]{1,0:T(8,128)(2,1)S(1)} %get-tuple-element.108), channel_id=1, source_target_pairs={{0,4},{1,5},{2,6},{3,7},{4,0},{5,1},{6,2},{7,3},{8,12},{9,13},{10,... | collective-permute-start | bytes 135176 | tf_op jit(solution)/shard_map/ppermute | solution.py:427
  152.8 2.7 %collective-permute-start.25 = (bf16[176,128]{1,0:T(8,128)(2,1)S(1)}, bf16[176,128]{1,0:T(8,128)(2,1)S(1)}, u32[]{:S(2)}, u32[]{:S(2)}) collective-permute-start(bf16[176,128]{1,0:T(8,128)(2,1)S(1)} %get-tuple-element.109), channel_id=1, source_target_pairs={{0,6},{1,7},{2,0},{3,1},{4,2},{5,3},{6,4},{7,5},{8,14},{9,15},{10,... | collective-permute-start | bytes 135176 | tf_op jit(solution)/shard_map/ppermute | solution.py:427
  155.4 2.2 %copy-done.1 = bf16[1024,2048]{1,0:T(8,128)(2,1)S(1)} copy-done((bf16[1024,2048]{1,0:T(8,128)(2,1)S(1)}, bf16[1024,2048]{1,0:T(8,128)(2,1)}, u32[]{:S(2)}) %copy-start.1) | copy-done | bytes 4194328
  158.6 1.0 copy-done.14
  159.6 1.0 copy-done.18
  160.6 1.0 copy-done.22
  161.6 3.8 %shard_map.143 = (bf16[128,1024]{1,0:T(8,128)(2,1)}, bf16[128,1024]{1,0:T(8,128)(2,1)}) custom-call(bf16[128,1024]{1,0:T(8,128)(2,1)S(1)} %bitcast.25, bf16[128,1024]{1,0:T(8,128)(2,1)S(1)} %bitcast.19, bf16[128,512]{1,0:T(8,128)(2,1)S(1)} %get-tuple-element.97.context, bf16[1664,128]{1,0:T(8,128)(2,1)S(1)} %copy-done.14, bf16[128,2048]{1,0:T(8,128)(2,1)S(1)} %copy-done.18, ...), custom_call_target="tpu_custom_call" | custom-call | tf_op jit(solution)/shard_map/pallas_call | solution.py:33
  165.5 1.3 shard_map.147
  (73 shorter events, 6.8 us)
Async XLA Ops:
  0.6 31.6 %collective-permute-start = (bf16[128,1024]{1,0:T(8,128)(2,1)}, bf16[128,1024]{1,0:T(8,128)(2,1)}, u32[]{:S(2)}, u32[]{:S(2)}) collective-permute-start(bf16[128,1024]{1,0:T(8,128)(2,1)} %bitcast.20), channel_id=1, source_target_pairs={{0,8},{8,16},{16,24},{24,0},{32,40},{40,48},{48,56},{56,32},{64,72... | collective-permute-start | bytes 786440 | tf_op jit(solution)/shard_map/ppermute | solution.py:420
  2.2 30.1 %collective-permute-start.1 = (bf16[128,1024]{1,0:T(8,128)(2,1)}, bf16[128,1024]{1,0:T(8,128)(2,1)}, u32[]{:S(2)}, u32[]{:S(2)}) collective-permute-start(bf16[128,1024]{1,0:T(8,128)(2,1)} %bitcast.21), channel_id=1, source_target_pairs={{0,16},{8,24},{16,0},{24,8},{32,48},{40,56},{48,32},{56,40},{64,80... | collective-permute-start | bytes 786440 | tf_op jit(solution)/shard_map/ppermute | solution.py:420
  4.9 29.0 %collective-permute-start.2 = (bf16[128,1024]{1,0:T(8,128)(2,1)}, bf16[128,1024]{1,0:T(8,128)(2,1)}, u32[]{:S(2)}, u32[]{:S(2)}) collective-permute-start(bf16[128,1024]{1,0:T(8,128)(2,1)} %bitcast.22), channel_id=1, source_target_pairs={{0,24},{8,0},{16,8},{24,16},{32,56},{40,32},{48,40},{56,48},{64,88... | collective-permute-start | bytes 786440 | tf_op jit(solution)/shard_map/ppermute | solution.py:420
  7.1 2.2 %copy-start = (bf16[1024,2048]{1,0:T(8,128)(2,1)S(1)}, bf16[1024,2048]{1,0:T(8,128)(2,1)}, u32[]{:S(2)}) copy-start(bf16[1024,2048]{1,0:T(8,128)(2,1)} %w_up.3) | copy-start | bytes 12582916
  9.3 1.6 copy-start.3
  12.8 11.6 %copy-start.19 = (f32[31,1024]{1,0:T(8,128)S(1)}, f32[31,1024]{1,0:T(8,128)}, u32[]{:S(2)}) copy-start(f32[31,1024]{1,0:T(8,128)} %taps.3) | copy-start | bytes 380932
  12.8 19.4 %copy-start.8 = (bf16[1,128,1024]{2,1,0:T(8,128)(2,1)S(1)}, bf16[1,128,1024]{2,1,0:T(8,128)(2,1)}, u32[]{:S(2)}) copy-start(bf16[1,128,1024]{2,1,0:T(8,128)(2,1)} %param.9) | copy-start | bytes 786436
  12.8 22.8 %copy-start.2 = (bf16[1024,1536]{1,0:T(8,128)(2,1)S(1)}, bf16[1024,1536]{1,0:T(8,128)(2,1)}, u32[]{:S(2)}) copy-start(bf16[1024,1536]{1,0:T(8,128)(2,1)} %w_qkv.3) | copy-start | bytes 9437188
  16.2 27.9 %copy-start.15 = (f32[128,2048]{1,0:T(8,128)S(1)}, f32[128,2048]{1,0:T(8,128)}, u32[]{:S(2)}) copy-start(f32[128,2048]{1,0:T(8,128)} %get-tuple-element.78.slope) | copy-start | bytes 3145732
  16.2 27.9 %copy-start.20 = (f32[128,1024]{1,0:T(8,128)S(1)}, f32[128,1024]{1,0:T(8,128)}, u32[]{:S(2)}) copy-start(f32[128,1024]{1,0:T(8,128)} %get-tuple-element.76.unit) | copy-start | bytes 1572868
  16.2 27.9 %copy-start.23 = (bf16[128,1024]{1,0:T(8,128)(2,1)S(1)}, bf16[128,1024]{1,0:T(8,128)(2,1)}, u32[]{:S(2)}) copy-start(bf16[128,1024]{1,0:T(8,128)(2,1)} %get-tuple-element.74.resid) | copy-start | bytes 786436
  16.2 27.9 %copy-start.24 = (bf16[128,1024]{1,0:T(8,128)(2,1)S(1)}, bf16[128,1024]{1,0:T(8,128)(2,1)}, u32[]{:S(2)}) copy-start(bf16[128,1024]{1,0:T(8,128)(2,1)} %get-tuple-element.75.d_gated) | copy-start | bytes 786436
  16.3 27.9 %copy-start.25 = (f32[128,128]{1,0:T(8,128)S(1)}, f32[128,128]{1,0:T(8,128)}, u32[]{:S(2)}) copy-start(f32[128,128]{1,0:T(8,128)} %get-tuple-element.77.inverse) | copy-start | bytes 196612
  16.3 21.8 %collective-permute-start.6 = (bf16[16,2048]{1,0:T(8,128)(2,1)S(1)}, bf16[16,2048]{1,0:T(8,128)(2,1)S(1)}, u32[]{:S(2)}, u32[]{:S(2)}) collective-permute-start(bf16[16,2048]{1,0:T(8,128)(2,1)S(1)} %get-tuple-element.79), channel_id=1, source_target_pairs={{0,8},{8,16},{16,24},{24,32},{32,40},{40,48},{48,56},{56,64},{64,7... | collective-permute-start | bytes 196616 | tf_op jit(solution)/shard_map/ppermute | solution.py:407
  18.9 22.7 %collective-permute-start.7 = (bf16[16,2048]{1,0:T(8,128)(2,1)S(1)}, bf16[16,2048]{1,0:T(8,128)(2,1)S(1)}, u32[]{:S(2)}, u32[]{:S(2)}) collective-permute-start(bf16[16,2048]{1,0:T(8,128)(2,1)S(1)} %get-tuple-element.80), channel_id=1, source_target_pairs={{8,0},{16,8},{24,16},{32,24},{40,32},{48,40},{56,48},{64,56},{72,6... | collective-permute-start | bytes 196616 | tf_op jit(solution)/shard_map/ppermute | solution.py:407
  32.2 17.6 %copy-start.5 = (bf16[512,1024]{1,0:T(8,128)(2,1)S(1)}, bf16[512,1024]{1,0:T(8,128)(2,1)}, u32[]{:S(2)}) copy-start(bf16[512,1024]{1,0:T(8,128)(2,1)} %w_out.3) | copy-start | bytes 3145732
  32.2 15.3 %collective-permute-start.3 = (bf16[128,1024]{1,0:T(8,128)(2,1)S(1)}, bf16[128,1024]{1,0:T(8,128)(2,1)S(1)}, u32[]{:S(2)}, u32[]{:S(2)}) collective-permute-start(bf16[128,1024]{1,0:T(8,128)(2,1)S(1)} %bitcast.14), channel_id=1, source_target_pairs={{0,8},{8,16},{16,24},{24,0},{32,40},{40,48},{48,56},{56,32},{64,72... | collective-permute-start | bytes 786440 | tf_op jit(solution)/shard_map/ppermute | solution.py:420
  32.3 15.2 %collective-permute-start.4 = (bf16[128,1024]{1,0:T(8,128)(2,1)S(1)}, bf16[128,1024]{1,0:T(8,128)(2,1)S(1)}, u32[]{:S(2)}, u32[]{:S(2)}) collective-permute-start(bf16[128,1024]{1,0:T(8,128)(2,1)S(1)} %bitcast.15), channel_id=1, source_target_pairs={{0,16},{8,24},{16,0},{24,8},{32,48},{40,56},{48,32},{56,40},{64,80... | collective-permute-start | bytes 786440 | tf_op jit(solution)/shard_map/ppermute | solution.py:420
  33.9 13.6 %collective-permute-start.5 = (bf16[128,1024]{1,0:T(8,128)(2,1)S(1)}, bf16[128,1024]{1,0:T(8,128)(2,1)S(1)}, u32[]{:S(2)}, u32[]{:S(2)}) collective-permute-start(bf16[128,1024]{1,0:T(8,128)(2,1)S(1)} %bitcast.16), channel_id=1, source_target_pairs={{0,24},{8,0},{16,8},{24,16},{32,56},{40,32},{48,40},{56,48},{64,88... | collective-permute-start | bytes 786440 | tf_op jit(solution)/shard_map/ppermute | solution.py:420
  38.1 9.5 %collective-permute-start.11 = (bf16[4,128,256]{2,1,0:T(8,128)(2,1)S(1)}, bf16[4,128,256]{2,1,0:T(8,128)(2,1)S(1)}, u32[]{:S(2)}, u32[]{:S(2)}) collective-permute-start(bf16[4,128,256]{2,1,0:T(8,128)(2,1)S(1)} %get-tuple-element.92.kv), channel_id=1, source_target_pairs={{0,32},{8,40},{16,48},{24,56},{32,64},{40,72},{48,80},{56,88},{64,... | collective-permute-start | bytes 786440 | tf_op jit(solution)/shard_map/ppermute | solution.py:407
  41.6 8.3 %collective-permute-start.12 = (bf16[4,128,256]{2,1,0:T(8,128)(2,1)S(1)}, bf16[4,128,256]{2,1,0:T(8,128)(2,1)S(1)}, u32[]{:S(2)}, u32[]{:S(2)}) collective-permute-start(bf16[4,128,256]{2,1,0:T(8,128)(2,1)S(1)} %get-tuple-element.92.kv), channel_id=1, source_target_pairs={{32,0},{40,8},{48,16},{56,24},{64,32},{72,40},{80,48},{88,56},{96,... | collective-permute-start | bytes 786440 | tf_op jit(solution)/shard_map/ppermute | solution.py:407
  47.5 52.2 %copy-start.13 = (bf16[1664,128]{1,0:T(8,128)(2,1)}, bf16[1664,128]{1,0:T(8,128)(2,1)S(1)}, u32[]{:S(2)}) copy-start(bf16[1664,128]{1,0:T(8,128)(2,1)S(1)} %get-tuple-element.86.gate_0.gate) | copy-start | bytes 1277956
  57.0 12.4 %collective-permute-start.16 = (bf16[4,128,256]{2,1,0:T(8,128)(2,1)S(1)}, bf16[4,128,256]{2,1,0:T(8,128)(2,1)S(1)}, u32[]{:S(2)}, u32[]{:S(2)}) collective-permute-start(bf16[4,128,256]{2,1,0:T(8,128)(2,1)S(1)} %get-tuple-element.95), channel_id=1, source_target_pairs={{0,32},{8,40},{16,48},{24,56},{32,64},{40,72},{48,80},{56,88},{64,... | collective-permute-start | bytes 786440 | tf_op jit(solution)/shard_map/ppermute | solution.py:407
  61.9 25.2 %collective-permute-start.8 = (bf16[1664,128]{1,0:T(8,128)(2,1)S(1)}, bf16[1664,128]{1,0:T(8,128)(2,1)S(1)}, u32[]{:S(2)}, u32[]{:S(2)}) collective-permute-start(bf16[1664,128]{1,0:T(8,128)(2,1)S(1)} %get-tuple-element.87), channel_id=1, source_target_pairs={{0,8},{8,16},{16,24},{24,0},{32,40},{40,48},{48,56},{56,32},{64,72... | collective-permute-start | bytes 1277960 | tf_op jit(solution)/shard_map/ppermute | solution.py:420
  62.8 24.3 %collective-permute-start.9 = (bf16[1664,128]{1,0:T(8,128)(2,1)S(1)}, bf16[1664,128]{1,0:T(8,128)(2,1)S(1)}, u32[]{:S(2)}, u32[]{:S(2)}) collective-permute-start(bf16[1664,128]{1,0:T(8,128)(2,1)S(1)} %get-tuple-element.88), channel_id=1, source_target_pairs={{0,16},{8,24},{16,0},{24,8},{32,48},{40,56},{48,32},{56,40},{64,80... | collective-permute-start | bytes 1277960 | tf_op jit(solution)/shard_map/ppermute | solution.py:420
  65.0 24.1 %collective-permute-start.10 = (bf16[1664,128]{1,0:T(8,128)(2,1)S(1)}, bf16[1664,128]{1,0:T(8,128)(2,1)S(1)}, u32[]{:S(2)}, u32[]{:S(2)}) collective-permute-start(bf16[1664,128]{1,0:T(8,128)(2,1)S(1)} %get-tuple-element.89), channel_id=1, source_target_pairs={{0,24},{8,0},{16,8},{24,16},{32,56},{40,32},{48,40},{56,48},{64,88... | collective-permute-start | bytes 1277960 | tf_op jit(solution)/shard_map/ppermute | solution.py:420
  67.5 10.4 %collective-permute-start.17 = (bf16[4,128,256]{2,1,0:T(8,128)(2,1)S(1)}, bf16[4,128,256]{2,1,0:T(8,128)(2,1)S(1)}, u32[]{:S(2)}, u32[]{:S(2)}) collective-permute-start(bf16[4,128,256]{2,1,0:T(8,128)(2,1)S(1)} %get-tuple-element.96), channel_id=1, source_target_pairs={{32,0},{40,8},{48,16},{56,24},{64,32},{72,40},{80,48},{88,56},{96,... | collective-permute-start | bytes 786440 | tf_op jit(solution)/shard_map/ppermute | solution.py:407
  69.4 27.2 %collective-permute-start.13 = (bf16[4,128,256]{2,1,0:T(8,128)(2,1)S(1)}, bf16[4,128,256]{2,1,0:T(8,128)(2,1)S(1)}, u32[]{:S(2)}, u32[]{:S(2)}) collective-permute-start(bf16[4,128,256]{2,1,0:T(8,128)(2,1)S(1)} %get-tuple-element.93.near_0), channel_id=1, source_target_pairs={{0,8},{8,16},{16,24},{24,0},{32,40},{40,48},{48,56},{56,32},{64,72... | collective-permute-start | bytes 786440 | tf_op jit(solution)/shard_map/ppermute | solution.py:420
  77.8 22.8 %collective-permute-start.14 = (bf16[4,128,256]{2,1,0:T(8,128)(2,1)S(1)}, bf16[4,128,256]{2,1,0:T(8,128)(2,1)S(1)}, u32[]{:S(2)}, u32[]{:S(2)}) collective-permute-start(bf16[4,128,256]{2,1,0:T(8,128)(2,1)S(1)} %get-tuple-element.93.near_0), channel_id=1, source_target_pairs={{0,16},{8,24},{16,0},{24,8},{32,48},{40,56},{48,32},{56,40},{64,80... | collective-permute-start | bytes 786440 | tf_op jit(solution)/shard_map/ppermute | solution.py:420
  87.1 13.6 %collective-permute-start.15 = (bf16[4,128,256]{2,1,0:T(8,128)(2,1)S(1)}, bf16[4,128,256]{2,1,0:T(8,128)(2,1)S(1)}, u32[]{:S(2)}, u32[]{:S(2)}) collective-permute-start(bf16[4,128,256]{2,1,0:T(8,128)(2,1)S(1)} %get-tuple-element.93.near_0), channel_id=1, source_target_pairs={{0,24},{8,0},{16,8},{24,16},{32,56},{40,32},{48,40},{56,48},{64,88... | collective-permute-start | bytes 786440 | tf_op jit(solution)/shard_map/ppermute | solution.py:420
  87.1 15.9 %collective-permute-start.18 = (bf16[4,128,256]{2,1,0:T(8,128)(2,1)S(1)}, bf16[4,128,256]{2,1,0:T(8,128)(2,1)S(1)}, u32[]{:S(2)}, u32[]{:S(2)}) collective-permute-start(bf16[4,128,256]{2,1,0:T(8,128)(2,1)S(1)} %shard_map.141.far_0), channel_id=1, source_target_pairs={{0,8},{8,16},{16,24},{24,0},{32,40},{40,48},{48,56},{56,32},{64,72... | collective-permute-start | bytes 786440 | tf_op jit(solution)/shard_map/ppermute | solution.py:420
  89.1 13.9 %collective-permute-start.19 = (bf16[4,128,256]{2,1,0:T(8,128)(2,1)S(1)}, bf16[4,128,256]{2,1,0:T(8,128)(2,1)S(1)}, u32[]{:S(2)}, u32[]{:S(2)}) collective-permute-start(bf16[4,128,256]{2,1,0:T(8,128)(2,1)S(1)} %shard_map.141.far_0), channel_id=1, source_target_pairs={{0,16},{8,24},{16,0},{24,8},{32,48},{40,56},{48,32},{56,40},{64,80... | collective-permute-start | bytes 786440 | tf_op jit(solution)/shard_map/ppermute | solution.py:420
  96.6 7.0 %collective-permute-start.20 = (bf16[4,128,256]{2,1,0:T(8,128)(2,1)S(1)}, bf16[4,128,256]{2,1,0:T(8,128)(2,1)S(1)}, u32[]{:S(2)}, u32[]{:S(2)}) collective-permute-start(bf16[4,128,256]{2,1,0:T(8,128)(2,1)S(1)} %shard_map.141.far_0), channel_id=1, source_target_pairs={{0,24},{8,0},{16,8},{24,16},{32,56},{40,32},{48,40},{56,48},{64,88... | collective-permute-start | bytes 786440 | tf_op jit(solution)/shard_map/ppermute | solution.py:420
  99.7 1.0 copy-start.16
  106.4 2.6 %collective-permute-start.22 = (bf16[8,64,512]{2,1,0:T(8,128)(2,1)S(1)}, bf16[8,64,512]{2,1,0:T(8,128)(2,1)S(1)}, u32[]{:S(2)}, u32[]{:S(2)}) collective-permute-start(bf16[8,64,512]{2,1,0:T(8,128)(2,1)S(1)} %get-tuple-element.105), channel_id=1, source_target_pairs={{0,1},{1,0},{2,3},{3,2},{4,5},{5,4},{6,7},{7,6},{8,9},{9,8},{10,11... | collective-permute-start | bytes 1572872 | tf_op jit(solution)/shard_map/ppermute | solution.py:411
  106.4 10.7 %collective-permute-start.21 = (bf16[8,112,512]{2,1,0:T(8,128)(2,1)}, bf16[8,112,512]{2,1,0:T(8,128)(2,1)}, u32[]{:S(2)}, u32[]{:S(2)}) collective-permute-start(bf16[8,112,512]{2,1,0:T(8,128)(2,1)} %get-tuple-element.103), channel_id=1, source_target_pairs={{0,1},{1,0},{2,3},{3,2},{4,5},{5,4},{6,7},{7,6},{8,9},{9,8},{10,11... | collective-permute-start | bytes 2752520 | tf_op jit(solution)/shard_map/ppermute | solution.py:411
  110.0 15.6 %all-to-all-start.1 = ((bf16[8,64,512]{2,1,0:T(8,128)(2,1)}), bf16[8,64,512]{2,1,0:T(8,128)(2,1)}, u32[]{:S(2)}, u32[]{:S(2)}) async-start(bf16[8,64,512]{2,1,0:T(8,128)(2,1)} %copy-done.12), calls=%async_computation.1 | async-start | bytes 1048576 | tf_op jit(solution)/shard_map/all_to_all | solution.py:415
  117.2 1.2 copy-start.17
  119.7 1.0 copy-start.9
  125.6 29.9 %copy-start.4 = (bf16[1024,1024]{1,0:T(8,128)(2,1)S(1)}, bf16[1024,1024]{1,0:T(8,128)(2,1)}, u32[]{:S(2)}) copy-start(bf16[1024,1024]{1,0:T(8,128)(2,1)} %w_down.3) | copy-start | bytes 6291460
  125.6 29.9 %copy-start.6 = (bf16[512,1024]{1,0:T(8,128)(2,1)S(1)}, bf16[512,1024]{1,0:T(8,128)(2,1)}, u32[]{:S(2)}) copy-start(bf16[512,1024]{1,0:T(8,128)(2,1)} %w_out.3) | copy-start | bytes 3145732
  144.9 20.5 %collective-permute-start.23 = (bf16[176,128]{1,0:T(8,128)(2,1)S(1)}, bf16[176,128]{1,0:T(8,128)(2,1)S(1)}, u32[]{:S(2)}, u32[]{:S(2)}) collective-permute-start(bf16[176,128]{1,0:T(8,128)(2,1)S(1)} %get-tuple-element.107), channel_id=1, source_target_pairs={{0,2},{1,3},{2,4},{3,5},{4,6},{5,7},{6,0},{7,1},{8,10},{9,11},{10,... | collective-permute-start | bytes 135176 | tf_op jit(solution)/shard_map/ppermute | solution.py:427
  148.3 17.2 %collective-permute-start.24 = (bf16[176,128]{1,0:T(8,128)(2,1)S(1)}, bf16[176,128]{1,0:T(8,128)(2,1)S(1)}, u32[]{:S(2)}, u32[]{:S(2)}) collective-permute-start(bf16[176,128]{1,0:T(8,128)(2,1)S(1)} %get-tuple-element.108), channel_id=1, source_target_pairs={{0,4},{1,5},{2,6},{3,7},{4,0},{5,1},{6,2},{7,3},{8,12},{9,13},{10,... | collective-permute-start | bytes 135176 | tf_op jit(solution)/shard_map/ppermute | solution.py:427
  152.8 12.7 %collective-permute-start.25 = (bf16[176,128]{1,0:T(8,128)(2,1)S(1)}, bf16[176,128]{1,0:T(8,128)(2,1)S(1)}, u32[]{:S(2)}, u32[]{:S(2)}) collective-permute-start(bf16[176,128]{1,0:T(8,128)(2,1)S(1)} %get-tuple-element.109), channel_id=1, source_target_pairs={{0,6},{1,7},{2,0},{3,1},{4,2},{5,3},{6,4},{7,5},{8,14},{9,15},{10,... | collective-permute-start | bytes 135176 | tf_op jit(solution)/shard_map/ppermute | solution.py:427
  155.4 2.2 %copy-start.1 = (bf16[1024,2048]{1,0:T(8,128)(2,1)S(1)}, bf16[1024,2048]{1,0:T(8,128)(2,1)}, u32[]{:S(2)}) copy-start(bf16[1024,2048]{1,0:T(8,128)(2,1)} %w_up.3) | copy-start | bytes 12582916
  158.6 1.0 copy-start.14
  159.6 1.0 copy-start.18
  160.6 1.0 copy-start.22
  (5 other events, 4.4 us)

commit v3 on v2

--- a/solution.py
+++ b/solution.py
@@ -44,6 +44,10 @@
     return run
 
 
+def in_hbm(*arrays):
+    return [pltpu.with_memory_space_constraint(array, HBM) for array in arrays]
+
+
 def dot(left, right, left_dim=1, right_dim=0):
     return lax.dot_general(
         left, right, (((left_dim,), (right_dim,)), ((), ())), preferred_element_type=F32
@@ -64,6 +68,11 @@
     )
 
 
+def locate(lengths):
+    seq, dp = lax.axis_index("seq"), lax.axis_index("dp")
+    return (seq * ROWS, lengths[0], dp & 1, (seq >> 2) * (GROUP * ROWS), seq & 3, dp >> 1)
+
+
 def slot(place, turn):
     return (place[4] + 4 - turn) & 3
 
@@ -72,7 +81,19 @@
     return pl.ds(pl.multiple_of(index * size, size), size)
 
 
-def project_kernel(place, frames_0, frames_1, frames_2, frames_3, w_qkv, normed, query, kv):
+def cotangent_kernel(lengths, cotangent, w_out, out_0, out_1, out_2, out_3, d_context, cot_t):
+    place = locate(lengths)
+    d_context[...] = dot(cotangent[...], w_out[...], 1, 1).astype(BF16)
+    cot_t[...] = cotangent[...].T
+    for turn, ref in enumerate((out_0, out_1, out_2, out_3)):
+        x = (place[4] + turn) & 3
+        ref[:128] = d_context[:, span(x, 128)]
+        for m in range(8):
+            ref[128 + 32 * m : 160 + 32 * m] = cot_t[span(4 * m + x, 32), :]
+
+
+def project_kernel(lengths, frames_0, frames_1, frames_2, frames_3, w_qkv, normed, query, kv):
+    place = locate(lengths)
     x = place[4]
     for turn, ref in enumerate((frames_0, frames_1, frames_2, frames_3)):
         unit_rows, _ = normalize(ref[...].astype(F32))
@@ -84,9 +105,10 @@
 
 
 def gate_kernel(
-    place, frames, cotangent, w_up, w_down,
+    lengths, frames, cotangent, w_up, w_down,
     resid, d_gated, gating, d_conv, unit, inverse, slope, top, bottom
 ):
+    place = locate(lengths)
     first_frame, length = place[0], place[1]
     unit_rows, _ = normalize(frames[...].astype(F32))
     upper = dot(unit_rows.astype(BF16), w_up[...])
@@ -145,9 +167,10 @@
 
 
 def conv_outer_kernel(
-    place, conv_in, d_gating_in, g_taps_in, d_conv, resid, d_gated, unit, inverse, slope, before, after, taps,
+    lengths, conv_in, d_gating_in, g_taps_in, d_conv, resid, d_gated, unit, inverse, slope, before, after, taps,
     d_upper, out_0, out_1, out_2, out_3, conv_out, d_gating, before_ext, after_ext, g_taps, d_upper_t, g_taps_t
 ):
+    place = locate(lengths)
     first_frame, length = place[0], place[1]
     conv_out[...] = conv_in[...]
     d_gating[...] = d_gating_in[...]
@@ -205,9 +228,10 @@
 
 
 def gate_grads_kernel(
-    place, normed, cot_0, cot_1, cot_2, cot_3, gate_0, gate_1, gate_2, gate_3,
-    keep, send, cot_own, d_upper_t, gated, cot_t
-):
+    lengths, normed, cot_0, cot_1, cot_2, cot_3, gate_0, gate_1, gate_2, gate_3,
+    keep, send, cot_own, d_upper_t, gated
+):
+    place = locate(lengths)
     x, core = place[4], place[2]
     gates = (gate_0, gate_1, gate_2, gate_3)
     g_taps = gate_0[512:640].astype(F32)
@@ -219,9 +243,7 @@
         d_upper_t[:, here] = gate[:512]
         for block in range(8):
             gated[here, 128 * block : 128 * block + 128] = gate[640 + 128 * block : 768 + 128 * block]
-        cot_t[:, here] = cot[...].T
-    for m in range(8):
-        cot_own[32 * m : 32 * m + 32] = cot_t[span(4 * m + x, 32), :]
+        cot_own[:, here] = cot[128:]
     for parity, out in ((core, keep), (1 - core, send)):
         grad = dot(d_upper_t[...], own_columns(normed, parity, 128))
         out[:, :64, :] = grad.astype(BF16).reshape(8, 64, 512)
@@ -232,23 +254,21 @@
 
 
 def attention_grads_kernel(
-    place, normed, cot_own, near_0, near_1, near_2, near_3, far_0, far_1, far_2, far_3,
-    keep, send, context_own, joined_own, joined_t, context, rows_t
-):
-    x, core = place[4], place[2]
-    nears, fars = (near_0, near_1, near_2, near_3), (far_0, far_1, far_2, far_3)
-    for turn, (near, far) in enumerate(zip(nears, fars)):
-        pair = slot(place, turn)
-        for block in range(GROUP):
-            tokens = slice(128 * block, 128 * block + 128)
-            context[tokens, span(pair, 128)] = near[block, :, :128]
-            joined_t[span(pair, 128), tokens] = near[block, :, 128:]
-            joined_t[span(pair + 4, 128), tokens] = far[block, :, :128]
-            joined_t[span(pair + 8, 128), tokens] = far[block, :, 128:]
-    for m in range(8):
-        rows_t[48 * m : 48 * m + 48] = joined_t[span(4 * m + x, 48), :]
-    context_own[...] = context[span(x, ROWS), :]
-    joined_own[...] = joined_t[:, span(x, ROWS)]
+    lengths, gate_keep, gate_send, normed, cot_own, near_0, near_1, near_2, near_3, far_0, far_1, far_2, far_3,
+    keep, send, context, rows_t
+):
+    place = locate(lengths)
+    core = place[2]
+    for turn, near in enumerate((near_0, near_1, near_2, near_3)):
+        context[:, span(slot(place, turn), 128)] = near[...].reshape(512, 128)
+    for x in range(4):
+
+        @pl.when(place[4] == x)
+        def _():
+            for turn, far in enumerate((far_0, far_1, far_2, far_3)):
+                for index, (_, there) in enumerate(unit_rows_of((x - turn) % 4, x)):
+                    rows_t[16 * there : 16 * there + 16] = far[16 * index : 16 * index + 16]
+
     lane = lax.broadcasted_iota(jnp.int32, (512, 128), 1)
     blocks, swapped = [], []
     for z in range(4):
@@ -256,25 +276,26 @@
         blocks.append(block)
         swapped.append(pltpu.roll(block, HEAD, 1))
     lane_out = lax.broadcasted_iota(jnp.int32, (8, 16, 512), 2)
-    for parity, out in ((core, keep), (1 - core, send)):
+    for parity, gate, out in ((core, gate_keep, keep), (1 - core, gate_send, send)):
+        out[:, :112, :] = gate[...]
         grad = dot(rows_t[...], own_columns(normed, parity, 128))
-        out[:, :48, :] = grad.astype(BF16).reshape(8, 48, 512)
+        out[:, 112:160, :] = grad.astype(BF16).reshape(8, 48, 512)
         mine = (lane < HEAD) == (parity == 0)
         doubled = jnp.concatenate(
             [jnp.where(mine, block, other) for block, other in zip(blocks, swapped)], axis=1
         ).astype(BF16)
         grad = dot(cot_own[...], doubled).reshape(8, 32, 512)
-        out[:, 48:, :] = jnp.where((lane_out & 127) < HEAD, grad[:, :16], grad[:, 16:]).astype(BF16)
+        out[:, 160:, :] = jnp.where((lane_out & 127) < HEAD, grad[:, :16], grad[:, 16:]).astype(BF16)
 
 
 def attend_kernel(
-    place, queries, kv, before, after, cot_0, cot_1, cot_2, cot_3, w_out, context_dq, d_before, d_after, d_own,
+    lengths, queries, kv, before, after, cot_0, cot_1, cot_2, cot_3, context_out, d_query, d_before, d_after, d_own,
     d_contexts, key, value, key_t, value_t, scores, weights, d_scores, d_key, d_value
 ):
+    place = locate(lengths)
     group_first, length = place[3], place[1]
-    w_pair = w_out[span(place[4], 128), :]
     for turn, ref in enumerate((cot_0, cot_1, cot_2, cot_3)):
-        d_contexts[slot(place, turn)] = dot(ref[...], w_pair, 1, 1).astype(BF16)
+        d_contexts[slot(place, turn)] = ref[:128]
     for part, ref in enumerate((before, kv, after)):
         for piece in range(GROUP):
             start = 512 * part + ROWS * piece
@@ -328,7 +349,7 @@
             weights[128 * index : 128 * index + 128] = part.astype(BF16)
         wide = dot(value_t[:, base : base + WINDOW], weights[...])
         context_t = jnp.concatenate([wide[:HEAD, :128], wide[HEAD:, 128:]], axis=0)
-        context_dq[block, :, :128] = context_t.T.astype(BF16)
+        context_out[block] = context_t.T.astype(BF16)
         product = context_t * d_context.T
         row_dot = jnp.concatenate(
             [
@@ -343,7 +364,7 @@
             d_scores[128 * index : 128 * index + 128] = part.astype(BF16)
         wide = dot(key_t[:, base : base + WINDOW], d_scores[...])
         d_query_t = jnp.concatenate([wide[:HEAD, :128], wide[HEAD:, 128:]], axis=0)
-        context_dq[block, :, 128:] = (d_query_t * 0.125).astype(BF16)
+        d_query[:, base : base + 128] = (d_query_t * 0.125).astype(BF16)
         d_key[base : base + WINDOW] += dot(d_scores[...], query_pair)
         d_value[base : base + WINDOW] += dot(weights[...], d_pair)
     for piece in range(GROUP):
@@ -353,17 +374,45 @@
             ref[piece, :, 128:] = d_value[start : start + ROWS].astype(ref.dtype)
 
 
-def join_kernel(own, from_before, from_after, out):
+def unit_rows_of(source, target):
+    units = [32 * part + 8 * source + row for part in range(3) for row in range(8)]
+    wanted = [unit for unit in units if (unit // 3) % 4 == target]
+    return [(units.index(unit), unit // 12 * 3 + unit % 3) for unit in wanted]
+
+
+def join_kernel(
+    lengths, d_query, own, from_before, from_after,
+    unit_0, unit_1, unit_2, unit_3, back_0, back_1, back_2, back_3, joined_t
+):
+    place = locate(lengths)
+    joined_t[:128] = d_query[...]
     for piece in range(GROUP):
         total = own[piece] + from_before[piece].astype(F32) + from_after[piece].astype(F32)
         total = total.astype(BF16)
-        out[piece, :, :128] = total[:, :128].T
-        out[piece, :, 128:] = total[:, 128:].T
+        joined_t[128:256, 128 * piece : 128 * piece + 128] = total[:, :128].T
+        joined_t[256:, 128 * piece : 128 * piece + 128] = total[:, 128:].T
+    for turn, ref in enumerate((back_0, back_1, back_2, back_3)):
+        ref[...] = joined_t[:, span((place[4] + turn) & 3, 128)]
+    for x in range(4):
+
+        @pl.when(place[4] == x)
+        def _():
+            for turn, ref in enumerate((unit_0, unit_1, unit_2, unit_3)):
+                for index, (here, _) in enumerate(unit_rows_of(x, (x + turn) % 4)):
+                    ref[16 * index : 16 * index + 16] = joined_t[16 * here : 16 * here + 16]
 
 
 def rows_kernel(
-    frames, cotangent, context, gate, d_upper, joined_t, w_qkv, w_out, w_up, w_down, layer_out, d_frames
-):
+    lengths, frames, cotangent, near_0, near_1, near_2, near_3, back_0, back_1, back_2, back_3, gate, d_upper,
+    w_qkv, w_out, w_up, w_down, layer_out, d_frames, context, joined_t
+):
+    place = locate(lengths)
+    for turn, near in enumerate((near_0, near_1, near_2, near_3)):
+        context[:, span(slot(place, turn), 128)] = near[place[4]]
+    for turn, back in enumerate((back_0, back_1, back_2, back_3)):
+        pair = slot(place, turn)
+        for part in range(3):
+            joined_t[span(pair + 4 * part, 128), :] = back[128 * part : 128 * part + 128]
     gated = jnp.concatenate([gate[640 + 128 * m : 768 + 128 * m] for m in range(8)], axis=1)
     values = frames[...].astype(F32)
     out = values + dot(context[...], w_out[...]) + dot(gated, w_down[...])
@@ -377,20 +426,21 @@
     out[...] = (near[...].astype(F32) + far[...].astype(F32)).astype(BF16)
 
 
-def chunk_sum_kernel(place, gate_parts, attention_parts, out_0, out_1, out_2, out_3, total):
-    for parts, start in ((gate_parts, 0), (attention_parts, 112)):
-        for first in range(0, parts.shape[1], 16):
-            rows = slice(first, first + 16)
-            acc = parts[0, rows, :].astype(F32)
-            for source in range(1, 8):
-                acc = acc + parts[source, rows, :].astype(F32)
-            for z in range(4):
-                total[z, start + first : start + first + 16, :] = acc[:, 128 * z : 128 * z + 128].astype(BF16)
+def chunk_sum_kernel(lengths, parts, out_0, out_1, out_2, out_3, total):
+    place = locate(lengths)
+    for first in range(0, parts.shape[1], 16):
+        rows = slice(first, first + 16)
+        acc = parts[0, rows, :].astype(F32)
+        for source in range(1, 8):
+            acc = acc + parts[source, rows, :].astype(F32)
+        for z in range(4):
+            total[z, rows, :] = acc[:, 128 * z : 128 * z + 128].astype(BF16)
     for turn, ref in enumerate((out_0, out_1, out_2, out_3)):
         ref[...] = total[(place[5] + turn) & 3]
 
 
-def final_kernel(place, part_0, part_1, part_2, part_3, g_qkv_t, g_out_t, g_up_t, g_down_t, g_taps, ordered):
+def final_kernel(lengths, part_0, part_1, part_2, part_3, g_qkv_t, g_out_t, g_up_t, g_down_t, g_taps, ordered):
+    place = locate(lengths)
     for turn, ref in enumerate((part_0, part_1, part_2, part_3)):
         ordered[(place[5] + 4 - turn) & 3] = ref[...].astype(F32)
     total = (ordered[0] + ordered[1]) + (ordered[2] + ordered[3])
@@ -430,35 +480,35 @@
 
 def local(frames, cotangent, lengths, w_qkv, w_out, w_up, w_down, conv_kernel):
     frames, cotangent = frames[0], cotangent[0]
-    seq_index = lax.axis_index("seq")
-    dp_index = lax.axis_index("dp")
-    place = jnp.stack(
-        [seq_index * ROWS, lengths[0], dp_index & 1, (seq_index >> 2) * (GROUP * ROWS), seq_index & 3, dp_index >> 1]
-    ).astype(jnp.int32)
-
     wide = ((ROWS, 1024), BF16)
     wide_f = ((ROWS, 1024), F32)
     quad = ((4, ROWS, 256), BF16)
     frames_x = turn_x([frames] * 4)
     resid, d_gated, gating, d_conv, unit, inverse, slope, top, bottom = call(
         gate_kernel,
-        [wide + (HBM,), wide + (HBM,), wide, wide, wide_f + (HBM,), ((ROWS, 128), F32, HBM),
-         ((ROWS, 2048), F32, HBM), ((16, 2048), BF16), ((16, 2048), BF16)],
+        [wide, wide, wide, wide, wide_f, ((ROWS, 128), F32), ((ROWS, 2048), F32),
+         ((16, 2048), BF16), ((16, 2048), BF16)],
         scalars=1,
-    )(place, frames, cotangent, w_up, w_down)
+    )(lengths, *in_hbm(frames, cotangent, w_up, w_down))
     before, after = shift(bottom, 1), shift(top, -1)
-    gating, d_conv, cot_later = lax.optimization_barrier((gating, d_conv, cotangent))
-    cot_x = turn_x([cot_later] * 4)
+    gating, frames_x, cot_later = lax.optimization_barrier((gating, frames_x, cotangent))
+    small = ((384, 128), BF16)
+    cot_x = turn_x(
+        call(
+            cotangent_kernel, [small] * 4, [pltpu.VMEM((ROWS, 512), BF16), pltpu.VMEM((1024, ROWS), BF16)], scalars=1
+        )(lengths, cot_later, w_out)
+    )
+    normed, query, kv = call(
+        project_kernel, [((512, 1024), BF16), ((4, ROWS, 128), BF16), quad], scalars=1
+    )(lengths, *frames_x, w_qkv)
+    gating, kv = lax.optimization_barrier((gating, kv))
+    kv_before, kv_after = shift(kv, 4), shift(kv, -4)
     conv_in, d_gating_in, g_taps_in = call(
         conv_inner_kernel,
         [wide_f, wide_f, ((32, 1024), F32)],
         [pltpu.VMEM((160, 1024), F32), pltpu.VMEM((160, 1024), F32)],
     )(gating, d_conv, conv_kernel)
-    normed, query, kv = call(
-        project_kernel, [((512, 1024), BF16), ((4, ROWS, 128), BF16), quad], scalars=1
-    )(place, *frames_x, w_qkv)
-    conv_in, normed, kv = lax.optimization_barrier((conv_in, normed, kv))
-    kv_before, kv_after = shift(kv, 4), shift(kv, -4)
+    conv_in, kv_before, kv_after, cot_x = lax.optimization_barrier((conv_in, kv_before, kv_after, cot_x))
     gate = ((1664, 128), BF16)
     d_upper, *gate_x = call(
         conv_outer_kernel,
@@ -467,51 +517,58 @@
          pltpu.VMEM((32, 2048), F32), pltpu.VMEM((32, 2048), F32),
          pltpu.VMEM((32, 1024), F32), pltpu.VMEM((2048, ROWS), BF16), pltpu.VMEM((32, 16, 128), BF16)],
         scalars=1,
-    )(place, conv_in, d_gating_in, g_taps_in, d_conv, resid, d_gated, unit, inverse, slope, before, after, conv_kernel)
-    query, d_upper, *gate_x = lax.optimization_barrier((query, d_upper, *gate_x))
+    )(lengths, conv_in, d_gating_in, g_taps_in, d_conv, resid, d_gated, unit, inverse, slope, before, after, conv_kernel)
+    query, gate_x = lax.optimization_barrier((query, gate_x))
     gate_x = turn_x(gate_x)
-    near, d_before, d_after, d_own = call(
+    near, d_query, d_before, d_after, d_own = call(
         attend_kernel,
-        [quad, quad, quad, ((4, ROWS, 256), F32)],
+        [((4, ROWS, 128), BF16), ((ROWS, 512), BF16), quad, quad, ((4, ROWS, 256), F32)],
         [pltpu.VMEM((4, ROWS, 128), BF16),
          pltpu.VMEM((1536, 128), BF16), pltpu.VMEM((1536, 128), BF16),
          pltpu.VMEM((128, 1536), BF16), pltpu.VMEM((128, 1536), BF16),
          pltpu.VMEM((WINDOW, 256), F32), pltpu.VMEM((WINDOW, 256), BF16), pltpu.VMEM((WINDOW, 256), BF16),
          pltpu.VMEM((1536, 128), F32), pltpu.VMEM((1536, 128), F32)],
         scalars=1,
-    )(place, query, kv, kv_before, kv_after, *cot_x, w_out)
+    )(lengths, query, kv, kv_before, kv_after, *cot_x)
     from_before, from_after = shift(d_after, 4), shift(d_before, -4)
     near_x = turn_x([near] * 4)
+    gate_x, d_own = lax.optimization_barrier((gate_x, d_own))
     keep, send, cot_own = call(
         gate_grads_kernel,
         [((8, 112, 512), BF16), ((8, 112, 512), BF16), ((256, 512), BF16)],
-        [pltpu.VMEM((512, 512), BF16), pltpu.VMEM((512, 1024), BF16), pltpu.VMEM((1024, 512), BF16)],
+        [pltpu.VMEM((512, 512), BF16), pltpu.VMEM((512, 1024), BF16)],
         scalars=1,
-    )(place, normed, *cot_x, *gate_x)
-    (far,) = call(join_kernel, [quad])(d_own, from_before, from_after)
-    far_x = turn_x([far] * 4)
-    (gate_parts,) = call(add_kernel, [((8, 112, 512), BF16)])(keep, other_core(send))
-    gate_parts = swap_rows(gate_parts)
-    keep, send, context, joined_t = call(
+    )(lengths, normed, *cot_x, *gate_x)
+    keep, d_own = lax.optimization_barrier((keep, d_own))
+    *far, back_0, back_1, back_2, back_3 = call(
+        join_kernel, [((96, 512), BF16)] * 4 + [small] * 4, [pltpu.VMEM((384, 512), BF16)], scalars=1
+    )(lengths, d_query, d_own, from_before, from_after)
+    far_x = turn_x(far)
+    keep, send = call(
         attention_grads_kernel,
-        [((8, 64, 512), BF16), ((8, 64, 512), BF16), ((ROWS, 512), BF16), ((1536, ROWS), BF16)],
-        [pltpu.VMEM((1536, 512), BF16), pltpu.VMEM((512, 512), BF16), pltpu.VMEM((384, 512), BF16)],
+        [((8, 176, 512), BF16), ((8, 176, 512), BF16)],
+        [pltpu.VMEM((512, 512), BF16), pltpu.VMEM((384, 512), BF16)],
         scalars=1,
-    )(place, normed, cot_own, *near_x, *far_x)
-    (attention_parts,) = call(add_kernel, [((8, 64, 512), BF16)])(keep, other_core(send))
-    attention_parts = swap_rows(attention_parts)
-    layer_out, d_frames = call(rows_kernel, [wide, wide])(
-        frames, cotangent, context, gate_x[0], d_upper, joined_t, w_qkv, w_out, w_up, w_down
+    )(lengths, keep, send, normed, cot_own, *near_x, *far_x)
+    keep, *back = lax.optimization_barrier((keep, back_0, back_1, back_2, back_3))
+    back_x = turn_x(back)
+    (parts,) = call(add_kernel, [((8, 176, 512), BF16, HBM)])(keep, other_core(send))
+    parts = swap_rows(parts)
+    layer_out, d_frames = call(
+        rows_kernel, [wide, wide], [pltpu.VMEM((ROWS, 512), BF16), pltpu.VMEM((1536, ROWS), BF16)], scalars=1
+    )(
+        lengths, frames, cotangent, *near_x, *back_x, gate_x[0], d_upper, *in_hbm(w_qkv, w_out, w_up, w_down)
     )
+    parts, layer_out, d_frames = lax.optimization_barrier((parts, layer_out, d_frames))
     parts = call(
         chunk_sum_kernel, [((176, 128), BF16)] * 4, [pltpu.VMEM((4, 176, 128), BF16)], scalars=1
-    )(place, gate_parts, attention_parts)
+    )(lengths, parts)
     g_qkv, g_out, g_up, g_down, g_kernel = call(
         final_kernel,
         [((48, 128), F32), ((32, HEAD), F32), ((64, 128), F32), ((32, 128), F32), ((TAPS, 32), F32)],
         [pltpu.VMEM((4, 176, 128), F32)],
         scalars=1,
-    )(place, *turn_z(parts))
+    )(lengths, *turn_z(parts))
     return (layer_out[None], d_frames[None], g_qkv.T, g_out.T, g_up.T, g_down.T, g_kernel)
 
 

time: 169 us -> 135 us (0.80)
  blocking collectives: 18.1 us -> 0 us
  local copies, waits for them, and re-layouts: 16.6 us -> 1.94 us
  starting transfers between devices: 58.7 us -> 61.3 us
  waiting for transfers between devices: 34.4 us -> 31.9 us
    all_to_all x1 -> x0, blocking collectives: 18.1 us -> none  [swap_rows(): return lax.all_to_all(array, 'seq', 0, 0, axis_index_groups=ROW_GROUPS)]
    unnamed x52 -> x32, local copies, waits for them, and re-layouts: 16.5 us -> 1.94 us
    ppermute x6, waiting for transfers between devices: 10.6 us -> 0.02 us  [shift(): lax.ppermute(array, 'seq', [(i, i + by) for i in range(32) if 0 <= i + by...]
    ppermute x15 -> x18, waiting for transfers between devices: 16.8 us -> 25.6 us  [turn_x(): lax.ppermute(pieces[by], 'seq', [(i, i // 4 * 4 + (i + by) % 4) for i in...]
    all_to_all x1, waiting for transfers between devices: 4.89 us -> 0.7 us  [swap_rows(): return lax.all_to_all(array, 'seq', 0, 0, axis_index_groups=ROW_GROUPS)]
    ppermute x15 -> x18, starting transfers between devices: 19.7 us -> 23.2 us  [turn_x(): lax.ppermute(pieces[by], 'seq', [(i, i // 4 * 4 + (i + by) % 4) for i in...]
    ppermute x3, waiting for transfers between devices: 0.01 us -> 2.4 us  [turn_z(): lax.ppermute(pieces[by], 'dp', [(i, (i + 2 * by) % 8) for i in range(8)])]
  transfers between devices with their start and end apart: 27 -> 29, of which waited for: 8 -> 13; matrix products, arithmetic and copies ran while one was open for 0% -> 0% of each run, Pallas kernels for 15% -> 22%
where the time goes in v3:
time: 135 us; the launch traced here: 134 us
  starting transfers between devices  61.3 us (45%)
  Pallas kernels  37.3 us (28%)
  waiting for transfers between devices  31.9 us (24%)
  local copies, waits for them, and re-layouts  1.94 us (1%)
  between operations  1.63 us (1%)
    pallas_call x13, Pallas kernels, run(): pl.pallas_call(body, out_shape=[HBM(*out[:2]) if len(out) > 2 else jax.Sh...  37.3 us
    ppermute x18, waiting for transfers between devices, turn_x(): lax.ppermute(pieces[by], 'seq', [(i, i // 4 * 4 + (i + by) % 4) for i in...  25.6 us
    ppermute x18, starting transfers between devices, turn_x(): lax.ppermute(pieces[by], 'seq', [(i, i // 4 * 4 + (i + by) % 4) for i in...  23.2 us
    ppermute x6, starting transfers between devices, shift(): lax.ppermute(array, 'seq', [(i, i + by) for i in range(32) if 0 <= i + by...  19.6 us
    ppermute x3, starting transfers between devices, turn_z(): lax.ppermute(pieces[by], 'dp', [(i, (i + 2 * by) % 8) for i in range(8)])  11.4 us
    all_to_all x1, starting transfers between devices, swap_rows(): return lax.all_to_all(array, 'seq', 0, 0, axis_index_groups=ROW_GROUPS)  7 us
    ppermute x1, waiting for transfers between devices, other_core(): return lax.ppermute(array, 'dp', [(i, i ^ 1) for i in range(8)])  3.21 us
  transfers between devices with their start and end apart: 29, of which 13 were waited for; matrix products, arithmetic and copies ran while one was open for 0% of the time, Pallas kernels for 22%

profile of v3, /device:TPU:8, one launch (start us, length us, event | category | flops | bytes accessed | tf_op | source)
XLA Modules:
  0.0 134.0 jit_solution(6736896513188036767)
XLA Ops:
  0.6 2.8 %collective-permute-start.2 = (bf16[128,1024]{1,0:T(8,128)(2,1)}, bf16[128,1024]{1,0:T(8,128)(2,1)S(1)}, u32[]{:S(2)}, u32[]{:S(2)}) collective-permute-start(bf16[128,1024]{1,0:T(8,128)(2,1)} %bitcast.8), channel_id=1, source_target_pairs={{0,24},{8,0},{16,8},{24,16},{32,56},{40,32},{48,40},{56,48},{64,88... | collective-permute-start | bytes 786440 | tf_op jit(solution)/shard_map/ppermute | solution.py:470
  3.5 0.8 collective-permute-start.1
  4.3 0.9 collective-permute-start
  5.8 5.0 %shard_map.135 = (bf16[128,1024]{1,0:T(8,128)(2,1)S(1)}, bf16[128,1024]{1,0:T(8,128)(2,1)S(1)}, bf16[128,1024]{1,0:T(8,128)(2,1)S(1)}, bf16[128,1024]{1,0:T(8,12...) custom-call(s32[1]{0:T(128)S(6)} %copy.15.lengths, ...), custom_call_target="tpu_custom_call" | custom-call | tf_op jit(solution)/shard_map/pallas_call | solution.py:33
  10.9 4.1 %collective-permute-done.2.frames_3 = bf16[128,1024]{1,0:T(8,128)(2,1)S(1)} collective-permute-done((bf16[128,1024]{1,0:T(8,128)(2,1)}, bf16[128,1024]{1,0:T(8,128)(2,1)S(1)}, u32[]{:S(2)}, u32[]{:S(2)}) %collective-permute-start.2) | collective-permute-done | bytes 262176 | tf_op jit(solution)/shard_map/ppermute | solution.py:470
  15.0 3.6 %collective-permute-done.frames_1 = bf16[128,1024]{1,0:T(8,128)(2,1)S(1)} collective-permute-done((bf16[128,1024]{1,0:T(8,128)(2,1)}, bf16[128,1024]{1,0:T(8,128)(2,1)S(1)}, u32[]{:S(2)}, u32[]{:S(2)}) %collective-permute-start) | collective-permute-done | bytes 262176 | tf_op jit(solution)/shard_map/ppermute | solution.py:470
  18.6 1.3 shard_map.136
  19.9 2.4 %collective-permute-start.4 = (bf16[4,128,256]{2,1,0:T(8,128)(2,1)S(1)}, bf16[4,128,256]{2,1,0:T(8,128)(2,1)S(1)}, u32[]{:S(2)}, u32[]{:S(2)}) collective-permute-start(bf16[4,128,256]{2,1,0:T(8,128)(2,1)S(1)} %get-tuple-element.106.kv), channel_id=1, source_target_pairs={{32,0},{40,8},{48,16},{56,24},{64,32},{72,40},{80,48},{88,56},{96,... | collective-permute-start | bytes 786440 | tf_op jit(solution)/shard_map/ppermute | solution.py:457
  22.3 3.5 %collective-permute-start.3 = (bf16[4,128,256]{2,1,0:T(8,128)(2,1)S(1)}, bf16[4,128,256]{2,1,0:T(8,128)(2,1)S(1)}, u32[]{:S(2)}, u32[]{:S(2)}) collective-permute-start(bf16[4,128,256]{2,1,0:T(8,128)(2,1)S(1)} %get-tuple-element.106.kv), channel_id=1, source_target_pairs={{0,32},{8,40},{16,48},{24,56},{32,64},{40,72},{48,80},{56,88},{64,... | collective-permute-start | bytes 786440 | tf_op jit(solution)/shard_map/ppermute | solution.py:457
  25.8 0.5 shard_map.138
  26.4 2.1 %collective-permute-start.6 = (bf16[384,128]{1,0:T(8,128)(2,1)S(1)}, bf16[384,128]{1,0:T(8,128)(2,1)S(1)}, u32[]{:S(2)}, u32[]{:S(2)}) collective-permute-start(bf16[384,128]{1,0:T(8,128)(2,1)S(1)} %get-tuple-element.110), channel_id=1, source_target_pairs={{0,16},{8,24},{16,0},{24,8},{32,48},{40,56},{48,32},{56,40},{64,80... | collective-permute-start | bytes 294920 | tf_op jit(solution)/shard_map/ppermute | solution.py:470
  28.5 1.4 %collective-permute-start.7 = (bf16[384,128]{1,0:T(8,128)(2,1)S(1)}, bf16[384,128]{1,0:T(8,128)(2,1)S(1)}, u32[]{:S(2)}, u32[]{:S(2)}) collective-permute-start(bf16[384,128]{1,0:T(8,128)(2,1)S(1)} %get-tuple-element.111), channel_id=1, source_target_pairs={{0,24},{8,0},{16,8},{24,16},{32,56},{40,32},{48,40},{56,48},{64,88... | collective-permute-start | bytes 294920 | tf_op jit(solution)/shard_map/ppermute | solution.py:470
  29.8 4.0 %collective-permute-done.5.cot_1 = bf16[384,128]{1,0:T(8,128)(2,1)S(1)} collective-permute-done((bf16[384,128]{1,0:T(8,128)(2,1)S(1)}, bf16[384,128]{1,0:T(8,128)(2,1)S(1)}, u32[]{:S(2)}, u32[]{:S(2)}) %collective-permute-start.5) | collective-permute-done | bytes 98336 | tf_op jit(solution)/shard_map/ppermute | solution.py:470
  33.9 1.9 %collective-permute-start.8 = (bf16[16,2048]{1,0:T(8,128)(2,1)S(1)}, bf16[16,2048]{1,0:T(8,128)(2,1)S(1)}, u32[]{:S(2)}, u32[]{:S(2)}) collective-permute-start(bf16[16,2048]{1,0:T(8,128)(2,1)S(1)} %get-tuple-element.125), channel_id=1, source_target_pairs={{0,8},{8,16},{16,24},{24,32},{32,40},{40,48},{48,56},{56,64},{64,7... | collective-permute-start | bytes 196616 | tf_op jit(solution)/shard_map/ppermute | solution.py:457
  35.8 6.0 %collective-permute-start.9 = (bf16[16,2048]{1,0:T(8,128)(2,1)S(1)}, bf16[16,2048]{1,0:T(8,128)(2,1)S(1)}, u32[]{:S(2)}, u32[]{:S(2)}) collective-permute-start(bf16[16,2048]{1,0:T(8,128)(2,1)S(1)} %get-tuple-element.126), channel_id=1, source_target_pairs={{8,0},{16,8},{24,16},{32,24},{40,32},{48,40},{56,48},{64,56},{72,6... | collective-permute-start | bytes 196616 | tf_op jit(solution)/shard_map/ppermute | solution.py:457
  41.8 7.8 %shard_map.137 = (f32[128,1024]{1,0:T(8,128)S(1)}, f32[128,1024]{1,0:T(8,128)S(1)}, f32[32,1024]{1,0:T(8,128)S(1)}) custom-call(bf16[128,1024]{1,0:T(8,128)(2,1)S(1)} %get-tuple-element.103.gating, bf16[128,1024]{1,0:T(8,128)(2,1)S(1)} %get-tuple-element.104.d_conv, f32[31,1024]{1,0:T(8,128)S(1)} %copy-done.12), custom_call_target="tpu_custom_call" | custom-call | tf_op jit(solution)/shard_map/pallas_call | solution.py:33
  49.7 2.8 %shard_map.139 = (bf16[128,2048]{1,0:T(8,128)(2,1)}, bf16[1664,128]{1,0:T(8,128)(2,1)S(1)}, bf16[1664,128]{1,0:T(8,128)(2,1)S(1)}, bf16[1664,128]{1,0:T(8,128)(2,1)S(1)}, bf16[1664,128]{1,0:T(8,128)(2,1)S(1)}) custom-call(s32[1]{0:T(128)S(6)} %copy.15.lengths, f32[128,1024]{1,0:T(8,128)S(1)} %get-tuple-element.117.conv_in, ...), custom_call_target="tpu_custom_call" | custom-call | tf_op jit(solution)/shard_map/pallas_call | solution.py:33
  52.5 1.6 %collective-permute-start.11 = (bf16[1664,128]{1,0:T(8,128)(2,1)S(1)}, bf16[1664,128]{1,0:T(8,128)(2,1)S(1)}, u32[]{:S(2)}, u32[]{:S(2)}) collective-permute-start(bf16[1664,128]{1,0:T(8,128)(2,1)S(1)} %get-tuple-element.133), channel_id=1, source_target_pairs={{0,16},{8,24},{16,0},{24,8},{32,48},{40,56},{48,32},{56,40},{64,80... | collective-permute-start | bytes 1277960 | tf_op jit(solution)/shard_map/ppermute | solution.py:470
  54.1 1.6 %collective-permute-start.12 = (bf16[1664,128]{1,0:T(8,128)(2,1)S(1)}, bf16[1664,128]{1,0:T(8,128)(2,1)S(1)}, u32[]{:S(2)}, u32[]{:S(2)}) collective-permute-start(bf16[1664,128]{1,0:T(8,128)(2,1)S(1)} %get-tuple-element.134), channel_id=1, source_target_pairs={{0,24},{8,0},{16,8},{24,16},{32,56},{40,32},{48,40},{56,48},{64,88... | collective-permute-start | bytes 1277960 | tf_op jit(solution)/shard_map/ppermute | solution.py:470
  55.7 6.5 %shard_map.140 = (bf16[4,128,128]{2,1,0:T(8,128)(2,1)S(1)}, bf16[128,512]{1,0:T(8,128)(2,1)S(1)}, bf16[4,128,256]{2,1,0:T(8,128)(2,1)S(1)}, bf16[4,128,256]{2,1,0:T(8,128)(2,1)S(1)}, f32[4,128,256]{2,1,0:T(8,128)S(1)}) custom-call(s32[1]{0:T(128)S(6)} %copy.15.lengths, bf16[4,128,128]{2,1,0:T(8,128)(2,1)S(1)} %get-tuple-element.135.queries, ...), custom_call_target="tpu_custom_call" | custom-call | tf_op jit(solution)/shard_map/pallas_call | solution.py:33
  62.3 3.7 %collective-permute-start.16 = (bf16[4,128,256]{2,1,0:T(8,128)(2,1)S(1)}, bf16[4,128,256]{2,1,0:T(8,128)(2,1)S(1)}, u32[]{:S(2)}, u32[]{:S(2)}) collective-permute-start(bf16[4,128,256]{2,1,0:T(8,128)(2,1)S(1)} %get-tuple-element.151), channel_id=1, source_target_pairs={{0,32},{8,40},{16,48},{24,56},{32,64},{40,72},{48,80},{56,88},{64,... | collective-permute-start | bytes 786440 | tf_op jit(solution)/shard_map/ppermute | solution.py:457
  65.9 2.2 %collective-permute-start.17 = (bf16[4,128,256]{2,1,0:T(8,128)(2,1)S(1)}, bf16[4,128,256]{2,1,0:T(8,128)(2,1)S(1)}, u32[]{:S(2)}, u32[]{:S(2)}) collective-permute-start(bf16[4,128,256]{2,1,0:T(8,128)(2,1)S(1)} %get-tuple-element.152), channel_id=1, source_target_pairs={{32,0},{40,8},{48,16},{56,24},{64,32},{72,40},{80,48},{88,56},{96,... | collective-permute-start | bytes 786440 | tf_op jit(solution)/shard_map/ppermute | solution.py:457
  68.1 4.9 %collective-permute-done.10.gate_1 = bf16[1664,128]{1,0:T(8,128)(2,1)S(1)} collective-permute-done((bf16[1664,128]{1,0:T(8,128)(2,1)S(1)}, bf16[1664,128]{1,0:T(8,128)(2,1)S(1)}, u32[]{:S(2)}, u32[]{:S(2)}) %collective-permute-start.10) | collective-permute-done | bytes 426016 | tf_op jit(solution)/shard_map/ppermute | solution.py:470
  73.1 2.0 %collective-permute-done.12.gate_3 = bf16[1664,128]{1,0:T(8,128)(2,1)S(1)} collective-permute-done((bf16[1664,128]{1,0:T(8,128)(2,1)S(1)}, bf16[1664,128]{1,0:T(8,128)(2,1)S(1)}, u32[]{:S(2)}, u32[]{:S(2)}) %collective-permute-start.12) | collective-permute-done | bytes 426016 | tf_op jit(solution)/shard_map/ppermute | solution.py:470
  75.2 1.4 %shard_map.141 = (bf16[8,112,512]{2,1,0:T(8,128)(2,1)S(1)}, bf16[8,112,512]{2,1,0:T(8,128)(2,1)S(1)}, bf16[256,512]{1,0:T(8,128)(2,1)S(1)}) custom-call(s32[1]{0:T(128)S(6)} %copy.15.lengths, bf16[512,1024]{1,0:T(8,128)(2,1)S(1)} %get-tuple-element.100.normed, bf16[384,128]{1,0:T(8,128)(2,1)S(1)} %get-tuple-element.112.cot_0, ...), custom_call_target="tpu_custom_call" | custom-call | tf_op jit(solution)/shard_map/pallas_call | solution.py:33
  76.9 0.6 copy-done.13
  77.5 0.6 copy-done.14
  78.1 0.6 copy-done.15
  78.7 1.4 %collective-permute-start.18 = (bf16[96,512]{1,0:T(8,128)(2,1)S(1)}, bf16[96,512]{1,0:T(8,128)(2,1)S(1)}, u32[]{:S(2)}, u32[]{:S(2)}) collective-permute-start(bf16[96,512]{1,0:T(8,128)(2,1)S(1)} %get-tuple-element.154), channel_id=1, source_target_pairs={{0,8},{8,16},{16,24},{24,0},{32,40},{40,48},{48,56},{56,32},{64,72... | collective-permute-start | bytes 294920 | tf_op jit(solution)/shard_map/ppermute | solution.py:470
  80.1 3.2 %collective-permute-start.19 = (bf16[96,512]{1,0:T(8,128)(2,1)S(1)}, bf16[96,512]{1,0:T(8,128)(2,1)S(1)}, u32[]{:S(2)}, u32[]{:S(2)}) collective-permute-start(bf16[96,512]{1,0:T(8,128)(2,1)S(1)} %get-tuple-element.155), channel_id=1, source_target_pairs={{0,16},{8,24},{16,0},{24,8},{32,48},{40,56},{48,32},{56,40},{64,80... | collective-permute-start | bytes 294920 | tf_op jit(solution)/shard_map/ppermute | solution.py:470
  83.4 2.1 %collective-permute-start.20 = (bf16[96,512]{1,0:T(8,128)(2,1)S(1)}, bf16[96,512]{1,0:T(8,128)(2,1)S(1)}, u32[]{:S(2)}, u32[]{:S(2)}) collective-permute-start(bf16[96,512]{1,0:T(8,128)(2,1)S(1)} %get-tuple-element.156), channel_id=1, source_target_pairs={{0,24},{8,0},{16,8},{24,16},{32,56},{40,32},{48,40},{56,48},{64,88... | collective-permute-start | bytes 294920 | tf_op jit(solution)/shard_map/ppermute | solution.py:470
  85.5 1.5 %collective-permute-done.19.far_2 = bf16[96,512]{1,0:T(8,128)(2,1)S(1)} collective-permute-done((bf16[96,512]{1,0:T(8,128)(2,1)S(1)}, bf16[96,512]{1,0:T(8,128)(2,1)S(1)}, u32[]{:S(2)}, u32[]{:S(2)}) %collective-permute-start.19) | collective-permute-done | bytes 98336 | tf_op jit(solution)/shard_map/ppermute | solution.py:470
  87.0 1.0 collective-permute-done.20.far_3
  88.0 1.3 shard_map.143
  89.4 3.2 %collective-permute-done.21.far = bf16[8,176,512]{2,1,0:T(8,128)(2,1)S(1)} collective-permute-done((bf16[8,176,512]{2,1,0:T(8,128)(2,1)S(1)}, bf16[8,176,512]{2,1,0:T(8,128)(2,1)S(1)}, u32[]{:S(2)}, u32[]{:S(2)}) %collective-permute-start.21) | collective-permute-done | bytes 1441824 | tf_op jit(solution)/shard_map/ppermute | solution.py:461
  92.6 1.5 %shard_map.144 = bf16[8,176,512]{2,1,0:T(8,128)(2,1)} custom-call(bf16[8,176,512]{2,1,0:T(8,128)(2,1)S(1)} %get-tuple-element.162.near, bf16[8,176,512]{2,1,0:T(8,128)(2,1)S(1)} %collective-permute-done.21.far), custom_call_target="tpu_custom_call" | custom-call | tf_op jit(solution)/shard_map/pallas_call | solution.py:33
  94.1 7.0 %all-to-all-start = ((bf16[8,176,512]{2,1,0:T(8,128)(2,1)}), bf16[8,176,512]{2,1,0:T(8,128)(2,1)S(1)}, u32[]{:S(2)}, u32[]{:S(2)}) async-start(bf16[8,176,512]{2,1,0:T(8,128)(2,1)} %shard_map.144), calls=%async_computation | async-start | bytes 2883584 | tf_op jit(solution)/shard_map/all_to_all | solution.py:465
  101.1 0.9 collective-permute-start.22
  102.0 3.8 %collective-permute-start.23 = (bf16[384,128]{1,0:T(8,128)(2,1)}, bf16[384,128]{1,0:T(8,128)(2,1)S(1)}, u32[]{:S(2)}, u32[]{:S(2)}) collective-permute-start(bf16[384,128]{1,0:T(8,128)(2,1)} %copy-done.14), channel_id=1, source_target_pairs={{0,16},{8,24},{16,0},{24,8},{32,48},{40,56},{48,32},{56,40},{64,80... | collective-permute-start | bytes 294920 | tf_op jit(solution)/shard_map/ppermute | solution.py:470
  106.2 0.9 collective-permute-done.22.back_1
  107.1 3.2 %collective-permute-done.23.back_2 = bf16[384,128]{1,0:T(8,128)(2,1)S(1)} collective-permute-done((bf16[384,128]{1,0:T(8,128)(2,1)}, bf16[384,128]{1,0:T(8,128)(2,1)S(1)}, u32[]{:S(2)}, u32[]{:S(2)}) %collective-permute-start.23) | collective-permute-done | bytes 98336 | tf_op jit(solution)/shard_map/ppermute | solution.py:470
  110.6 7.9 %shard_map.145 = (bf16[128,1024]{1,0:T(8,128)(2,1)}, bf16[128,1024]{1,0:T(8,128)(2,1)}) custom-call(s32[1]{0:T(128)S(6)} %copy.15.lengths, bf16[128,1024]{1,0:T(8,128)(2,1)S(1)} %bitcast.13, bf16[128,1024]{1,0:T(8,128)(2,1)S(1)} %bitcast.16, bf16[4,128,128]{2,1,0:T(8,128)(2,1)S(1)} %get-tuple-element.148.near_0, bf16[4,128,128]{2,1,0:T(8,128)(2,1)S(1)} %copy-done.10, ...), custom_call_target="tpu_custom_call" | custom-call | tf_op jit(solution)/shard_map/pallas_call | solution.py:33
  118.5 0.7 all-to-all-done.parts
  119.4 3.3 %collective-permute-start.25 = (bf16[176,128]{1,0:T(8,128)(2,1)S(1)}, bf16[176,128]{1,0:T(8,128)(2,1)S(1)}, u32[]{:S(2)}, u32[]{:S(2)}) collective-permute-start(bf16[176,128]{1,0:T(8,128)(2,1)S(1)} %get-tuple-element.175), channel_id=1, source_target_pairs={{0,2},{1,3},{2,4},{3,5},{4,6},{5,7},{6,0},{7,1},{8,10},{9,11},{10,... | collective-permute-start | bytes 135176 | tf_op jit(solution)/shard_map/ppermute | solution.py:477
  122.8 5.4 %collective-permute-start.26 = (bf16[176,128]{1,0:T(8,128)(2,1)S(1)}, bf16[176,128]{1,0:T(8,128)(2,1)S(1)}, u32[]{:S(2)}, u32[]{:S(2)}) collective-permute-start(bf16[176,128]{1,0:T(8,128)(2,1)S(1)} %get-tuple-element.176), channel_id=1, source_target_pairs={{0,4},{1,5},{2,6},{3,7},{4,0},{5,1},{6,2},{7,3},{8,12},{9,13},{10,... | collective-permute-start | bytes 135176 | tf_op jit(solution)/shard_map/ppermute | solution.py:477
  128.2 2.7 %collective-permute-start.27 = (bf16[176,128]{1,0:T(8,128)(2,1)S(1)}, bf16[176,128]{1,0:T(8,128)(2,1)S(1)}, u32[]{:S(2)}, u32[]{:S(2)}) collective-permute-start(bf16[176,128]{1,0:T(8,128)(2,1)S(1)} %get-tuple-element.177), channel_id=1, source_target_pairs={{0,6},{1,7},{2,0},{3,1},{4,2},{5,3},{6,4},{7,5},{8,14},{9,15},{10,... | collective-permute-start | bytes 135176 | tf_op jit(solution)/shard_map/ppermute | solution.py:477
  130.9 2.4 %collective-permute-done.27.part_3 = bf16[176,128]{1,0:T(8,128)(2,1)S(1)} collective-permute-done((bf16[176,128]{1,0:T(8,128)(2,1)S(1)}, bf16[176,128]{1,0:T(8,128)(2,1)S(1)}, u32[]{:S(2)}, u32[]{:S(2)}) %collective-permute-start.27) | collective-permute-done | bytes 45088 | tf_op jit(solution)/shard_map/ppermute | solution.py:477
  133.2 0.8 shard_map.147
  (55 shorter events, 1.6 us)
Async XLA Ops:
  0.6 14.4 %collective-permute-start.2 = (bf16[128,1024]{1,0:T(8,128)(2,1)}, bf16[128,1024]{1,0:T(8,128)(2,1)S(1)}, u32[]{:S(2)}, u32[]{:S(2)}) collective-permute-start(bf16[128,1024]{1,0:T(8,128)(2,1)} %bitcast.8), channel_id=1, source_target_pairs={{0,24},{8,0},{16,8},{24,16},{32,56},{40,32},{48,40},{56,48},{64,88... | collective-permute-start | bytes 786440 | tf_op jit(solution)/shard_map/ppermute | solution.py:470
  3.5 11.5 %collective-permute-start.1 = (bf16[128,1024]{1,0:T(8,128)(2,1)}, bf16[128,1024]{1,0:T(8,128)(2,1)S(1)}, u32[]{:S(2)}, u32[]{:S(2)}) collective-permute-start(bf16[128,1024]{1,0:T(8,128)(2,1)} %bitcast.9), channel_id=1, source_target_pairs={{0,16},{8,24},{16,0},{24,8},{32,48},{40,56},{48,32},{56,40},{64,80... | collective-permute-start | bytes 786440 | tf_op jit(solution)/shard_map/ppermute | solution.py:470
  4.3 14.3 %collective-permute-start = (bf16[128,1024]{1,0:T(8,128)(2,1)}, bf16[128,1024]{1,0:T(8,128)(2,1)S(1)}, u32[]{:S(2)}, u32[]{:S(2)}) collective-permute-start(bf16[128,1024]{1,0:T(8,128)(2,1)} %bitcast.10), channel_id=1, source_target_pairs={{0,8},{8,16},{16,24},{24,0},{32,40},{40,48},{48,56},{56,32},{64,72... | collective-permute-start | bytes 786440 | tf_op jit(solution)/shard_map/ppermute | solution.py:470
  5.8 12.8 %copy-start = (bf16[1024,1536]{1,0:T(8,128)(2,1)S(1)}, bf16[1024,1536]{1,0:T(8,128)(2,1)}, u32[]{:S(2)}) copy-start(bf16[1024,1536]{1,0:T(8,128)(2,1)} %w_qkv.3) | copy-start | bytes 9437188
  5.8 12.8 %copy-start.2 = (bf16[1,128,1024]{2,1,0:T(8,128)(2,1)S(1)}, bf16[1,128,1024]{2,1,0:T(8,128)(2,1)}, u32[]{:S(2)}) copy-start(bf16[1,128,1024]{2,1,0:T(8,128)(2,1)} %param.8) | copy-start | bytes 786436
  18.6 7.2 %copy-start.1 = (bf16[512,1024]{1,0:T(8,128)(2,1)S(1)}, bf16[512,1024]{1,0:T(8,128)(2,1)}, u32[]{:S(2)}) copy-start(bf16[512,1024]{1,0:T(8,128)(2,1)} %w_out.3) | copy-start | bytes 3145732
  18.6 7.2 %copy-start.3 = (bf16[1,128,1024]{2,1,0:T(8,128)(2,1)S(1)}, bf16[1,128,1024]{2,1,0:T(8,128)(2,1)}, u32[]{:S(2)}) copy-start(bf16[1,128,1024]{2,1,0:T(8,128)(2,1)} %param.9) | copy-start | bytes 786436
  18.6 23.2 %copy-start.12 = (f32[31,1024]{1,0:T(8,128)S(1)}, f32[31,1024]{1,0:T(8,128)}, u32[]{:S(2)}) copy-start(f32[31,1024]{1,0:T(8,128)} %taps.3) | copy-start | bytes 380932
  19.9 29.8 %collective-permute-start.4 = (bf16[4,128,256]{2,1,0:T(8,128)(2,1)S(1)}, bf16[4,128,256]{2,1,0:T(8,128)(2,1)S(1)}, u32[]{:S(2)}, u32[]{:S(2)}) collective-permute-start(bf16[4,128,256]{2,1,0:T(8,128)(2,1)S(1)} %get-tuple-element.106.kv), channel_id=1, source_target_pairs={{32,0},{40,8},{48,16},{56,24},{64,32},{72,40},{80,48},{88,56},{96,... | collective-permute-start | bytes 786440 | tf_op jit(solution)/shard_map/ppermute | solution.py:457
  22.3 27.4 %collective-permute-start.3 = (bf16[4,128,256]{2,1,0:T(8,128)(2,1)S(1)}, bf16[4,128,256]{2,1,0:T(8,128)(2,1)S(1)}, u32[]{:S(2)}, u32[]{:S(2)}) collective-permute-start(bf16[4,128,256]{2,1,0:T(8,128)(2,1)S(1)} %get-tuple-element.106.kv), channel_id=1, source_target_pairs={{0,32},{8,40},{16,48},{24,56},{32,64},{40,72},{48,80},{56,88},{64,... | collective-permute-start | bytes 786440 | tf_op jit(solution)/shard_map/ppermute | solution.py:457
  26.3 7.6 %collective-permute-start.5 = (bf16[384,128]{1,0:T(8,128)(2,1)S(1)}, bf16[384,128]{1,0:T(8,128)(2,1)S(1)}, u32[]{:S(2)}, u32[]{:S(2)}) collective-permute-start(bf16[384,128]{1,0:T(8,128)(2,1)S(1)} %get-tuple-element.109), channel_id=1, source_target_pairs={{0,8},{8,16},{16,24},{24,0},{32,40},{40,48},{48,56},{56,32},{64,72... | collective-permute-start | bytes 294920 | tf_op jit(solution)/shard_map/ppermute | solution.py:470
  26.4 9.4 %collective-permute-start.6 = (bf16[384,128]{1,0:T(8,128)(2,1)S(1)}, bf16[384,128]{1,0:T(8,128)(2,1)S(1)}, u32[]{:S(2)}, u32[]{:S(2)}) collective-permute-start(bf16[384,128]{1,0:T(8,128)(2,1)S(1)} %get-tuple-element.110), channel_id=1, source_target_pairs={{0,16},{8,24},{16,0},{24,8},{32,48},{40,56},{48,32},{56,40},{64,80... | collective-permute-start | bytes 294920 | tf_op jit(solution)/shard_map/ppermute | solution.py:470
  28.5 21.2 %collective-permute-start.7 = (bf16[384,128]{1,0:T(8,128)(2,1)S(1)}, bf16[384,128]{1,0:T(8,128)(2,1)S(1)}, u32[]{:S(2)}, u32[]{:S(2)}) collective-permute-start(bf16[384,128]{1,0:T(8,128)(2,1)S(1)} %get-tuple-element.111), channel_id=1, source_target_pairs={{0,24},{8,0},{16,8},{24,16},{32,56},{40,32},{48,40},{56,48},{64,88... | collective-permute-start | bytes 294920 | tf_op jit(solution)/shard_map/ppermute | solution.py:470
  33.9 15.8 %collective-permute-start.8 = (bf16[16,2048]{1,0:T(8,128)(2,1)S(1)}, bf16[16,2048]{1,0:T(8,128)(2,1)S(1)}, u32[]{:S(2)}, u32[]{:S(2)}) collective-permute-start(bf16[16,2048]{1,0:T(8,128)(2,1)S(1)} %get-tuple-element.125), channel_id=1, source_target_pairs={{0,8},{8,16},{16,24},{24,32},{32,40},{40,48},{48,56},{56,64},{64,7... | collective-permute-start | bytes 196616 | tf_op jit(solution)/shard_map/ppermute | solution.py:457
  35.8 13.9 %collective-permute-start.9 = (bf16[16,2048]{1,0:T(8,128)(2,1)S(1)}, bf16[16,2048]{1,0:T(8,128)(2,1)S(1)}, u32[]{:S(2)}, u32[]{:S(2)}) collective-permute-start(bf16[16,2048]{1,0:T(8,128)(2,1)S(1)} %get-tuple-element.126), channel_id=1, source_target_pairs={{8,0},{16,8},{24,16},{32,24},{40,32},{48,40},{56,48},{64,56},{72,6... | collective-permute-start | bytes 196616 | tf_op jit(solution)/shard_map/ppermute | solution.py:457
  52.5 20.6 %collective-permute-start.10 = (bf16[1664,128]{1,0:T(8,128)(2,1)S(1)}, bf16[1664,128]{1,0:T(8,128)(2,1)S(1)}, u32[]{:S(2)}, u32[]{:S(2)}) collective-permute-start(bf16[1664,128]{1,0:T(8,128)(2,1)S(1)} %get-tuple-element.132), channel_id=1, source_target_pairs={{0,8},{8,16},{16,24},{24,0},{32,40},{40,48},{48,56},{56,32},{64,72... | collective-permute-start | bytes 1277960 | tf_op jit(solution)/shard_map/ppermute | solution.py:470
  52.5 20.6 %collective-permute-start.11 = (bf16[1664,128]{1,0:T(8,128)(2,1)S(1)}, bf16[1664,128]{1,0:T(8,128)(2,1)S(1)}, u32[]{:S(2)}, u32[]{:S(2)}) collective-permute-start(bf16[1664,128]{1,0:T(8,128)(2,1)S(1)} %get-tuple-element.133), channel_id=1, source_target_pairs={{0,16},{8,24},{16,0},{24,8},{32,48},{40,56},{48,32},{56,40},{64,80... | collective-permute-start | bytes 1277960 | tf_op jit(solution)/shard_map/ppermute | solution.py:470
  54.1 21.0 %collective-permute-start.12 = (bf16[1664,128]{1,0:T(8,128)(2,1)S(1)}, bf16[1664,128]{1,0:T(8,128)(2,1)S(1)}, u32[]{:S(2)}, u32[]{:S(2)}) collective-permute-start(bf16[1664,128]{1,0:T(8,128)(2,1)S(1)} %get-tuple-element.134), channel_id=1, source_target_pairs={{0,24},{8,0},{16,8},{24,16},{32,56},{40,32},{48,40},{56,48},{64,88... | collective-permute-start | bytes 1277960 | tf_op jit(solution)/shard_map/ppermute | solution.py:470
  62.3 14.3 %collective-permute-start.16 = (bf16[4,128,256]{2,1,0:T(8,128)(2,1)S(1)}, bf16[4,128,256]{2,1,0:T(8,128)(2,1)S(1)}, u32[]{:S(2)}, u32[]{:S(2)}) collective-permute-start(bf16[4,128,256]{2,1,0:T(8,128)(2,1)S(1)} %get-tuple-element.151), channel_id=1, source_target_pairs={{0,32},{8,40},{16,48},{24,56},{32,64},{40,72},{48,80},{56,88},{64,... | collective-permute-start | bytes 786440 | tf_op jit(solution)/shard_map/ppermute | solution.py:457
  65.9 10.6 %collective-permute-start.17 = (bf16[4,128,256]{2,1,0:T(8,128)(2,1)S(1)}, bf16[4,128,256]{2,1,0:T(8,128)(2,1)S(1)}, u32[]{:S(2)}, u32[]{:S(2)}) collective-permute-start(bf16[4,128,256]{2,1,0:T(8,128)(2,1)S(1)} %get-tuple-element.152), channel_id=1, source_target_pairs={{32,0},{40,8},{48,16},{56,24},{64,32},{72,40},{80,48},{88,56},{96,... | collective-permute-start | bytes 786440 | tf_op jit(solution)/shard_map/ppermute | solution.py:457
  73.1 10.3 %collective-permute-start.15 = (bf16[4,128,128]{2,1,0:T(8,128)(2,1)S(1)}, bf16[4,128,128]{2,1,0:T(8,128)(2,1)S(1)}, u32[]{:S(2)}, u32[]{:S(2)}) collective-permute-start(bf16[4,128,128]{2,1,0:T(8,128)(2,1)S(1)} %get-tuple-element.148.near_0), channel_id=1, source_target_pairs={{0,24},{8,0},{16,8},{24,16},{32,56},{40,32},{48,40},{56,48},{64,88... | collective-permute-start | bytes 393224 | tf_op jit(solution)/shard_map/ppermute | solution.py:470
  73.1 12.4 %collective-permute-start.14 = (bf16[4,128,128]{2,1,0:T(8,128)(2,1)S(1)}, bf16[4,128,128]{2,1,0:T(8,128)(2,1)S(1)}, u32[]{:S(2)}, u32[]{:S(2)}) collective-permute-start(bf16[4,128,128]{2,1,0:T(8,128)(2,1)S(1)} %get-tuple-element.148.near_0), channel_id=1, source_target_pairs={{0,16},{8,24},{16,0},{24,8},{32,48},{40,56},{48,32},{56,40},{64,80... | collective-permute-start | bytes 393224 | tf_op jit(solution)/shard_map/ppermute | solution.py:470
  75.1 10.3 %collective-permute-start.13 = (bf16[4,128,128]{2,1,0:T(8,128)(2,1)S(1)}, bf16[4,128,128]{2,1,0:T(8,128)(2,1)S(1)}, u32[]{:S(2)}, u32[]{:S(2)}) collective-permute-start(bf16[4,128,128]{2,1,0:T(8,128)(2,1)S(1)} %get-tuple-element.148.near_0), channel_id=1, source_target_pairs={{0,8},{8,16},{16,24},{24,0},{32,40},{40,48},{48,56},{56,32},{64,72... | collective-permute-start | bytes 393224 | tf_op jit(solution)/shard_map/ppermute | solution.py:470
  76.8 0.6 copy-start.13
  77.5 0.6 copy-start.14
  78.1 0.6 copy-start.15
  78.7 6.7 %collective-permute-start.18 = (bf16[96,512]{1,0:T(8,128)(2,1)S(1)}, bf16[96,512]{1,0:T(8,128)(2,1)S(1)}, u32[]{:S(2)}, u32[]{:S(2)}) collective-permute-start(bf16[96,512]{1,0:T(8,128)(2,1)S(1)} %get-tuple-element.154), channel_id=1, source_target_pairs={{0,8},{8,16},{16,24},{24,0},{32,40},{40,48},{48,56},{56,32},{64,72... | collective-permute-start | bytes 294920 | tf_op jit(solution)/shard_map/ppermute | solution.py:470
  80.1 6.9 %collective-permute-start.19 = (bf16[96,512]{1,0:T(8,128)(2,1)S(1)}, bf16[96,512]{1,0:T(8,128)(2,1)S(1)}, u32[]{:S(2)}, u32[]{:S(2)}) collective-permute-start(bf16[96,512]{1,0:T(8,128)(2,1)S(1)} %get-tuple-element.155), channel_id=1, source_target_pairs={{0,16},{8,24},{16,0},{24,8},{32,48},{40,56},{48,32},{56,40},{64,80... | collective-permute-start | bytes 294920 | tf_op jit(solution)/shard_map/ppermute | solution.py:470
  83.4 5.9 %copy-start.5 = (bf16[4,128,128]{2,1,0:T(8,128)(2,1)}, bf16[4,128,128]{2,1,0:T(8,128)(2,1)S(1)}, u32[]{:S(2)}) copy-start(bf16[4,128,128]{2,1,0:T(8,128)(2,1)S(1)} %collective-permute-done.15.near_3) | copy-start | bytes 393220
  83.4 4.6 %collective-permute-start.20 = (bf16[96,512]{1,0:T(8,128)(2,1)S(1)}, bf16[96,512]{1,0:T(8,128)(2,1)S(1)}, u32[]{:S(2)}, u32[]{:S(2)}) collective-permute-start(bf16[96,512]{1,0:T(8,128)(2,1)S(1)} %get-tuple-element.156), channel_id=1, source_target_pairs={{0,24},{8,0},{16,8},{24,16},{32,56},{40,32},{48,40},{56,48},{64,88... | collective-permute-start | bytes 294920 | tf_op jit(solution)/shard_map/ppermute | solution.py:470
  85.4 3.8 %copy-start.7 = (bf16[4,128,128]{2,1,0:T(8,128)(2,1)}, bf16[4,128,128]{2,1,0:T(8,128)(2,1)S(1)}, u32[]{:S(2)}) copy-start(bf16[4,128,128]{2,1,0:T(8,128)(2,1)S(1)} %collective-permute-done.14.near_2) | copy-start | bytes 393220
  85.5 3.8 %copy-start.9 = (bf16[4,128,128]{2,1,0:T(8,128)(2,1)}, bf16[4,128,128]{2,1,0:T(8,128)(2,1)S(1)}, u32[]{:S(2)}) copy-start(bf16[4,128,128]{2,1,0:T(8,128)(2,1)S(1)} %collective-permute-done.13.near_1) | copy-start | bytes 393220
  89.3 3.3 %collective-permute-start.21 = (bf16[8,176,512]{2,1,0:T(8,128)(2,1)S(1)}, bf16[8,176,512]{2,1,0:T(8,128)(2,1)S(1)}, u32[]{:S(2)}, u32[]{:S(2)}) collective-permute-start(bf16[8,176,512]{2,1,0:T(8,128)(2,1)S(1)} %get-tuple-element.163), channel_id=1, source_target_pairs={{0,1},{1,0},{2,3},{3,2},{4,5},{5,4},{6,7},{7,6},{8,9},{9,8},{10,11... | collective-permute-start | bytes 4325384 | tf_op jit(solution)/shard_map/ppermute | solution.py:461
  94.1 16.5 %copy-start.4 = (bf16[1,128,1024]{2,1,0:T(8,128)(2,1)S(1)}, bf16[1,128,1024]{2,1,0:T(8,128)(2,1)}, u32[]{:S(2)}) copy-start(bf16[1,128,1024]{2,1,0:T(8,128)(2,1)} %param.9) | copy-start | bytes 786436
  94.1 16.5 %copy-start.6 = (bf16[4,128,128]{2,1,0:T(8,128)(2,1)S(1)}, bf16[4,128,128]{2,1,0:T(8,128)(2,1)}, u32[]{:S(2)}) copy-start(bf16[4,128,128]{2,1,0:T(8,128)(2,1)} %copy-done.5) | copy-start | bytes 393220
  94.1 16.5 %copy-start.8 = (bf16[4,128,128]{2,1,0:T(8,128)(2,1)S(1)}, bf16[4,128,128]{2,1,0:T(8,128)(2,1)}, u32[]{:S(2)}) copy-start(bf16[4,128,128]{2,1,0:T(8,128)(2,1)} %copy-done.7) | copy-start | bytes 393220
  94.1 16.5 %copy-start.10 = (bf16[4,128,128]{2,1,0:T(8,128)(2,1)S(1)}, bf16[4,128,128]{2,1,0:T(8,128)(2,1)}, u32[]{:S(2)}) copy-start(bf16[4,128,128]{2,1,0:T(8,128)(2,1)} %copy-done.9) | copy-start | bytes 393220
  94.1 16.5 %copy-start.11 = (bf16[128,2048]{1,0:T(8,128)(2,1)S(1)}, bf16[128,2048]{1,0:T(8,128)(2,1)}, u32[]{:S(2)}) copy-start(bf16[128,2048]{1,0:T(8,128)(2,1)} %get-tuple-element.168.d_upper) | copy-start | bytes 1572868
  94.1 25.2 %all-to-all-start = ((bf16[8,176,512]{2,1,0:T(8,128)(2,1)}), bf16[8,176,512]{2,1,0:T(8,128)(2,1)S(1)}, u32[]{:S(2)}, u32[]{:S(2)}) async-start(bf16[8,176,512]{2,1,0:T(8,128)(2,1)} %shard_map.144), calls=%async_computation | async-start | bytes 2883584 | tf_op jit(solution)/shard_map/all_to_all | solution.py:465
  101.1 6.0 %collective-permute-start.22 = (bf16[384,128]{1,0:T(8,128)(2,1)}, bf16[384,128]{1,0:T(8,128)(2,1)S(1)}, u32[]{:S(2)}, u32[]{:S(2)}) collective-permute-start(bf16[384,128]{1,0:T(8,128)(2,1)} %copy-done.15), channel_id=1, source_target_pairs={{0,8},{8,16},{16,24},{24,0},{32,40},{40,48},{48,56},{56,32},{64,72... | collective-permute-start | bytes 294920 | tf_op jit(solution)/shard_map/ppermute | solution.py:470
  102.0 8.3 %collective-permute-start.23 = (bf16[384,128]{1,0:T(8,128)(2,1)}, bf16[384,128]{1,0:T(8,128)(2,1)S(1)}, u32[]{:S(2)}, u32[]{:S(2)}) collective-permute-start(bf16[384,128]{1,0:T(8,128)(2,1)} %copy-done.14), channel_id=1, source_target_pairs={{0,16},{8,24},{16,0},{24,8},{32,48},{40,56},{48,32},{56,40},{64,80... | collective-permute-start | bytes 294920 | tf_op jit(solution)/shard_map/ppermute | solution.py:470
  105.8 4.8 %collective-permute-start.24 = (bf16[384,128]{1,0:T(8,128)(2,1)}, bf16[384,128]{1,0:T(8,128)(2,1)S(1)}, u32[]{:S(2)}, u32[]{:S(2)}) collective-permute-start(bf16[384,128]{1,0:T(8,128)(2,1)} %copy-done.13), channel_id=1, source_target_pairs={{0,24},{8,0},{16,8},{24,16},{32,56},{40,32},{48,40},{56,48},{64,88... | collective-permute-start | bytes 294920 | tf_op jit(solution)/shard_map/ppermute | solution.py:470
  119.4 11.4 %collective-permute-start.25 = (bf16[176,128]{1,0:T(8,128)(2,1)S(1)}, bf16[176,128]{1,0:T(8,128)(2,1)S(1)}, u32[]{:S(2)}, u32[]{:S(2)}) collective-permute-start(bf16[176,128]{1,0:T(8,128)(2,1)S(1)} %get-tuple-element.175), channel_id=1, source_target_pairs={{0,2},{1,3},{2,4},{3,5},{4,6},{5,7},{6,0},{7,1},{8,10},{9,11},{10,... | collective-permute-start | bytes 135176 | tf_op jit(solution)/shard_map/ppermute | solution.py:477
  122.8 8.1 %collective-permute-start.26 = (bf16[176,128]{1,0:T(8,128)(2,1)S(1)}, bf16[176,128]{1,0:T(8,128)(2,1)S(1)}, u32[]{:S(2)}, u32[]{:S(2)}) collective-permute-start(bf16[176,128]{1,0:T(8,128)(2,1)S(1)} %get-tuple-element.176), channel_id=1, source_target_pairs={{0,4},{1,5},{2,6},{3,7},{4,0},{5,1},{6,2},{7,3},{8,12},{9,13},{10,... | collective-permute-start | bytes 135176 | tf_op jit(solution)/shard_map/ppermute | solution.py:477
  128.2 5.1 %collective-permute-start.27 = (bf16[176,128]{1,0:T(8,128)(2,1)S(1)}, bf16[176,128]{1,0:T(8,128)(2,1)S(1)}, u32[]{:S(2)}, u32[]{:S(2)}) collective-permute-start(bf16[176,128]{1,0:T(8,128)(2,1)S(1)} %get-tuple-element.177), channel_id=1, source_target_pairs={{0,6},{1,7},{2,0},{3,1},{4,2},{5,3},{6,4},{7,5},{8,14},{9,15},{10,... | collective-permute-start | bytes 135176 | tf_op jit(solution)/shard_map/ppermute | solution.py:477

commit v4 on v3

--- a/solution.py
+++ b/solution.py
@@ -81,22 +81,24 @@
     return pl.ds(pl.multiple_of(index * size, size), size)
 
 
-def cotangent_kernel(lengths, cotangent, w_out, out_0, out_1, out_2, out_3, d_context, cot_t):
+def send_kernel(lengths, frames, cotangent, w_out, out_0, out_1, out_2, out_3, d_context, cot_t):
     place = locate(lengths)
     d_context[...] = dot(cotangent[...], w_out[...], 1, 1).astype(BF16)
     cot_t[...] = cotangent[...].T
     for turn, ref in enumerate((out_0, out_1, out_2, out_3)):
         x = (place[4] + turn) & 3
-        ref[:128] = d_context[:, span(x, 128)]
+        ref[:, :1024] = frames[...]
+        ref[:, 1024:1152] = d_context[:, span(x, 128)]
         for m in range(8):
-            ref[128 + 32 * m : 160 + 32 * m] = cot_t[span(4 * m + x, 32), :]
+            lanes = slice(1152 + 128 * (m // 4), 1280 + 128 * (m // 4))
+            ref[32 * (m % 4) : 32 * (m % 4) + 32, lanes] = cot_t[span(4 * m + x, 32), :]
 
 
 def project_kernel(lengths, frames_0, frames_1, frames_2, frames_3, w_qkv, normed, query, kv):
     place = locate(lengths)
     x = place[4]
     for turn, ref in enumerate((frames_0, frames_1, frames_2, frames_3)):
-        unit_rows, _ = normalize(ref[...].astype(F32))
+        unit_rows, _ = normalize(ref[:, :1024].astype(F32))
         normed[span(slot(place, turn), ROWS), :] = unit_rows.astype(BF16)
     weight = jnp.concatenate([w_qkv[:, span(x + 4 * part, 128)] for part in range(3)], axis=1)
     joined = dot(normed[...], weight).astype(BF16)
@@ -141,26 +143,27 @@
 
     def chunk(index, _):
         lanes = pl.ds(pl.multiple_of(index * 128, 128), 128)
-        own = conv_ext[16:144, lanes]
-        forward = jnp.zeros((ROWS, 128), F32)
-        for shift in range(8):
-            moved = gate_ext[pl.ds(shift, 152), lanes]
-            for step in range(4):
-                offset = 8 * step + shift
-                if 1 <= offset <= TAPS:
-                    part = moved[8 * step : 8 * step + ROWS]
-                    forward = forward + taps[offset - 1 : offset, lanes] * part
-                    g_taps[offset - 1 : offset, lanes] = jnp.sum(part * own, axis=0, keepdims=True)
-        conv_out[:, lanes] = forward
-        backward = jnp.zeros((ROWS, 128), F32)
-        for shift in range(8):
-            moved = conv_ext[pl.ds(shift, 152), lanes]
-            for step in range(4):
-                offset = 8 * step + shift
-                if 1 <= offset <= TAPS:
-                    part = moved[8 * step : 8 * step + ROWS]
-                    backward = backward + taps[TAPS - offset : TAPS - offset + 1, lanes] * part
-        d_gating[:, lanes] = backward
+        for first in (0, 64):
+            own = conv_ext[16 + first : 80 + first, lanes]
+            forward = jnp.zeros((64, 128), F32)
+            for shift in range(8):
+                moved = gate_ext[pl.ds(first + shift, 88), lanes]
+                for step in range(4):
+                    offset = 8 * step + shift
+                    if 1 <= offset <= TAPS:
+                        part = moved[8 * step : 8 * step + 64]
+                        forward = forward + taps[offset - 1 : offset, lanes] * part
+                        g_taps[offset - 1 : offset, lanes] += jnp.sum(part * own, axis=0, keepdims=True)
+            conv_out[first : first + 64, lanes] = forward
+            backward = jnp.zeros((64, 128), F32)
+            for shift in range(8):
+                moved = conv_ext[pl.ds(first + shift, 88), lanes]
+                for step in range(4):
+                    offset = 8 * step + shift
+                    if 1 <= offset <= TAPS:
+                        part = moved[8 * step : 8 * step + 64]
+                        backward = backward + taps[TAPS - offset : TAPS - offset + 1, lanes] * part
+            d_gating[first : first + 64, lanes] = backward
         return 0
 
     lax.fori_loop(0, 8, chunk, 0)
@@ -243,7 +246,8 @@
         d_upper_t[:, here] = gate[:512]
         for block in range(8):
             gated[here, 128 * block : 128 * block + 128] = gate[640 + 128 * block : 768 + 128 * block]
-        cot_own[:, here] = cot[128:]
+        cot_own[:128, here] = cot[:, 1152:1280]
+        cot_own[128:, here] = cot[:, 1280:]
     for parity, out in ((core, keep), (1 - core, send)):
         grad = dot(d_upper_t[...], own_columns(normed, parity, 128))
         out[:, :64, :] = grad.astype(BF16).reshape(8, 64, 512)
@@ -254,13 +258,15 @@
 
 
 def attention_grads_kernel(
-    lengths, gate_keep, gate_send, normed, cot_own, near_0, near_1, near_2, near_3, far_0, far_1, far_2, far_3,
+    lengths, normed, cot_own, far_0, far_1, far_2, far_3,
     keep, send, context, rows_t
 ):
     place = locate(lengths)
     core = place[2]
-    for turn, near in enumerate((near_0, near_1, near_2, near_3)):
-        context[:, span(slot(place, turn), 128)] = near[...].reshape(512, 128)
+    for turn, far in enumerate((far_0, far_1, far_2, far_3)):
+        for block in range(GROUP):
+            tokens = slice(128 * block, 128 * block + 128)
+            context[tokens, span(slot(place, turn), 128)] = far[96:, tokens]
     for x in range(4):
 
         @pl.when(place[4] == x)
@@ -276,16 +282,15 @@
         blocks.append(block)
         swapped.append(pltpu.roll(block, HEAD, 1))
     lane_out = lax.broadcasted_iota(jnp.int32, (8, 16, 512), 2)
-    for parity, gate, out in ((core, gate_keep, keep), (1 - core, gate_send, send)):
-        out[:, :112, :] = gate[...]
+    for parity, out in ((core, keep), (1 - core, send)):
         grad = dot(rows_t[...], own_columns(normed, parity, 128))
-        out[:, 112:160, :] = grad.astype(BF16).reshape(8, 48, 512)
+        out[:, :48, :] = grad.astype(BF16).reshape(8, 48, 512)
         mine = (lane < HEAD) == (parity == 0)
         doubled = jnp.concatenate(
             [jnp.where(mine, block, other) for block, other in zip(blocks, swapped)], axis=1
         ).astype(BF16)
         grad = dot(cot_own[...], doubled).reshape(8, 32, 512)
-        out[:, 160:, :] = jnp.where((lane_out & 127) < HEAD, grad[:, :16], grad[:, 16:]).astype(BF16)
+        out[:, 48:, :] = jnp.where((lane_out & 127) < HEAD, grad[:, :16], grad[:, 16:]).astype(BF16)
 
 
 def attend_kernel(
@@ -295,7 +300,7 @@
     place = locate(lengths)
     group_first, length = place[3], place[1]
     for turn, ref in enumerate((cot_0, cot_1, cot_2, cot_3)):
-        d_contexts[slot(place, turn)] = ref[:128]
+        d_contexts[slot(place, turn)] = ref[:, 1024:1152]
     for part, ref in enumerate((before, kv, after)):
         for piece in range(GROUP):
             start = 512 * part + ROWS * piece
@@ -381,7 +386,7 @@
 
 
 def join_kernel(
-    lengths, d_query, own, from_before, from_after,
+    lengths, context, d_query, own, from_before, from_after,
     unit_0, unit_1, unit_2, unit_3, back_0, back_1, back_2, back_3, joined_t
 ):
     place = locate(lengths)
@@ -393,6 +398,9 @@
         joined_t[256:, 128 * piece : 128 * piece + 128] = total[:, 128:].T
     for turn, ref in enumerate((back_0, back_1, back_2, back_3)):
         ref[...] = joined_t[:, span((place[4] + turn) & 3, 128)]
+    for ref in (unit_0, unit_1, unit_2, unit_3):
+        for block in range(GROUP):
+            ref[96:, 128 * block : 128 * block + 128] = context[block]
     for x in range(4):
 
         @pl.when(place[4] == x)
@@ -402,28 +410,32 @@
                     ref[16 * index : 16 * index + 16] = joined_t[16 * here : 16 * here + 16]
 
 
+def gate_rows_kernel(frames, gate, d_upper, w_up, w_down, layer_part, d_normed):
+    gated = jnp.concatenate([gate[640 + 128 * m : 768 + 128 * m] for m in range(8)], axis=1)
+    layer_part[...] = frames[...].astype(F32) + dot(gated, w_down[...])
+    d_normed[...] = dot(d_upper[...], w_up[...], 1, 1)
+
+
 def rows_kernel(
-    lengths, frames, cotangent, near_0, near_1, near_2, near_3, back_0, back_1, back_2, back_3, gate, d_upper,
-    w_qkv, w_out, w_up, w_down, layer_out, d_frames, context, joined_t
+    lengths, frames, cotangent, far_0, far_1, far_2, far_3, back_0, back_1, back_2, back_3, layer_part, d_normed,
+    w_qkv, w_out, layer_out, d_frames, context, joined_t
 ):
     place = locate(lengths)
-    for turn, near in enumerate((near_0, near_1, near_2, near_3)):
-        context[:, span(slot(place, turn), 128)] = near[place[4]]
+    for turn, far in enumerate((far_0, far_1, far_2, far_3)):
+        context[:, span(slot(place, turn), 128)] = far[96:, span(place[4], 128)]
     for turn, back in enumerate((back_0, back_1, back_2, back_3)):
         pair = slot(place, turn)
         for part in range(3):
             joined_t[span(pair + 4 * part, 128), :] = back[128 * part : 128 * part + 128]
-    gated = jnp.concatenate([gate[640 + 128 * m : 768 + 128 * m] for m in range(8)], axis=1)
-    values = frames[...].astype(F32)
-    out = values + dot(context[...], w_out[...]) + dot(gated, w_down[...])
-    layer_out[...] = out.astype(BF16)
-    unit_rows, inverse = normalize(values)
-    d_normed = dot(d_upper[...], w_up[...], 1, 1) + dot(joined_t[...].T, w_qkv[...], 1, 1)
-    d_frames[...] = (cotangent[...].astype(F32) + norm_back(d_normed, unit_rows, inverse)).astype(BF16)
-
-
-def add_kernel(near, far, out):
-    out[...] = (near[...].astype(F32) + far[...].astype(F32)).astype(BF16)
+    layer_out[...] = (layer_part[...] + dot(context[...], w_out[...])).astype(BF16)
+    unit_rows, inverse = normalize(frames[...].astype(F32))
+    d_rows = d_normed[...] + dot(joined_t[...].T, w_qkv[...], 1, 1)
+    d_frames[...] = (cotangent[...].astype(F32) + norm_back(d_rows, unit_rows, inverse)).astype(BF16)
+
+
+def add_kernel(gate, gate_far, attention, attention_far, out):
+    out[:, :112] = (gate[...].astype(F32) + gate_far[...].astype(F32)).astype(BF16)
+    out[:, 112:] = (attention[...].astype(F32) + attention_far[...].astype(F32)).astype(BF16)
 
 
 def chunk_sum_kernel(lengths, parts, out_0, out_1, out_2, out_3, total):
@@ -483,32 +495,24 @@
     wide = ((ROWS, 1024), BF16)
     wide_f = ((ROWS, 1024), F32)
     quad = ((4, ROWS, 256), BF16)
-    frames_x = turn_x([frames] * 4)
+    piece = ((ROWS, 1408), BF16)
+    pieces = call(
+        send_kernel, [piece] * 4, [pltpu.VMEM((ROWS, 512), BF16), pltpu.VMEM((1024, ROWS), BF16)], scalars=1
+    )(lengths, *in_hbm(frames, cotangent, w_out))
+    pieces, frames_later = lax.optimization_barrier((pieces, frames))
+    in_x = turn_x(pieces)
     resid, d_gated, gating, d_conv, unit, inverse, slope, top, bottom = call(
         gate_kernel,
         [wide, wide, wide, wide, wide_f, ((ROWS, 128), F32), ((ROWS, 2048), F32),
          ((16, 2048), BF16), ((16, 2048), BF16)],
         scalars=1,
-    )(lengths, *in_hbm(frames, cotangent, w_up, w_down))
+    )(lengths, *in_hbm(frames_later, cotangent, w_up, w_down))
     before, after = shift(bottom, 1), shift(top, -1)
-    gating, frames_x, cot_later = lax.optimization_barrier((gating, frames_x, cotangent))
-    small = ((384, 128), BF16)
-    cot_x = turn_x(
-        call(
-            cotangent_kernel, [small] * 4, [pltpu.VMEM((ROWS, 512), BF16), pltpu.VMEM((1024, ROWS), BF16)], scalars=1
-        )(lengths, cot_later, w_out)
-    )
-    normed, query, kv = call(
-        project_kernel, [((512, 1024), BF16), ((4, ROWS, 128), BF16), quad], scalars=1
-    )(lengths, *frames_x, w_qkv)
-    gating, kv = lax.optimization_barrier((gating, kv))
-    kv_before, kv_after = shift(kv, 4), shift(kv, -4)
     conv_in, d_gating_in, g_taps_in = call(
         conv_inner_kernel,
         [wide_f, wide_f, ((32, 1024), F32)],
         [pltpu.VMEM((160, 1024), F32), pltpu.VMEM((160, 1024), F32)],
     )(gating, d_conv, conv_kernel)
-    conv_in, kv_before, kv_after, cot_x = lax.optimization_barrier((conv_in, kv_before, kv_after, cot_x))
     gate = ((1664, 128), BF16)
     d_upper, *gate_x = call(
         conv_outer_kernel,
@@ -518,9 +522,13 @@
          pltpu.VMEM((32, 1024), F32), pltpu.VMEM((2048, ROWS), BF16), pltpu.VMEM((32, 16, 128), BF16)],
         scalars=1,
     )(lengths, conv_in, d_gating_in, g_taps_in, d_conv, resid, d_gated, unit, inverse, slope, before, after, conv_kernel)
-    query, gate_x = lax.optimization_barrier((query, gate_x))
+    in_x, gate_x = lax.optimization_barrier((in_x, gate_x))
+    normed, query, kv = call(
+        project_kernel, [((512, 1024), BF16), ((4, ROWS, 128), BF16), quad], scalars=1
+    )(lengths, *in_x, w_qkv)
+    kv_before, kv_after = shift(kv, 4), shift(kv, -4)
     gate_x = turn_x(gate_x)
-    near, d_query, d_before, d_after, d_own = call(
+    context, d_query, d_before, d_after, d_own = call(
         attend_kernel,
         [((4, ROWS, 128), BF16), ((ROWS, 512), BF16), quad, quad, ((4, ROWS, 256), F32)],
         [pltpu.VMEM((4, ROWS, 128), BF16),
@@ -529,35 +537,40 @@
          pltpu.VMEM((WINDOW, 256), F32), pltpu.VMEM((WINDOW, 256), BF16), pltpu.VMEM((WINDOW, 256), BF16),
          pltpu.VMEM((1536, 128), F32), pltpu.VMEM((1536, 128), F32)],
         scalars=1,
-    )(lengths, query, kv, kv_before, kv_after, *cot_x)
+    )(lengths, query, kv, kv_before, kv_after, *in_x)
     from_before, from_after = shift(d_after, 4), shift(d_before, -4)
-    near_x = turn_x([near] * 4)
-    gate_x, d_own = lax.optimization_barrier((gate_x, d_own))
+    frames_later, d_own = lax.optimization_barrier((frames, d_own))
+    layer_part, d_normed = call(gate_rows_kernel, [wide_f + (HBM,), wide_f + (HBM,)])(
+        *in_hbm(frames_later), gate_x[0], *in_hbm(d_upper), w_up, w_down
+    )
+    gate_x, d_normed, d_own = lax.optimization_barrier((gate_x, d_normed, d_own))
+    small = ((384, 128), BF16)
+    *far, back_0, back_1, back_2, back_3 = call(
+        join_kernel, [((224, 512), BF16)] * 4 + [small + (HBM,)] * 4, [pltpu.VMEM((384, 512), BF16)], scalars=1
+    )(lengths, context, d_query, d_own, from_before, from_after)
+    far, gate_x = lax.optimization_barrier((far, gate_x))
+    far_x = turn_x(far)
     keep, send, cot_own = call(
         gate_grads_kernel,
         [((8, 112, 512), BF16), ((8, 112, 512), BF16), ((256, 512), BF16)],
         [pltpu.VMEM((512, 512), BF16), pltpu.VMEM((512, 1024), BF16)],
         scalars=1,
-    )(lengths, normed, *cot_x, *gate_x)
-    keep, d_own = lax.optimization_barrier((keep, d_own))
-    *far, back_0, back_1, back_2, back_3 = call(
-        join_kernel, [((96, 512), BF16)] * 4 + [small] * 4, [pltpu.VMEM((384, 512), BF16)], scalars=1
-    )(lengths, d_query, d_own, from_before, from_after)
-    far_x = turn_x(far)
-    keep, send = call(
+    )(lengths, normed, *in_x, *gate_x)
+    gate_far = other_core(send)
+    attention_keep, send = call(
         attention_grads_kernel,
-        [((8, 176, 512), BF16), ((8, 176, 512), BF16)],
+        [((8, 64, 512), BF16), ((8, 64, 512), BF16)],
         [pltpu.VMEM((512, 512), BF16), pltpu.VMEM((384, 512), BF16)],
         scalars=1,
-    )(lengths, keep, send, normed, cot_own, *near_x, *far_x)
-    keep, *back = lax.optimization_barrier((keep, back_0, back_1, back_2, back_3))
+    )(lengths, normed, cot_own, *far_x)
+    send, *back = lax.optimization_barrier((send, back_0, back_1, back_2, back_3))
     back_x = turn_x(back)
-    (parts,) = call(add_kernel, [((8, 176, 512), BF16, HBM)])(keep, other_core(send))
+    (parts,) = call(add_kernel, [((8, 176, 512), BF16, HBM)])(keep, gate_far, attention_keep, other_core(send))
     parts = swap_rows(parts)
     layer_out, d_frames = call(
         rows_kernel, [wide, wide], [pltpu.VMEM((ROWS, 512), BF16), pltpu.VMEM((1536, ROWS), BF16)], scalars=1
     )(
-        lengths, frames, cotangent, *near_x, *back_x, gate_x[0], d_upper, *in_hbm(w_qkv, w_out, w_up, w_down)
+        lengths, frames, cotangent, *far_x, *back_x, layer_part, d_normed, *in_hbm(w_qkv, w_out)
     )
     parts, layer_out, d_frames = lax.optimization_barrier((parts, layer_out, d_frames))
     parts = call(

time: 135 us -> 130 us (0.963)
  waiting for transfers between devices: 31.9 us -> 26.9 us
  Pallas kernels: 37.3 us -> 38.9 us
    ppermute x18 -> x12, waiting for transfers between devices: 25.6 us -> 14.6 us  [turn_x(): lax.ppermute(pieces[by], 'seq', [(i, i // 4 * 4 + (i + by) % 4) for i in...]
    ppermute x18 -> x12, starting transfers between devices: 23.2 us -> 18 us  [turn_x(): lax.ppermute(pieces[by], 'seq', [(i, i // 4 * 4 + (i + by) % 4) for i in...]
    ppermute x6, waiting for transfers between devices: 0.02 us -> 4.07 us  [shift(): lax.ppermute(array, 'seq', [(i, i + by) for i in range(32) if 0 <= i + by...]
    all_to_all x1, starting transfers between devices: 7 us -> 10.8 us  [swap_rows(): return lax.all_to_all(array, 'seq', 0, 0, axis_index_groups=ROW_GROUPS)]
    all_to_all x1, waiting for transfers between devices: 0.7 us -> 3.89 us  [swap_rows(): return lax.all_to_all(array, 'seq', 0, 0, axis_index_groups=ROW_GROUPS)]
    pallas_call x13 -> x14, Pallas kernels: 37.3 us -> 38.9 us  [run(): pl.pallas_call(body, out_shape=[HBM(*out[:2]) if len(out) > 2 else jax.Sh...]
    ppermute x1 -> x2, waiting for transfers between devices: 3.21 us -> 1.9 us  [other_core(): return lax.ppermute(array, 'dp', [(i, i ^ 1) for i in range(8)])]
  transfers between devices with their start and end apart: 29 -> 24, of which waited for: 13 -> 10; matrix products, arithmetic and copies ran while one was open for 0% -> 0% of each run, Pallas kernels for 22% -> 24%
where the time goes in v4:
time: 130 us; the launch traced here: 129 us
  starting transfers between devices  60.1 us (46%)
  Pallas kernels  38.9 us (30%)
  waiting for transfers between devices  26.9 us (21%)
  between operations  1.53 us (1%)
    pallas_call x14, Pallas kernels, run(): pl.pallas_call(body, out_shape=[HBM(*out[:2]) if len(out) > 2 else jax.Sh...  38.9 us
    ppermute x6, starting transfers between devices, shift(): lax.ppermute(array, 'seq', [(i, i + by) for i in range(32) if 0 <= i + by...  19.8 us
    ppermute x12, starting transfers between devices, turn_x(): lax.ppermute(pieces[by], 'seq', [(i, i // 4 * 4 + (i + by) % 4) for i in...  18 us
    ppermute x12, waiting for transfers between devices, turn_x(): lax.ppermute(pieces[by], 'seq', [(i, i // 4 * 4 + (i + by) % 4) for i in...  14.6 us
    ppermute x3, starting transfers between devices, turn_z(): lax.ppermute(pieces[by], 'dp', [(i, (i + 2 * by) % 8) for i in range(8)])  11.4 us
    all_to_all x1, starting transfers between devices, swap_rows(): return lax.all_to_all(array, 'seq', 0, 0, axis_index_groups=ROW_GROUPS)  10.8 us
    ppermute x6, waiting for transfers between devices, shift(): lax.ppermute(array, 'seq', [(i, i + by) for i in range(32) if 0 <= i + by...  4.07 us
    all_to_all x1, waiting for transfers between devices, swap_rows(): return lax.all_to_all(array, 'seq', 0, 0, axis_index_groups=ROW_GROUPS)  3.89 us
  transfers between devices with their start and end apart: 24, of which 10 were waited for; matrix products, arithmetic and copies ran while one was open for 0% of the time, Pallas kernels for 24%

profile of v4, /device:TPU:8, one launch (start us, length us, event | category | flops | bytes accessed | tf_op | source)
XLA Modules:
  0.0 128.5 jit_solution(13820879935557680125)
XLA Ops:
  1.3 2.0 %shard_map.135 = (bf16[128,1408]{1,0:T(8,128)(2,1)S(1)}, bf16[128,1408]{1,0:T(8,128)(2,1)S(1)}, bf16[128,1408]{1,0:T(8,128)(2,1)S(1)}, bf16[128,1408]{1,0:T(8,128)(2,1)S(1)}) custom-call(s32[1]{0:T(128)S(6)} %copy.15.lengths, bf16[128,1024]{1,0:T(8,128)(2,1)} %bitcast.8, bf16[128,1024]{1,0:T(8,128)(2,1)} %bitcast.12, bf16[512,1024]{1,0:T(8,128)(2,1)} %w_out.3), custom_call_target="tpu_custom_call" | custom-call | tf_op jit(solution)/shard_map/pallas_call | solution.py:33
  3.3 1.6 %collective-permute-start = (bf16[128,1408]{1,0:T(8,128)(2,1)S(1)}, bf16[128,1408]{1,0:T(8,128)(2,1)S(1)}, u32[]{:S(2)}, u32[]{:S(2)}) collective-permute-start(bf16[128,1408]{1,0:T(8,128)(2,1)S(1)} %get-tuple-element.104), channel_id=1, source_target_pairs={{0,8},{8,16},{16,24},{24,0},{32,40},{40,48},{48,56},{56,32},{64,72... | collective-permute-start | bytes 1081352 | tf_op jit(solution)/shard_map/ppermute | solution.py:482
  4.8 2.7 %collective-permute-start.1 = (bf16[128,1408]{1,0:T(8,128)(2,1)S(1)}, bf16[128,1408]{1,0:T(8,128)(2,1)S(1)}, u32[]{:S(2)}, u32[]{:S(2)}) collective-permute-start(bf16[128,1408]{1,0:T(8,128)(2,1)S(1)} %get-tuple-element.105), channel_id=1, source_target_pairs={{0,16},{8,24},{16,0},{24,8},{32,48},{40,56},{48,32},{56,40},{64,80... | collective-permute-start | bytes 1081352 | tf_op jit(solution)/shard_map/ppermute | solution.py:482
  7.6 1.4 %collective-permute-start.2 = (bf16[128,1408]{1,0:T(8,128)(2,1)S(1)}, bf16[128,1408]{1,0:T(8,128)(2,1)S(1)}, u32[]{:S(2)}, u32[]{:S(2)}) collective-permute-start(bf16[128,1408]{1,0:T(8,128)(2,1)S(1)} %get-tuple-element.106), channel_id=1, source_target_pairs={{0,24},{8,0},{16,8},{24,16},{32,56},{40,32},{48,40},{56,48},{64,88... | collective-permute-start | bytes 1081352 | tf_op jit(solution)/shard_map/ppermute | solution.py:482
  9.0 4.9 %shard_map.136 = (bf16[128,1024]{1,0:T(8,128)(2,1)S(1)}, bf16[128,1024]{1,0:T(8,128)(2,1)S(1)}, bf16[128,1024]{1,0:T(8,128)(2,1)S(1)}, bf16[128,1024]{1,0:T(8,12...) custom-call(s32[1]{0:T(128)S(6)} %copy.15.lengths, ...), custom_call_target="tpu_custom_call" | custom-call | tf_op jit(solution)/shard_map/pallas_call | solution.py:33
  13.9 2.5 %collective-permute-start.3 = (bf16[16,2048]{1,0:T(8,128)(2,1)S(1)}, bf16[16,2048]{1,0:T(8,128)(2,1)S(1)}, u32[]{:S(2)}, u32[]{:S(2)}) collective-permute-start(bf16[16,2048]{1,0:T(8,128)(2,1)S(1)} %get-tuple-element.118), channel_id=1, source_target_pairs={{0,8},{8,16},{16,24},{24,32},{32,40},{40,48},{48,56},{56,64},{64,7... | collective-permute-start | bytes 196616 | tf_op jit(solution)/shard_map/ppermute | solution.py:469
  16.4 5.4 %collective-permute-start.4 = (bf16[16,2048]{1,0:T(8,128)(2,1)S(1)}, bf16[16,2048]{1,0:T(8,128)(2,1)S(1)}, u32[]{:S(2)}, u32[]{:S(2)}) collective-permute-start(bf16[16,2048]{1,0:T(8,128)(2,1)S(1)} %get-tuple-element.119), channel_id=1, source_target_pairs={{8,0},{16,8},{24,16},{32,24},{40,32},{48,40},{56,48},{64,56},{72,6... | collective-permute-start | bytes 196616 | tf_op jit(solution)/shard_map/ppermute | solution.py:469
  21.9 7.1 %shard_map.137 = (f32[128,1024]{1,0:T(8,128)S(1)}, f32[128,1024]{1,0:T(8,128)S(1)}, f32[32,1024]{1,0:T(8,128)S(1)}) custom-call(bf16[128,1024]{1,0:T(8,128)(2,1)S(1)} %get-tuple-element.108.gating, bf16[128,1024]{1,0:T(8,128)(2,1)S(1)} %get-tuple-element.109.d_conv, f32[31,1024]{1,0:T(8,128)S(1)} %copy-done.7), custom_call_target="tpu_custom_call" | custom-call | tf_op jit(solution)/shard_map/pallas_call | solution.py:33
  29.0 2.8 %shard_map.138 = (bf16[128,2048]{1,0:T(8,128)(2,1)}, bf16[1664,128]{1,0:T(8,128)(2,1)S(1)}, bf16[1664,128]{1,0:T(8,128)(2,1)S(1)}, bf16[1664,128]{1,0:T(8,128)(2,1)S(1)}, bf16[1664,128]{1,0:T(8,128)(2,1)S(1)}) custom-call(s32[1]{0:T(128)S(6)} %copy.15.lengths, f32[128,1024]{1,0:T(8,128)S(1)} %get-tuple-element.110.conv_in, ...), custom_call_target="tpu_custom_call" | custom-call | tf_op jit(solution)/shard_map/pallas_call | solution.py:33
  31.8 1.3 %shard_map.139 = (bf16[512,1024]{1,0:T(8,128)(2,1)S(1)}, bf16[4,128,128]{2,1,0:T(8,128)(2,1)S(1)}, bf16[4,128,256]{2,1,0:T(8,128)(2,1)S(1)}) custom-call(s32[1]{0:T(128)S(6)} %copy.15.lengths, bf16[128,1408]{1,0:T(8,128)(2,1)S(1)} %get-tuple-element.124.frames_0.cot_0, bf16[128,1408]{1,0:T(8,128)(2,1)S(1)} %collective-permute-done.frames_1.cot_1, ...), custom_call_target="tpu_custom_call" | custom-call | tf_op jit(solution)/shard_map/pallas_call | solution.py:33
  33.1 2.1 %collective-permute-start.6 = (bf16[4,128,256]{2,1,0:T(8,128)(2,1)S(1)}, bf16[4,128,256]{2,1,0:T(8,128)(2,1)S(1)}, u32[]{:S(2)}, u32[]{:S(2)}) collective-permute-start(bf16[4,128,256]{2,1,0:T(8,128)(2,1)S(1)} %get-tuple-element.130.kv), channel_id=1, source_target_pairs={{32,0},{40,8},{48,16},{56,24},{64,32},{72,40},{80,48},{88,56},{96,... | collective-permute-start | bytes 786440 | tf_op jit(solution)/shard_map/ppermute | solution.py:469
  35.2 3.9 %collective-permute-start.5 = (bf16[4,128,256]{2,1,0:T(8,128)(2,1)S(1)}, bf16[4,128,256]{2,1,0:T(8,128)(2,1)S(1)}, u32[]{:S(2)}, u32[]{:S(2)}) collective-permute-start(bf16[4,128,256]{2,1,0:T(8,128)(2,1)S(1)} %get-tuple-element.130.kv), channel_id=1, source_target_pairs={{0,32},{8,40},{16,48},{24,56},{32,64},{40,72},{48,80},{56,88},{64,... | collective-permute-start | bytes 786440 | tf_op jit(solution)/shard_map/ppermute | solution.py:469
  39.1 0.1 collective-permute-start.7
  39.2 1.6 %collective-permute-start.8 = (bf16[1664,128]{1,0:T(8,128)(2,1)S(1)}, bf16[1664,128]{1,0:T(8,128)(2,1)S(1)}, u32[]{:S(2)}, u32[]{:S(2)}) collective-permute-start(bf16[1664,128]{1,0:T(8,128)(2,1)S(1)} %get-tuple-element.135), channel_id=1, source_target_pairs={{0,16},{8,24},{16,0},{24,8},{32,48},{40,56},{48,32},{56,40},{64,80... | collective-permute-start | bytes 1277960 | tf_op jit(solution)/shard_map/ppermute | solution.py:482
  40.8 1.6 %collective-permute-start.9 = (bf16[1664,128]{1,0:T(8,128)(2,1)S(1)}, bf16[1664,128]{1,0:T(8,128)(2,1)S(1)}, u32[]{:S(2)}, u32[]{:S(2)}) collective-permute-start(bf16[1664,128]{1,0:T(8,128)(2,1)S(1)} %get-tuple-element.136), channel_id=1, source_target_pairs={{0,24},{8,0},{16,8},{24,16},{32,56},{40,32},{48,40},{56,48},{64,88... | collective-permute-start | bytes 1277960 | tf_op jit(solution)/shard_map/ppermute | solution.py:482
  42.5 1.3 %collective-permute-done.5.before = bf16[4,128,256]{2,1,0:T(8,128)(2,1)S(1)} collective-permute-done((bf16[4,128,256]{2,1,0:T(8,128)(2,1)S(1)}, bf16[4,128,256]{2,1,0:T(8,128)(2,1)S(1)}, u32[]{:S(2)}, u32[]{:S(2)}) %collective-permute-start.5) | collective-permute-done | bytes 262176 | tf_op jit(solution)/shard_map/ppermute | solution.py:469
  43.7 6.6 %shard_map.140 = (bf16[4,128,128]{2,1,0:T(8,128)(2,1)S(1)}, bf16[128,512]{1,0:T(8,128)(2,1)S(1)}, bf16[4,128,256]{2,1,0:T(8,128)(2,1)S(1)}, bf16[4,128,256]{2,1,0:T(8,128)(2,1)S(1)}, f32[4,128,256]{2,1,0:T(8,128)S(1)}) custom-call(s32[1]{0:T(128)S(6)} %copy.15.lengths, bf16[4,128,128]{2,1,0:T(8,128)(2,1)S(1)} %get-tuple-element.129.queries, ...), custom_call_target="tpu_custom_call" | custom-call | tf_op jit(solution)/shard_map/pallas_call | solution.py:33
  50.3 3.6 %collective-permute-start.10 = (bf16[4,128,256]{2,1,0:T(8,128)(2,1)S(1)}, bf16[4,128,256]{2,1,0:T(8,128)(2,1)S(1)}, u32[]{:S(2)}, u32[]{:S(2)}) collective-permute-start(bf16[4,128,256]{2,1,0:T(8,128)(2,1)S(1)} %get-tuple-element.143), channel_id=1, source_target_pairs={{0,32},{8,40},{16,48},{24,56},{32,64},{40,72},{48,80},{56,88},{64,... | collective-permute-start | bytes 786440 | tf_op jit(solution)/shard_map/ppermute | solution.py:469
  54.0 2.2 %collective-permute-start.11 = (bf16[4,128,256]{2,1,0:T(8,128)(2,1)S(1)}, bf16[4,128,256]{2,1,0:T(8,128)(2,1)S(1)}, u32[]{:S(2)}, u32[]{:S(2)}) collective-permute-start(bf16[4,128,256]{2,1,0:T(8,128)(2,1)S(1)} %get-tuple-element.144), channel_id=1, source_target_pairs={{32,0},{40,8},{48,16},{56,24},{64,32},{72,40},{80,48},{88,56},{96,... | collective-permute-start | bytes 786440 | tf_op jit(solution)/shard_map/ppermute | solution.py:469
  56.2 3.7 %shard_map.141 = (f32[128,1024]{1,0:T(8,128)}, f32[128,1024]{1,0:T(8,128)}) custom-call(bf16[128,1024]{1,0:T(8,128)(2,1)} %bitcast.10, bf16[1664,128]{1,0:T(8,128)(2,1)S(1)} %get-tuple-element.153.gate.gate_0, bf16[128,2048]{1,0:T(8,128)(2,1)} %get-tuple-element.139.d_upper, bf16[1024,2048]{1,0:T(8,128)(2,1)S(1)} %copy-done, bf16[1024,1024]{1,0:T(8,128)(2,1)S(1)} %copy-done.2), custom_call_target="tpu_custom_call" | custom-call | tf_op jit(solution)/shard_map/pallas_call | solution.py:33
  59.9 2.8 %collective-permute-done.11.from_after = bf16[4,128,256]{2,1,0:T(8,128)(2,1)S(1)} collective-permute-done((bf16[4,128,256]{2,1,0:T(8,128)(2,1)S(1)}, bf16[4,128,256]{2,1,0:T(8,128)(2,1)S(1)}, u32[]{:S(2)}, u32[]{:S(2)}) %collective-permute-start.11) | collective-permute-done | bytes 262176 | tf_op jit(solution)/shard_map/ppermute | solution.py:469
  62.7 1.0 shard_map.142
  63.7 1.4 %shard_map.143 = (bf16[8,112,512]{2,1,0:T(8,128)(2,1)S(1)}, bf16[8,112,512]{2,1,0:T(8,128)(2,1)S(1)}, bf16[256,512]{1,0:T(8,128)(2,1)S(1)}) custom-call(s32[1]{0:T(128)S(6)} %copy.15.lengths, bf16[512,1024]{1,0:T(8,128)(2,1)S(1)} %get-tuple-element.128.normed, bf16[128,1408]{1,0:T(8,128)(2,1)S(1)} %get-tuple-element.124.frames_0.cot_0, ...), custom_call_target="tpu_custom_call" | custom-call | tf_op jit(solution)/shard_map/pallas_call | solution.py:33
  65.1 0.1 collective-permute-start.12
  65.2 1.3 collective-permute-start.13
  66.5 1.8 %collective-permute-start.14 = (bf16[224,512]{1,0:T(8,128)(2,1)S(1)}, bf16[224,512]{1,0:T(8,128)(2,1)S(1)}, u32[]{:S(2)}, u32[]{:S(2)}) collective-permute-start(bf16[224,512]{1,0:T(8,128)(2,1)S(1)} %get-tuple-element.162), channel_id=1, source_target_pairs={{0,16},{8,24},{16,0},{24,8},{32,48},{40,56},{48,32},{56,40},{64,80... | collective-permute-start | bytes 688136 | tf_op jit(solution)/shard_map/ppermute | solution.py:482
  68.2 2.1 %collective-permute-start.15 = (bf16[224,512]{1,0:T(8,128)(2,1)S(1)}, bf16[224,512]{1,0:T(8,128)(2,1)S(1)}, u32[]{:S(2)}, u32[]{:S(2)}) collective-permute-start(bf16[224,512]{1,0:T(8,128)(2,1)S(1)} %get-tuple-element.163), channel_id=1, source_target_pairs={{0,24},{8,0},{16,8},{24,16},{32,56},{40,32},{48,40},{56,48},{64,88... | collective-permute-start | bytes 688136 | tf_op jit(solution)/shard_map/ppermute | solution.py:482
  70.3 9.0 %collective-permute-done.13.far_1 = bf16[224,512]{1,0:T(8,128)(2,1)S(1)} collective-permute-done((bf16[224,512]{1,0:T(8,128)(2,1)S(1)}, bf16[224,512]{1,0:T(8,128)(2,1)S(1)}, u32[]{:S(2)}, u32[]{:S(2)}) %collective-permute-start.13) | collective-permute-done | bytes 229408 | tf_op jit(solution)/shard_map/ppermute | solution.py:482
  79.4 0.6 collective-permute-done.15.far_3
  80.0 1.4 %shard_map.144 = (bf16[8,64,512]{2,1,0:T(8,128)(2,1)S(1)}, bf16[8,64,512]{2,1,0:T(8,128)(2,1)S(1)}) custom-call(s32[1]{0:T(128)S(6)} %copy.15.lengths, bf16[512,1024]{1,0:T(8,128)(2,1)S(1)} %get-tuple-element.128.normed, bf16[256,512]{1,0:T(8,128)(2,1)S(1)} %get-tuple-element.159.cot_own, bf16[224,512]{1,0:T(8,128)(2,1)S(1)} %get-tuple-element.160.far_0, ...), custom_call_target="tpu_custom_call" | custom-call | tf_op jit(solution)/shard_map/pallas_call | solution.py:33
  81.3 0.1 collective-permute-start.16
  81.4 1.9 %collective-permute-done.16.attention_far = bf16[8,64,512]{2,1,0:T(8,128)(2,1)S(1)} collective-permute-done((bf16[8,64,512]{2,1,0:T(8,128)(2,1)S(1)}, bf16[8,64,512]{2,1,0:T(8,128)(2,1)S(1)}, u32[]{:S(2)}, u32[]{:S(2)}) %collective-permute-start.16) | collective-permute-done | bytes 524320 | tf_op jit(solution)/shard_map/ppermute | solution.py:473
  83.3 1.5 %shard_map.145 = bf16[8,176,512]{2,1,0:T(8,128)(2,1)} custom-call(bf16[8,112,512]{2,1,0:T(8,128)(2,1)S(1)} %get-tuple-element.157.gate, bf16[8,112,512]{2,1,0:T(8,128)(2,1)S(1)} %collective-permute-done.12.gate_far, bf16[8,64,512]{2,1,0:T(8,128)(2,1)S(1)} %get-tuple-element.164.attention, bf16[8,64,512]{2,1,0:T(8,128)(2,1)S(1)} %collective-permute-done.16.attention_far), custom_call_target="tpu_custom_call" | custom-call | tf_op jit(solution)/shard_map/pallas_call | solution.py:33
  84.8 10.8 %all-to-all-start = ((bf16[8,176,512]{2,1,0:T(8,128)(2,1)}), bf16[8,176,512]{2,1,0:T(8,128)(2,1)S(1)}, u32[]{:S(2)}, u32[]{:S(2)}) async-start(bf16[8,176,512]{2,1,0:T(8,128)(2,1)} %shard_map.145), calls=%async_computation | async-start | bytes 2883584 | tf_op jit(solution)/shard_map/all_to_all | solution.py:477
  95.6 0.2 collective-permute-start.17
  95.8 3.6 %collective-permute-start.18 = (bf16[384,128]{1,0:T(8,128)(2,1)}, bf16[384,128]{1,0:T(8,128)(2,1)S(1)}, u32[]{:S(2)}, u32[]{:S(2)}) collective-permute-start(bf16[384,128]{1,0:T(8,128)(2,1)} %get-tuple-element.173), channel_id=1, source_target_pairs={{0,16},{8,24},{16,0},{24,8},{32,48},{40,56},{48,32},{56,40},{64,80... | collective-permute-start | bytes 294920 | tf_op jit(solution)/shard_map/ppermute | solution.py:482
  99.4 3.3 %collective-permute-done.17.back_1 = bf16[384,128]{1,0:T(8,128)(2,1)S(1)} collective-permute-done((bf16[384,128]{1,0:T(8,128)(2,1)}, bf16[384,128]{1,0:T(8,128)(2,1)S(1)}, u32[]{:S(2)}, u32[]{:S(2)}) %collective-permute-start.17) | collective-permute-done | bytes 98336 | tf_op jit(solution)/shard_map/ppermute | solution.py:482
  102.7 1.3 collective-permute-done.18.back_2
  104.0 0.4 collective-permute-done.19.back_3
  104.4 1.0 copy-done.6
  105.4 4.4 %shard_map.146 = (bf16[128,1024]{1,0:T(8,128)(2,1)}, bf16[128,1024]{1,0:T(8,128)(2,1)}) custom-call(s32[1]{0:T(128)S(6)} %copy.15.lengths, bf16[128,1024]{1,0:T(8,128)(2,1)S(1)} %bitcast.11, bf16[128,1024]{1,0:T(8,128)(2,1)S(1)} %bitcast.14, bf16[224,512]{1,0:T(8,128)(2,1)S(1)} %get-tuple-element.160.far_0, ...), custom_call_target="tpu_custom_call" | custom-call | tf_op jit(solution)/shard_map/pallas_call | solution.py:33
  109.8 3.9 %all-to-all-done.parts = bf16[8,176,512]{2,1,0:T(8,128)(2,1)S(1)} async-done(((bf16[8,176,512]{2,1,0:T(8,128)(2,1)}), bf16[8,176,512]{2,1,0:T(8,128)(2,1)S(1)}, u32[]{:S(2)}, u32[]{:S(2)}) %all-to-all-start) | async-done | bytes 1441824 | tf_op jit(solution)/shard_map/all_to_all | solution.py:477
  113.7 0.2 shard_map.147
  113.9 3.3 %collective-permute-start.20 = (bf16[176,128]{1,0:T(8,128)(2,1)S(1)}, bf16[176,128]{1,0:T(8,128)(2,1)S(1)}, u32[]{:S(2)}, u32[]{:S(2)}) collective-permute-start(bf16[176,128]{1,0:T(8,128)(2,1)S(1)} %get-tuple-element.183), channel_id=1, source_target_pairs={{0,2},{1,3},{2,4},{3,5},{4,6},{5,7},{6,0},{7,1},{8,10},{9,11},{10,... | collective-permute-start | bytes 135176 | tf_op jit(solution)/shard_map/ppermute | solution.py:489
  117.3 5.4 %collective-permute-start.21 = (bf16[176,128]{1,0:T(8,128)(2,1)S(1)}, bf16[176,128]{1,0:T(8,128)(2,1)S(1)}, u32[]{:S(2)}, u32[]{:S(2)}) collective-permute-start(bf16[176,128]{1,0:T(8,128)(2,1)S(1)} %get-tuple-element.184), channel_id=1, source_target_pairs={{0,4},{1,5},{2,6},{3,7},{4,0},{5,1},{6,2},{7,3},{8,12},{9,13},{10,... | collective-permute-start | bytes 135176 | tf_op jit(solution)/shard_map/ppermute | solution.py:489
  122.7 2.7 %collective-permute-start.22 = (bf16[176,128]{1,0:T(8,128)(2,1)S(1)}, bf16[176,128]{1,0:T(8,128)(2,1)S(1)}, u32[]{:S(2)}, u32[]{:S(2)}) collective-permute-start(bf16[176,128]{1,0:T(8,128)(2,1)S(1)} %get-tuple-element.185), channel_id=1, source_target_pairs={{0,6},{1,7},{2,0},{3,1},{4,2},{5,3},{6,4},{7,5},{8,14},{9,15},{10,... | collective-permute-start | bytes 135176 | tf_op jit(solution)/shard_map/ppermute | solution.py:489
  125.4 2.4 %collective-permute-done.22.part_3 = bf16[176,128]{1,0:T(8,128)(2,1)S(1)} collective-permute-done((bf16[176,128]{1,0:T(8,128)(2,1)S(1)}, bf16[176,128]{1,0:T(8,128)(2,1)S(1)}, u32[]{:S(2)}, u32[]{:S(2)}) %collective-permute-start.22) | collective-permute-done | bytes 45088 | tf_op jit(solution)/shard_map/ppermute | solution.py:489
  127.7 0.8 shard_map.148
  (32 shorter events, 0.1 us)
Async XLA Ops:
  3.2 18.6 %copy-start.7 = (f32[31,1024]{1,0:T(8,128)S(1)}, f32[31,1024]{1,0:T(8,128)}, u32[]{:S(2)}) copy-start(f32[31,1024]{1,0:T(8,128)} %taps.3) | copy-start | bytes 380932
  3.3 28.5 %collective-permute-start = (bf16[128,1408]{1,0:T(8,128)(2,1)S(1)}, bf16[128,1408]{1,0:T(8,128)(2,1)S(1)}, u32[]{:S(2)}, u32[]{:S(2)}) collective-permute-start(bf16[128,1408]{1,0:T(8,128)(2,1)S(1)} %get-tuple-element.104), channel_id=1, source_target_pairs={{0,8},{8,16},{16,24},{24,0},{32,40},{40,48},{48,56},{56,32},{64,72... | collective-permute-start | bytes 1081352 | tf_op jit(solution)/shard_map/ppermute | solution.py:482
  4.8 27.0 %collective-permute-start.1 = (bf16[128,1408]{1,0:T(8,128)(2,1)S(1)}, bf16[128,1408]{1,0:T(8,128)(2,1)S(1)}, u32[]{:S(2)}, u32[]{:S(2)}) collective-permute-start(bf16[128,1408]{1,0:T(8,128)(2,1)S(1)} %get-tuple-element.105), channel_id=1, source_target_pairs={{0,16},{8,24},{16,0},{24,8},{32,48},{40,56},{48,32},{56,40},{64,80... | collective-permute-start | bytes 1081352 | tf_op jit(solution)/shard_map/ppermute | solution.py:482
  7.6 24.2 %collective-permute-start.2 = (bf16[128,1408]{1,0:T(8,128)(2,1)S(1)}, bf16[128,1408]{1,0:T(8,128)(2,1)S(1)}, u32[]{:S(2)}, u32[]{:S(2)}) collective-permute-start(bf16[128,1408]{1,0:T(8,128)(2,1)S(1)} %get-tuple-element.106), channel_id=1, source_target_pairs={{0,24},{8,0},{16,8},{24,16},{32,56},{40,32},{48,40},{56,48},{64,88... | collective-permute-start | bytes 1081352 | tf_op jit(solution)/shard_map/ppermute | solution.py:482
  13.9 15.1 %collective-permute-start.3 = (bf16[16,2048]{1,0:T(8,128)(2,1)S(1)}, bf16[16,2048]{1,0:T(8,128)(2,1)S(1)}, u32[]{:S(2)}, u32[]{:S(2)}) collective-permute-start(bf16[16,2048]{1,0:T(8,128)(2,1)S(1)} %get-tuple-element.118), channel_id=1, source_target_pairs={{0,8},{8,16},{16,24},{24,32},{32,40},{40,48},{48,56},{56,64},{64,7... | collective-permute-start | bytes 196616 | tf_op jit(solution)/shard_map/ppermute | solution.py:469
  16.4 12.6 %collective-permute-start.4 = (bf16[16,2048]{1,0:T(8,128)(2,1)S(1)}, bf16[16,2048]{1,0:T(8,128)(2,1)S(1)}, u32[]{:S(2)}, u32[]{:S(2)}) collective-permute-start(bf16[16,2048]{1,0:T(8,128)(2,1)S(1)} %get-tuple-element.119), channel_id=1, source_target_pairs={{8,0},{16,8},{24,16},{32,24},{40,32},{48,40},{56,48},{64,56},{72,6... | collective-permute-start | bytes 196616 | tf_op jit(solution)/shard_map/ppermute | solution.py:469
  29.0 2.8 %copy-start.1 = (bf16[1024,1536]{1,0:T(8,128)(2,1)S(1)}, bf16[1024,1536]{1,0:T(8,128)(2,1)}, u32[]{:S(2)}) copy-start(bf16[1024,1536]{1,0:T(8,128)(2,1)} %w_qkv.3) | copy-start | bytes 9437188
  31.8 24.4 %copy-start = (bf16[1024,2048]{1,0:T(8,128)(2,1)S(1)}, bf16[1024,2048]{1,0:T(8,128)(2,1)}, u32[]{:S(2)}) copy-start(bf16[1024,2048]{1,0:T(8,128)(2,1)} %w_up.3) | copy-start | bytes 12582916
  33.1 23.1 %copy-start.2 = (bf16[1024,1024]{1,0:T(8,128)(2,1)S(1)}, bf16[1024,1024]{1,0:T(8,128)(2,1)}, u32[]{:S(2)}) copy-start(bf16[1024,1024]{1,0:T(8,128)(2,1)} %w_down.3) | copy-start | bytes 6291460
  33.1 9.3 %collective-permute-start.6 = (bf16[4,128,256]{2,1,0:T(8,128)(2,1)S(1)}, bf16[4,128,256]{2,1,0:T(8,128)(2,1)S(1)}, u32[]{:S(2)}, u32[]{:S(2)}) collective-permute-start(bf16[4,128,256]{2,1,0:T(8,128)(2,1)S(1)} %get-tuple-element.130.kv), channel_id=1, source_target_pairs={{32,0},{40,8},{48,16},{56,24},{64,32},{72,40},{80,48},{88,56},{96,... | collective-permute-start | bytes 786440 | tf_op jit(solution)/shard_map/ppermute | solution.py:469
  35.2 8.5 %collective-permute-start.5 = (bf16[4,128,256]{2,1,0:T(8,128)(2,1)S(1)}, bf16[4,128,256]{2,1,0:T(8,128)(2,1)S(1)}, u32[]{:S(2)}, u32[]{:S(2)}) collective-permute-start(bf16[4,128,256]{2,1,0:T(8,128)(2,1)S(1)} %get-tuple-element.130.kv), channel_id=1, source_target_pairs={{0,32},{8,40},{16,48},{24,56},{32,64},{40,72},{48,80},{56,88},{64,... | collective-permute-start | bytes 786440 | tf_op jit(solution)/shard_map/ppermute | solution.py:469
  39.1 20.8 %collective-permute-start.7 = (bf16[1664,128]{1,0:T(8,128)(2,1)S(1)}, bf16[1664,128]{1,0:T(8,128)(2,1)S(1)}, u32[]{:S(2)}, u32[]{:S(2)}) collective-permute-start(bf16[1664,128]{1,0:T(8,128)(2,1)S(1)} %get-tuple-element.134), channel_id=1, source_target_pairs={{0,8},{8,16},{16,24},{24,0},{32,40},{40,48},{48,56},{56,32},{64,72... | collective-permute-start | bytes 1277960 | tf_op jit(solution)/shard_map/ppermute | solution.py:482
  39.2 20.7 %collective-permute-start.8 = (bf16[1664,128]{1,0:T(8,128)(2,1)S(1)}, bf16[1664,128]{1,0:T(8,128)(2,1)S(1)}, u32[]{:S(2)}, u32[]{:S(2)}) collective-permute-start(bf16[1664,128]{1,0:T(8,128)(2,1)S(1)} %get-tuple-element.135), channel_id=1, source_target_pairs={{0,16},{8,24},{16,0},{24,8},{32,48},{40,56},{48,32},{56,40},{64,80... | collective-permute-start | bytes 1277960 | tf_op jit(solution)/shard_map/ppermute | solution.py:482
  40.8 19.1 %collective-permute-start.9 = (bf16[1664,128]{1,0:T(8,128)(2,1)S(1)}, bf16[1664,128]{1,0:T(8,128)(2,1)S(1)}, u32[]{:S(2)}, u32[]{:S(2)}) collective-permute-start(bf16[1664,128]{1,0:T(8,128)(2,1)S(1)} %get-tuple-element.136), channel_id=1, source_target_pairs={{0,24},{8,0},{16,8},{24,16},{32,56},{40,32},{48,40},{56,48},{64,88... | collective-permute-start | bytes 1277960 | tf_op jit(solution)/shard_map/ppermute | solution.py:482
  50.3 9.6 %collective-permute-start.10 = (bf16[4,128,256]{2,1,0:T(8,128)(2,1)S(1)}, bf16[4,128,256]{2,1,0:T(8,128)(2,1)S(1)}, u32[]{:S(2)}, u32[]{:S(2)}) collective-permute-start(bf16[4,128,256]{2,1,0:T(8,128)(2,1)S(1)} %get-tuple-element.143), channel_id=1, source_target_pairs={{0,32},{8,40},{16,48},{24,56},{32,64},{40,72},{48,80},{56,88},{64,... | collective-permute-start | bytes 786440 | tf_op jit(solution)/shard_map/ppermute | solution.py:469
  54.0 8.7 %collective-permute-start.11 = (bf16[4,128,256]{2,1,0:T(8,128)(2,1)S(1)}, bf16[4,128,256]{2,1,0:T(8,128)(2,1)S(1)}, u32[]{:S(2)}, u32[]{:S(2)}) collective-permute-start(bf16[4,128,256]{2,1,0:T(8,128)(2,1)S(1)} %get-tuple-element.144), channel_id=1, source_target_pairs={{32,0},{40,8},{48,16},{56,24},{64,32},{72,40},{80,48},{88,56},{96,... | collective-permute-start | bytes 786440 | tf_op jit(solution)/shard_map/ppermute | solution.py:469
  65.1 18.2 %collective-permute-start.12 = (bf16[8,112,512]{2,1,0:T(8,128)(2,1)S(1)}, bf16[8,112,512]{2,1,0:T(8,128)(2,1)S(1)}, u32[]{:S(2)}, u32[]{:S(2)}) collective-permute-start(bf16[8,112,512]{2,1,0:T(8,128)(2,1)S(1)} %get-tuple-element.158), channel_id=1, source_target_pairs={{0,1},{1,0},{2,3},{3,2},{4,5},{5,4},{6,7},{7,6},{8,9},{9,8},{10,11... | collective-permute-start | bytes 2752520 | tf_op jit(solution)/shard_map/ppermute | solution.py:473
  65.2 14.1 %collective-permute-start.13 = (bf16[224,512]{1,0:T(8,128)(2,1)S(1)}, bf16[224,512]{1,0:T(8,128)(2,1)S(1)}, u32[]{:S(2)}, u32[]{:S(2)}) collective-permute-start(bf16[224,512]{1,0:T(8,128)(2,1)S(1)} %get-tuple-element.161), channel_id=1, source_target_pairs={{0,8},{8,16},{16,24},{24,0},{32,40},{40,48},{48,56},{56,32},{64,72... | collective-permute-start | bytes 688136 | tf_op jit(solution)/shard_map/ppermute | solution.py:482
  66.5 12.9 %collective-permute-start.14 = (bf16[224,512]{1,0:T(8,128)(2,1)S(1)}, bf16[224,512]{1,0:T(8,128)(2,1)S(1)}, u32[]{:S(2)}, u32[]{:S(2)}) collective-permute-start(bf16[224,512]{1,0:T(8,128)(2,1)S(1)} %get-tuple-element.162), channel_id=1, source_target_pairs={{0,16},{8,24},{16,0},{24,8},{32,48},{40,56},{48,32},{56,40},{64,80... | collective-permute-start | bytes 688136 | tf_op jit(solution)/shard_map/ppermute | solution.py:482
  68.2 11.8 %collective-permute-start.15 = (bf16[224,512]{1,0:T(8,128)(2,1)S(1)}, bf16[224,512]{1,0:T(8,128)(2,1)S(1)}, u32[]{:S(2)}, u32[]{:S(2)}) collective-permute-start(bf16[224,512]{1,0:T(8,128)(2,1)S(1)} %get-tuple-element.163), channel_id=1, source_target_pairs={{0,24},{8,0},{16,8},{24,16},{32,56},{40,32},{48,40},{56,48},{64,88... | collective-permute-start | bytes 688136 | tf_op jit(solution)/shard_map/ppermute | solution.py:482
  81.3 2.0 %collective-permute-start.16 = (bf16[8,64,512]{2,1,0:T(8,128)(2,1)S(1)}, bf16[8,64,512]{2,1,0:T(8,128)(2,1)S(1)}, u32[]{:S(2)}, u32[]{:S(2)}) collective-permute-start(bf16[8,64,512]{2,1,0:T(8,128)(2,1)S(1)} %get-tuple-element.170), channel_id=1, source_target_pairs={{0,1},{1,0},{2,3},{3,2},{4,5},{5,4},{6,7},{7,6},{8,9},{9,8},{10,11... | collective-permute-start | bytes 1572872 | tf_op jit(solution)/shard_map/ppermute | solution.py:473
  84.8 19.5 %copy-start.3 = (bf16[1,128,1024]{2,1,0:T(8,128)(2,1)S(1)}, bf16[1,128,1024]{2,1,0:T(8,128)(2,1)}, u32[]{:S(2)}) copy-start(bf16[1,128,1024]{2,1,0:T(8,128)(2,1)} %param.8) | copy-start | bytes 786436
  84.8 19.5 %copy-start.4 = (bf16[1,128,1024]{2,1,0:T(8,128)(2,1)S(1)}, bf16[1,128,1024]{2,1,0:T(8,128)(2,1)}, u32[]{:S(2)}) copy-start(bf16[1,128,1024]{2,1,0:T(8,128)(2,1)} %param.9) | copy-start | bytes 786436
  84.8 19.5 %copy-start.5 = (f32[128,1024]{1,0:T(8,128)S(1)}, f32[128,1024]{1,0:T(8,128)}, u32[]{:S(2)}) copy-start(f32[128,1024]{1,0:T(8,128)} %get-tuple-element.175.layer_part) | copy-start | bytes 1572868
  84.8 19.6 %copy-start.8 = (bf16[384,128]{1,0:T(8,128)(2,1)S(1)}, bf16[384,128]{1,0:T(8,128)(2,1)}, u32[]{:S(2)}) copy-start(bf16[384,128]{1,0:T(8,128)(2,1)} %get-tuple-element.171.back_0) | copy-start | bytes 294916
  84.8 28.9 %all-to-all-start = ((bf16[8,176,512]{2,1,0:T(8,128)(2,1)}), bf16[8,176,512]{2,1,0:T(8,128)(2,1)S(1)}, u32[]{:S(2)}, u32[]{:S(2)}) async-start(bf16[8,176,512]{2,1,0:T(8,128)(2,1)} %shard_map.145), calls=%async_computation | async-start | bytes 2883584 | tf_op jit(solution)/shard_map/all_to_all | solution.py:477
  95.6 7.1 %collective-permute-start.17 = (bf16[384,128]{1,0:T(8,128)(2,1)}, bf16[384,128]{1,0:T(8,128)(2,1)S(1)}, u32[]{:S(2)}, u32[]{:S(2)}) collective-permute-start(bf16[384,128]{1,0:T(8,128)(2,1)} %get-tuple-element.172), channel_id=1, source_target_pairs={{0,8},{8,16},{16,24},{24,0},{32,40},{40,48},{48,56},{56,32},{64,72... | collective-permute-start | bytes 294920 | tf_op jit(solution)/shard_map/ppermute | solution.py:482
  95.8 8.1 %collective-permute-start.18 = (bf16[384,128]{1,0:T(8,128)(2,1)}, bf16[384,128]{1,0:T(8,128)(2,1)S(1)}, u32[]{:S(2)}, u32[]{:S(2)}) collective-permute-start(bf16[384,128]{1,0:T(8,128)(2,1)} %get-tuple-element.173), channel_id=1, source_target_pairs={{0,16},{8,24},{16,0},{24,8},{32,48},{40,56},{48,32},{56,40},{64,80... | collective-permute-start | bytes 294920 | tf_op jit(solution)/shard_map/ppermute | solution.py:482
  99.4 5.0 %collective-permute-start.19 = (bf16[384,128]{1,0:T(8,128)(2,1)}, bf16[384,128]{1,0:T(8,128)(2,1)S(1)}, u32[]{:S(2)}, u32[]{:S(2)}) collective-permute-start(bf16[384,128]{1,0:T(8,128)(2,1)} %get-tuple-element.174), channel_id=1, source_target_pairs={{0,24},{8,0},{16,8},{24,16},{32,56},{40,32},{48,40},{56,48},{64,88... | collective-permute-start | bytes 294920 | tf_op jit(solution)/shard_map/ppermute | solution.py:482
  104.4 1.0 copy-start.6
  113.9 11.4 %collective-permute-start.20 = (bf16[176,128]{1,0:T(8,128)(2,1)S(1)}, bf16[176,128]{1,0:T(8,128)(2,1)S(1)}, u32[]{:S(2)}, u32[]{:S(2)}) collective-permute-start(bf16[176,128]{1,0:T(8,128)(2,1)S(1)} %get-tuple-element.183), channel_id=1, source_target_pairs={{0,2},{1,3},{2,4},{3,5},{4,6},{5,7},{6,0},{7,1},{8,10},{9,11},{10,... | collective-permute-start | bytes 135176 | tf_op jit(solution)/shard_map/ppermute | solution.py:489
  117.3 8.1 %collective-permute-start.21 = (bf16[176,128]{1,0:T(8,128)(2,1)S(1)}, bf16[176,128]{1,0:T(8,128)(2,1)S(1)}, u32[]{:S(2)}, u32[]{:S(2)}) collective-permute-start(bf16[176,128]{1,0:T(8,128)(2,1)S(1)} %get-tuple-element.184), channel_id=1, source_target_pairs={{0,4},{1,5},{2,6},{3,7},{4,0},{5,1},{6,2},{7,3},{8,12},{9,13},{10,... | collective-permute-start | bytes 135176 | tf_op jit(solution)/shard_map/ppermute | solution.py:489
  122.7 5.1 %collective-permute-start.22 = (bf16[176,128]{1,0:T(8,128)(2,1)S(1)}, bf16[176,128]{1,0:T(8,128)(2,1)S(1)}, u32[]{:S(2)}, u32[]{:S(2)}) collective-permute-start(bf16[176,128]{1,0:T(8,128)(2,1)S(1)} %get-tuple-element.185), channel_id=1, source_target_pairs={{0,6},{1,7},{2,0},{3,1},{4,2},{5,3},{6,4},{7,5},{8,14},{9,15},{10,... | collective-permute-start | bytes 135176 | tf_op jit(solution)/shard_map/ppermute | solution.py:489

commit v5 on v4

--- a/solution.py
+++ b/solution.py
@@ -3,7 +3,7 @@
 from jax import lax
 from jax.experimental import pallas as pl
 from jax.experimental.pallas import tpu as pltpu
-from jax.sharding import PartitionSpec as P
+from jax.sharding import Mesh, PartitionSpec as P
 
 HEAD = 64
 BAND = 512
@@ -14,7 +14,7 @@
 TAPS = 31
 
 EPSILON = 1e-05
-NEG_LARGE = -1e30
+NEG_LARGE = -3e38
 HALF_ROOT = 0.7071067811865476
 NORMAL_PEAK = 0.3989422804014327
 
@@ -22,8 +22,6 @@
 F32 = jnp.float32
 HBM = pltpu.HBM
 VMEM_LIMIT = 24 * 2**20
-
-ROW_GROUPS = [[4 * m + x for m in range(8)] for x in range(4)]
 
 
 def call(body, outs, scratch=(), scalars=0):
@@ -69,8 +67,9 @@
 
 
 def locate(lengths):
-    seq, dp = lax.axis_index("seq"), lax.axis_index("dp")
-    return (seq * ROWS, lengths[0], dp & 1, (seq >> 2) * (GROUP * ROWS), seq & 3, dp >> 1)
+    z_low, y, x = lax.axis_index("z_low"), lax.axis_index("y"), lax.axis_index("x")
+    row = 4 * z_low + y
+    return ((4 * row + x) * ROWS, lengths[0], lax.axis_index("core"), row * (GROUP * ROWS), x, lax.axis_index("z_high"))
 
 
 def slot(place, turn):
@@ -134,30 +133,31 @@
     bottom[:, 1024:] = conv_back[112:]
 
 
-def conv_inner_kernel(gating, d_conv, taps, conv_out, d_gating, g_taps, gate_ext, conv_ext):
+def conv_inner_kernel(gating, d_conv, taps, conv_out, d_gating, g_taps, gate_ext, conv_ext, sums):
     for ext, ref in ((gate_ext, gating), (conv_ext, d_conv)):
-        ext[:16] = jnp.zeros((16, 1024), F32)
-        ext[16:144] = ref[...].astype(F32)
-        ext[144:] = jnp.zeros((16, 1024), F32)
-    g_taps[...] = jnp.zeros_like(g_taps)
+        ext[:, :16] = jnp.zeros((8, 16, 128), F32)
+        ext[:, 144:] = jnp.zeros((8, 16, 128), F32)
+        for block in range(8):
+            ext[block, 16:144] = ref[:, 128 * block : 128 * block + 128].astype(F32)
+    sums[...] = jnp.zeros_like(sums)
 
     def chunk(index, _):
         lanes = pl.ds(pl.multiple_of(index * 128, 128), 128)
         for first in (0, 64):
-            own = conv_ext[16 + first : 80 + first, lanes]
+            own = conv_ext[index, 16 + first : 80 + first, :]
             forward = jnp.zeros((64, 128), F32)
             for shift in range(8):
-                moved = gate_ext[pl.ds(first + shift, 88), lanes]
+                moved = gate_ext[index, pl.ds(first + shift, 88), :]
                 for step in range(4):
                     offset = 8 * step + shift
                     if 1 <= offset <= TAPS:
                         part = moved[8 * step : 8 * step + 64]
                         forward = forward + taps[offset - 1 : offset, lanes] * part
-                        g_taps[offset - 1 : offset, lanes] += jnp.sum(part * own, axis=0, keepdims=True)
+                        sums[offset - 1, :, lanes] += jnp.sum((part * own).reshape(8, 8, 128), axis=0)
             conv_out[first : first + 64, lanes] = forward
             backward = jnp.zeros((64, 128), F32)
             for shift in range(8):
-                moved = conv_ext[pl.ds(first + shift, 88), lanes]
+                moved = conv_ext[index, pl.ds(first + shift, 88), :]
                 for step in range(4):
                     offset = 8 * step + shift
                     if 1 <= offset <= TAPS:
@@ -167,6 +167,7 @@
         return 0
 
     lax.fori_loop(0, 8, chunk, 0)
+    g_taps[...] = jnp.sum(sums[...], axis=1)
 
 
 def conv_outer_kernel(
@@ -345,10 +346,11 @@
         total = jnp.zeros((128, 256), F32)
         for index in range(chunks):
             part = scores[128 * index : 128 * index + 128]
-            part = jnp.where(allowed_of(index), jnp.exp(part - peak), 0.0)
+            part = jnp.exp(part - peak)
             scores[128 * index : 128 * index + 128] = part
             total = total + part
-        scale = 1.0 / jnp.maximum(jnp.sum(total, axis=0, keepdims=True), 1.0)
+        some = jnp.maximum(low, 0) <= jnp.minimum(high, WINDOW - 1)
+        scale = jnp.where(some, 1.0 / jnp.maximum(jnp.sum(total, axis=0, keepdims=True), 1.0), 0.0)
         for index in range(chunks):
             part = scores[128 * index : 128 * index + 128] * scale
             weights[128 * index : 128 * index + 128] = part.astype(BF16)
@@ -465,28 +467,26 @@
     g_out_t[16:] = total[160:, HEAD:]
 
 
+SEQ = ("z_low", "y", "x")
+
+
 def shift(array, by):
-    return lax.ppermute(array, "seq", [(i, i + by) for i in range(32) if 0 <= i + by < 32])
+    return lax.ppermute(array, SEQ, [(i, i + by) for i in range(32) if 0 <= i + by < 32])
 
 
 def other_core(array):
-    return lax.ppermute(array, "dp", [(i, i ^ 1) for i in range(8)])
-
-
-def swap_rows(array):
-    return lax.all_to_all(array, "seq", 0, 0, axis_index_groups=ROW_GROUPS)
+    return lax.ppermute(array, "core", [(0, 1), (1, 0)])
 
 
 def turn_x(pieces):
     return [pieces[0]] + [
-        lax.ppermute(pieces[by], "seq", [(i, i // 4 * 4 + (i + by) % 4) for i in range(32)])
-        for by in range(1, 4)
+        lax.ppermute(pieces[by], "x", [(i, (i + by) % 4) for i in range(4)]) for by in range(1, 4)
     ]
 
 
 def turn_z(pieces):
     return [pieces[0]] + [
-        lax.ppermute(pieces[by], "dp", [(i, (i + 2 * by) % 8) for i in range(8)]) for by in range(1, 4)
+        lax.ppermute(pieces[by], "z_high", [(i, (i + by) % 4) for i in range(4)]) for by in range(1, 4)
     ]
 
 
@@ -511,8 +511,14 @@
     conv_in, d_gating_in, g_taps_in = call(
         conv_inner_kernel,
         [wide_f, wide_f, ((32, 1024), F32)],
-        [pltpu.VMEM((160, 1024), F32), pltpu.VMEM((160, 1024), F32)],
+        [pltpu.VMEM((8, 160, 128), F32), pltpu.VMEM((8, 160, 128), F32), pltpu.VMEM((32, 8, 1024), F32)],
     )(gating, d_conv, conv_kernel)
+    in_x, conv_in, before, after = lax.optimization_barrier((in_x, conv_in, before, after))
+    normed, query, kv = call(
+        project_kernel, [((512, 1024), BF16), ((4, ROWS, 128), BF16), quad], scalars=1
+    )(lengths, *in_x, w_qkv)
+    kv_before, kv_after = shift(kv, 4), shift(kv, -4)
+    conv_in, kv = lax.optimization_barrier((conv_in, kv))
     gate = ((1664, 128), BF16)
     d_upper, *gate_x = call(
         conv_outer_kernel,
@@ -522,11 +528,7 @@
          pltpu.VMEM((32, 1024), F32), pltpu.VMEM((2048, ROWS), BF16), pltpu.VMEM((32, 16, 128), BF16)],
         scalars=1,
     )(lengths, conv_in, d_gating_in, g_taps_in, d_conv, resid, d_gated, unit, inverse, slope, before, after, conv_kernel)
-    in_x, gate_x = lax.optimization_barrier((in_x, gate_x))
-    normed, query, kv = call(
-        project_kernel, [((512, 1024), BF16), ((4, ROWS, 128), BF16), quad], scalars=1
-    )(lengths, *in_x, w_qkv)
-    kv_before, kv_after = shift(kv, 4), shift(kv, -4)
+    gate_x, kv_before = lax.optimization_barrier((gate_x, kv_before))
     gate_x = turn_x(gate_x)
     context, d_query, d_before, d_after, d_own = call(
         attend_kernel,
@@ -539,11 +541,7 @@
         scalars=1,
     )(lengths, query, kv, kv_before, kv_after, *in_x)
     from_before, from_after = shift(d_after, 4), shift(d_before, -4)
-    frames_later, d_own = lax.optimization_barrier((frames, d_own))
-    layer_part, d_normed = call(gate_rows_kernel, [wide_f + (HBM,), wide_f + (HBM,)])(
-        *in_hbm(frames_later), gate_x[0], *in_hbm(d_upper), w_up, w_down
-    )
-    gate_x, d_normed, d_own = lax.optimization_barrier((gate_x, d_normed, d_own))
+    gate_x, d_own = lax.optimization_barrier((gate_x, d_own))
     small = ((384, 128), BF16)
     *far, back_0, back_1, back_2, back_3 = call(
         join_kernel, [((224, 512), BF16)] * 4 + [small + (HBM,)] * 4, [pltpu.VMEM((384, 512), BF16)], scalars=1
@@ -563,10 +561,13 @@
         [pltpu.VMEM((512, 512), BF16), pltpu.VMEM((384, 512), BF16)],
         scalars=1,
     )(lengths, normed, cot_own, *far_x)
-    send, *back = lax.optimization_barrier((send, back_0, back_1, back_2, back_3))
+    send, frames_later, *back = lax.optimization_barrier((send, frames, back_0, back_1, back_2, back_3))
     back_x = turn_x(back)
+    layer_part, d_normed = call(gate_rows_kernel, [wide_f, wide_f])(
+        frames_later, gate_x[0], *in_hbm(d_upper, w_up, w_down)
+    )
     (parts,) = call(add_kernel, [((8, 176, 512), BF16, HBM)])(keep, gate_far, attention_keep, other_core(send))
-    parts = swap_rows(parts)
+    parts = lax.all_to_all(parts, ("z_low", "y"), 0, 0)
     layer_out, d_frames = call(
         rows_kernel, [wide, wide], [pltpu.VMEM((ROWS, 512), BF16), pltpu.VMEM((1536, ROWS), BF16)], scalars=1
     )(
@@ -586,18 +587,20 @@
 
 
 def solution(mesh):
+    split = Mesh(mesh.devices.reshape(2, 4, 4, 4, 2), SEQ + ("z_high", "core"))
+    dp = ("z_high", "core")
     return jax.shard_map(
         local,
-        mesh=mesh,
-        in_specs=(P("dp", "seq", None), P("dp", "seq", None), P("dp"), P(), P(), P(), P(), P()),
+        mesh=split,
+        in_specs=(P(dp, SEQ, None), P(dp, SEQ, None), P(dp), P(), P(), P(), P(), P()),
         out_specs=(
-            P("dp", "seq", None),
-            P("dp", "seq", None),
-            P("dp", "seq"),
-            P("dp", "seq"),
-            P("dp", "seq"),
-            P("dp", "seq"),
-            P(None, "seq"),
+            P(dp, SEQ, None),
+            P(dp, SEQ, None),
+            P(dp, SEQ),
+            P(dp, SEQ),
+            P(dp, SEQ),
+            P(dp, SEQ),
+            P(None, SEQ),
         ),
         check_vma=False,
     )

time: 130 us -> 123 us (0.946)
  Pallas kernels: 38.9 us -> 35.8 us
  starting transfers between devices: 60.1 us -> 58.2 us
    pallas_call x14, Pallas kernels: 38.9 us -> 35.8 us  [run(): pl.pallas_call(body, out_shape=[HBM(*out[:2]) if len(out) > 2 else jax.Sh...]
    all_to_all x1, starting transfers between devices: 10.8 us -> 7.83 us  [local(): parts = lax.all_to_all(parts, ('z_low', 'y'), 0, 0)]
  transfers between devices with their start and end apart: 24 -> 24, of which waited for: 10 -> 10; matrix products, arithmetic and copies ran while one was open for 0% -> 0% of each run, Pallas kernels for 24% -> 23%
where the time goes in v5:
time: 123 us; the launch traced here: 122 us
  starting transfers between devices  58.2 us (47%)
  Pallas kernels  35.8 us (29%)
  waiting for transfers between devices  26.7 us (22%)
  between operations  1.54 us (1%)
    pallas_call x14, Pallas kernels, run(): pl.pallas_call(body, out_shape=[HBM(*out[:2]) if len(out) > 2 else jax.Sh...  35.8 us
    ppermute x6, starting transfers between devices, shift(): lax.ppermute(array, SEQ, [(i, i + by) for i in range(32) if 0 <= i + by <...  20.1 us
    ppermute x12, starting transfers between devices, turn_x(): lax.ppermute(pieces[by], 'x', [(i, (i + by) % 4) for i in range(4)])  19.3 us
    ppermute x12, waiting for transfers between devices, turn_x(): lax.ppermute(pieces[by], 'x', [(i, (i + by) % 4) for i in range(4)])  15.4 us
    ppermute x3, starting transfers between devices, turn_z(): lax.ppermute(pieces[by], 'z_high', [(i, (i + by) % 4) for i in range(4)])  10.5 us
    all_to_all x1, starting transfers between devices, local(): parts = lax.all_to_all(parts, ('z_low', 'y'), 0, 0)  7.83 us
    ppermute x6, waiting for transfers between devices, shift(): lax.ppermute(array, SEQ, [(i, i + by) for i in range(32) if 0 <= i + by <...  3.44 us
    all_to_all x1, waiting for transfers between devices, local(): parts = lax.all_to_all(parts, ('z_low', 'y'), 0, 0)  3.27 us
  transfers between devices with their start and end apart: 24, of which 10 were waited for; matrix products, arithmetic and copies ran while one was open for 0% of the time, Pallas kernels for 23%

profile of v5, /device:TPU:8, one launch (start us, length us, event | category | flops | bytes accessed | tf_op | source)
XLA Modules:
  0.0 122.3 jit_solution(10761015080564707441)
XLA Ops:
  1.3 2.0 %shard_map.135 = (bf16[128,1408]{1,0:T(8,128)(2,1)S(1)}, bf16[128,1408]{1,0:T(8,128)(2,1)S(1)}, bf16[128,1408]{1,0:T(8,128)(2,1)S(1)}, bf16[128,1408]{1,0:T(8,128)(2,1)S(1)}) custom-call(s32[1]{0:T(128)S(6)} %copy.15.lengths, bf16[128,1024]{1,0:T(8,128)(2,1)} %bitcast.8, bf16[128,1024]{1,0:T(8,128)(2,1)} %bitcast.12, bf16[512,1024]{1,0:T(8,128)(2,1)} %w_out.3), custom_call_target="tpu_custom_call" | custom-call | tf_op jit(solution)/shard_map/pallas_call | solution.py:31
  3.3 1.6 %collective-permute-start = (bf16[128,1408]{1,0:T(8,128)(2,1)S(1)}, bf16[128,1408]{1,0:T(8,128)(2,1)S(1)}, u32[]{:S(2)}, u32[]{:S(2)}) collective-permute-start(bf16[128,1408]{1,0:T(8,128)(2,1)S(1)} %get-tuple-element.108), channel_id=1, source_target_pairs={{0,8},{8,16},{16,24},{24,0},{1,9},{9,17},{17,25},{25,1},{2,10},{10... | collective-permute-start | bytes 1081352 | tf_op jit(solution)/shard_map/ppermute | solution.py:483
  4.8 2.7 %collective-permute-start.1 = (bf16[128,1408]{1,0:T(8,128)(2,1)S(1)}, bf16[128,1408]{1,0:T(8,128)(2,1)S(1)}, u32[]{:S(2)}, u32[]{:S(2)}) collective-permute-start(bf16[128,1408]{1,0:T(8,128)(2,1)S(1)} %get-tuple-element.109), channel_id=1, source_target_pairs={{0,16},{8,24},{16,0},{24,8},{1,17},{9,25},{17,1},{25,9},{2,18},{10... | collective-permute-start | bytes 1081352 | tf_op jit(solution)/shard_map/ppermute | solution.py:483
  7.6 1.4 %collective-permute-start.2 = (bf16[128,1408]{1,0:T(8,128)(2,1)S(1)}, bf16[128,1408]{1,0:T(8,128)(2,1)S(1)}, u32[]{:S(2)}, u32[]{:S(2)}) collective-permute-start(bf16[128,1408]{1,0:T(8,128)(2,1)S(1)} %get-tuple-element.110), channel_id=1, source_target_pairs={{0,24},{8,0},{16,8},{24,16},{1,25},{9,1},{17,9},{25,17},{2,26},{10... | collective-permute-start | bytes 1081352 | tf_op jit(solution)/shard_map/ppermute | solution.py:483
  9.0 4.9 %shard_map.136 = (bf16[128,1024]{1,0:T(8,128)(2,1)S(1)}, bf16[128,1024]{1,0:T(8,128)(2,1)S(1)}, bf16[128,1024]{1,0:T(8,128)(2,1)S(1)}, bf16[128,1024]{1,0:T(8,12...) custom-call(s32[1]{0:T(128)S(6)} %copy.15.lengths, ...), custom_call_target="tpu_custom_call" | custom-call | tf_op jit(solution)/shard_map/pallas_call | solution.py:31
  13.9 2.5 %collective-permute-start.3 = (bf16[16,2048]{1,0:T(8,128)(2,1)S(1)}, bf16[16,2048]{1,0:T(8,128)(2,1)S(1)}, u32[]{:S(2)}, u32[]{:S(2)}) collective-permute-start(bf16[16,2048]{1,0:T(8,128)(2,1)S(1)} %get-tuple-element.115), channel_id=1, source_target_pairs={{0,8},{8,16},{16,24},{24,32},{32,40},{40,48},{48,56},{56,64},{64,7... | collective-permute-start | bytes 196616 | tf_op jit(solution)/shard_map/ppermute | solution.py:474
  16.4 5.4 %collective-permute-start.4 = (bf16[16,2048]{1,0:T(8,128)(2,1)S(1)}, bf16[16,2048]{1,0:T(8,128)(2,1)S(1)}, u32[]{:S(2)}, u32[]{:S(2)}) collective-permute-start(bf16[16,2048]{1,0:T(8,128)(2,1)S(1)} %get-tuple-element.116), channel_id=1, source_target_pairs={{8,0},{16,8},{24,16},{32,24},{40,32},{48,40},{56,48},{64,56},{72,6... | collective-permute-start | bytes 196616 | tf_op jit(solution)/shard_map/ppermute | solution.py:474
  21.9 3.6 %shard_map.137 = (f32[128,1024]{1,0:T(8,128)S(1)}, f32[128,1024]{1,0:T(8,128)S(1)}, f32[32,1024]{1,0:T(8,128)S(1)}) custom-call(bf16[128,1024]{1,0:T(8,128)(2,1)S(1)} %get-tuple-element.112.gating, bf16[128,1024]{1,0:T(8,128)(2,1)S(1)} %get-tuple-element.113.d_conv, f32[31,1024]{1,0:T(8,128)S(1)} %copy-done.3), custom_call_target="tpu_custom_call" | custom-call | tf_op jit(solution)/shard_map/pallas_call | solution.py:31
  25.6 1.3 %shard_map.138 = (bf16[512,1024]{1,0:T(8,128)(2,1)S(1)}, bf16[4,128,128]{2,1,0:T(8,128)(2,1)S(1)}, bf16[4,128,256]{2,1,0:T(8,128)(2,1)S(1)}) custom-call(s32[1]{0:T(128)S(6)} %copy.15.lengths, bf16[128,1408]{1,0:T(8,128)(2,1)S(1)} %get-tuple-element.117.frames_0.cot_0, bf16[128,1408]{1,0:T(8,128)(2,1)S(1)} %collective-permute-done.frames_1.cot_1, ...), custom_call_target="tpu_custom_call" | custom-call | tf_op jit(solution)/shard_map/pallas_call | solution.py:31
  26.9 3.5 %collective-permute-start.5 = (bf16[4,128,256]{2,1,0:T(8,128)(2,1)S(1)}, bf16[4,128,256]{2,1,0:T(8,128)(2,1)S(1)}, u32[]{:S(2)}, u32[]{:S(2)}) collective-permute-start(bf16[4,128,256]{2,1,0:T(8,128)(2,1)S(1)} %get-tuple-element.125.kv), channel_id=1, source_target_pairs={{0,32},{8,40},{16,48},{24,56},{32,64},{40,72},{48,80},{56,88},{64,... | collective-permute-start | bytes 786440 | tf_op jit(solution)/shard_map/ppermute | solution.py:474
  30.4 2.4 %collective-permute-start.6 = (bf16[4,128,256]{2,1,0:T(8,128)(2,1)S(1)}, bf16[4,128,256]{2,1,0:T(8,128)(2,1)S(1)}, u32[]{:S(2)}, u32[]{:S(2)}) collective-permute-start(bf16[4,128,256]{2,1,0:T(8,128)(2,1)S(1)} %get-tuple-element.125.kv), channel_id=1, source_target_pairs={{32,0},{40,8},{48,16},{56,24},{64,32},{72,40},{80,48},{88,56},{96,... | collective-permute-start | bytes 786440 | tf_op jit(solution)/shard_map/ppermute | solution.py:474
  32.8 2.8 %shard_map.139 = (bf16[128,2048]{1,0:T(8,128)(2,1)}, bf16[1664,128]{1,0:T(8,128)(2,1)S(1)}, bf16[1664,128]{1,0:T(8,128)(2,1)S(1)}, bf16[1664,128]{1,0:T(8,128)(2,1)S(1)}, bf16[1664,128]{1,0:T(8,128)(2,1)S(1)}) custom-call(s32[1]{0:T(128)S(6)} %copy.15.lengths, f32[128,1024]{1,0:T(8,128)S(1)} %get-tuple-element.126.conv_in, ...), custom_call_target="tpu_custom_call" | custom-call | tf_op jit(solution)/shard_map/pallas_call | solution.py:31
  35.5 0.7 collective-permute-done.5.before
  36.2 0.7 collective-permute-start.7
  36.9 3.3 %collective-permute-start.8 = (bf16[1664,128]{1,0:T(8,128)(2,1)S(1)}, bf16[1664,128]{1,0:T(8,128)(2,1)S(1)}, u32[]{:S(2)}, u32[]{:S(2)}) collective-permute-start(bf16[1664,128]{1,0:T(8,128)(2,1)S(1)} %get-tuple-element.145), channel_id=1, source_target_pairs={{0,16},{8,24},{16,0},{24,8},{1,17},{9,25},{17,1},{25,9},{2,18},{10... | collective-permute-start | bytes 1277960 | tf_op jit(solution)/shard_map/ppermute | solution.py:483
  40.1 0.1 collective-permute-start.9
  40.3 6.0 %shard_map.140 = (bf16[4,128,128]{2,1,0:T(8,128)(2,1)S(1)}, bf16[128,512]{1,0:T(8,128)(2,1)S(1)}, bf16[4,128,256]{2,1,0:T(8,128)(2,1)S(1)}, bf16[4,128,256]{2,1,0:T(8,128)(2,1)S(1)}, f32[4,128,256]{2,1,0:T(8,128)S(1)}) custom-call(s32[1]{0:T(128)S(6)} %copy.15.lengths, bf16[4,128,128]{2,1,0:T(8,128)(2,1)S(1)} %get-tuple-element.122.queries, ...), custom_call_target="tpu_custom_call" | custom-call | tf_op jit(solution)/shard_map/pallas_call | solution.py:31
  46.3 4.4 %collective-permute-start.10 = (bf16[4,128,256]{2,1,0:T(8,128)(2,1)S(1)}, bf16[4,128,256]{2,1,0:T(8,128)(2,1)S(1)}, u32[]{:S(2)}, u32[]{:S(2)}) collective-permute-start(bf16[4,128,256]{2,1,0:T(8,128)(2,1)S(1)} %get-tuple-element.149), channel_id=1, source_target_pairs={{0,32},{8,40},{16,48},{24,56},{32,64},{40,72},{48,80},{56,88},{64,... | collective-permute-start | bytes 786440 | tf_op jit(solution)/shard_map/ppermute | solution.py:474
  50.7 1.9 %collective-permute-start.11 = (bf16[4,128,256]{2,1,0:T(8,128)(2,1)S(1)}, bf16[4,128,256]{2,1,0:T(8,128)(2,1)S(1)}, u32[]{:S(2)}, u32[]{:S(2)}) collective-permute-start(bf16[4,128,256]{2,1,0:T(8,128)(2,1)S(1)} %get-tuple-element.150), channel_id=1, source_target_pairs={{32,0},{40,8},{48,16},{56,24},{64,32},{72,40},{80,48},{88,56},{96,... | collective-permute-start | bytes 786440 | tf_op jit(solution)/shard_map/ppermute | solution.py:474
  52.6 4.3 %collective-permute-done.8.gate_2 = bf16[1664,128]{1,0:T(8,128)(2,1)S(1)} collective-permute-done((bf16[1664,128]{1,0:T(8,128)(2,1)S(1)}, bf16[1664,128]{1,0:T(8,128)(2,1)S(1)}, u32[]{:S(2)}, u32[]{:S(2)}) %collective-permute-start.8) | collective-permute-done | bytes 426016 | tf_op jit(solution)/shard_map/ppermute | solution.py:483
  56.9 0.2 collective-permute-done.9.gate_3
  57.1 2.8 %collective-permute-done.11.from_after = bf16[4,128,256]{2,1,0:T(8,128)(2,1)S(1)} collective-permute-done((bf16[4,128,256]{2,1,0:T(8,128)(2,1)S(1)}, bf16[4,128,256]{2,1,0:T(8,128)(2,1)S(1)}, u32[]{:S(2)}, u32[]{:S(2)}) %collective-permute-start.11) | collective-permute-done | bytes 262176 | tf_op jit(solution)/shard_map/ppermute | solution.py:474
  59.9 1.1 shard_map.141
  61.0 1.3 %shard_map.142 = (bf16[8,112,512]{2,1,0:T(8,128)(2,1)S(1)}, bf16[8,112,512]{2,1,0:T(8,128)(2,1)S(1)}, bf16[256,512]{1,0:T(8,128)(2,1)S(1)}) custom-call(s32[1]{0:T(128)S(6)} %copy.15.lengths, bf16[512,1024]{1,0:T(8,128)(2,1)S(1)} %get-tuple-element.121.normed, bf16[128,1408]{1,0:T(8,128)(2,1)S(1)} %get-tuple-element.117.frames_0.cot_0, ...), custom_call_target="tpu_custom_call" | custom-call | tf_op jit(solution)/shard_map/pallas_call | solution.py:31
  62.3 0.1 collective-permute-start.12
  62.4 1.1 collective-permute-start.13
  63.5 1.7 %collective-permute-start.14 = (bf16[224,512]{1,0:T(8,128)(2,1)S(1)}, bf16[224,512]{1,0:T(8,128)(2,1)S(1)}, u32[]{:S(2)}, u32[]{:S(2)}) collective-permute-start(bf16[224,512]{1,0:T(8,128)(2,1)S(1)} %get-tuple-element.168), channel_id=1, source_target_pairs={{0,16},{8,24},{16,0},{24,8},{1,17},{9,25},{17,1},{25,9},{2,18},{10... | collective-permute-start | bytes 688136 | tf_op jit(solution)/shard_map/ppermute | solution.py:483
  65.2 1.1 collective-permute-start.15
  66.3 10.2 %collective-permute-done.13.far_1 = bf16[224,512]{1,0:T(8,128)(2,1)S(1)} collective-permute-done((bf16[224,512]{1,0:T(8,128)(2,1)S(1)}, bf16[224,512]{1,0:T(8,128)(2,1)S(1)}, u32[]{:S(2)}, u32[]{:S(2)}) %collective-permute-start.13) | collective-permute-done | bytes 229408 | tf_op jit(solution)/shard_map/ppermute | solution.py:483
  76.6 0.6 collective-permute-done.15.far_3
  77.2 1.1 shard_map.143
  78.3 0.3 collective-permute-start.16
  78.6 1.9 %collective-permute-done.16.attention_far = bf16[8,64,512]{2,1,0:T(8,128)(2,1)S(1)} collective-permute-done((bf16[8,64,512]{2,1,0:T(8,128)(2,1)S(1)}, bf16[8,64,512]{2,1,0:T(8,128)(2,1)S(1)}, u32[]{:S(2)}, u32[]{:S(2)}) %collective-permute-start.16) | collective-permute-done | bytes 524320 | tf_op jit(solution)/shard_map/ppermute | solution.py:478
  80.5 1.5 %shard_map.144 = bf16[8,176,512]{2,1,0:T(8,128)(2,1)} custom-call(bf16[8,112,512]{2,1,0:T(8,128)(2,1)S(1)} %get-tuple-element.163.gate, bf16[8,112,512]{2,1,0:T(8,128)(2,1)S(1)} %collective-permute-done.12.gate_far, bf16[8,64,512]{2,1,0:T(8,128)(2,1)S(1)} %get-tuple-element.170.attention, bf16[8,64,512]{2,1,0:T(8,128)(2,1)S(1)} %collective-permute-done.16.attention_far), custom_call_target="tpu_custom_call" | custom-call | tf_op jit(solution)/shard_map/pallas_call | solution.py:31
  82.0 7.8 %all-to-all-start = ((bf16[8,176,512]{2,1,0:T(8,128)(2,1)}), bf16[8,176,512]{2,1,0:T(8,128)(2,1)S(1)}, u32[]{:S(2)}, u32[]{:S(2)}) async-start(bf16[8,176,512]{2,1,0:T(8,128)(2,1)} %shard_map.144), calls=%async_computation | async-start | bytes 2883584 | tf_op jit(solution)/shard_map/all_to_all | solution.py:570
  89.8 1.7 %collective-permute-start.17 = (bf16[384,128]{1,0:T(8,128)(2,1)S(1)}, bf16[384,128]{1,0:T(8,128)(2,1)S(1)}, u32[]{:S(2)}, u32[]{:S(2)}) collective-permute-start(bf16[384,128]{1,0:T(8,128)(2,1)S(1)} %copy-done.7), channel_id=1, source_target_pairs={{0,8},{8,16},{16,24},{24,0},{1,9},{9,17},{17,25},{25,1},{2,10},{10... | collective-permute-start | bytes 294920 | tf_op jit(solution)/shard_map/ppermute | solution.py:483
  91.5 2.4 %collective-permute-start.18 = (bf16[384,128]{1,0:T(8,128)(2,1)S(1)}, bf16[384,128]{1,0:T(8,128)(2,1)S(1)}, u32[]{:S(2)}, u32[]{:S(2)}) collective-permute-start(bf16[384,128]{1,0:T(8,128)(2,1)S(1)} %copy-done.6), channel_id=1, source_target_pairs={{0,16},{8,24},{16,0},{24,8},{1,17},{9,25},{17,1},{25,9},{2,18},{10... | collective-permute-start | bytes 294920 | tf_op jit(solution)/shard_map/ppermute | solution.py:483
  93.9 1.5 %collective-permute-start.19 = (bf16[384,128]{1,0:T(8,128)(2,1)S(1)}, bf16[384,128]{1,0:T(8,128)(2,1)S(1)}, u32[]{:S(2)}, u32[]{:S(2)}) collective-permute-start(bf16[384,128]{1,0:T(8,128)(2,1)S(1)} %copy-done.5), channel_id=1, source_target_pairs={{0,24},{8,0},{16,8},{24,16},{1,25},{9,1},{17,9},{25,17},{2,26},{10... | collective-permute-start | bytes 294920 | tf_op jit(solution)/shard_map/ppermute | solution.py:483
  95.4 4.8 %shard_map.145 = (f32[128,1024]{1,0:T(8,128)S(1)}, f32[128,1024]{1,0:T(8,128)S(1)}) custom-call(bf16[128,1024]{1,0:T(8,128)(2,1)S(1)} %bitcast.10, bf16[1664,128]{1,0:T(8,128)(2,1)S(1)} %get-tuple-element.159.gate_0.gate, bf16[128,2048]{1,0:T(8,128)(2,1)} %get-tuple-element.182.d_upper, bf16[1024,2048]{1,0:T(8,128)(2,1)} %w_up.3, bf16[1024,1024]{1,0:T(8,128)(2,1)} %w_down.3), custom_call_target="tpu_custom_call" | custom-call | tf_op jit(solution)/shard_map/pallas_call | solution.py:31
  100.3 4.4 %shard_map.146 = (bf16[128,1024]{1,0:T(8,128)(2,1)}, bf16[128,1024]{1,0:T(8,128)(2,1)}) custom-call(s32[1]{0:T(128)S(6)} %copy.15.lengths, bf16[128,1024]{1,0:T(8,128)(2,1)S(1)} %bitcast.11, bf16[128,1024]{1,0:T(8,128)(2,1)S(1)} %bitcast.14, bf16[224,512]{1,0:T(8,128)(2,1)S(1)} %get-tuple-element.166.far_0, ...), custom_call_target="tpu_custom_call" | custom-call | tf_op jit(solution)/shard_map/pallas_call | solution.py:31
  104.7 3.3 %all-to-all-done.parts = bf16[8,176,512]{2,1,0:T(8,128)(2,1)S(1)} async-done(((bf16[8,176,512]{2,1,0:T(8,128)(2,1)}), bf16[8,176,512]{2,1,0:T(8,128)(2,1)S(1)}, u32[]{:S(2)}, u32[]{:S(2)}) %all-to-all-start) | async-done | bytes 1441824 | tf_op jit(solution)/shard_map/all_to_all | solution.py:570
  108.0 0.2 shard_map.147
  108.2 3.3 %collective-permute-start.20 = (bf16[176,128]{1,0:T(8,128)(2,1)S(1)}, bf16[176,128]{1,0:T(8,128)(2,1)S(1)}, u32[]{:S(2)}, u32[]{:S(2)}) collective-permute-start(bf16[176,128]{1,0:T(8,128)(2,1)S(1)} %get-tuple-element.191), channel_id=1, source_target_pairs={{0,2},{2,4},{4,6},{6,0},{1,3},{3,5},{5,7},{7,1},{8,10},{10,12},{12... | collective-permute-start | bytes 135176 | tf_op jit(solution)/shard_map/ppermute | solution.py:489
  111.5 4.5 %collective-permute-start.21 = (bf16[176,128]{1,0:T(8,128)(2,1)S(1)}, bf16[176,128]{1,0:T(8,128)(2,1)S(1)}, u32[]{:S(2)}, u32[]{:S(2)}) collective-permute-start(bf16[176,128]{1,0:T(8,128)(2,1)S(1)} %get-tuple-element.192), channel_id=1, source_target_pairs={{0,4},{2,6},{4,0},{6,2},{1,5},{3,7},{5,1},{7,3},{8,12},{10,14},{12... | collective-permute-start | bytes 135176 | tf_op jit(solution)/shard_map/ppermute | solution.py:489
  116.0 2.7 %collective-permute-start.22 = (bf16[176,128]{1,0:T(8,128)(2,1)S(1)}, bf16[176,128]{1,0:T(8,128)(2,1)S(1)}, u32[]{:S(2)}, u32[]{:S(2)}) collective-permute-start(bf16[176,128]{1,0:T(8,128)(2,1)S(1)} %get-tuple-element.193), channel_id=1, source_target_pairs={{0,6},{2,0},{4,2},{6,4},{1,7},{3,1},{5,3},{7,5},{8,14},{10,8},{12,... | collective-permute-start | bytes 135176 | tf_op jit(solution)/shard_map/ppermute | solution.py:489
  118.7 1.5 %collective-permute-done.21.part_2 = bf16[176,128]{1,0:T(8,128)(2,1)S(1)} collective-permute-done((bf16[176,128]{1,0:T(8,128)(2,1)S(1)}, bf16[176,128]{1,0:T(8,128)(2,1)S(1)}, u32[]{:S(2)}, u32[]{:S(2)}) %collective-permute-start.21) | collective-permute-done | bytes 45088 | tf_op jit(solution)/shard_map/ppermute | solution.py:489
  120.2 1.3 %collective-permute-done.22.part_3 = bf16[176,128]{1,0:T(8,128)(2,1)S(1)} collective-permute-done((bf16[176,128]{1,0:T(8,128)(2,1)S(1)}, bf16[176,128]{1,0:T(8,128)(2,1)S(1)}, u32[]{:S(2)}, u32[]{:S(2)}) %collective-permute-start.22) | collective-permute-done | bytes 45088 | tf_op jit(solution)/shard_map/ppermute | solution.py:489
  121.5 0.8 shard_map.148
  (30 shorter events, 0.1 us)
Async XLA Ops:
  3.2 18.6 %copy-start.3 = (f32[31,1024]{1,0:T(8,128)S(1)}, f32[31,1024]{1,0:T(8,128)}, u32[]{:S(2)}) copy-start(f32[31,1024]{1,0:T(8,128)} %taps.3) | copy-start | bytes 380932
  3.3 22.3 %copy-start = (bf16[1024,1536]{1,0:T(8,128)(2,1)S(1)}, bf16[1024,1536]{1,0:T(8,128)(2,1)}, u32[]{:S(2)}) copy-start(bf16[1024,1536]{1,0:T(8,128)(2,1)} %w_qkv.3) | copy-start | bytes 9437188
  3.3 22.3 %collective-permute-start = (bf16[128,1408]{1,0:T(8,128)(2,1)S(1)}, bf16[128,1408]{1,0:T(8,128)(2,1)S(1)}, u32[]{:S(2)}, u32[]{:S(2)}) collective-permute-start(bf16[128,1408]{1,0:T(8,128)(2,1)S(1)} %get-tuple-element.108), channel_id=1, source_target_pairs={{0,8},{8,16},{16,24},{24,0},{1,9},{9,17},{17,25},{25,1},{2,10},{10... | collective-permute-start | bytes 1081352 | tf_op jit(solution)/shard_map/ppermute | solution.py:483
  4.8 20.7 %collective-permute-start.1 = (bf16[128,1408]{1,0:T(8,128)(2,1)S(1)}, bf16[128,1408]{1,0:T(8,128)(2,1)S(1)}, u32[]{:S(2)}, u32[]{:S(2)}) collective-permute-start(bf16[128,1408]{1,0:T(8,128)(2,1)S(1)} %get-tuple-element.109), channel_id=1, source_target_pairs={{0,16},{8,24},{16,0},{24,8},{1,17},{9,25},{17,1},{25,9},{2,18},{10... | collective-permute-start | bytes 1081352 | tf_op jit(solution)/shard_map/ppermute | solution.py:483
  7.6 18.0 %collective-permute-start.2 = (bf16[128,1408]{1,0:T(8,128)(2,1)S(1)}, bf16[128,1408]{1,0:T(8,128)(2,1)S(1)}, u32[]{:S(2)}, u32[]{:S(2)}) collective-permute-start(bf16[128,1408]{1,0:T(8,128)(2,1)S(1)} %get-tuple-element.110), channel_id=1, source_target_pairs={{0,24},{8,0},{16,8},{24,16},{1,25},{9,1},{17,9},{25,17},{2,26},{10... | collective-permute-start | bytes 1081352 | tf_op jit(solution)/shard_map/ppermute | solution.py:483
  13.9 11.6 %collective-permute-start.3 = (bf16[16,2048]{1,0:T(8,128)(2,1)S(1)}, bf16[16,2048]{1,0:T(8,128)(2,1)S(1)}, u32[]{:S(2)}, u32[]{:S(2)}) collective-permute-start(bf16[16,2048]{1,0:T(8,128)(2,1)S(1)} %get-tuple-element.115), channel_id=1, source_target_pairs={{0,8},{8,16},{16,24},{24,32},{32,40},{40,48},{48,56},{56,64},{64,7... | collective-permute-start | bytes 196616 | tf_op jit(solution)/shard_map/ppermute | solution.py:474
  16.4 9.1 %collective-permute-start.4 = (bf16[16,2048]{1,0:T(8,128)(2,1)S(1)}, bf16[16,2048]{1,0:T(8,128)(2,1)S(1)}, u32[]{:S(2)}, u32[]{:S(2)}) collective-permute-start(bf16[16,2048]{1,0:T(8,128)(2,1)S(1)} %get-tuple-element.116), channel_id=1, source_target_pairs={{8,0},{16,8},{24,16},{32,24},{40,32},{48,40},{56,48},{64,56},{72,6... | collective-permute-start | bytes 196616 | tf_op jit(solution)/shard_map/ppermute | solution.py:474
  26.9 9.3 %collective-permute-start.5 = (bf16[4,128,256]{2,1,0:T(8,128)(2,1)S(1)}, bf16[4,128,256]{2,1,0:T(8,128)(2,1)S(1)}, u32[]{:S(2)}, u32[]{:S(2)}) collective-permute-start(bf16[4,128,256]{2,1,0:T(8,128)(2,1)S(1)} %get-tuple-element.125.kv), channel_id=1, source_target_pairs={{0,32},{8,40},{16,48},{24,56},{32,64},{40,72},{48,80},{56,88},{64,... | collective-permute-start | bytes 786440 | tf_op jit(solution)/shard_map/ppermute | solution.py:474
  30.4 9.9 %collective-permute-start.6 = (bf16[4,128,256]{2,1,0:T(8,128)(2,1)S(1)}, bf16[4,128,256]{2,1,0:T(8,128)(2,1)S(1)}, u32[]{:S(2)}, u32[]{:S(2)}) collective-permute-start(bf16[4,128,256]{2,1,0:T(8,128)(2,1)S(1)} %get-tuple-element.125.kv), channel_id=1, source_target_pairs={{32,0},{40,8},{48,16},{56,24},{64,32},{72,40},{80,48},{88,56},{96,... | collective-permute-start | bytes 786440 | tf_op jit(solution)/shard_map/ppermute | solution.py:474
  36.2 16.4 %collective-permute-start.7 = (bf16[1664,128]{1,0:T(8,128)(2,1)S(1)}, bf16[1664,128]{1,0:T(8,128)(2,1)S(1)}, u32[]{:S(2)}, u32[]{:S(2)}) collective-permute-start(bf16[1664,128]{1,0:T(8,128)(2,1)S(1)} %get-tuple-element.144), channel_id=1, source_target_pairs={{0,8},{8,16},{16,24},{24,0},{1,9},{9,17},{17,25},{25,1},{2,10},{10... | collective-permute-start | bytes 1277960 | tf_op jit(solution)/shard_map/ppermute | solution.py:483
  36.9 20.1 %collective-permute-start.8 = (bf16[1664,128]{1,0:T(8,128)(2,1)S(1)}, bf16[1664,128]{1,0:T(8,128)(2,1)S(1)}, u32[]{:S(2)}, u32[]{:S(2)}) collective-permute-start(bf16[1664,128]{1,0:T(8,128)(2,1)S(1)} %get-tuple-element.145), channel_id=1, source_target_pairs={{0,16},{8,24},{16,0},{24,8},{1,17},{9,25},{17,1},{25,9},{2,18},{10... | collective-permute-start | bytes 1277960 | tf_op jit(solution)/shard_map/ppermute | solution.py:483
  40.1 17.0 %collective-permute-start.9 = (bf16[1664,128]{1,0:T(8,128)(2,1)S(1)}, bf16[1664,128]{1,0:T(8,128)(2,1)S(1)}, u32[]{:S(2)}, u32[]{:S(2)}) collective-permute-start(bf16[1664,128]{1,0:T(8,128)(2,1)S(1)} %get-tuple-element.146), channel_id=1, source_target_pairs={{0,24},{8,0},{16,8},{24,16},{1,25},{9,1},{17,9},{25,17},{2,26},{10... | collective-permute-start | bytes 1277960 | tf_op jit(solution)/shard_map/ppermute | solution.py:483
  46.3 10.9 %collective-permute-start.10 = (bf16[4,128,256]{2,1,0:T(8,128)(2,1)S(1)}, bf16[4,128,256]{2,1,0:T(8,128)(2,1)S(1)}, u32[]{:S(2)}, u32[]{:S(2)}) collective-permute-start(bf16[4,128,256]{2,1,0:T(8,128)(2,1)S(1)} %get-tuple-element.149), channel_id=1, source_target_pairs={{0,32},{8,40},{16,48},{24,56},{32,64},{40,72},{48,80},{56,88},{64,... | collective-permute-start | bytes 786440 | tf_op jit(solution)/shard_map/ppermute | solution.py:474
  50.7 9.2 %collective-permute-start.11 = (bf16[4,128,256]{2,1,0:T(8,128)(2,1)S(1)}, bf16[4,128,256]{2,1,0:T(8,128)(2,1)S(1)}, u32[]{:S(2)}, u32[]{:S(2)}) collective-permute-start(bf16[4,128,256]{2,1,0:T(8,128)(2,1)S(1)} %get-tuple-element.150), channel_id=1, source_target_pairs={{32,0},{40,8},{48,16},{56,24},{64,32},{72,40},{80,48},{88,56},{96,... | collective-permute-start | bytes 786440 | tf_op jit(solution)/shard_map/ppermute | solution.py:474
  62.3 18.2 %collective-permute-start.12 = (bf16[8,112,512]{2,1,0:T(8,128)(2,1)S(1)}, bf16[8,112,512]{2,1,0:T(8,128)(2,1)S(1)}, u32[]{:S(2)}, u32[]{:S(2)}) collective-permute-start(bf16[8,112,512]{2,1,0:T(8,128)(2,1)S(1)} %get-tuple-element.164), channel_id=1, source_target_pairs={{0,1},{1,0},{2,3},{3,2},{4,5},{5,4},{6,7},{7,6},{8,9},{9,8},{10,11... | collective-permute-start | bytes 2752520 | tf_op jit(solution)/shard_map/ppermute | solution.py:478
  62.4 14.1 %collective-permute-start.13 = (bf16[224,512]{1,0:T(8,128)(2,1)S(1)}, bf16[224,512]{1,0:T(8,128)(2,1)S(1)}, u32[]{:S(2)}, u32[]{:S(2)}) collective-permute-start(bf16[224,512]{1,0:T(8,128)(2,1)S(1)} %get-tuple-element.167), channel_id=1, source_target_pairs={{0,8},{8,16},{16,24},{24,0},{1,9},{9,17},{17,25},{25,1},{2,10},{10... | collective-permute-start | bytes 688136 | tf_op jit(solution)/shard_map/ppermute | solution.py:483
  63.5 13.0 %collective-permute-start.14 = (bf16[224,512]{1,0:T(8,128)(2,1)S(1)}, bf16[224,512]{1,0:T(8,128)(2,1)S(1)}, u32[]{:S(2)}, u32[]{:S(2)}) collective-permute-start(bf16[224,512]{1,0:T(8,128)(2,1)S(1)} %get-tuple-element.168), channel_id=1, source_target_pairs={{0,16},{8,24},{16,0},{24,8},{1,17},{9,25},{17,1},{25,9},{2,18},{10... | collective-permute-start | bytes 688136 | tf_op jit(solution)/shard_map/ppermute | solution.py:483
  65.2 12.0 %collective-permute-start.15 = (bf16[224,512]{1,0:T(8,128)(2,1)S(1)}, bf16[224,512]{1,0:T(8,128)(2,1)S(1)}, u32[]{:S(2)}, u32[]{:S(2)}) collective-permute-start(bf16[224,512]{1,0:T(8,128)(2,1)S(1)} %get-tuple-element.169), channel_id=1, source_target_pairs={{0,24},{8,0},{16,8},{24,16},{1,25},{9,1},{17,9},{25,17},{2,26},{10... | collective-permute-start | bytes 688136 | tf_op jit(solution)/shard_map/ppermute | solution.py:483
  78.3 2.2 %collective-permute-start.16 = (bf16[8,64,512]{2,1,0:T(8,128)(2,1)S(1)}, bf16[8,64,512]{2,1,0:T(8,128)(2,1)S(1)}, u32[]{:S(2)}, u32[]{:S(2)}) collective-permute-start(bf16[8,64,512]{2,1,0:T(8,128)(2,1)S(1)} %get-tuple-element.176), channel_id=1, source_target_pairs={{0,1},{1,0},{2,3},{3,2},{4,5},{5,4},{6,7},{7,6},{8,9},{9,8},{10,11... | collective-permute-start | bytes 1572872 | tf_op jit(solution)/shard_map/ppermute | solution.py:478
  82.0 7.8 %copy-start.7 = (bf16[384,128]{1,0:T(8,128)(2,1)S(1)}, bf16[384,128]{1,0:T(8,128)(2,1)}, u32[]{:S(2)}) copy-start(bf16[384,128]{1,0:T(8,128)(2,1)} %get-tuple-element.178) | copy-start | bytes 294916
  82.0 9.5 %copy-start.6 = (bf16[384,128]{1,0:T(8,128)(2,1)S(1)}, bf16[384,128]{1,0:T(8,128)(2,1)}, u32[]{:S(2)}) copy-start(bf16[384,128]{1,0:T(8,128)(2,1)} %get-tuple-element.179) | copy-start | bytes 294916
  82.0 11.9 %copy-start.5 = (bf16[384,128]{1,0:T(8,128)(2,1)S(1)}, bf16[384,128]{1,0:T(8,128)(2,1)}, u32[]{:S(2)}) copy-start(bf16[384,128]{1,0:T(8,128)(2,1)} %get-tuple-element.180) | copy-start | bytes 294916
  82.0 13.4 %copy-start.1 = (bf16[1,128,1024]{2,1,0:T(8,128)(2,1)S(1)}, bf16[1,128,1024]{2,1,0:T(8,128)(2,1)}, u32[]{:S(2)}) copy-start(bf16[1,128,1024]{2,1,0:T(8,128)(2,1)} %param.8) | copy-start | bytes 786436
  82.0 26.0 %all-to-all-start = ((bf16[8,176,512]{2,1,0:T(8,128)(2,1)}), bf16[8,176,512]{2,1,0:T(8,128)(2,1)S(1)}, u32[]{:S(2)}, u32[]{:S(2)}) async-start(bf16[8,176,512]{2,1,0:T(8,128)(2,1)} %shard_map.144), calls=%async_computation | async-start | bytes 2883584 | tf_op jit(solution)/shard_map/all_to_all | solution.py:570
  89.8 10.4 %collective-permute-start.17 = (bf16[384,128]{1,0:T(8,128)(2,1)S(1)}, bf16[384,128]{1,0:T(8,128)(2,1)S(1)}, u32[]{:S(2)}, u32[]{:S(2)}) collective-permute-start(bf16[384,128]{1,0:T(8,128)(2,1)S(1)} %copy-done.7), channel_id=1, source_target_pairs={{0,8},{8,16},{16,24},{24,0},{1,9},{9,17},{17,25},{25,1},{2,10},{10... | collective-permute-start | bytes 294920 | tf_op jit(solution)/shard_map/ppermute | solution.py:483
  91.5 8.7 %collective-permute-start.18 = (bf16[384,128]{1,0:T(8,128)(2,1)S(1)}, bf16[384,128]{1,0:T(8,128)(2,1)S(1)}, u32[]{:S(2)}, u32[]{:S(2)}) collective-permute-start(bf16[384,128]{1,0:T(8,128)(2,1)S(1)} %copy-done.6), channel_id=1, source_target_pairs={{0,16},{8,24},{16,0},{24,8},{1,17},{9,25},{17,1},{25,9},{2,18},{10... | collective-permute-start | bytes 294920 | tf_op jit(solution)/shard_map/ppermute | solution.py:483
  93.9 6.4 %collective-permute-start.19 = (bf16[384,128]{1,0:T(8,128)(2,1)S(1)}, bf16[384,128]{1,0:T(8,128)(2,1)S(1)}, u32[]{:S(2)}, u32[]{:S(2)}) collective-permute-start(bf16[384,128]{1,0:T(8,128)(2,1)S(1)} %copy-done.5), channel_id=1, source_target_pairs={{0,24},{8,0},{16,8},{24,16},{1,25},{9,1},{17,9},{25,17},{2,26},{10... | collective-permute-start | bytes 294920 | tf_op jit(solution)/shard_map/ppermute | solution.py:483
  95.4 4.9 %copy-start.2 = (bf16[1,128,1024]{2,1,0:T(8,128)(2,1)S(1)}, bf16[1,128,1024]{2,1,0:T(8,128)(2,1)}, u32[]{:S(2)}) copy-start(bf16[1,128,1024]{2,1,0:T(8,128)(2,1)} %param.9) | copy-start | bytes 786436
  95.4 4.9 %copy-start.4 = (bf16[384,128]{1,0:T(8,128)(2,1)S(1)}, bf16[384,128]{1,0:T(8,128)(2,1)}, u32[]{:S(2)}) copy-start(bf16[384,128]{1,0:T(8,128)(2,1)} %get-tuple-element.177.back_0) | copy-start | bytes 294916
  108.2 10.5 %collective-permute-start.20 = (bf16[176,128]{1,0:T(8,128)(2,1)S(1)}, bf16[176,128]{1,0:T(8,128)(2,1)S(1)}, u32[]{:S(2)}, u32[]{:S(2)}) collective-permute-start(bf16[176,128]{1,0:T(8,128)(2,1)S(1)} %get-tuple-element.191), channel_id=1, source_target_pairs={{0,2},{2,4},{4,6},{6,0},{1,3},{3,5},{5,7},{7,1},{8,10},{10,12},{12... | collective-permute-start | bytes 135176 | tf_op jit(solution)/shard_map/ppermute | solution.py:489
  111.5 8.6 %collective-permute-start.21 = (bf16[176,128]{1,0:T(8,128)(2,1)S(1)}, bf16[176,128]{1,0:T(8,128)(2,1)S(1)}, u32[]{:S(2)}, u32[]{:S(2)}) collective-permute-start(bf16[176,128]{1,0:T(8,128)(2,1)S(1)} %get-tuple-element.192), channel_id=1, source_target_pairs={{0,4},{2,6},{4,0},{6,2},{1,5},{3,7},{5,1},{7,3},{8,12},{10,14},{12... | collective-permute-start | bytes 135176 | tf_op jit(solution)/shard_map/ppermute | solution.py:489
  116.0 5.4 %collective-permute-start.22 = (bf16[176,128]{1,0:T(8,128)(2,1)S(1)}, bf16[176,128]{1,0:T(8,128)(2,1)S(1)}, u32[]{:S(2)}, u32[]{:S(2)}) collective-permute-start(bf16[176,128]{1,0:T(8,128)(2,1)S(1)} %get-tuple-element.193), channel_id=1, source_target_pairs={{0,6},{2,0},{4,2},{6,4},{1,7},{3,1},{5,3},{7,5},{8,14},{10,8},{12,... | collective-permute-start | bytes 135176 | tf_op jit(solution)/shard_map/ppermute | solution.py:489

commit v6 on v5

--- a/solution.py
+++ b/solution.py
@@ -24,10 +24,11 @@
 VMEM_LIMIT = 24 * 2**20
 
 
-def call(body, outs, scratch=(), scalars=0):
+def call(body, outs, scratch=(), scalars=0, left=0):
     def run(*args):
         specs = [pl.BlockSpec(memory_space=pltpu.SMEM)] * scalars
-        specs += [pl.BlockSpec(memory_space=pltpu.VMEM)] * (len(args) - scalars)
+        specs += [pl.BlockSpec(memory_space=pltpu.VMEM)] * (len(args) - scalars - left)
+        specs += [pl.BlockSpec(memory_space=HBM)] * left
         return pl.pallas_call(
             body,
             out_shape=[
@@ -69,7 +70,7 @@
 def locate(lengths):
     z_low, y, x = lax.axis_index("z_low"), lax.axis_index("y"), lax.axis_index("x")
     row = 4 * z_low + y
-    return ((4 * row + x) * ROWS, lengths[0], lax.axis_index("core"), row * (GROUP * ROWS), x, lax.axis_index("z_high"))
+    return ((4 * row + x) * ROWS, lengths[0], lax.axis_index("core"), row * (GROUP * ROWS), x, lax.axis_index("z_high"), y, z_low)
 
 
 def slot(place, turn):
@@ -107,25 +108,36 @@
 
 def gate_kernel(
     lengths, frames, cotangent, w_up, w_down,
-    resid, d_gated, gating, d_conv, unit, inverse, slope, top, bottom
+    resid, d_gated, gating, d_conv, unit, inverse, slope, top, bottom,
+    up, down, copied
 ):
     place = locate(lengths)
     first_frame, length = place[0], place[1]
+    copies = [
+        pltpu.make_async_copy(w_up.at[:, pl.ds(1024 * half, 1024)], up.at[half], copied.at[half]) for half in (1, 0)
+    ] + [pltpu.make_async_copy(w_down, down, copied.at[2])]
+    for copy in copies:
+        copy.start()
     unit_rows, _ = normalize(frames[...].astype(F32))
-    upper = dot(unit_rows.astype(BF16), w_up[...])
-    phi = 0.5 * (1.0 + lax.erf(upper * HALF_ROOT))
-    slope[...] = phi + upper * jnp.exp(-0.5 * upper * upper) * NORMAL_PEAK
-    hidden = (upper * phi).astype(BF16)
-    gate_unit, gate_inv = normalize(hidden[:, 1024:].astype(F32))
+    unit_rows = unit_rows.astype(BF16)
+    hidden = [None, None]
+    for half, copy in ((1, copies[0]), (0, copies[1])):
+        copy.wait()
+        upper = dot(unit_rows, up[half])
+        phi = 0.5 * (1.0 + lax.erf(upper * HALF_ROOT))
+        slope[:, 1024 * half : 1024 * half + 1024] = phi + upper * jnp.exp(-0.5 * upper * upper) * NORMAL_PEAK
+        hidden[half] = (upper * phi).astype(BF16)
+    gate_unit, gate_inv = normalize(hidden[1].astype(F32))
     unit[...] = gate_unit
     inverse[...] = jnp.broadcast_to(gate_inv, inverse.shape)
     rows = first_frame + lax.broadcasted_iota(jnp.int32, (ROWS, 1024), 0)
     masked = jnp.where(rows < length, gate_unit, 0.0).astype(BF16)
     gating[...] = masked
-    resid[...] = hidden[:, :1024]
-    back = dot(cotangent[...], w_down[...], 1, 1).astype(BF16)
+    resid[...] = hidden[0]
+    copies[2].wait()
+    back = dot(cotangent[...], down[...], 1, 1).astype(BF16)
     d_gated[...] = back
-    conv_back = (back.astype(F32) * hidden[:, :1024].astype(F32)).astype(BF16)
+    conv_back = (back.astype(F32) * hidden[0].astype(F32)).astype(BF16)
     d_conv[...] = conv_back
     top[:, :1024] = masked[:16]
     top[:, 1024:] = conv_back[:16]
@@ -179,24 +191,24 @@
     conv_out[...] = conv_in[...]
     d_gating[...] = d_gating_in[...]
     g_taps[...] = g_taps_in[...]
-    before_ext[:16] = before[...].astype(F32)
-    before_ext[16:] = jnp.zeros((16, 2048), F32)
-    after_ext[:16] = jnp.zeros((16, 2048), F32)
-    after_ext[16:] = after[...].astype(F32)
+    before_ext[:, 16:] = jnp.zeros((16, 16, 128), F32)
+    after_ext[:, :16] = jnp.zeros((16, 16, 128), F32)
+    for block in range(16):
+        before_ext[block, :16] = before[:, 128 * block : 128 * block + 128].astype(F32)
+        after_ext[block, 16:] = after[:, 128 * block : 128 * block + 128].astype(F32)
 
     def chunk(index, _):
         lanes = pl.ds(pl.multiple_of(index * 128, 128), 128)
-        far = pl.ds(pl.multiple_of(index * 128 + 1024, 128), 128)
         for ext, first, skip in ((before_ext, 0, 0), (after_ext, 112, 16)):
             own = d_conv[first : first + 16, lanes].astype(F32)
             forward = conv_out[first : first + 16, lanes]
             backward = d_gating[first : first + 16, lanes]
             for step in range(1, 16):
                 offset = step + skip
-                part = ext[pl.ds(step, 16), lanes]
+                part = ext[index, pl.ds(step, 16), :]
                 forward = forward + taps[offset - 1 : offset, lanes] * part
                 g_taps[offset - 1 : offset, lanes] += jnp.sum(part * own, axis=0, keepdims=True)
-                part = ext[pl.ds(step, 16), far]
+                part = ext[index + 8, pl.ds(step, 16), :]
                 backward = backward + taps[TAPS - offset : TAPS - offset + 1, lanes] * part
             conv_out[first : first + 16, lanes] = forward
             d_gating[first : first + 16, lanes] = backward
@@ -267,7 +279,7 @@
     for turn, far in enumerate((far_0, far_1, far_2, far_3)):
         for block in range(GROUP):
             tokens = slice(128 * block, 128 * block + 128)
-            context[tokens, span(slot(place, turn), 128)] = far[96:, tokens]
+            context[tokens, span(slot(place, turn), 128)] = far[96:224, tokens]
     for x in range(4):
 
         @pl.when(place[4] == x)
@@ -389,7 +401,7 @@
 
 def join_kernel(
     lengths, context, d_query, own, from_before, from_after,
-    unit_0, unit_1, unit_2, unit_3, back_0, back_1, back_2, back_3, joined_t
+    unit_0, unit_1, unit_2, unit_3, joined_t
 ):
     place = locate(lengths)
     joined_t[:128] = d_query[...]
@@ -398,11 +410,11 @@
         total = total.astype(BF16)
         joined_t[128:256, 128 * piece : 128 * piece + 128] = total[:, :128].T
         joined_t[256:, 128 * piece : 128 * piece + 128] = total[:, 128:].T
-    for turn, ref in enumerate((back_0, back_1, back_2, back_3)):
-        ref[...] = joined_t[:, span((place[4] + turn) & 3, 128)]
-    for ref in (unit_0, unit_1, unit_2, unit_3):
+    for turn, ref in enumerate((unit_0, unit_1, unit_2, unit_3)):
         for block in range(GROUP):
-            ref[96:, 128 * block : 128 * block + 128] = context[block]
+            lanes = slice(128 * block, 128 * block + 128)
+            ref[96:224, lanes] = context[block]
+            ref[224:, lanes] = joined_t[96 * block : 96 * block + 96, span((place[4] + turn) & 3, 128)]
     for x in range(4):
 
         @pl.when(place[4] == x)
@@ -419,14 +431,15 @@
 
 
 def rows_kernel(
-    lengths, frames, cotangent, far_0, far_1, far_2, far_3, back_0, back_1, back_2, back_3, layer_part, d_normed,
-    w_qkv, w_out, layer_out, d_frames, context, joined_t
+    lengths, frames, cotangent, far_0, far_1, far_2, far_3, layer_part, d_normed,
+    w_qkv, w_out, layer_out, d_frames, context, joined_t, back
 ):
     place = locate(lengths)
     for turn, far in enumerate((far_0, far_1, far_2, far_3)):
-        context[:, span(slot(place, turn), 128)] = far[96:, span(place[4], 128)]
-    for turn, back in enumerate((back_0, back_1, back_2, back_3)):
         pair = slot(place, turn)
+        context[:, span(pair, 128)] = far[96:224, span(place[4], 128)]
+        for block in range(4):
+            back[96 * block : 96 * block + 96] = far[224:, 128 * block : 128 * block + 128]
         for part in range(3):
             joined_t[span(pair + 4 * part, 128), :] = back[128 * part : 128 * part + 128]
     layer_out[...] = (layer_part[...] + dot(context[...], w_out[...])).astype(BF16)
@@ -435,18 +448,37 @@
     d_frames[...] = (cotangent[...].astype(F32) + norm_back(d_rows, unit_rows, inverse)).astype(BF16)
 
 
-def add_kernel(gate, gate_far, attention, attention_far, out):
-    out[:, :112] = (gate[...].astype(F32) + gate_far[...].astype(F32)).astype(BF16)
-    out[:, 112:] = (attention[...].astype(F32) + attention_far[...].astype(F32)).astype(BF16)
-
-
-def chunk_sum_kernel(lengths, parts, out_0, out_1, out_2, out_3, total):
-    place = locate(lengths)
-    for first in range(0, parts.shape[1], 16):
+def add_kernel(near, far, out):
+    out[...] = (near[...].astype(F32) + far[...].astype(F32)).astype(BF16)
+
+
+def turn_add_kernel(lengths, near, far, out_0, out_1, out_2, out_3):
+    place = locate(lengths)
+    for turn, ref in enumerate((out_0, out_1, out_2, out_3)):
+        for z_low in range(2):
+            m = 4 * z_low + ((place[6] + turn) & 3)
+            ref[z_low] = (near[m].astype(F32) + far[m].astype(F32)).astype(BF16)
+
+
+def gate_sum_kernel(lengths, part_0, part_1, part_2, part_3, keep, send):
+    place = locate(lengths)
+    for out, z_low in ((keep, place[7]), (send, 1 - place[7])):
+        total = part_0[z_low].astype(F32)
+        for part in (part_1, part_2, part_3):
+            total = total + part[z_low].astype(F32)
+        out[...] = total.astype(BF16)
+
+
+def chunk_sum_kernel(lengths, gate, gate_far, parts, out_0, out_1, out_2, out_3, total):
+    place = locate(lengths)
+    for first in range(0, 176, 16):
         rows = slice(first, first + 16)
-        acc = parts[0, rows, :].astype(F32)
-        for source in range(1, 8):
-            acc = acc + parts[source, rows, :].astype(F32)
+        if first < 112:
+            acc = gate[rows].astype(F32) + gate_far[rows].astype(F32)
+        else:
+            acc = parts[0, first - 112 : first - 96].astype(F32)
+            for source in range(1, 8):
+                acc = acc + parts[source, first - 112 : first - 96].astype(F32)
         for z in range(4):
             total[z, rows, :] = acc[:, 128 * z : 128 * z + 128].astype(BF16)
     for turn, ref in enumerate((out_0, out_1, out_2, out_3)):
@@ -481,6 +513,12 @@
 def turn_x(pieces):
     return [pieces[0]] + [
         lax.ppermute(pieces[by], "x", [(i, (i + by) % 4) for i in range(4)]) for by in range(1, 4)
+    ]
+
+
+def turn_y(pieces):
+    return [pieces[0]] + [
+        lax.ppermute(pieces[by], "y", [(i, (i + by) % 4) for i in range(4)]) for by in range(1, 4)
     ]
 
 
@@ -505,7 +543,9 @@
         gate_kernel,
         [wide, wide, wide, wide, wide_f, ((ROWS, 128), F32), ((ROWS, 2048), F32),
          ((16, 2048), BF16), ((16, 2048), BF16)],
+        [pltpu.VMEM((2, 1024, 1024), BF16), pltpu.VMEM((1024, 1024), BF16), pltpu.SemaphoreType.DMA((3,))],
         scalars=1,
+        left=2,
     )(lengths, *in_hbm(frames_later, cotangent, w_up, w_down))
     before, after = shift(bottom, 1), shift(top, -1)
     conv_in, d_gating_in, g_taps_in = call(
@@ -524,7 +564,7 @@
         conv_outer_kernel,
         [((ROWS, 2048), BF16, HBM), gate, gate, gate, gate],
         [pltpu.VMEM((ROWS, 1024), F32), pltpu.VMEM((ROWS, 1024), F32),
-         pltpu.VMEM((32, 2048), F32), pltpu.VMEM((32, 2048), F32),
+         pltpu.VMEM((16, 32, 128), F32), pltpu.VMEM((16, 32, 128), F32),
          pltpu.VMEM((32, 1024), F32), pltpu.VMEM((2048, ROWS), BF16), pltpu.VMEM((32, 16, 128), BF16)],
         scalars=1,
     )(lengths, conv_in, d_gating_in, g_taps_in, d_conv, resid, d_gated, unit, inverse, slope, before, after, conv_kernel)
@@ -541,11 +581,14 @@
         scalars=1,
     )(lengths, query, kv, kv_before, kv_after, *in_x)
     from_before, from_after = shift(d_after, 4), shift(d_before, -4)
-    gate_x, d_own = lax.optimization_barrier((gate_x, d_own))
-    small = ((384, 128), BF16)
-    *far, back_0, back_1, back_2, back_3 = call(
-        join_kernel, [((224, 512), BF16)] * 4 + [small + (HBM,)] * 4, [pltpu.VMEM((384, 512), BF16)], scalars=1
-    )(lengths, context, d_query, d_own, from_before, from_after)
+    frames_later, d_own = lax.optimization_barrier((frames, d_own))
+    layer_part, d_normed = call(gate_rows_kernel, [wide_f + (HBM,), wide_f + (HBM,)])(
+        *in_hbm(frames_later), gate_x[0], *in_hbm(d_upper), w_up, w_down
+    )
+    gate_x, d_normed, d_own = lax.optimization_barrier((gate_x, d_normed, d_own))
+    far = call(join_kernel, [((320, 512), BF16)] * 4, [pltpu.VMEM((384, 512), BF16)], scalars=1)(
+        lengths, context, d_query, d_own, from_before, from_after
+    )
     far, gate_x = lax.optimization_barrier((far, gate_x))
     far_x = turn_x(far)
     keep, send, cot_own = call(
@@ -554,29 +597,34 @@
         [pltpu.VMEM((512, 512), BF16), pltpu.VMEM((512, 1024), BF16)],
         scalars=1,
     )(lengths, normed, *in_x, *gate_x)
-    gate_far = other_core(send)
+    gate_y = turn_y(
+        call(turn_add_kernel, [((2, 112, 512), BF16)] * 4, scalars=1)(lengths, keep, other_core(send))
+    )
+    far_x, gate_y = lax.optimization_barrier((far_x, gate_y))
     attention_keep, send = call(
         attention_grads_kernel,
         [((8, 64, 512), BF16), ((8, 64, 512), BF16)],
         [pltpu.VMEM((512, 512), BF16), pltpu.VMEM((384, 512), BF16)],
         scalars=1,
     )(lengths, normed, cot_own, *far_x)
-    send, frames_later, *back = lax.optimization_barrier((send, frames, back_0, back_1, back_2, back_3))
-    back_x = turn_x(back)
-    layer_part, d_normed = call(gate_rows_kernel, [wide_f, wide_f])(
-        frames_later, gate_x[0], *in_hbm(d_upper, w_up, w_down)
-    )
-    (parts,) = call(add_kernel, [((8, 176, 512), BF16, HBM)])(keep, gate_far, attention_keep, other_core(send))
+    send, gate_y = lax.optimization_barrier((send, gate_y))
+    gate_keep, gate_send = call(gate_sum_kernel, [((112, 512), BF16, HBM)] * 2, scalars=1)(lengths, *gate_y)
+    attention_keep, gate_send = lax.optimization_barrier((attention_keep, gate_send))
+    (parts,) = call(add_kernel, [((8, 64, 512), BF16, HBM)])(attention_keep, other_core(send))
     parts = lax.all_to_all(parts, ("z_low", "y"), 0, 0)
+    gate_far = lax.ppermute(gate_send, "z_low", [(0, 1), (1, 0)])
     layer_out, d_frames = call(
-        rows_kernel, [wide, wide], [pltpu.VMEM((ROWS, 512), BF16), pltpu.VMEM((1536, ROWS), BF16)], scalars=1
+        rows_kernel,
+        [wide, wide],
+        [pltpu.VMEM((ROWS, 512), BF16), pltpu.VMEM((1536, ROWS), BF16), pltpu.VMEM((384, ROWS), BF16)],
+        scalars=1,
     )(
-        lengths, frames, cotangent, *far_x, *back_x, layer_part, d_normed, *in_hbm(w_qkv, w_out)
+        lengths, frames, cotangent, *far_x, layer_part, d_normed, *in_hbm(w_qkv, w_out)
     )
     parts, layer_out, d_frames = lax.optimization_barrier((parts, layer_out, d_frames))
     parts = call(
         chunk_sum_kernel, [((176, 128), BF16)] * 4, [pltpu.VMEM((4, 176, 128), BF16)], scalars=1
-    )(lengths, parts)
+    )(lengths, gate_keep, gate_far, parts)
     g_qkv, g_out, g_up, g_down, g_kernel = call(
         final_kernel,
         [((48, 128), F32), ((32, HEAD), F32), ((64, 128), F32), ((32, 128), F32), ((TAPS, 32), F32)],

time: 123 us -> 121 us (0.984)
    ppermute x0 -> x4, starting transfers between devices: none -> 9.11 us  [the longest x3 7.64 us: turn_y(): lax.ppermute(pieces[by], 'y', [(i, (i + by) % 4) for i in range(4)])]
    ppermute x0 -> x4, waiting for transfers between devices: none -> 6.88 us  [the longest x3 5.39 us: turn_y(): lax.ppermute(pieces[by], 'y', [(i, (i + by) % 4) for i in range(4)])]
    ppermute x12 -> x9, waiting for transfers between devices: 15.4 us -> 8.91 us  [turn_x(): lax.ppermute(pieces[by], 'x', [(i, (i + by) % 4) for i in range(4)])]
    ppermute x12 -> x9, starting transfers between devices: 19.3 us -> 13.4 us  [turn_x(): lax.ppermute(pieces[by], 'x', [(i, (i + by) % 4) for i in range(4)])]
    all_to_all x1, starting transfers between devices: 7.83 us -> 5.35 us  [local(): parts = lax.all_to_all(parts, ('z_low', 'y'), 0, 0)]
    pallas_call x14 -> x16, Pallas kernels: 35.8 us -> 34.6 us  [run(): pl.pallas_call(body, out_shape=[HBM(*out[:2]) if len(out) > 2 else jax.Sh...]
  transfers between devices with their start and end apart: 24 -> 25, of which waited for: 10 -> 12; matrix products, arithmetic and copies ran while one was open for 0% -> 0% of each run, Pallas kernels for 23% -> 21%
where the time goes in v6:
time: 121 us
  starting transfers between devices  58.4 us (48%)
  Pallas kernels  34.6 us (29%)
  waiting for transfers between devices  26.4 us (22%)
  between operations  1.57 us (1%)
    pallas_call x16, Pallas kernels, run(): pl.pallas_call(body, out_shape=[HBM(*out[:2]) if len(out) > 2 else jax.Sh...  34.6 us
    ppermute x6, starting transfers between devices, shift(): lax.ppermute(array, SEQ, [(i, i + by) for i in range(32) if 0 <= i + by <...  19.9 us
    ppermute x9, starting transfers between devices, turn_x(): lax.ppermute(pieces[by], 'x', [(i, (i + by) % 4) for i in range(4)])  13.4 us
    ppermute x3, starting transfers between devices, turn_z(): lax.ppermute(pieces[by], 'z_high', [(i, (i + by) % 4) for i in range(4)])  10.5 us
    ppermute x9, waiting for transfers between devices, turn_x(): lax.ppermute(pieces[by], 'x', [(i, (i + by) % 4) for i in range(4)])  8.91 us
    ppermute x3, starting transfers between devices, turn_y(): lax.ppermute(pieces[by], 'y', [(i, (i + by) % 4) for i in range(4)])  7.64 us
    ppermute x3, waiting for transfers between devices, turn_y(): lax.ppermute(pieces[by], 'y', [(i, (i + by) % 4) for i in range(4)])  5.39 us
    all_to_all x1, starting transfers between devices, local(): parts = lax.all_to_all(parts, ('z_low', 'y'), 0, 0)  5.35 us
  transfers between devices with their start and end apart: 25, of which 12 were waited for; matrix products, arithmetic and copies ran while one was open for 0% of the time, Pallas kernels for 21%

profile of v6, /device:TPU:8, one launch (start us, length us, event | category | flops | bytes accessed | tf_op | source)
XLA Modules:
  0.0 121.0 jit_solution(8369068476933469881)
XLA Ops:
  1.3 2.0 %shard_map.135 = (bf16[128,1408]{1,0:T(8,128)(2,1)S(1)}, bf16[128,1408]{1,0:T(8,128)(2,1)S(1)}, bf16[128,1408]{1,0:T(8,128)(2,1)S(1)}, bf16[128,1408]{1,0:T(8,128)(2,1)S(1)}) custom-call(s32[1]{0:T(128)S(6)} %copy.15.lengths, bf16[128,1024]{1,0:T(8,128)(2,1)} %bitcast.8, bf16[128,1024]{1,0:T(8,128)(2,1)} %bitcast.12, bf16[512,1024]{1,0:T(8,128)(2,1)} %w_out.3), custom_call_target="tpu_custom_call" | custom-call | tf_op jit(solution)/shard_map/pallas_call | solution.py:32
  3.3 1.6 %collective-permute-start = (bf16[128,1408]{1,0:T(8,128)(2,1)S(1)}, bf16[128,1408]{1,0:T(8,128)(2,1)S(1)}, u32[]{:S(2)}, u32[]{:S(2)}) collective-permute-start(bf16[128,1408]{1,0:T(8,128)(2,1)S(1)} %get-tuple-element.122), channel_id=1, source_target_pairs={{0,8},{8,16},{16,24},{24,0},{1,9},{9,17},{17,25},{25,1},{2,10},{10... | collective-permute-start | bytes 1081352 | tf_op jit(solution)/shard_map/ppermute | solution.py:515
  4.8 2.7 %collective-permute-start.1 = (bf16[128,1408]{1,0:T(8,128)(2,1)S(1)}, bf16[128,1408]{1,0:T(8,128)(2,1)S(1)}, u32[]{:S(2)}, u32[]{:S(2)}) collective-permute-start(bf16[128,1408]{1,0:T(8,128)(2,1)S(1)} %get-tuple-element.123), channel_id=1, source_target_pairs={{0,16},{8,24},{16,0},{24,8},{1,17},{9,25},{17,1},{25,9},{2,18},{10... | collective-permute-start | bytes 1081352 | tf_op jit(solution)/shard_map/ppermute | solution.py:515
  7.6 1.4 %collective-permute-start.2 = (bf16[128,1408]{1,0:T(8,128)(2,1)S(1)}, bf16[128,1408]{1,0:T(8,128)(2,1)S(1)}, u32[]{:S(2)}, u32[]{:S(2)}) collective-permute-start(bf16[128,1408]{1,0:T(8,128)(2,1)S(1)} %get-tuple-element.124), channel_id=1, source_target_pairs={{0,24},{8,0},{16,8},{24,16},{1,25},{9,1},{17,9},{25,17},{2,26},{10... | collective-permute-start | bytes 1081352 | tf_op jit(solution)/shard_map/ppermute | solution.py:515
  9.0 4.8 %shard_map.136 = (bf16[128,1024]{1,0:T(8,128)(2,1)S(1)}, bf16[128,1024]{1,0:T(8,128)(2,1)S(1)}, bf16[128,1024]{1,0:T(8,128)(2,1)S(1)}, bf16[128,1024]{1,0:T(8,12...) custom-call(s32[1]{0:T(128)S(6)} %copy.15.lengths, ...), custom_call_target="tpu_custom_call" | custom-call | tf_op jit(solution)/shard_map/pallas_call | solution.py:32
  13.8 2.5 %collective-permute-start.3 = (bf16[16,2048]{1,0:T(8,128)(2,1)S(1)}, bf16[16,2048]{1,0:T(8,128)(2,1)S(1)}, u32[]{:S(2)}, u32[]{:S(2)}) collective-permute-start(bf16[16,2048]{1,0:T(8,128)(2,1)S(1)} %get-tuple-element.129), channel_id=1, source_target_pairs={{0,8},{8,16},{16,24},{24,32},{32,40},{40,48},{48,56},{56,64},{64,7... | collective-permute-start | bytes 196616 | tf_op jit(solution)/shard_map/ppermute | solution.py:506
  16.3 5.4 %collective-permute-start.4 = (bf16[16,2048]{1,0:T(8,128)(2,1)S(1)}, bf16[16,2048]{1,0:T(8,128)(2,1)S(1)}, u32[]{:S(2)}, u32[]{:S(2)}) collective-permute-start(bf16[16,2048]{1,0:T(8,128)(2,1)S(1)} %get-tuple-element.130), channel_id=1, source_target_pairs={{8,0},{16,8},{24,16},{32,24},{40,32},{48,40},{56,48},{64,56},{72,6... | collective-permute-start | bytes 196616 | tf_op jit(solution)/shard_map/ppermute | solution.py:506
  21.8 3.6 %shard_map.137 = (f32[128,1024]{1,0:T(8,128)S(1)}, f32[128,1024]{1,0:T(8,128)S(1)}, f32[32,1024]{1,0:T(8,128)S(1)}) custom-call(bf16[128,1024]{1,0:T(8,128)(2,1)S(1)} %get-tuple-element.126.gating, bf16[128,1024]{1,0:T(8,128)(2,1)S(1)} %get-tuple-element.127.d_conv, f32[31,1024]{1,0:T(8,128)S(1)} %copy-done.7), custom_call_target="tpu_custom_call" | custom-call | tf_op jit(solution)/shard_map/pallas_call | solution.py:32
  25.5 1.3 %shard_map.138 = (bf16[512,1024]{1,0:T(8,128)(2,1)S(1)}, bf16[4,128,128]{2,1,0:T(8,128)(2,1)S(1)}, bf16[4,128,256]{2,1,0:T(8,128)(2,1)S(1)}) custom-call(s32[1]{0:T(128)S(6)} %copy.15.lengths, bf16[128,1408]{1,0:T(8,128)(2,1)S(1)} %get-tuple-element.131.frames_0.cot_0, bf16[128,1408]{1,0:T(8,128)(2,1)S(1)} %collective-permute-done.frames_1.cot_1, ...), custom_call_target="tpu_custom_call" | custom-call | tf_op jit(solution)/shard_map/pallas_call | solution.py:32
  26.8 3.7 %collective-permute-start.5 = (bf16[4,128,256]{2,1,0:T(8,128)(2,1)S(1)}, bf16[4,128,256]{2,1,0:T(8,128)(2,1)S(1)}, u32[]{:S(2)}, u32[]{:S(2)}) collective-permute-start(bf16[4,128,256]{2,1,0:T(8,128)(2,1)S(1)} %get-tuple-element.139.kv), channel_id=1, source_target_pairs={{0,32},{8,40},{16,48},{24,56},{32,64},{40,72},{48,80},{56,88},{64,... | collective-permute-start | bytes 786440 | tf_op jit(solution)/shard_map/ppermute | solution.py:506
  30.5 2.4 %collective-permute-start.6 = (bf16[4,128,256]{2,1,0:T(8,128)(2,1)S(1)}, bf16[4,128,256]{2,1,0:T(8,128)(2,1)S(1)}, u32[]{:S(2)}, u32[]{:S(2)}) collective-permute-start(bf16[4,128,256]{2,1,0:T(8,128)(2,1)S(1)} %get-tuple-element.139.kv), channel_id=1, source_target_pairs={{32,0},{40,8},{48,16},{56,24},{64,32},{72,40},{80,48},{88,56},{96,... | collective-permute-start | bytes 786440 | tf_op jit(solution)/shard_map/ppermute | solution.py:506
  32.9 2.2 %shard_map.139 = (bf16[128,2048]{1,0:T(8,128)(2,1)}, bf16[1664,128]{1,0:T(8,128)(2,1)S(1)}, bf16[1664,128]{1,0:T(8,128)(2,1)S(1)}, bf16[1664,128]{1,0:T(8,128)(2,1)S(1)}, bf16[1664,128]{1,0:T(8,128)(2,1)S(1)}) custom-call(s32[1]{0:T(128)S(6)} %copy.15.lengths, f32[128,1024]{1,0:T(8,128)S(1)} %get-tuple-element.140.conv_in, ...), custom_call_target="tpu_custom_call" | custom-call | tf_op jit(solution)/shard_map/pallas_call | solution.py:32
  35.2 1.3 %collective-permute-done.5.before = bf16[4,128,256]{2,1,0:T(8,128)(2,1)S(1)} collective-permute-done((bf16[4,128,256]{2,1,0:T(8,128)(2,1)S(1)}, bf16[4,128,256]{2,1,0:T(8,128)(2,1)S(1)}, u32[]{:S(2)}, u32[]{:S(2)}) %collective-permute-start.5) | collective-permute-done | bytes 262176 | tf_op jit(solution)/shard_map/ppermute | solution.py:506
  36.5 0.7 collective-permute-start.7
  37.2 3.3 %collective-permute-start.8 = (bf16[1664,128]{1,0:T(8,128)(2,1)S(1)}, bf16[1664,128]{1,0:T(8,128)(2,1)S(1)}, u32[]{:S(2)}, u32[]{:S(2)}) collective-permute-start(bf16[1664,128]{1,0:T(8,128)(2,1)S(1)} %get-tuple-element.159), channel_id=1, source_target_pairs={{0,16},{8,24},{16,0},{24,8},{1,17},{9,25},{17,1},{25,9},{2,18},{10... | collective-permute-start | bytes 1277960 | tf_op jit(solution)/shard_map/ppermute | solution.py:515
  40.6 6.0 %shard_map.140 = (bf16[4,128,128]{2,1,0:T(8,128)(2,1)S(1)}, bf16[128,512]{1,0:T(8,128)(2,1)S(1)}, bf16[4,128,256]{2,1,0:T(8,128)(2,1)S(1)}, bf16[4,128,256]{2,1,0:T(8,128)(2,1)S(1)}, f32[4,128,256]{2,1,0:T(8,128)S(1)}) custom-call(s32[1]{0:T(128)S(6)} %copy.15.lengths, bf16[4,128,128]{2,1,0:T(8,128)(2,1)S(1)} %get-tuple-element.136.queries, ...), custom_call_target="tpu_custom_call" | custom-call | tf_op jit(solution)/shard_map/pallas_call | solution.py:32
  46.6 3.7 %collective-permute-start.10 = (bf16[4,128,256]{2,1,0:T(8,128)(2,1)S(1)}, bf16[4,128,256]{2,1,0:T(8,128)(2,1)S(1)}, u32[]{:S(2)}, u32[]{:S(2)}) collective-permute-start(bf16[4,128,256]{2,1,0:T(8,128)(2,1)S(1)} %get-tuple-element.167), channel_id=1, source_target_pairs={{0,32},{8,40},{16,48},{24,56},{32,64},{40,72},{48,80},{56,88},{64,... | collective-permute-start | bytes 786440 | tf_op jit(solution)/shard_map/ppermute | solution.py:506
  50.3 2.1 %collective-permute-start.11 = (bf16[4,128,256]{2,1,0:T(8,128)(2,1)S(1)}, bf16[4,128,256]{2,1,0:T(8,128)(2,1)S(1)}, u32[]{:S(2)}, u32[]{:S(2)}) collective-permute-start(bf16[4,128,256]{2,1,0:T(8,128)(2,1)S(1)} %get-tuple-element.168), channel_id=1, source_target_pairs={{32,0},{40,8},{48,16},{56,24},{64,32},{72,40},{80,48},{88,56},{96,... | collective-permute-start | bytes 786440 | tf_op jit(solution)/shard_map/ppermute | solution.py:506
  52.5 3.7 %shard_map.141 = (f32[128,1024]{1,0:T(8,128)}, f32[128,1024]{1,0:T(8,128)}) custom-call(bf16[128,1024]{1,0:T(8,128)(2,1)} %bitcast.10, bf16[1664,128]{1,0:T(8,128)(2,1)S(1)} %get-tuple-element.177.gate.gate_0, bf16[128,2048]{1,0:T(8,128)(2,1)} %get-tuple-element.163.d_upper, bf16[1024,2048]{1,0:T(8,128)(2,1)S(1)} %copy-done, bf16[1024,1024]{1,0:T(8,128)(2,1)S(1)} %copy-done.2), custom_call_target="tpu_custom_call" | custom-call | tf_op jit(solution)/shard_map/pallas_call | solution.py:32
  56.2 1.2 collective-permute-done.8.gate_2
  57.6 2.5 %collective-permute-done.11.from_after = bf16[4,128,256]{2,1,0:T(8,128)(2,1)S(1)} collective-permute-done((bf16[4,128,256]{2,1,0:T(8,128)(2,1)S(1)}, bf16[4,128,256]{2,1,0:T(8,128)(2,1)S(1)}, u32[]{:S(2)}, u32[]{:S(2)}) %collective-permute-start.11) | collective-permute-done | bytes 262176 | tf_op jit(solution)/shard_map/ppermute | solution.py:506
  60.1 0.3 shard_map.142
  60.4 1.3 %shard_map.143 = (bf16[8,112,512]{2,1,0:T(8,128)(2,1)S(1)}, bf16[8,112,512]{2,1,0:T(8,128)(2,1)S(1)}, bf16[256,512]{1,0:T(8,128)(2,1)S(1)}) custom-call(s32[1]{0:T(128)S(6)} %copy.15.lengths, bf16[512,1024]{1,0:T(8,128)(2,1)S(1)} %get-tuple-element.135.normed, bf16[128,1408]{1,0:T(8,128)(2,1)S(1)} %get-tuple-element.131.frames_0.cot_0, ...), custom_call_target="tpu_custom_call" | custom-call | tf_op jit(solution)/shard_map/pallas_call | solution.py:32
  61.8 0.8 collective-permute-start.12
  62.6 2.0 %collective-permute-start.13 = (bf16[320,512]{1,0:T(8,128)(2,1)S(1)}, bf16[320,512]{1,0:T(8,128)(2,1)S(1)}, u32[]{:S(2)}, u32[]{:S(2)}) collective-permute-start(bf16[320,512]{1,0:T(8,128)(2,1)S(1)} %get-tuple-element.184), channel_id=1, source_target_pairs={{0,16},{8,24},{16,0},{24,8},{1,17},{9,25},{17,1},{25,9},{2,18},{10... | collective-permute-start | bytes 983048 | tf_op jit(solution)/shard_map/ppermute | solution.py:515
  64.6 0.7 collective-permute-start.14
  65.4 0.2 shard_map.144
  65.6 3.8 %collective-permute-start.16 = (bf16[2,112,512]{2,1,0:T(8,128)(2,1)S(1)}, bf16[2,112,512]{2,1,0:T(8,128)(2,1)S(1)}, u32[]{:S(2)}, u32[]{:S(2)}) collective-permute-start(bf16[2,112,512]{2,1,0:T(8,128)(2,1)S(1)} %get-tuple-element.189), channel_id=1, source_target_pairs={{0,32},{32,64},{64,96},{96,0},{1,33},{33,65},{65,97},{97,1},{2,34}... | collective-permute-start | bytes 688136 | tf_op jit(solution)/shard_map/ppermute | solution.py:521
  69.4 3.9 %collective-permute-start.17 = (bf16[2,112,512]{2,1,0:T(8,128)(2,1)S(1)}, bf16[2,112,512]{2,1,0:T(8,128)(2,1)S(1)}, u32[]{:S(2)}, u32[]{:S(2)}) collective-permute-start(bf16[2,112,512]{2,1,0:T(8,128)(2,1)S(1)} %get-tuple-element.190), channel_id=1, source_target_pairs={{0,64},{32,96},{64,0},{96,32},{1,65},{33,97},{65,1},{97,33},{2,66}... | collective-permute-start | bytes 688136 | tf_op jit(solution)/shard_map/ppermute | solution.py:521
  73.3 6.9 %collective-permute-done.12.far_1 = bf16[320,512]{1,0:T(8,128)(2,1)S(1)} collective-permute-done((bf16[320,512]{1,0:T(8,128)(2,1)S(1)}, bf16[320,512]{1,0:T(8,128)(2,1)S(1)}, u32[]{:S(2)}, u32[]{:S(2)}) %collective-permute-start.12) | collective-permute-done | bytes 327712 | tf_op jit(solution)/shard_map/ppermute | solution.py:515
  80.2 0.6 collective-permute-done.14.far_3
  80.8 5.4 %collective-permute-done.18.part_3 = bf16[2,112,512]{2,1,0:T(8,128)(2,1)S(1)} collective-permute-done((bf16[2,112,512]{2,1,0:T(8,128)(2,1)S(1)}, bf16[2,112,512]{2,1,0:T(8,128)(2,1)S(1)}, u32[]{:S(2)}, u32[]{:S(2)}) %collective-permute-start.18) | collective-permute-done | bytes 229408 | tf_op jit(solution)/shard_map/ppermute | solution.py:521
  86.2 1.1 shard_map.145
  87.5 0.8 shard_map.146
  88.2 1.1 collective-permute-done.19.far
  89.3 0.9 shard_map.147
  90.3 5.3 %all-to-all-start = ((bf16[8,64,512]{2,1,0:T(8,128)(2,1)}), bf16[8,64,512]{2,1,0:T(8,128)(2,1)S(1)}, u32[]{:S(2)}, u32[]{:S(2)}) async-start(bf16[8,64,512]{2,1,0:T(8,128)(2,1)} %shard_map.147), calls=%async_computation | async-start | bytes 1048576 | tf_op jit(solution)/shard_map/all_to_all | solution.py:614
  95.6 1.5 %collective-permute-start.20 = (bf16[112,512]{1,0:T(8,128)(2,1)}, bf16[112,512]{1,0:T(8,128)(2,1)}, u32[]{:S(2)}, u32[]{:S(2)}) collective-permute-start(bf16[112,512]{1,0:T(8,128)(2,1)} %get-tuple-element.216), channel_id=1, source_target_pairs={{0,128},{128,0},{1,129},{129,1},{2,130},{130,2},{3,131},{131,3},{4... | collective-permute-start | bytes 344072 | tf_op jit(solution)/shard_map/ppermute | solution.py:615
  97.1 4.5 %shard_map.148 = (bf16[128,1024]{1,0:T(8,128)(2,1)}, bf16[128,1024]{1,0:T(8,128)(2,1)}) custom-call(s32[1]{0:T(128)S(6)} %copy.15.lengths, bf16[128,1024]{1,0:T(8,128)(2,1)S(1)} %bitcast.11, bf16[128,1024]{1,0:T(8,128)(2,1)S(1)} %bitcast.14, bf16[320,512]{1,0:T(8,128)(2,1)S(1)} %get-tuple-element.192.far_0, ...), custom_call_target="tpu_custom_call" | custom-call | tf_op jit(solution)/shard_map/pallas_call | solution.py:32
  101.6 2.9 %all-to-all-done.parts = bf16[8,64,512]{2,1,0:T(8,128)(2,1)S(1)} async-done(((bf16[8,64,512]{2,1,0:T(8,128)(2,1)}), bf16[8,64,512]{2,1,0:T(8,128)(2,1)S(1)}, u32[]{:S(2)}, u32[]{:S(2)}) %all-to-all-start) | async-done | bytes 524320 | tf_op jit(solution)/shard_map/all_to_all | solution.py:614
  104.5 1.5 %collective-permute-done.20.gate_far = bf16[112,512]{1,0:T(8,128)(2,1)} collective-permute-done((bf16[112,512]{1,0:T(8,128)(2,1)}, bf16[112,512]{1,0:T(8,128)(2,1)}, u32[]{:S(2)}, u32[]{:S(2)}) %collective-permute-start.20) | collective-permute-done | bytes 114720 | tf_op jit(solution)/shard_map/ppermute | solution.py:615
  106.0 1.0 shard_map.149
  107.0 3.3 %collective-permute-start.21 = (bf16[176,128]{1,0:T(8,128)(2,1)S(1)}, bf16[176,128]{1,0:T(8,128)(2,1)S(1)}, u32[]{:S(2)}, u32[]{:S(2)}) collective-permute-start(bf16[176,128]{1,0:T(8,128)(2,1)S(1)} %get-tuple-element.219), channel_id=1, source_target_pairs={{0,2},{2,4},{4,6},{6,0},{1,3},{3,5},{5,7},{7,1},{8,10},{10,12},{12... | collective-permute-start | bytes 135176 | tf_op jit(solution)/shard_map/ppermute | solution.py:527
  110.3 4.5 %collective-permute-start.22 = (bf16[176,128]{1,0:T(8,128)(2,1)S(1)}, bf16[176,128]{1,0:T(8,128)(2,1)S(1)}, u32[]{:S(2)}, u32[]{:S(2)}) collective-permute-start(bf16[176,128]{1,0:T(8,128)(2,1)S(1)} %get-tuple-element.220), channel_id=1, source_target_pairs={{0,4},{2,6},{4,0},{6,2},{1,5},{3,7},{5,1},{7,3},{8,12},{10,14},{12... | collective-permute-start | bytes 135176 | tf_op jit(solution)/shard_map/ppermute | solution.py:527
  114.8 2.7 %collective-permute-start.23 = (bf16[176,128]{1,0:T(8,128)(2,1)S(1)}, bf16[176,128]{1,0:T(8,128)(2,1)S(1)}, u32[]{:S(2)}, u32[]{:S(2)}) collective-permute-start(bf16[176,128]{1,0:T(8,128)(2,1)S(1)} %get-tuple-element.221), channel_id=1, source_target_pairs={{0,6},{2,0},{4,2},{6,4},{1,7},{3,1},{5,3},{7,5},{8,14},{10,8},{12,... | collective-permute-start | bytes 135176 | tf_op jit(solution)/shard_map/ppermute | solution.py:527
  117.5 1.5 %collective-permute-done.22.part_2 = bf16[176,128]{1,0:T(8,128)(2,1)S(1)} collective-permute-done((bf16[176,128]{1,0:T(8,128)(2,1)S(1)}, bf16[176,128]{1,0:T(8,128)(2,1)S(1)}, u32[]{:S(2)}, u32[]{:S(2)}) %collective-permute-start.22) | collective-permute-done | bytes 45088 | tf_op jit(solution)/shard_map/ppermute | solution.py:527
  118.9 1.3 %collective-permute-done.23.part_3 = bf16[176,128]{1,0:T(8,128)(2,1)S(1)} collective-permute-done((bf16[176,128]{1,0:T(8,128)(2,1)S(1)}, bf16[176,128]{1,0:T(8,128)(2,1)S(1)}, u32[]{:S(2)}, u32[]{:S(2)}) %collective-permute-start.23) | collective-permute-done | bytes 45088 | tf_op jit(solution)/shard_map/ppermute | solution.py:527
  120.2 0.8 shard_map.150
  (36 shorter events, 0.6 us)
Async XLA Ops:
  3.2 18.5 %copy-start.7 = (f32[31,1024]{1,0:T(8,128)S(1)}, f32[31,1024]{1,0:T(8,128)}, u32[]{:S(2)}) copy-start(f32[31,1024]{1,0:T(8,128)} %taps.3) | copy-start | bytes 380932
  3.3 22.2 %copy-start.1 = (bf16[1024,1536]{1,0:T(8,128)(2,1)S(1)}, bf16[1024,1536]{1,0:T(8,128)(2,1)}, u32[]{:S(2)}) copy-start(bf16[1024,1536]{1,0:T(8,128)(2,1)} %w_qkv.3) | copy-start | bytes 9437188
  3.3 22.1 %collective-permute-start = (bf16[128,1408]{1,0:T(8,128)(2,1)S(1)}, bf16[128,1408]{1,0:T(8,128)(2,1)S(1)}, u32[]{:S(2)}, u32[]{:S(2)}) collective-permute-start(bf16[128,1408]{1,0:T(8,128)(2,1)S(1)} %get-tuple-element.122), channel_id=1, source_target_pairs={{0,8},{8,16},{16,24},{24,0},{1,9},{9,17},{17,25},{25,1},{2,10},{10... | collective-permute-start | bytes 1081352 | tf_op jit(solution)/shard_map/ppermute | solution.py:515
  4.8 20.6 %collective-permute-start.1 = (bf16[128,1408]{1,0:T(8,128)(2,1)S(1)}, bf16[128,1408]{1,0:T(8,128)(2,1)S(1)}, u32[]{:S(2)}, u32[]{:S(2)}) collective-permute-start(bf16[128,1408]{1,0:T(8,128)(2,1)S(1)} %get-tuple-element.123), channel_id=1, source_target_pairs={{0,16},{8,24},{16,0},{24,8},{1,17},{9,25},{17,1},{25,9},{2,18},{10... | collective-permute-start | bytes 1081352 | tf_op jit(solution)/shard_map/ppermute | solution.py:515
  7.6 17.9 %collective-permute-start.2 = (bf16[128,1408]{1,0:T(8,128)(2,1)S(1)}, bf16[128,1408]{1,0:T(8,128)(2,1)S(1)}, u32[]{:S(2)}, u32[]{:S(2)}) collective-permute-start(bf16[128,1408]{1,0:T(8,128)(2,1)S(1)} %get-tuple-element.124), channel_id=1, source_target_pairs={{0,24},{8,0},{16,8},{24,16},{1,25},{9,1},{17,9},{25,17},{2,26},{10... | collective-permute-start | bytes 1081352 | tf_op jit(solution)/shard_map/ppermute | solution.py:515
  13.8 11.6 %collective-permute-start.3 = (bf16[16,2048]{1,0:T(8,128)(2,1)S(1)}, bf16[16,2048]{1,0:T(8,128)(2,1)S(1)}, u32[]{:S(2)}, u32[]{:S(2)}) collective-permute-start(bf16[16,2048]{1,0:T(8,128)(2,1)S(1)} %get-tuple-element.129), channel_id=1, source_target_pairs={{0,8},{8,16},{16,24},{24,32},{32,40},{40,48},{48,56},{56,64},{64,7... | collective-permute-start | bytes 196616 | tf_op jit(solution)/shard_map/ppermute | solution.py:506
  16.3 9.1 %collective-permute-start.4 = (bf16[16,2048]{1,0:T(8,128)(2,1)S(1)}, bf16[16,2048]{1,0:T(8,128)(2,1)S(1)}, u32[]{:S(2)}, u32[]{:S(2)}) collective-permute-start(bf16[16,2048]{1,0:T(8,128)(2,1)S(1)} %get-tuple-element.130), channel_id=1, source_target_pairs={{8,0},{16,8},{24,16},{32,24},{40,32},{48,40},{56,48},{64,56},{72,6... | collective-permute-start | bytes 196616 | tf_op jit(solution)/shard_map/ppermute | solution.py:506
  25.4 27.0 %copy-start.2 = (bf16[1024,1024]{1,0:T(8,128)(2,1)S(1)}, bf16[1024,1024]{1,0:T(8,128)(2,1)}, u32[]{:S(2)}) copy-start(bf16[1024,1024]{1,0:T(8,128)(2,1)} %w_down.3) | copy-start | bytes 6291460
  26.8 25.7 %copy-start = (bf16[1024,2048]{1,0:T(8,128)(2,1)S(1)}, bf16[1024,2048]{1,0:T(8,128)(2,1)}, u32[]{:S(2)}) copy-start(bf16[1024,2048]{1,0:T(8,128)(2,1)} %w_up.3) | copy-start | bytes 12582916
  26.8 9.7 %collective-permute-start.5 = (bf16[4,128,256]{2,1,0:T(8,128)(2,1)S(1)}, bf16[4,128,256]{2,1,0:T(8,128)(2,1)S(1)}, u32[]{:S(2)}, u32[]{:S(2)}) collective-permute-start(bf16[4,128,256]{2,1,0:T(8,128)(2,1)S(1)} %get-tuple-element.139.kv), channel_id=1, source_target_pairs={{0,32},{8,40},{16,48},{24,56},{32,64},{40,72},{48,80},{56,88},{64,... | collective-permute-start | bytes 786440 | tf_op jit(solution)/shard_map/ppermute | solution.py:506
  30.5 10.0 %collective-permute-start.6 = (bf16[4,128,256]{2,1,0:T(8,128)(2,1)S(1)}, bf16[4,128,256]{2,1,0:T(8,128)(2,1)S(1)}, u32[]{:S(2)}, u32[]{:S(2)}) collective-permute-start(bf16[4,128,256]{2,1,0:T(8,128)(2,1)S(1)} %get-tuple-element.139.kv), channel_id=1, source_target_pairs={{32,0},{40,8},{48,16},{56,24},{64,32},{72,40},{80,48},{88,56},{96,... | collective-permute-start | bytes 786440 | tf_op jit(solution)/shard_map/ppermute | solution.py:506
  36.5 19.7 %collective-permute-start.7 = (bf16[1664,128]{1,0:T(8,128)(2,1)S(1)}, bf16[1664,128]{1,0:T(8,128)(2,1)S(1)}, u32[]{:S(2)}, u32[]{:S(2)}) collective-permute-start(bf16[1664,128]{1,0:T(8,128)(2,1)S(1)} %get-tuple-element.158), channel_id=1, source_target_pairs={{0,8},{8,16},{16,24},{24,0},{1,9},{9,17},{17,25},{25,1},{2,10},{10... | collective-permute-start | bytes 1277960 | tf_op jit(solution)/shard_map/ppermute | solution.py:515
  37.2 20.2 %collective-permute-start.8 = (bf16[1664,128]{1,0:T(8,128)(2,1)S(1)}, bf16[1664,128]{1,0:T(8,128)(2,1)S(1)}, u32[]{:S(2)}, u32[]{:S(2)}) collective-permute-start(bf16[1664,128]{1,0:T(8,128)(2,1)S(1)} %get-tuple-element.159), channel_id=1, source_target_pairs={{0,16},{8,24},{16,0},{24,8},{1,17},{9,25},{17,1},{25,9},{2,18},{10... | collective-permute-start | bytes 1277960 | tf_op jit(solution)/shard_map/ppermute | solution.py:515
  40.4 17.1 %collective-permute-start.9 = (bf16[1664,128]{1,0:T(8,128)(2,1)S(1)}, bf16[1664,128]{1,0:T(8,128)(2,1)S(1)}, u32[]{:S(2)}, u32[]{:S(2)}) collective-permute-start(bf16[1664,128]{1,0:T(8,128)(2,1)S(1)} %get-tuple-element.160), channel_id=1, source_target_pairs={{0,24},{8,0},{16,8},{24,16},{1,25},{9,1},{17,9},{25,17},{2,26},{10... | collective-permute-start | bytes 1277960 | tf_op jit(solution)/shard_map/ppermute | solution.py:515
  46.6 11.0 %collective-permute-start.10 = (bf16[4,128,256]{2,1,0:T(8,128)(2,1)S(1)}, bf16[4,128,256]{2,1,0:T(8,128)(2,1)S(1)}, u32[]{:S(2)}, u32[]{:S(2)}) collective-permute-start(bf16[4,128,256]{2,1,0:T(8,128)(2,1)S(1)} %get-tuple-element.167), channel_id=1, source_target_pairs={{0,32},{8,40},{16,48},{24,56},{32,64},{40,72},{48,80},{56,88},{64,... | collective-permute-start | bytes 786440 | tf_op jit(solution)/shard_map/ppermute | solution.py:506
  50.3 9.7 %collective-permute-start.11 = (bf16[4,128,256]{2,1,0:T(8,128)(2,1)S(1)}, bf16[4,128,256]{2,1,0:T(8,128)(2,1)S(1)}, u32[]{:S(2)}, u32[]{:S(2)}) collective-permute-start(bf16[4,128,256]{2,1,0:T(8,128)(2,1)S(1)} %get-tuple-element.168), channel_id=1, source_target_pairs={{32,0},{40,8},{48,16},{56,24},{64,32},{72,40},{80,48},{88,56},{96,... | collective-permute-start | bytes 786440 | tf_op jit(solution)/shard_map/ppermute | solution.py:506
  61.7 3.7 %collective-permute-start.15 = (bf16[8,112,512]{2,1,0:T(8,128)(2,1)S(1)}, bf16[8,112,512]{2,1,0:T(8,128)(2,1)S(1)}, u32[]{:S(2)}, u32[]{:S(2)}) collective-permute-start(bf16[8,112,512]{2,1,0:T(8,128)(2,1)S(1)} %get-tuple-element.187), channel_id=1, source_target_pairs={{0,1},{1,0},{2,3},{3,2},{4,5},{5,4},{6,7},{7,6},{8,9},{9,8},{10,11... | collective-permute-start | bytes 2752520 | tf_op jit(solution)/shard_map/ppermute | solution.py:510
  61.8 18.4 %collective-permute-start.12 = (bf16[320,512]{1,0:T(8,128)(2,1)S(1)}, bf16[320,512]{1,0:T(8,128)(2,1)S(1)}, u32[]{:S(2)}, u32[]{:S(2)}) collective-permute-start(bf16[320,512]{1,0:T(8,128)(2,1)S(1)} %get-tuple-element.183), channel_id=1, source_target_pairs={{0,8},{8,16},{16,24},{24,0},{1,9},{9,17},{17,25},{25,1},{2,10},{10... | collective-permute-start | bytes 983048 | tf_op jit(solution)/shard_map/ppermute | solution.py:515
  62.6 17.6 %collective-permute-start.13 = (bf16[320,512]{1,0:T(8,128)(2,1)S(1)}, bf16[320,512]{1,0:T(8,128)(2,1)S(1)}, u32[]{:S(2)}, u32[]{:S(2)}) collective-permute-start(bf16[320,512]{1,0:T(8,128)(2,1)S(1)} %get-tuple-element.184), channel_id=1, source_target_pairs={{0,16},{8,24},{16,0},{24,8},{1,17},{9,25},{17,1},{25,9},{2,18},{10... | collective-permute-start | bytes 983048 | tf_op jit(solution)/shard_map/ppermute | solution.py:515
  64.6 16.2 %collective-permute-start.14 = (bf16[320,512]{1,0:T(8,128)(2,1)S(1)}, bf16[320,512]{1,0:T(8,128)(2,1)S(1)}, u32[]{:S(2)}, u32[]{:S(2)}) collective-permute-start(bf16[320,512]{1,0:T(8,128)(2,1)S(1)} %get-tuple-element.185), channel_id=1, source_target_pairs={{0,24},{8,0},{16,8},{24,16},{1,25},{9,1},{17,9},{25,17},{2,26},{10... | collective-permute-start | bytes 983048 | tf_op jit(solution)/shard_map/ppermute | solution.py:515
  65.6 31.5 %copy-start.3 = (bf16[1,128,1024]{2,1,0:T(8,128)(2,1)S(1)}, bf16[1,128,1024]{2,1,0:T(8,128)(2,1)}, u32[]{:S(2)}) copy-start(bf16[1,128,1024]{2,1,0:T(8,128)(2,1)} %param.8) | copy-start | bytes 786436
  65.6 31.5 %copy-start.4 = (bf16[1,128,1024]{2,1,0:T(8,128)(2,1)S(1)}, bf16[1,128,1024]{2,1,0:T(8,128)(2,1)}, u32[]{:S(2)}) copy-start(bf16[1,128,1024]{2,1,0:T(8,128)(2,1)} %param.9) | copy-start | bytes 786436
  65.6 31.5 %copy-start.5 = (f32[128,1024]{1,0:T(8,128)S(1)}, f32[128,1024]{1,0:T(8,128)}, u32[]{:S(2)}) copy-start(f32[128,1024]{1,0:T(8,128)} %get-tuple-element.209.layer_part) | copy-start | bytes 1572868
  65.6 31.5 %copy-start.6 = (f32[128,1024]{1,0:T(8,128)S(1)}, f32[128,1024]{1,0:T(8,128)}, u32[]{:S(2)}) copy-start(f32[128,1024]{1,0:T(8,128)} %get-tuple-element.210.d_normed) | copy-start | bytes 1572868
  65.6 15.2 %collective-permute-start.16 = (bf16[2,112,512]{2,1,0:T(8,128)(2,1)S(1)}, bf16[2,112,512]{2,1,0:T(8,128)(2,1)S(1)}, u32[]{:S(2)}, u32[]{:S(2)}) collective-permute-start(bf16[2,112,512]{2,1,0:T(8,128)(2,1)S(1)} %get-tuple-element.189), channel_id=1, source_target_pairs={{0,32},{32,64},{64,96},{96,0},{1,33},{33,65},{65,97},{97,1},{2,34}... | collective-permute-start | bytes 688136 | tf_op jit(solution)/shard_map/ppermute | solution.py:521
  69.4 11.4 %collective-permute-start.17 = (bf16[2,112,512]{2,1,0:T(8,128)(2,1)S(1)}, bf16[2,112,512]{2,1,0:T(8,128)(2,1)S(1)}, u32[]{:S(2)}, u32[]{:S(2)}) collective-permute-start(bf16[2,112,512]{2,1,0:T(8,128)(2,1)S(1)} %get-tuple-element.190), channel_id=1, source_target_pairs={{0,64},{32,96},{64,0},{96,32},{1,65},{33,97},{65,1},{97,33},{2,66}... | collective-permute-start | bytes 688136 | tf_op jit(solution)/shard_map/ppermute | solution.py:521
  80.2 6.0 %collective-permute-start.18 = (bf16[2,112,512]{2,1,0:T(8,128)(2,1)S(1)}, bf16[2,112,512]{2,1,0:T(8,128)(2,1)S(1)}, u32[]{:S(2)}, u32[]{:S(2)}) collective-permute-start(bf16[2,112,512]{2,1,0:T(8,128)(2,1)S(1)} %get-tuple-element.191), channel_id=1, source_target_pairs={{0,96},{32,0},{64,32},{96,64},{1,97},{33,1},{65,33},{97,65},{2,98}... | collective-permute-start | bytes 688136 | tf_op jit(solution)/shard_map/ppermute | solution.py:521
  87.4 2.0 %collective-permute-start.19 = (bf16[8,64,512]{2,1,0:T(8,128)(2,1)S(1)}, bf16[8,64,512]{2,1,0:T(8,128)(2,1)S(1)}, u32[]{:S(2)}, u32[]{:S(2)}) collective-permute-start(bf16[8,64,512]{2,1,0:T(8,128)(2,1)S(1)} %get-tuple-element.208), channel_id=1, source_target_pairs={{0,1},{1,0},{2,3},{3,2},{4,5},{5,4},{6,7},{7,6},{8,9},{9,8},{10,11... | collective-permute-start | bytes 1572872 | tf_op jit(solution)/shard_map/ppermute | solution.py:510
  90.3 14.2 %all-to-all-start = ((bf16[8,64,512]{2,1,0:T(8,128)(2,1)}), bf16[8,64,512]{2,1,0:T(8,128)(2,1)S(1)}, u32[]{:S(2)}, u32[]{:S(2)}) async-start(bf16[8,64,512]{2,1,0:T(8,128)(2,1)} %shard_map.147), calls=%async_computation | async-start | bytes 1048576 | tf_op jit(solution)/shard_map/all_to_all | solution.py:614
  95.6 10.3 %collective-permute-start.20 = (bf16[112,512]{1,0:T(8,128)(2,1)}, bf16[112,512]{1,0:T(8,128)(2,1)}, u32[]{:S(2)}, u32[]{:S(2)}) collective-permute-start(bf16[112,512]{1,0:T(8,128)(2,1)} %get-tuple-element.216), channel_id=1, source_target_pairs={{0,128},{128,0},{1,129},{129,1},{2,130},{130,2},{3,131},{131,3},{4... | collective-permute-start | bytes 344072 | tf_op jit(solution)/shard_map/ppermute | solution.py:615
  97.1 8.8 %copy-start.8 = (bf16[112,512]{1,0:T(8,128)(2,1)S(1)}, bf16[112,512]{1,0:T(8,128)(2,1)}, u32[]{:S(2)}) copy-start(bf16[112,512]{1,0:T(8,128)(2,1)} %get-tuple-element.215.gate) | copy-start | bytes 344068
  107.0 10.5 %collective-permute-start.21 = (bf16[176,128]{1,0:T(8,128)(2,1)S(1)}, bf16[176,128]{1,0:T(8,128)(2,1)S(1)}, u32[]{:S(2)}, u32[]{:S(2)}) collective-permute-start(bf16[176,128]{1,0:T(8,128)(2,1)S(1)} %get-tuple-element.219), channel_id=1, source_target_pairs={{0,2},{2,4},{4,6},{6,0},{1,3},{3,5},{5,7},{7,1},{8,10},{10,12},{12... | collective-permute-start | bytes 135176 | tf_op jit(solution)/shard_map/ppermute | solution.py:527
  110.3 8.6 %collective-permute-start.22 = (bf16[176,128]{1,0:T(8,128)(2,1)S(1)}, bf16[176,128]{1,0:T(8,128)(2,1)S(1)}, u32[]{:S(2)}, u32[]{:S(2)}) collective-permute-start(bf16[176,128]{1,0:T(8,128)(2,1)S(1)} %get-tuple-element.220), channel_id=1, source_target_pairs={{0,4},{2,6},{4,0},{6,2},{1,5},{3,7},{5,1},{7,3},{8,12},{10,14},{12... | collective-permute-start | bytes 135176 | tf_op jit(solution)/shard_map/ppermute | solution.py:527
  114.8 5.4 %collective-permute-start.23 = (bf16[176,128]{1,0:T(8,128)(2,1)S(1)}, bf16[176,128]{1,0:T(8,128)(2,1)S(1)}, u32[]{:S(2)}, u32[]{:S(2)}) collective-permute-start(bf16[176,128]{1,0:T(8,128)(2,1)S(1)} %get-tuple-element.221), channel_id=1, source_target_pairs={{0,6},{2,0},{4,2},{6,4},{1,7},{3,1},{5,3},{7,5},{8,14},{10,8},{12,... | collective-permute-start | bytes 135176 | tf_op jit(solution)/shard_map/ppermute | solution.py:527

commit v7 on v6

--- a/solution.py
+++ b/solution.py
@@ -232,8 +232,10 @@
         x = (place[4] + turn) & 3
         for m in range(8):
             ref[64 * m : 64 * m + 64] = d_upper_t[span(4 * m + x, 64), :]
-            ref[512 + 16 * m : 528 + 16 * m] = g_taps_t[4 * m + x]
-            ref[640 + 128 * m : 768 + 128 * m] = gated[:, 128 * m : 128 * m + 128]
+            ref[576 + 128 * m : 704 + 128 * m] = gated[:, 128 * m : 128 * m + 128]
+        for pair in range(4):
+            right = pltpu.roll(g_taps_t[8 * pair + 4 + x].astype(F32), 64, 1)
+            ref[512 + 16 * pair : 528 + 16 * pair] = (g_taps_t[8 * pair + x].astype(F32) + right).astype(BF16)
 
 
 def own_columns(array, core, width):
@@ -250,15 +252,16 @@
     place = locate(lengths)
     x, core = place[4], place[2]
     gates = (gate_0, gate_1, gate_2, gate_3)
-    g_taps = gate_0[512:640].astype(F32)
+    g_taps = gate_0[512:576].astype(F32)
     for ref in gates[1:]:
-        g_taps = g_taps + ref[512:640].astype(F32)
-    g_taps = g_taps.astype(BF16).reshape(8, 16, 128)
+        g_taps = g_taps + ref[512:576].astype(F32)
+    left = g_taps.reshape(4, 16, 128)
+    g_taps = jnp.stack([left, pltpu.roll(left, 64, 2)], axis=1).reshape(8, 16, 128).astype(BF16)
     for turn, (gate, cot) in enumerate(zip(gates, (cot_0, cot_1, cot_2, cot_3))):
         here = span(slot(place, turn), 128)
         d_upper_t[:, here] = gate[:512]
         for block in range(8):
-            gated[here, 128 * block : 128 * block + 128] = gate[640 + 128 * block : 768 + 128 * block]
+            gated[here, 128 * block : 128 * block + 128] = gate[576 + 128 * block : 704 + 128 * block]
         cot_own[:128, here] = cot[:, 1152:1280]
         cot_own[128:, here] = cot[:, 1280:]
     for parity, out in ((core, keep), (1 - core, send)):
@@ -346,6 +349,9 @@
 
         def allowed_of(index):
             position = 128 * index + lax.broadcasted_iota(jnp.int32, (128, 256), 0)
+            if 0 < index < chunks - 1:
+                last = length - group_first + 511 - base
+                return position <= jnp.where(128 * index >= 512 - group_first - base, last, -1)
             return (position >= low) & (position <= high)
 
         peak = jnp.full((128, 256), NEG_LARGE, F32)
@@ -425,7 +431,7 @@
 
 
 def gate_rows_kernel(frames, gate, d_upper, w_up, w_down, layer_part, d_normed):
-    gated = jnp.concatenate([gate[640 + 128 * m : 768 + 128 * m] for m in range(8)], axis=1)
+    gated = jnp.concatenate([gate[576 + 128 * m : 704 + 128 * m] for m in range(8)], axis=1)
     layer_part[...] = frames[...].astype(F32) + dot(gated, w_down[...])
     d_normed[...] = dot(d_upper[...], w_up[...], 1, 1)
 
@@ -559,7 +565,7 @@
     )(lengths, *in_x, w_qkv)
     kv_before, kv_after = shift(kv, 4), shift(kv, -4)
     conv_in, kv = lax.optimization_barrier((conv_in, kv))
-    gate = ((1664, 128), BF16)
+    gate = ((1600, 128), BF16)
     d_upper, *gate_x = call(
         conv_outer_kernel,
         [((ROWS, 2048), BF16, HBM), gate, gate, gate, gate],

time: 121 us -> 121 us (level)
  no operation moved by 1% of the time
where the time goes in v7:
time: 121 us
  starting transfers between devices  58.5 us (48%)
  Pallas kernels  34.5 us (29%)
  waiting for transfers between devices  26.4 us (22%)
  between operations  1.57 us (1%)
    pallas_call x16, Pallas kernels, run(): pl.pallas_call(body, out_shape=[HBM(*out[:2]) if len(out) > 2 else jax.Sh...  34.5 us
    ppermute x6, starting transfers between devices, shift(): lax.ppermute(array, SEQ, [(i, i + by) for i in range(32) if 0 <= i + by <...  19.9 us
    ppermute x9, starting transfers between devices, turn_x(): lax.ppermute(pieces[by], 'x', [(i, (i + by) % 4) for i in range(4)])  13.4 us
    ppermute x3, starting transfers between devices, turn_z(): lax.ppermute(pieces[by], 'z_high', [(i, (i + by) % 4) for i in range(4)])  10.5 us
    ppermute x9, waiting for transfers between devices, turn_x(): lax.ppermute(pieces[by], 'x', [(i, (i + by) % 4) for i in range(4)])  8.21 us
    ppermute x3, starting transfers between devices, turn_y(): lax.ppermute(pieces[by], 'y', [(i, (i + by) % 4) for i in range(4)])  7.64 us
    ppermute x3, waiting for transfers between devices, turn_y(): lax.ppermute(pieces[by], 'y', [(i, (i + by) % 4) for i in range(4)])  5.4 us
    all_to_all x1, starting transfers between devices, local(): parts = lax.all_to_all(parts, ('z_low', 'y'), 0, 0)  5.36 us
  transfers between devices with their start and end apart: 25, of which 12 were waited for; matrix products, arithmetic and copies ran while one was open for 0% of the time, Pallas kernels for 21%

profile of v7, /device:TPU:8, one launch (start us, length us, event | category | flops | bytes accessed | tf_op | source)
XLA Modules:
  0.0 121.0 jit_solution(12290991606983500589)
XLA Ops:
  1.3 2.0 %shard_map.135 = (bf16[128,1408]{1,0:T(8,128)(2,1)S(1)}, bf16[128,1408]{1,0:T(8,128)(2,1)S(1)}, bf16[128,1408]{1,0:T(8,128)(2,1)S(1)}, bf16[128,1408]{1,0:T(8,128)(2,1)S(1)}) custom-call(s32[1]{0:T(128)S(6)} %copy.15.lengths, bf16[128,1024]{1,0:T(8,128)(2,1)} %bitcast.8, bf16[128,1024]{1,0:T(8,128)(2,1)} %bitcast.12, bf16[512,1024]{1,0:T(8,128)(2,1)} %w_out.3), custom_call_target="tpu_custom_call" | custom-call | tf_op jit(solution)/shard_map/pallas_call | solution.py:32
  3.3 1.6 %collective-permute-start = (bf16[128,1408]{1,0:T(8,128)(2,1)S(1)}, bf16[128,1408]{1,0:T(8,128)(2,1)S(1)}, u32[]{:S(2)}, u32[]{:S(2)}) collective-permute-start(bf16[128,1408]{1,0:T(8,128)(2,1)S(1)} %get-tuple-element.122), channel_id=1, source_target_pairs={{0,8},{8,16},{16,24},{24,0},{1,9},{9,17},{17,25},{25,1},{2,10},{10... | collective-permute-start | bytes 1081352 | tf_op jit(solution)/shard_map/ppermute | solution.py:521
  4.8 2.7 %collective-permute-start.1 = (bf16[128,1408]{1,0:T(8,128)(2,1)S(1)}, bf16[128,1408]{1,0:T(8,128)(2,1)S(1)}, u32[]{:S(2)}, u32[]{:S(2)}) collective-permute-start(bf16[128,1408]{1,0:T(8,128)(2,1)S(1)} %get-tuple-element.123), channel_id=1, source_target_pairs={{0,16},{8,24},{16,0},{24,8},{1,17},{9,25},{17,1},{25,9},{2,18},{10... | collective-permute-start | bytes 1081352 | tf_op jit(solution)/shard_map/ppermute | solution.py:521
  7.6 1.4 %collective-permute-start.2 = (bf16[128,1408]{1,0:T(8,128)(2,1)S(1)}, bf16[128,1408]{1,0:T(8,128)(2,1)S(1)}, u32[]{:S(2)}, u32[]{:S(2)}) collective-permute-start(bf16[128,1408]{1,0:T(8,128)(2,1)S(1)} %get-tuple-element.124), channel_id=1, source_target_pairs={{0,24},{8,0},{16,8},{24,16},{1,25},{9,1},{17,9},{25,17},{2,26},{10... | collective-permute-start | bytes 1081352 | tf_op jit(solution)/shard_map/ppermute | solution.py:521
  9.0 4.8 %shard_map.136 = (bf16[128,1024]{1,0:T(8,128)(2,1)S(1)}, bf16[128,1024]{1,0:T(8,128)(2,1)S(1)}, bf16[128,1024]{1,0:T(8,128)(2,1)S(1)}, bf16[128,1024]{1,0:T(8,12...) custom-call(s32[1]{0:T(128)S(6)} %copy.15.lengths, ...), custom_call_target="tpu_custom_call" | custom-call | tf_op jit(solution)/shard_map/pallas_call | solution.py:32
  13.8 2.5 %collective-permute-start.3 = (bf16[16,2048]{1,0:T(8,128)(2,1)S(1)}, bf16[16,2048]{1,0:T(8,128)(2,1)S(1)}, u32[]{:S(2)}, u32[]{:S(2)}) collective-permute-start(bf16[16,2048]{1,0:T(8,128)(2,1)S(1)} %get-tuple-element.129), channel_id=1, source_target_pairs={{0,8},{8,16},{16,24},{24,32},{32,40},{40,48},{48,56},{56,64},{64,7... | collective-permute-start | bytes 196616 | tf_op jit(solution)/shard_map/ppermute | solution.py:512
  16.3 5.4 %collective-permute-start.4 = (bf16[16,2048]{1,0:T(8,128)(2,1)S(1)}, bf16[16,2048]{1,0:T(8,128)(2,1)S(1)}, u32[]{:S(2)}, u32[]{:S(2)}) collective-permute-start(bf16[16,2048]{1,0:T(8,128)(2,1)S(1)} %get-tuple-element.130), channel_id=1, source_target_pairs={{8,0},{16,8},{24,16},{32,24},{40,32},{48,40},{56,48},{64,56},{72,6... | collective-permute-start | bytes 196616 | tf_op jit(solution)/shard_map/ppermute | solution.py:512
  21.8 3.6 %shard_map.137 = (f32[128,1024]{1,0:T(8,128)S(1)}, f32[128,1024]{1,0:T(8,128)S(1)}, f32[32,1024]{1,0:T(8,128)S(1)}) custom-call(bf16[128,1024]{1,0:T(8,128)(2,1)S(1)} %get-tuple-element.126.gating, bf16[128,1024]{1,0:T(8,128)(2,1)S(1)} %get-tuple-element.127.d_conv, f32[31,1024]{1,0:T(8,128)S(1)} %copy-done.7), custom_call_target="tpu_custom_call" | custom-call | tf_op jit(solution)/shard_map/pallas_call | solution.py:32
  25.5 1.3 %shard_map.138 = (bf16[512,1024]{1,0:T(8,128)(2,1)S(1)}, bf16[4,128,128]{2,1,0:T(8,128)(2,1)S(1)}, bf16[4,128,256]{2,1,0:T(8,128)(2,1)S(1)}) custom-call(s32[1]{0:T(128)S(6)} %copy.15.lengths, bf16[128,1408]{1,0:T(8,128)(2,1)S(1)} %get-tuple-element.131.frames_0.cot_0, bf16[128,1408]{1,0:T(8,128)(2,1)S(1)} %collective-permute-done.frames_1.cot_1, ...), custom_call_target="tpu_custom_call" | custom-call | tf_op jit(solution)/shard_map/pallas_call | solution.py:32
  26.8 3.7 %collective-permute-start.5 = (bf16[4,128,256]{2,1,0:T(8,128)(2,1)S(1)}, bf16[4,128,256]{2,1,0:T(8,128)(2,1)S(1)}, u32[]{:S(2)}, u32[]{:S(2)}) collective-permute-start(bf16[4,128,256]{2,1,0:T(8,128)(2,1)S(1)} %get-tuple-element.139.kv), channel_id=1, source_target_pairs={{0,32},{8,40},{16,48},{24,56},{32,64},{40,72},{48,80},{56,88},{64,... | collective-permute-start | bytes 786440 | tf_op jit(solution)/shard_map/ppermute | solution.py:512
  30.5 2.4 %collective-permute-start.6 = (bf16[4,128,256]{2,1,0:T(8,128)(2,1)S(1)}, bf16[4,128,256]{2,1,0:T(8,128)(2,1)S(1)}, u32[]{:S(2)}, u32[]{:S(2)}) collective-permute-start(bf16[4,128,256]{2,1,0:T(8,128)(2,1)S(1)} %get-tuple-element.139.kv), channel_id=1, source_target_pairs={{32,0},{40,8},{48,16},{56,24},{64,32},{72,40},{80,48},{88,56},{96,... | collective-permute-start | bytes 786440 | tf_op jit(solution)/shard_map/ppermute | solution.py:512
  32.9 2.2 %shard_map.139 = (bf16[128,2048]{1,0:T(8,128)(2,1)}, bf16[1600,128]{1,0:T(8,128)(2,1)S(1)}, bf16[1600,128]{1,0:T(8,128)(2,1)S(1)}, bf16[1600,128]{1,0:T(8,128)(2,1)S(1)}, bf16[1600,128]{1,0:T(8,128)(2,1)S(1)}) custom-call(s32[1]{0:T(128)S(6)} %copy.15.lengths, f32[128,1024]{1,0:T(8,128)S(1)} %get-tuple-element.140.conv_in, ...), custom_call_target="tpu_custom_call" | custom-call | tf_op jit(solution)/shard_map/pallas_call | solution.py:32
  35.1 1.4 %collective-permute-done.5.before = bf16[4,128,256]{2,1,0:T(8,128)(2,1)S(1)} collective-permute-done((bf16[4,128,256]{2,1,0:T(8,128)(2,1)S(1)}, bf16[4,128,256]{2,1,0:T(8,128)(2,1)S(1)}, u32[]{:S(2)}, u32[]{:S(2)}) %collective-permute-start.5) | collective-permute-done | bytes 262176 | tf_op jit(solution)/shard_map/ppermute | solution.py:512
  36.5 0.7 collective-permute-start.7
  37.2 3.3 %collective-permute-start.8 = (bf16[1600,128]{1,0:T(8,128)(2,1)S(1)}, bf16[1600,128]{1,0:T(8,128)(2,1)S(1)}, u32[]{:S(2)}, u32[]{:S(2)}) collective-permute-start(bf16[1600,128]{1,0:T(8,128)(2,1)S(1)} %get-tuple-element.159), channel_id=1, source_target_pairs={{0,16},{8,24},{16,0},{24,8},{1,17},{9,25},{17,1},{25,9},{2,18},{10... | collective-permute-start | bytes 1228808 | tf_op jit(solution)/shard_map/ppermute | solution.py:521
  40.6 6.0 %shard_map.140 = (bf16[4,128,128]{2,1,0:T(8,128)(2,1)S(1)}, bf16[128,512]{1,0:T(8,128)(2,1)S(1)}, bf16[4,128,256]{2,1,0:T(8,128)(2,1)S(1)}, bf16[4,128,256]{2,1,0:T(8,128)(2,1)S(1)}, f32[4,128,256]{2,1,0:T(8,128)S(1)}) custom-call(s32[1]{0:T(128)S(6)} %copy.15.lengths, bf16[4,128,128]{2,1,0:T(8,128)(2,1)S(1)} %get-tuple-element.136.queries, ...), custom_call_target="tpu_custom_call" | custom-call | tf_op jit(solution)/shard_map/pallas_call | solution.py:32
  46.5 3.7 %collective-permute-start.10 = (bf16[4,128,256]{2,1,0:T(8,128)(2,1)S(1)}, bf16[4,128,256]{2,1,0:T(8,128)(2,1)S(1)}, u32[]{:S(2)}, u32[]{:S(2)}) collective-permute-start(bf16[4,128,256]{2,1,0:T(8,128)(2,1)S(1)} %get-tuple-element.167), channel_id=1, source_target_pairs={{0,32},{8,40},{16,48},{24,56},{32,64},{40,72},{48,80},{56,88},{64,... | collective-permute-start | bytes 786440 | tf_op jit(solution)/shard_map/ppermute | solution.py:512
  50.3 2.2 %collective-permute-start.11 = (bf16[4,128,256]{2,1,0:T(8,128)(2,1)S(1)}, bf16[4,128,256]{2,1,0:T(8,128)(2,1)S(1)}, u32[]{:S(2)}, u32[]{:S(2)}) collective-permute-start(bf16[4,128,256]{2,1,0:T(8,128)(2,1)S(1)} %get-tuple-element.168), channel_id=1, source_target_pairs={{32,0},{40,8},{48,16},{56,24},{64,32},{72,40},{80,48},{88,56},{96,... | collective-permute-start | bytes 786440 | tf_op jit(solution)/shard_map/ppermute | solution.py:512
  52.4 3.7 %shard_map.141 = (f32[128,1024]{1,0:T(8,128)}, f32[128,1024]{1,0:T(8,128)}) custom-call(bf16[128,1024]{1,0:T(8,128)(2,1)} %bitcast.10, bf16[1600,128]{1,0:T(8,128)(2,1)S(1)} %get-tuple-element.177.gate.gate_0, bf16[128,2048]{1,0:T(8,128)(2,1)} %get-tuple-element.163.d_upper, bf16[1024,2048]{1,0:T(8,128)(2,1)S(1)} %copy-done, bf16[1024,1024]{1,0:T(8,128)(2,1)S(1)} %copy-done.2), custom_call_target="tpu_custom_call" | custom-call | tf_op jit(solution)/shard_map/pallas_call | solution.py:32
  56.2 0.5 collective-permute-done.8.gate_2
  56.8 3.2 %collective-permute-done.11.from_after = bf16[4,128,256]{2,1,0:T(8,128)(2,1)S(1)} collective-permute-done((bf16[4,128,256]{2,1,0:T(8,128)(2,1)S(1)}, bf16[4,128,256]{2,1,0:T(8,128)(2,1)S(1)}, u32[]{:S(2)}, u32[]{:S(2)}) %collective-permute-start.11) | collective-permute-done | bytes 262176 | tf_op jit(solution)/shard_map/ppermute | solution.py:512
  60.0 0.3 shard_map.142
  60.4 1.3 %shard_map.143 = (bf16[8,112,512]{2,1,0:T(8,128)(2,1)S(1)}, bf16[8,112,512]{2,1,0:T(8,128)(2,1)S(1)}, bf16[256,512]{1,0:T(8,128)(2,1)S(1)}) custom-call(s32[1]{0:T(128)S(6)} %copy.15.lengths, bf16[512,1024]{1,0:T(8,128)(2,1)S(1)} %get-tuple-element.135.normed, bf16[128,1408]{1,0:T(8,128)(2,1)S(1)} %get-tuple-element.131.frames_0.cot_0, ...), custom_call_target="tpu_custom_call" | custom-call | tf_op jit(solution)/shard_map/pallas_call | solution.py:32
  61.8 0.8 collective-permute-start.12
  62.6 2.0 %collective-permute-start.13 = (bf16[320,512]{1,0:T(8,128)(2,1)S(1)}, bf16[320,512]{1,0:T(8,128)(2,1)S(1)}, u32[]{:S(2)}, u32[]{:S(2)}) collective-permute-start(bf16[320,512]{1,0:T(8,128)(2,1)S(1)} %get-tuple-element.184), channel_id=1, source_target_pairs={{0,16},{8,24},{16,0},{24,8},{1,17},{9,25},{17,1},{25,9},{2,18},{10... | collective-permute-start | bytes 983048 | tf_op jit(solution)/shard_map/ppermute | solution.py:521
  64.6 0.7 collective-permute-start.14
  65.4 0.2 shard_map.144
  65.6 3.8 %collective-permute-start.16 = (bf16[2,112,512]{2,1,0:T(8,128)(2,1)S(1)}, bf16[2,112,512]{2,1,0:T(8,128)(2,1)S(1)}, u32[]{:S(2)}, u32[]{:S(2)}) collective-permute-start(bf16[2,112,512]{2,1,0:T(8,128)(2,1)S(1)} %get-tuple-element.189), channel_id=1, source_target_pairs={{0,32},{32,64},{64,96},{96,0},{1,33},{33,65},{65,97},{97,1},{2,34}... | collective-permute-start | bytes 688136 | tf_op jit(solution)/shard_map/ppermute | solution.py:527
  69.4 3.9 %collective-permute-start.17 = (bf16[2,112,512]{2,1,0:T(8,128)(2,1)S(1)}, bf16[2,112,512]{2,1,0:T(8,128)(2,1)S(1)}, u32[]{:S(2)}, u32[]{:S(2)}) collective-permute-start(bf16[2,112,512]{2,1,0:T(8,128)(2,1)S(1)} %get-tuple-element.190), channel_id=1, source_target_pairs={{0,64},{32,96},{64,0},{96,32},{1,65},{33,97},{65,1},{97,33},{2,66}... | collective-permute-start | bytes 688136 | tf_op jit(solution)/shard_map/ppermute | solution.py:527
  73.3 6.9 %collective-permute-done.12.far_1 = bf16[320,512]{1,0:T(8,128)(2,1)S(1)} collective-permute-done((bf16[320,512]{1,0:T(8,128)(2,1)S(1)}, bf16[320,512]{1,0:T(8,128)(2,1)S(1)}, u32[]{:S(2)}, u32[]{:S(2)}) %collective-permute-start.12) | collective-permute-done | bytes 327712 | tf_op jit(solution)/shard_map/ppermute | solution.py:521
  80.2 0.6 collective-permute-done.14.far_3
  80.8 5.4 %collective-permute-done.18.part_3 = bf16[2,112,512]{2,1,0:T(8,128)(2,1)S(1)} collective-permute-done((bf16[2,112,512]{2,1,0:T(8,128)(2,1)S(1)}, bf16[2,112,512]{2,1,0:T(8,128)(2,1)S(1)}, u32[]{:S(2)}, u32[]{:S(2)}) %collective-permute-start.18) | collective-permute-done | bytes 229408 | tf_op jit(solution)/shard_map/ppermute | solution.py:527
  86.2 1.1 shard_map.145
  87.4 0.8 shard_map.146
  88.2 1.1 collective-permute-done.19.far
  89.3 0.9 shard_map.147
  90.3 5.4 %all-to-all-start = ((bf16[8,64,512]{2,1,0:T(8,128)(2,1)}), bf16[8,64,512]{2,1,0:T(8,128)(2,1)S(1)}, u32[]{:S(2)}, u32[]{:S(2)}) async-start(bf16[8,64,512]{2,1,0:T(8,128)(2,1)} %shard_map.147), calls=%async_computation | async-start | bytes 1048576 | tf_op jit(solution)/shard_map/all_to_all | solution.py:620
  95.6 1.5 %collective-permute-start.20 = (bf16[112,512]{1,0:T(8,128)(2,1)}, bf16[112,512]{1,0:T(8,128)(2,1)}, u32[]{:S(2)}, u32[]{:S(2)}) collective-permute-start(bf16[112,512]{1,0:T(8,128)(2,1)} %get-tuple-element.216), channel_id=1, source_target_pairs={{0,128},{128,0},{1,129},{129,1},{2,130},{130,2},{3,131},{131,3},{4... | collective-permute-start | bytes 344072 | tf_op jit(solution)/shard_map/ppermute | solution.py:621
  97.1 4.5 %shard_map.148 = (bf16[128,1024]{1,0:T(8,128)(2,1)}, bf16[128,1024]{1,0:T(8,128)(2,1)}) custom-call(s32[1]{0:T(128)S(6)} %copy.15.lengths, bf16[128,1024]{1,0:T(8,128)(2,1)S(1)} %bitcast.11, bf16[128,1024]{1,0:T(8,128)(2,1)S(1)} %bitcast.14, bf16[320,512]{1,0:T(8,128)(2,1)S(1)} %get-tuple-element.192.far_0, ...), custom_call_target="tpu_custom_call" | custom-call | tf_op jit(solution)/shard_map/pallas_call | solution.py:32
  101.6 2.9 %all-to-all-done.parts = bf16[8,64,512]{2,1,0:T(8,128)(2,1)S(1)} async-done(((bf16[8,64,512]{2,1,0:T(8,128)(2,1)}), bf16[8,64,512]{2,1,0:T(8,128)(2,1)S(1)}, u32[]{:S(2)}, u32[]{:S(2)}) %all-to-all-start) | async-done | bytes 524320 | tf_op jit(solution)/shard_map/all_to_all | solution.py:620
  104.5 1.5 %collective-permute-done.20.gate_far = bf16[112,512]{1,0:T(8,128)(2,1)} collective-permute-done((bf16[112,512]{1,0:T(8,128)(2,1)}, bf16[112,512]{1,0:T(8,128)(2,1)}, u32[]{:S(2)}, u32[]{:S(2)}) %collective-permute-start.20) | collective-permute-done | bytes 114720 | tf_op jit(solution)/shard_map/ppermute | solution.py:621
  105.9 1.0 shard_map.149
  107.0 3.3 %collective-permute-start.21 = (bf16[176,128]{1,0:T(8,128)(2,1)S(1)}, bf16[176,128]{1,0:T(8,128)(2,1)S(1)}, u32[]{:S(2)}, u32[]{:S(2)}) collective-permute-start(bf16[176,128]{1,0:T(8,128)(2,1)S(1)} %get-tuple-element.219), channel_id=1, source_target_pairs={{0,2},{2,4},{4,6},{6,0},{1,3},{3,5},{5,7},{7,1},{8,10},{10,12},{12... | collective-permute-start | bytes 135176 | tf_op jit(solution)/shard_map/ppermute | solution.py:533
  110.3 4.5 %collective-permute-start.22 = (bf16[176,128]{1,0:T(8,128)(2,1)S(1)}, bf16[176,128]{1,0:T(8,128)(2,1)S(1)}, u32[]{:S(2)}, u32[]{:S(2)}) collective-permute-start(bf16[176,128]{1,0:T(8,128)(2,1)S(1)} %get-tuple-element.220), channel_id=1, source_target_pairs={{0,4},{2,6},{4,0},{6,2},{1,5},{3,7},{5,1},{7,3},{8,12},{10,14},{12... | collective-permute-start | bytes 135176 | tf_op jit(solution)/shard_map/ppermute | solution.py:533
  114.8 2.7 %collective-permute-start.23 = (bf16[176,128]{1,0:T(8,128)(2,1)S(1)}, bf16[176,128]{1,0:T(8,128)(2,1)S(1)}, u32[]{:S(2)}, u32[]{:S(2)}) collective-permute-start(bf16[176,128]{1,0:T(8,128)(2,1)S(1)} %get-tuple-element.221), channel_id=1, source_target_pairs={{0,6},{2,0},{4,2},{6,4},{1,7},{3,1},{5,3},{7,5},{8,14},{10,8},{12,... | collective-permute-start | bytes 135176 | tf_op jit(solution)/shard_map/ppermute | solution.py:533
  117.5 1.5 %collective-permute-done.22.part_2 = bf16[176,128]{1,0:T(8,128)(2,1)S(1)} collective-permute-done((bf16[176,128]{1,0:T(8,128)(2,1)S(1)}, bf16[176,128]{1,0:T(8,128)(2,1)S(1)}, u32[]{:S(2)}, u32[]{:S(2)}) %collective-permute-start.22) | collective-permute-done | bytes 45088 | tf_op jit(solution)/shard_map/ppermute | solution.py:533
  118.9 1.3 %collective-permute-done.23.part_3 = bf16[176,128]{1,0:T(8,128)(2,1)S(1)} collective-permute-done((bf16[176,128]{1,0:T(8,128)(2,1)S(1)}, bf16[176,128]{1,0:T(8,128)(2,1)S(1)}, u32[]{:S(2)}, u32[]{:S(2)}) %collective-permute-start.23) | collective-permute-done | bytes 45088 | tf_op jit(solution)/shard_map/ppermute | solution.py:533
  120.2 0.8 shard_map.150
  (36 shorter events, 0.6 us)
Async XLA Ops:
  3.2 18.5 %copy-start.7 = (f32[31,1024]{1,0:T(8,128)S(1)}, f32[31,1024]{1,0:T(8,128)}, u32[]{:S(2)}) copy-start(f32[31,1024]{1,0:T(8,128)} %taps.3) | copy-start | bytes 380932
  3.3 22.2 %copy-start.1 = (bf16[1024,1536]{1,0:T(8,128)(2,1)S(1)}, bf16[1024,1536]{1,0:T(8,128)(2,1)}, u32[]{:S(2)}) copy-start(bf16[1024,1536]{1,0:T(8,128)(2,1)} %w_qkv.3) | copy-start | bytes 9437188
  3.3 22.1 %collective-permute-start = (bf16[128,1408]{1,0:T(8,128)(2,1)S(1)}, bf16[128,1408]{1,0:T(8,128)(2,1)S(1)}, u32[]{:S(2)}, u32[]{:S(2)}) collective-permute-start(bf16[128,1408]{1,0:T(8,128)(2,1)S(1)} %get-tuple-element.122), channel_id=1, source_target_pairs={{0,8},{8,16},{16,24},{24,0},{1,9},{9,17},{17,25},{25,1},{2,10},{10... | collective-permute-start | bytes 1081352 | tf_op jit(solution)/shard_map/ppermute | solution.py:521
  4.8 20.6 %collective-permute-start.1 = (bf16[128,1408]{1,0:T(8,128)(2,1)S(1)}, bf16[128,1408]{1,0:T(8,128)(2,1)S(1)}, u32[]{:S(2)}, u32[]{:S(2)}) collective-permute-start(bf16[128,1408]{1,0:T(8,128)(2,1)S(1)} %get-tuple-element.123), channel_id=1, source_target_pairs={{0,16},{8,24},{16,0},{24,8},{1,17},{9,25},{17,1},{25,9},{2,18},{10... | collective-permute-start | bytes 1081352 | tf_op jit(solution)/shard_map/ppermute | solution.py:521
  7.6 17.9 %collective-permute-start.2 = (bf16[128,1408]{1,0:T(8,128)(2,1)S(1)}, bf16[128,1408]{1,0:T(8,128)(2,1)S(1)}, u32[]{:S(2)}, u32[]{:S(2)}) collective-permute-start(bf16[128,1408]{1,0:T(8,128)(2,1)S(1)} %get-tuple-element.124), channel_id=1, source_target_pairs={{0,24},{8,0},{16,8},{24,16},{1,25},{9,1},{17,9},{25,17},{2,26},{10... | collective-permute-start | bytes 1081352 | tf_op jit(solution)/shard_map/ppermute | solution.py:521
  13.8 11.6 %collective-permute-start.3 = (bf16[16,2048]{1,0:T(8,128)(2,1)S(1)}, bf16[16,2048]{1,0:T(8,128)(2,1)S(1)}, u32[]{:S(2)}, u32[]{:S(2)}) collective-permute-start(bf16[16,2048]{1,0:T(8,128)(2,1)S(1)} %get-tuple-element.129), channel_id=1, source_target_pairs={{0,8},{8,16},{16,24},{24,32},{32,40},{40,48},{48,56},{56,64},{64,7... | collective-permute-start | bytes 196616 | tf_op jit(solution)/shard_map/ppermute | solution.py:512
  16.3 9.1 %collective-permute-start.4 = (bf16[16,2048]{1,0:T(8,128)(2,1)S(1)}, bf16[16,2048]{1,0:T(8,128)(2,1)S(1)}, u32[]{:S(2)}, u32[]{:S(2)}) collective-permute-start(bf16[16,2048]{1,0:T(8,128)(2,1)S(1)} %get-tuple-element.130), channel_id=1, source_target_pairs={{8,0},{16,8},{24,16},{32,24},{40,32},{48,40},{56,48},{64,56},{72,6... | collective-permute-start | bytes 196616 | tf_op jit(solution)/shard_map/ppermute | solution.py:512
  25.4 27.0 %copy-start.2 = (bf16[1024,1024]{1,0:T(8,128)(2,1)S(1)}, bf16[1024,1024]{1,0:T(8,128)(2,1)}, u32[]{:S(2)}) copy-start(bf16[1024,1024]{1,0:T(8,128)(2,1)} %w_down.3) | copy-start | bytes 6291460
  26.8 25.7 %copy-start = (bf16[1024,2048]{1,0:T(8,128)(2,1)S(1)}, bf16[1024,2048]{1,0:T(8,128)(2,1)}, u32[]{:S(2)}) copy-start(bf16[1024,2048]{1,0:T(8,128)(2,1)} %w_up.3) | copy-start | bytes 12582916
  26.8 9.7 %collective-permute-start.5 = (bf16[4,128,256]{2,1,0:T(8,128)(2,1)S(1)}, bf16[4,128,256]{2,1,0:T(8,128)(2,1)S(1)}, u32[]{:S(2)}, u32[]{:S(2)}) collective-permute-start(bf16[4,128,256]{2,1,0:T(8,128)(2,1)S(1)} %get-tuple-element.139.kv), channel_id=1, source_target_pairs={{0,32},{8,40},{16,48},{24,56},{32,64},{40,72},{48,80},{56,88},{64,... | collective-permute-start | bytes 786440 | tf_op jit(solution)/shard_map/ppermute | solution.py:512
  30.5 10.0 %collective-permute-start.6 = (bf16[4,128,256]{2,1,0:T(8,128)(2,1)S(1)}, bf16[4,128,256]{2,1,0:T(8,128)(2,1)S(1)}, u32[]{:S(2)}, u32[]{:S(2)}) collective-permute-start(bf16[4,128,256]{2,1,0:T(8,128)(2,1)S(1)} %get-tuple-element.139.kv), channel_id=1, source_target_pairs={{32,0},{40,8},{48,16},{56,24},{64,32},{72,40},{80,48},{88,56},{96,... | collective-permute-start | bytes 786440 | tf_op jit(solution)/shard_map/ppermute | solution.py:512
  36.5 19.7 %collective-permute-start.7 = (bf16[1600,128]{1,0:T(8,128)(2,1)S(1)}, bf16[1600,128]{1,0:T(8,128)(2,1)S(1)}, u32[]{:S(2)}, u32[]{:S(2)}) collective-permute-start(bf16[1600,128]{1,0:T(8,128)(2,1)S(1)} %get-tuple-element.158), channel_id=1, source_target_pairs={{0,8},{8,16},{16,24},{24,0},{1,9},{9,17},{17,25},{25,1},{2,10},{10... | collective-permute-start | bytes 1228808 | tf_op jit(solution)/shard_map/ppermute | solution.py:521
  37.2 19.5 %collective-permute-start.8 = (bf16[1600,128]{1,0:T(8,128)(2,1)S(1)}, bf16[1600,128]{1,0:T(8,128)(2,1)S(1)}, u32[]{:S(2)}, u32[]{:S(2)}) collective-permute-start(bf16[1600,128]{1,0:T(8,128)(2,1)S(1)} %get-tuple-element.159), channel_id=1, source_target_pairs={{0,16},{8,24},{16,0},{24,8},{1,17},{9,25},{17,1},{25,9},{2,18},{10... | collective-permute-start | bytes 1228808 | tf_op jit(solution)/shard_map/ppermute | solution.py:521
  40.4 16.4 %collective-permute-start.9 = (bf16[1600,128]{1,0:T(8,128)(2,1)S(1)}, bf16[1600,128]{1,0:T(8,128)(2,1)S(1)}, u32[]{:S(2)}, u32[]{:S(2)}) collective-permute-start(bf16[1600,128]{1,0:T(8,128)(2,1)S(1)} %get-tuple-element.160), channel_id=1, source_target_pairs={{0,24},{8,0},{16,8},{24,16},{1,25},{9,1},{17,9},{25,17},{2,26},{10... | collective-permute-start | bytes 1228808 | tf_op jit(solution)/shard_map/ppermute | solution.py:521
  46.5 10.3 %collective-permute-start.10 = (bf16[4,128,256]{2,1,0:T(8,128)(2,1)S(1)}, bf16[4,128,256]{2,1,0:T(8,128)(2,1)S(1)}, u32[]{:S(2)}, u32[]{:S(2)}) collective-permute-start(bf16[4,128,256]{2,1,0:T(8,128)(2,1)S(1)} %get-tuple-element.167), channel_id=1, source_target_pairs={{0,32},{8,40},{16,48},{24,56},{32,64},{40,72},{48,80},{56,88},{64,... | collective-permute-start | bytes 786440 | tf_op jit(solution)/shard_map/ppermute | solution.py:512
  50.3 9.8 %collective-permute-start.11 = (bf16[4,128,256]{2,1,0:T(8,128)(2,1)S(1)}, bf16[4,128,256]{2,1,0:T(8,128)(2,1)S(1)}, u32[]{:S(2)}, u32[]{:S(2)}) collective-permute-start(bf16[4,128,256]{2,1,0:T(8,128)(2,1)S(1)} %get-tuple-element.168), channel_id=1, source_target_pairs={{32,0},{40,8},{48,16},{56,24},{64,32},{72,40},{80,48},{88,56},{96,... | collective-permute-start | bytes 786440 | tf_op jit(solution)/shard_map/ppermute | solution.py:512
  61.7 3.7 %collective-permute-start.15 = (bf16[8,112,512]{2,1,0:T(8,128)(2,1)S(1)}, bf16[8,112,512]{2,1,0:T(8,128)(2,1)S(1)}, u32[]{:S(2)}, u32[]{:S(2)}) collective-permute-start(bf16[8,112,512]{2,1,0:T(8,128)(2,1)S(1)} %get-tuple-element.187), channel_id=1, source_target_pairs={{0,1},{1,0},{2,3},{3,2},{4,5},{5,4},{6,7},{7,6},{8,9},{9,8},{10,11... | collective-permute-start | bytes 2752520 | tf_op jit(solution)/shard_map/ppermute | solution.py:516
  61.8 18.4 %collective-permute-start.12 = (bf16[320,512]{1,0:T(8,128)(2,1)S(1)}, bf16[320,512]{1,0:T(8,128)(2,1)S(1)}, u32[]{:S(2)}, u32[]{:S(2)}) collective-permute-start(bf16[320,512]{1,0:T(8,128)(2,1)S(1)} %get-tuple-element.183), channel_id=1, source_target_pairs={{0,8},{8,16},{16,24},{24,0},{1,9},{9,17},{17,25},{25,1},{2,10},{10... | collective-permute-start | bytes 983048 | tf_op jit(solution)/shard_map/ppermute | solution.py:521
  62.6 17.6 %collective-permute-start.13 = (bf16[320,512]{1,0:T(8,128)(2,1)S(1)}, bf16[320,512]{1,0:T(8,128)(2,1)S(1)}, u32[]{:S(2)}, u32[]{:S(2)}) collective-permute-start(bf16[320,512]{1,0:T(8,128)(2,1)S(1)} %get-tuple-element.184), channel_id=1, source_target_pairs={{0,16},{8,24},{16,0},{24,8},{1,17},{9,25},{17,1},{25,9},{2,18},{10... | collective-permute-start | bytes 983048 | tf_op jit(solution)/shard_map/ppermute | solution.py:521
  64.6 16.2 %collective-permute-start.14 = (bf16[320,512]{1,0:T(8,128)(2,1)S(1)}, bf16[320,512]{1,0:T(8,128)(2,1)S(1)}, u32[]{:S(2)}, u32[]{:S(2)}) collective-permute-start(bf16[320,512]{1,0:T(8,128)(2,1)S(1)} %get-tuple-element.185), channel_id=1, source_target_pairs={{0,24},{8,0},{16,8},{24,16},{1,25},{9,1},{17,9},{25,17},{2,26},{10... | collective-permute-start | bytes 983048 | tf_op jit(solution)/shard_map/ppermute | solution.py:521
  65.6 31.5 %copy-start.3 = (bf16[1,128,1024]{2,1,0:T(8,128)(2,1)S(1)}, bf16[1,128,1024]{2,1,0:T(8,128)(2,1)}, u32[]{:S(2)}) copy-start(bf16[1,128,1024]{2,1,0:T(8,128)(2,1)} %param.8) | copy-start | bytes 786436
  65.6 31.5 %copy-start.4 = (bf16[1,128,1024]{2,1,0:T(8,128)(2,1)S(1)}, bf16[1,128,1024]{2,1,0:T(8,128)(2,1)}, u32[]{:S(2)}) copy-start(bf16[1,128,1024]{2,1,0:T(8,128)(2,1)} %param.9) | copy-start | bytes 786436
  65.6 31.5 %copy-start.5 = (f32[128,1024]{1,0:T(8,128)S(1)}, f32[128,1024]{1,0:T(8,128)}, u32[]{:S(2)}) copy-start(f32[128,1024]{1,0:T(8,128)} %get-tuple-element.209.layer_part) | copy-start | bytes 1572868
  65.6 31.5 %copy-start.6 = (f32[128,1024]{1,0:T(8,128)S(1)}, f32[128,1024]{1,0:T(8,128)}, u32[]{:S(2)}) copy-start(f32[128,1024]{1,0:T(8,128)} %get-tuple-element.210.d_normed) | copy-start | bytes 1572868
  65.6 15.2 %collective-permute-start.16 = (bf16[2,112,512]{2,1,0:T(8,128)(2,1)S(1)}, bf16[2,112,512]{2,1,0:T(8,128)(2,1)S(1)}, u32[]{:S(2)}, u32[]{:S(2)}) collective-permute-start(bf16[2,112,512]{2,1,0:T(8,128)(2,1)S(1)} %get-tuple-element.189), channel_id=1, source_target_pairs={{0,32},{32,64},{64,96},{96,0},{1,33},{33,65},{65,97},{97,1},{2,34}... | collective-permute-start | bytes 688136 | tf_op jit(solution)/shard_map/ppermute | solution.py:527
  69.4 11.4 %collective-permute-start.17 = (bf16[2,112,512]{2,1,0:T(8,128)(2,1)S(1)}, bf16[2,112,512]{2,1,0:T(8,128)(2,1)S(1)}, u32[]{:S(2)}, u32[]{:S(2)}) collective-permute-start(bf16[2,112,512]{2,1,0:T(8,128)(2,1)S(1)} %get-tuple-element.190), channel_id=1, source_target_pairs={{0,64},{32,96},{64,0},{96,32},{1,65},{33,97},{65,1},{97,33},{2,66}... | collective-permute-start | bytes 688136 | tf_op jit(solution)/shard_map/ppermute | solution.py:527
  80.2 6.0 %collective-permute-start.18 = (bf16[2,112,512]{2,1,0:T(8,128)(2,1)S(1)}, bf16[2,112,512]{2,1,0:T(8,128)(2,1)S(1)}, u32[]{:S(2)}, u32[]{:S(2)}) collective-permute-start(bf16[2,112,512]{2,1,0:T(8,128)(2,1)S(1)} %get-tuple-element.191), channel_id=1, source_target_pairs={{0,96},{32,0},{64,32},{96,64},{1,97},{33,1},{65,33},{97,65},{2,98}... | collective-permute-start | bytes 688136 | tf_op jit(solution)/shard_map/ppermute | solution.py:527
  87.3 2.0 %collective-permute-start.19 = (bf16[8,64,512]{2,1,0:T(8,128)(2,1)S(1)}, bf16[8,64,512]{2,1,0:T(8,128)(2,1)S(1)}, u32[]{:S(2)}, u32[]{:S(2)}) collective-permute-start(bf16[8,64,512]{2,1,0:T(8,128)(2,1)S(1)} %get-tuple-element.208), channel_id=1, source_target_pairs={{0,1},{1,0},{2,3},{3,2},{4,5},{5,4},{6,7},{7,6},{8,9},{9,8},{10,11... | collective-permute-start | bytes 1572872 | tf_op jit(solution)/shard_map/ppermute | solution.py:516
  90.3 14.2 %all-to-all-start = ((bf16[8,64,512]{2,1,0:T(8,128)(2,1)}), bf16[8,64,512]{2,1,0:T(8,128)(2,1)S(1)}, u32[]{:S(2)}, u32[]{:S(2)}) async-start(bf16[8,64,512]{2,1,0:T(8,128)(2,1)} %shard_map.147), calls=%async_computation | async-start | bytes 1048576 | tf_op jit(solution)/shard_map/all_to_all | solution.py:620
  95.6 10.3 %collective-permute-start.20 = (bf16[112,512]{1,0:T(8,128)(2,1)}, bf16[112,512]{1,0:T(8,128)(2,1)}, u32[]{:S(2)}, u32[]{:S(2)}) collective-permute-start(bf16[112,512]{1,0:T(8,128)(2,1)} %get-tuple-element.216), channel_id=1, source_target_pairs={{0,128},{128,0},{1,129},{129,1},{2,130},{130,2},{3,131},{131,3},{4... | collective-permute-start | bytes 344072 | tf_op jit(solution)/shard_map/ppermute | solution.py:621
  97.1 8.8 %copy-start.8 = (bf16[112,512]{1,0:T(8,128)(2,1)S(1)}, bf16[112,512]{1,0:T(8,128)(2,1)}, u32[]{:S(2)}) copy-start(bf16[112,512]{1,0:T(8,128)(2,1)} %get-tuple-element.215.gate) | copy-start | bytes 344068
  107.0 10.5 %collective-permute-start.21 = (bf16[176,128]{1,0:T(8,128)(2,1)S(1)}, bf16[176,128]{1,0:T(8,128)(2,1)S(1)}, u32[]{:S(2)}, u32[]{:S(2)}) collective-permute-start(bf16[176,128]{1,0:T(8,128)(2,1)S(1)} %get-tuple-element.219), channel_id=1, source_target_pairs={{0,2},{2,4},{4,6},{6,0},{1,3},{3,5},{5,7},{7,1},{8,10},{10,12},{12... | collective-permute-start | bytes 135176 | tf_op jit(solution)/shard_map/ppermute | solution.py:533
  110.3 8.6 %collective-permute-start.22 = (bf16[176,128]{1,0:T(8,128)(2,1)S(1)}, bf16[176,128]{1,0:T(8,128)(2,1)S(1)}, u32[]{:S(2)}, u32[]{:S(2)}) collective-permute-start(bf16[176,128]{1,0:T(8,128)(2,1)S(1)} %get-tuple-element.220), channel_id=1, source_target_pairs={{0,4},{2,6},{4,0},{6,2},{1,5},{3,7},{5,1},{7,3},{8,12},{10,14},{12... | collective-permute-start | bytes 135176 | tf_op jit(solution)/shard_map/ppermute | solution.py:533
  114.8 5.4 %collective-permute-start.23 = (bf16[176,128]{1,0:T(8,128)(2,1)S(1)}, bf16[176,128]{1,0:T(8,128)(2,1)S(1)}, u32[]{:S(2)}, u32[]{:S(2)}) collective-permute-start(bf16[176,128]{1,0:T(8,128)(2,1)S(1)} %get-tuple-element.221), channel_id=1, source_target_pairs={{0,6},{2,0},{4,2},{6,4},{1,7},{3,1},{5,3},{7,5},{8,14},{10,8},{12,... | collective-permute-start | bytes 135176 | tf_op jit(solution)/shard_map/ppermute | solution.py:533

commit v8 on v7

--- a/solution.py
+++ b/solution.py
@@ -606,14 +606,14 @@
     gate_y = turn_y(
         call(turn_add_kernel, [((2, 112, 512), BF16)] * 4, scalars=1)(lengths, keep, other_core(send))
     )
-    far_x, gate_y = lax.optimization_barrier((far_x, gate_y))
+    far_x, gate_y[1] = lax.optimization_barrier((far_x, gate_y[1]))
     attention_keep, send = call(
         attention_grads_kernel,
         [((8, 64, 512), BF16), ((8, 64, 512), BF16)],
         [pltpu.VMEM((512, 512), BF16), pltpu.VMEM((384, 512), BF16)],
         scalars=1,
     )(lengths, normed, cot_own, *far_x)
-    send, gate_y = lax.optimization_barrier((send, gate_y))
+    attention_keep, gate_y = lax.optimization_barrier((attention_keep, gate_y))
     gate_keep, gate_send = call(gate_sum_kernel, [((112, 512), BF16, HBM)] * 2, scalars=1)(lengths, *gate_y)
     attention_keep, gate_send = lax.optimization_barrier((attention_keep, gate_send))
     (parts,) = call(add_kernel, [((8, 64, 512), BF16, HBM)])(attention_keep, other_core(send))

time: 121 us -> 131 us (1.083)
  waiting for transfers between devices: 26.4 us -> 34.5 us
  starting transfers between devices: 58.5 us -> 60.1 us
    ppermute x3, waiting for transfers between devices: 5.4 us -> 11.1 us  [turn_y(): lax.ppermute(pieces[by], 'y', [(i, (i + by) % 4) for i in range(4)])]
    ppermute x9, waiting for transfers between devices: 8.21 us -> 11.9 us  [turn_x(): lax.ppermute(pieces[by], 'x', [(i, (i + by) % 4) for i in range(4)])]
    ppermute x3, starting transfers between devices: 7.64 us -> 9.24 us  [turn_y(): lax.ppermute(pieces[by], 'y', [(i, (i + by) % 4) for i in range(4)])]
  transfers between devices with their start and end apart: 25 -> 25, of which waited for: 12 -> 12; matrix products, arithmetic and copies ran while one was open for 0% -> 0% of each run, Pallas kernels for 21% -> 20%
where the time goes in v8:
time: 131 us
  starting transfers between devices  60.1 us (46%)
  Pallas kernels  34.5 us (26%)
  waiting for transfers between devices  34.5 us (26%)
  between operations  1.57 us (1%)
    pallas_call x16, Pallas kernels, run(): pl.pallas_call(body, out_shape=[HBM(*out[:2]) if len(out) > 2 else jax.Sh...  34.5 us
    ppermute x6, starting transfers between devices, shift(): lax.ppermute(array, SEQ, [(i, i + by) for i in range(32) if 0 <= i + by <...  19.9 us
    ppermute x9, starting transfers between devices, turn_x(): lax.ppermute(pieces[by], 'x', [(i, (i + by) % 4) for i in range(4)])  13.4 us
    ppermute x9, waiting for transfers between devices, turn_x(): lax.ppermute(pieces[by], 'x', [(i, (i + by) % 4) for i in range(4)])  11.9 us
    ppermute x3, waiting for transfers between devices, turn_y(): lax.ppermute(pieces[by], 'y', [(i, (i + by) % 4) for i in range(4)])  11.1 us
    ppermute x3, starting transfers between devices, turn_z(): lax.ppermute(pieces[by], 'z_high', [(i, (i + by) % 4) for i in range(4)])  10.5 us
    ppermute x3, starting transfers between devices, turn_y(): lax.ppermute(pieces[by], 'y', [(i, (i + by) % 4) for i in range(4)])  9.24 us
    all_to_all x1, starting transfers between devices, local(): parts = lax.all_to_all(parts, ('z_low', 'y'), 0, 0)  5.4 us
  transfers between devices with their start and end apart: 25, of which 12 were waited for; matrix products, arithmetic and copies ran while one was open for 0% of the time, Pallas kernels for 20%

profile of v8, /device:TPU:8, one launch (start us, length us, event | category | flops | bytes accessed | tf_op | source)
XLA Modules:
  0.0 130.7 jit_solution(15737678886030082310)
XLA Ops:
  1.3 2.0 %shard_map.135 = (bf16[128,1408]{1,0:T(8,128)(2,1)S(1)}, bf16[128,1408]{1,0:T(8,128)(2,1)S(1)}, bf16[128,1408]{1,0:T(8,128)(2,1)S(1)}, bf16[128,1408]{1,0:T(8,128)(2,1)S(1)}) custom-call(s32[1]{0:T(128)S(6)} %copy.15.lengths, bf16[128,1024]{1,0:T(8,128)(2,1)} %bitcast.8, bf16[128,1024]{1,0:T(8,128)(2,1)} %bitcast.12, bf16[512,1024]{1,0:T(8,128)(2,1)} %w_out.3), custom_call_target="tpu_custom_call" | custom-call | tf_op jit(solution)/shard_map/pallas_call | solution.py:32
  3.3 1.6 %collective-permute-start = (bf16[128,1408]{1,0:T(8,128)(2,1)S(1)}, bf16[128,1408]{1,0:T(8,128)(2,1)S(1)}, u32[]{:S(2)}, u32[]{:S(2)}) collective-permute-start(bf16[128,1408]{1,0:T(8,128)(2,1)S(1)} %get-tuple-element.119), channel_id=1, source_target_pairs={{0,8},{8,16},{16,24},{24,0},{1,9},{9,17},{17,25},{25,1},{2,10},{10... | collective-permute-start | bytes 1081352 | tf_op jit(solution)/shard_map/ppermute | solution.py:521
  4.8 2.7 %collective-permute-start.1 = (bf16[128,1408]{1,0:T(8,128)(2,1)S(1)}, bf16[128,1408]{1,0:T(8,128)(2,1)S(1)}, u32[]{:S(2)}, u32[]{:S(2)}) collective-permute-start(bf16[128,1408]{1,0:T(8,128)(2,1)S(1)} %get-tuple-element.120), channel_id=1, source_target_pairs={{0,16},{8,24},{16,0},{24,8},{1,17},{9,25},{17,1},{25,9},{2,18},{10... | collective-permute-start | bytes 1081352 | tf_op jit(solution)/shard_map/ppermute | solution.py:521
  7.6 1.4 %collective-permute-start.2 = (bf16[128,1408]{1,0:T(8,128)(2,1)S(1)}, bf16[128,1408]{1,0:T(8,128)(2,1)S(1)}, u32[]{:S(2)}, u32[]{:S(2)}) collective-permute-start(bf16[128,1408]{1,0:T(8,128)(2,1)S(1)} %get-tuple-element.121), channel_id=1, source_target_pairs={{0,24},{8,0},{16,8},{24,16},{1,25},{9,1},{17,9},{25,17},{2,26},{10... | collective-permute-start | bytes 1081352 | tf_op jit(solution)/shard_map/ppermute | solution.py:521
  9.0 4.8 %shard_map.136 = (bf16[128,1024]{1,0:T(8,128)(2,1)S(1)}, bf16[128,1024]{1,0:T(8,128)(2,1)S(1)}, bf16[128,1024]{1,0:T(8,128)(2,1)S(1)}, bf16[128,1024]{1,0:T(8,12...) custom-call(s32[1]{0:T(128)S(6)} %copy.15.lengths, ...), custom_call_target="tpu_custom_call" | custom-call | tf_op jit(solution)/shard_map/pallas_call | solution.py:32
  13.8 2.5 %collective-permute-start.3 = (bf16[16,2048]{1,0:T(8,128)(2,1)S(1)}, bf16[16,2048]{1,0:T(8,128)(2,1)S(1)}, u32[]{:S(2)}, u32[]{:S(2)}) collective-permute-start(bf16[16,2048]{1,0:T(8,128)(2,1)S(1)} %get-tuple-element.126), channel_id=1, source_target_pairs={{0,8},{8,16},{16,24},{24,32},{32,40},{40,48},{48,56},{56,64},{64,7... | collective-permute-start | bytes 196616 | tf_op jit(solution)/shard_map/ppermute | solution.py:512
  16.3 5.4 %collective-permute-start.4 = (bf16[16,2048]{1,0:T(8,128)(2,1)S(1)}, bf16[16,2048]{1,0:T(8,128)(2,1)S(1)}, u32[]{:S(2)}, u32[]{:S(2)}) collective-permute-start(bf16[16,2048]{1,0:T(8,128)(2,1)S(1)} %get-tuple-element.127), channel_id=1, source_target_pairs={{8,0},{16,8},{24,16},{32,24},{40,32},{48,40},{56,48},{64,56},{72,6... | collective-permute-start | bytes 196616 | tf_op jit(solution)/shard_map/ppermute | solution.py:512
  21.8 3.6 %shard_map.137 = (f32[128,1024]{1,0:T(8,128)S(1)}, f32[128,1024]{1,0:T(8,128)S(1)}, f32[32,1024]{1,0:T(8,128)S(1)}) custom-call(bf16[128,1024]{1,0:T(8,128)(2,1)S(1)} %get-tuple-element.123.gating, bf16[128,1024]{1,0:T(8,128)(2,1)S(1)} %get-tuple-element.124.d_conv, f32[31,1024]{1,0:T(8,128)S(1)} %copy-done.7), custom_call_target="tpu_custom_call" | custom-call | tf_op jit(solution)/shard_map/pallas_call | solution.py:32
  25.5 1.3 shard_map.138
  26.8 3.7 %collective-permute-start.5 = (bf16[4,128,256]{2,1,0:T(8,128)(2,1)S(1)}, bf16[4,128,256]{2,1,0:T(8,128)(2,1)S(1)}, u32[]{:S(2)}, u32[]{:S(2)}) collective-permute-start(bf16[4,128,256]{2,1,0:T(8,128)(2,1)S(1)} %get-tuple-element.136.kv), channel_id=1, source_target_pairs={{0,32},{8,40},{16,48},{24,56},{32,64},{40,72},{48,80},{56,88},{64,... | collective-permute-start | bytes 786440 | tf_op jit(solution)/shard_map/ppermute | solution.py:512
  30.5 2.4 %collective-permute-start.6 = (bf16[4,128,256]{2,1,0:T(8,128)(2,1)S(1)}, bf16[4,128,256]{2,1,0:T(8,128)(2,1)S(1)}, u32[]{:S(2)}, u32[]{:S(2)}) collective-permute-start(bf16[4,128,256]{2,1,0:T(8,128)(2,1)S(1)} %get-tuple-element.136.kv), channel_id=1, source_target_pairs={{32,0},{40,8},{48,16},{56,24},{64,32},{72,40},{80,48},{88,56},{96,... | collective-permute-start | bytes 786440 | tf_op jit(solution)/shard_map/ppermute | solution.py:512
  32.9 2.2 %shard_map.139 = (bf16[128,2048]{1,0:T(8,128)(2,1)}, bf16[1600,128]{1,0:T(8,128)(2,1)S(1)}, bf16[1600,128]{1,0:T(8,128)(2,1)S(1)}, bf16[1600,128]{1,0:T(8,128)(2,1)S(1)}, bf16[1600,128]{1,0:T(8,128)(2,1)S(1)}) custom-call(s32[1]{0:T(128)S(6)} %copy.15.lengths, f32[128,1024]{1,0:T(8,128)S(1)} %get-tuple-element.137.conv_in, ...), custom_call_target="tpu_custom_call" | custom-call | tf_op jit(solution)/shard_map/pallas_call | solution.py:32
  35.1 1.4 %collective-permute-done.5.before = bf16[4,128,256]{2,1,0:T(8,128)(2,1)S(1)} collective-permute-done((bf16[4,128,256]{2,1,0:T(8,128)(2,1)S(1)}, bf16[4,128,256]{2,1,0:T(8,128)(2,1)S(1)}, u32[]{:S(2)}, u32[]{:S(2)}) %collective-permute-start.5) | collective-permute-done | bytes 262176 | tf_op jit(solution)/shard_map/ppermute | solution.py:512
  36.5 0.7 collective-permute-start.7
  37.2 3.3 %collective-permute-start.8 = (bf16[1600,128]{1,0:T(8,128)(2,1)S(1)}, bf16[1600,128]{1,0:T(8,128)(2,1)S(1)}, u32[]{:S(2)}, u32[]{:S(2)}) collective-permute-start(bf16[1600,128]{1,0:T(8,128)(2,1)S(1)} %get-tuple-element.156), channel_id=1, source_target_pairs={{0,16},{8,24},{16,0},{24,8},{1,17},{9,25},{17,1},{25,9},{2,18},{10... | collective-permute-start | bytes 1228808 | tf_op jit(solution)/shard_map/ppermute | solution.py:521
  40.6 6.0 %shard_map.140 = (bf16[4,128,128]{2,1,0:T(8,128)(2,1)S(1)}, bf16[128,512]{1,0:T(8,128)(2,1)S(1)}, bf16[4,128,256]{2,1,0:T(8,128)(2,1)S(1)}, bf16[4,128,256]{2,1,0:T(8,128)(2,1)S(1)}, f32[4,128,256]{2,1,0:T(8,128)S(1)}) custom-call(s32[1]{0:T(128)S(6)} %copy.15.lengths, bf16[4,128,128]{2,1,0:T(8,128)(2,1)S(1)} %get-tuple-element.133.queries, ...), custom_call_target="tpu_custom_call" | custom-call | tf_op jit(solution)/shard_map/pallas_call | solution.py:32
  46.5 3.7 %collective-permute-start.10 = (bf16[4,128,256]{2,1,0:T(8,128)(2,1)S(1)}, bf16[4,128,256]{2,1,0:T(8,128)(2,1)S(1)}, u32[]{:S(2)}, u32[]{:S(2)}) collective-permute-start(bf16[4,128,256]{2,1,0:T(8,128)(2,1)S(1)} %get-tuple-element.164), channel_id=1, source_target_pairs={{0,32},{8,40},{16,48},{24,56},{32,64},{40,72},{48,80},{56,88},{64,... | collective-permute-start | bytes 786440 | tf_op jit(solution)/shard_map/ppermute | solution.py:512
  50.3 2.2 %collective-permute-start.11 = (bf16[4,128,256]{2,1,0:T(8,128)(2,1)S(1)}, bf16[4,128,256]{2,1,0:T(8,128)(2,1)S(1)}, u32[]{:S(2)}, u32[]{:S(2)}) collective-permute-start(bf16[4,128,256]{2,1,0:T(8,128)(2,1)S(1)} %get-tuple-element.165), channel_id=1, source_target_pairs={{32,0},{40,8},{48,16},{56,24},{64,32},{72,40},{80,48},{88,56},{96,... | collective-permute-start | bytes 786440 | tf_op jit(solution)/shard_map/ppermute | solution.py:512
  52.4 3.7 %shard_map.141 = (f32[128,1024]{1,0:T(8,128)}, f32[128,1024]{1,0:T(8,128)}) custom-call(bf16[128,1024]{1,0:T(8,128)(2,1)} %bitcast.10, bf16[1600,128]{1,0:T(8,128)(2,1)S(1)} %get-tuple-element.174.gate.gate_0, bf16[128,2048]{1,0:T(8,128)(2,1)} %get-tuple-element.160.d_upper, bf16[1024,2048]{1,0:T(8,128)(2,1)S(1)} %copy-done, bf16[1024,1024]{1,0:T(8,128)(2,1)S(1)} %copy-done.2), custom_call_target="tpu_custom_call" | custom-call | tf_op jit(solution)/shard_map/pallas_call | solution.py:32
  56.2 0.5 collective-permute-done.8.gate_2
  56.8 3.2 %collective-permute-done.11.from_after = bf16[4,128,256]{2,1,0:T(8,128)(2,1)S(1)} collective-permute-done((bf16[4,128,256]{2,1,0:T(8,128)(2,1)S(1)}, bf16[4,128,256]{2,1,0:T(8,128)(2,1)S(1)}, u32[]{:S(2)}, u32[]{:S(2)}) %collective-permute-start.11) | collective-permute-done | bytes 262176 | tf_op jit(solution)/shard_map/ppermute | solution.py:512
  60.0 0.3 shard_map.142
  60.4 1.3 %shard_map.143 = (bf16[8,112,512]{2,1,0:T(8,128)(2,1)S(1)}, bf16[8,112,512]{2,1,0:T(8,128)(2,1)S(1)}, bf16[256,512]{1,0:T(8,128)(2,1)S(1)}) custom-call(s32[1]{0:T(128)S(6)} %copy.15.lengths, bf16[512,1024]{1,0:T(8,128)(2,1)S(1)} %get-tuple-element.132.normed, bf16[128,1408]{1,0:T(8,128)(2,1)S(1)} %get-tuple-element.128.frames_0.cot_0, ...), custom_call_target="tpu_custom_call" | custom-call | tf_op jit(solution)/shard_map/pallas_call | solution.py:32
  61.8 0.8 collective-permute-start.12
  62.6 2.0 %collective-permute-start.13 = (bf16[320,512]{1,0:T(8,128)(2,1)S(1)}, bf16[320,512]{1,0:T(8,128)(2,1)S(1)}, u32[]{:S(2)}, u32[]{:S(2)}) collective-permute-start(bf16[320,512]{1,0:T(8,128)(2,1)S(1)} %get-tuple-element.181), channel_id=1, source_target_pairs={{0,16},{8,24},{16,0},{24,8},{1,17},{9,25},{17,1},{25,9},{2,18},{10... | collective-permute-start | bytes 983048 | tf_op jit(solution)/shard_map/ppermute | solution.py:521
  64.6 0.7 collective-permute-start.14
  65.4 0.2 shard_map.144
  65.6 4.0 %collective-permute-start.16 = (bf16[2,112,512]{2,1,0:T(8,128)(2,1)S(1)}, bf16[2,112,512]{2,1,0:T(8,128)(2,1)S(1)}, u32[]{:S(2)}, u32[]{:S(2)}) collective-permute-start(bf16[2,112,512]{2,1,0:T(8,128)(2,1)S(1)} %get-tuple-element.185), channel_id=1, source_target_pairs={{0,32},{32,64},{64,96},{96,0},{1,33},{33,65},{65,97},{97,1},{2,34}... | collective-permute-start | bytes 688136 | tf_op jit(solution)/shard_map/ppermute | solution.py:527
  69.6 10.6 %collective-permute-done.12.far_1 = bf16[320,512]{1,0:T(8,128)(2,1)S(1)} collective-permute-done((bf16[320,512]{1,0:T(8,128)(2,1)S(1)}, bf16[320,512]{1,0:T(8,128)(2,1)S(1)}, u32[]{:S(2)}, u32[]{:S(2)}) %collective-permute-start.12) | collective-permute-done | bytes 327712 | tf_op jit(solution)/shard_map/ppermute | solution.py:521
  80.2 0.6 collective-permute-done.14.far_3
  80.8 1.1 shard_map.145
  82.0 5.3 %collective-permute-start.17 = (bf16[2,112,512]{2,1,0:T(8,128)(2,1)S(1)}, bf16[2,112,512]{2,1,0:T(8,128)(2,1)S(1)}, u32[]{:S(2)}, u32[]{:S(2)}) collective-permute-start(bf16[2,112,512]{2,1,0:T(8,128)(2,1)S(1)} %get-tuple-element.193), channel_id=1, source_target_pairs={{0,64},{32,96},{64,0},{96,32},{1,65},{33,97},{65,1},{97,33},{2,66}... | collective-permute-start | bytes 688136 | tf_op jit(solution)/shard_map/ppermute | solution.py:527
  87.3 6.5 %collective-permute-done.17.part_2 = bf16[2,112,512]{2,1,0:T(8,128)(2,1)S(1)} collective-permute-done((bf16[2,112,512]{2,1,0:T(8,128)(2,1)S(1)}, bf16[2,112,512]{2,1,0:T(8,128)(2,1)S(1)}, u32[]{:S(2)}, u32[]{:S(2)}) %collective-permute-start.17) | collective-permute-done | bytes 229408 | tf_op jit(solution)/shard_map/ppermute | solution.py:527
  93.8 4.6 %collective-permute-done.18.part_3 = bf16[2,112,512]{2,1,0:T(8,128)(2,1)S(1)} collective-permute-done((bf16[2,112,512]{2,1,0:T(8,128)(2,1)S(1)}, bf16[2,112,512]{2,1,0:T(8,128)(2,1)S(1)}, u32[]{:S(2)}, u32[]{:S(2)}) %collective-permute-start.18) | collective-permute-done | bytes 229408 | tf_op jit(solution)/shard_map/ppermute | solution.py:527
  98.4 0.8 shard_map.146
  99.1 0.9 shard_map.147
  100.1 5.4 %all-to-all-start = ((bf16[8,64,512]{2,1,0:T(8,128)(2,1)}), bf16[8,64,512]{2,1,0:T(8,128)(2,1)S(1)}, u32[]{:S(2)}, u32[]{:S(2)}) async-start(bf16[8,64,512]{2,1,0:T(8,128)(2,1)} %shard_map.147), calls=%async_computation | async-start | bytes 1048576 | tf_op jit(solution)/shard_map/all_to_all | solution.py:620
  105.5 1.5 %collective-permute-start.20 = (bf16[112,512]{1,0:T(8,128)(2,1)}, bf16[112,512]{1,0:T(8,128)(2,1)}, u32[]{:S(2)}, u32[]{:S(2)}) collective-permute-start(bf16[112,512]{1,0:T(8,128)(2,1)} %get-tuple-element.210), channel_id=1, source_target_pairs={{0,128},{128,0},{1,129},{129,1},{2,130},{130,2},{3,131},{131,3},{4... | collective-permute-start | bytes 344072 | tf_op jit(solution)/shard_map/ppermute | solution.py:621
  107.0 4.5 %shard_map.148 = (bf16[128,1024]{1,0:T(8,128)(2,1)}, bf16[128,1024]{1,0:T(8,128)(2,1)}) custom-call(s32[1]{0:T(128)S(6)} %copy.15.lengths, bf16[128,1024]{1,0:T(8,128)(2,1)S(1)} %bitcast.11, bf16[128,1024]{1,0:T(8,128)(2,1)S(1)} %bitcast.14, bf16[320,512]{1,0:T(8,128)(2,1)S(1)} %get-tuple-element.186.far_0, ...), custom_call_target="tpu_custom_call" | custom-call | tf_op jit(solution)/shard_map/pallas_call | solution.py:32
  111.4 2.6 %all-to-all-done.parts = bf16[8,64,512]{2,1,0:T(8,128)(2,1)S(1)} async-done(((bf16[8,64,512]{2,1,0:T(8,128)(2,1)}), bf16[8,64,512]{2,1,0:T(8,128)(2,1)S(1)}, u32[]{:S(2)}, u32[]{:S(2)}) %all-to-all-start) | async-done | bytes 524320 | tf_op jit(solution)/shard_map/all_to_all | solution.py:620
  114.1 1.3 %collective-permute-done.20.gate_far = bf16[112,512]{1,0:T(8,128)(2,1)} collective-permute-done((bf16[112,512]{1,0:T(8,128)(2,1)}, bf16[112,512]{1,0:T(8,128)(2,1)}, u32[]{:S(2)}, u32[]{:S(2)}) %collective-permute-start.20) | collective-permute-done | bytes 114720 | tf_op jit(solution)/shard_map/ppermute | solution.py:621
  115.4 1.0 shard_map.149
  116.4 3.3 %collective-permute-start.21 = (bf16[176,128]{1,0:T(8,128)(2,1)S(1)}, bf16[176,128]{1,0:T(8,128)(2,1)S(1)}, u32[]{:S(2)}, u32[]{:S(2)}) collective-permute-start(bf16[176,128]{1,0:T(8,128)(2,1)S(1)} %get-tuple-element.213), channel_id=1, source_target_pairs={{0,2},{2,4},{4,6},{6,0},{1,3},{3,5},{5,7},{7,1},{8,10},{10,12},{12... | collective-permute-start | bytes 135176 | tf_op jit(solution)/shard_map/ppermute | solution.py:533
  119.8 4.5 %collective-permute-start.22 = (bf16[176,128]{1,0:T(8,128)(2,1)S(1)}, bf16[176,128]{1,0:T(8,128)(2,1)S(1)}, u32[]{:S(2)}, u32[]{:S(2)}) collective-permute-start(bf16[176,128]{1,0:T(8,128)(2,1)S(1)} %get-tuple-element.214), channel_id=1, source_target_pairs={{0,4},{2,6},{4,0},{6,2},{1,5},{3,7},{5,1},{7,3},{8,12},{10,14},{12... | collective-permute-start | bytes 135176 | tf_op jit(solution)/shard_map/ppermute | solution.py:533
  124.2 2.7 %collective-permute-start.23 = (bf16[176,128]{1,0:T(8,128)(2,1)S(1)}, bf16[176,128]{1,0:T(8,128)(2,1)S(1)}, u32[]{:S(2)}, u32[]{:S(2)}) collective-permute-start(bf16[176,128]{1,0:T(8,128)(2,1)S(1)} %get-tuple-element.215), channel_id=1, source_target_pairs={{0,6},{2,0},{4,2},{6,4},{1,7},{3,1},{5,3},{7,5},{8,14},{10,8},{12,... | collective-permute-start | bytes 135176 | tf_op jit(solution)/shard_map/ppermute | solution.py:533
  126.9 1.0 collective-permute-done.22.part_2
  127.9 2.0 %collective-permute-done.23.part_3 = bf16[176,128]{1,0:T(8,128)(2,1)S(1)} collective-permute-done((bf16[176,128]{1,0:T(8,128)(2,1)S(1)}, bf16[176,128]{1,0:T(8,128)(2,1)S(1)}, u32[]{:S(2)}, u32[]{:S(2)}) %collective-permute-start.23) | collective-permute-done | bytes 45088 | tf_op jit(solution)/shard_map/ppermute | solution.py:533
  129.9 0.8 shard_map.150
  (36 shorter events, 0.6 us)
Async XLA Ops:
  3.2 18.5 %copy-start.7 = (f32[31,1024]{1,0:T(8,128)S(1)}, f32[31,1024]{1,0:T(8,128)}, u32[]{:S(2)}) copy-start(f32[31,1024]{1,0:T(8,128)} %taps.3) | copy-start | bytes 380932
  3.3 22.2 %copy-start.1 = (bf16[1024,1536]{1,0:T(8,128)(2,1)S(1)}, bf16[1024,1536]{1,0:T(8,128)(2,1)}, u32[]{:S(2)}) copy-start(bf16[1024,1536]{1,0:T(8,128)(2,1)} %w_qkv.3) | copy-start | bytes 9437188
  3.3 22.1 %collective-permute-start = (bf16[128,1408]{1,0:T(8,128)(2,1)S(1)}, bf16[128,1408]{1,0:T(8,128)(2,1)S(1)}, u32[]{:S(2)}, u32[]{:S(2)}) collective-permute-start(bf16[128,1408]{1,0:T(8,128)(2,1)S(1)} %get-tuple-element.119), channel_id=1, source_target_pairs={{0,8},{8,16},{16,24},{24,0},{1,9},{9,17},{17,25},{25,1},{2,10},{10... | collective-permute-start | bytes 1081352 | tf_op jit(solution)/shard_map/ppermute | solution.py:521
  4.8 20.6 %collective-permute-start.1 = (bf16[128,1408]{1,0:T(8,128)(2,1)S(1)}, bf16[128,1408]{1,0:T(8,128)(2,1)S(1)}, u32[]{:S(2)}, u32[]{:S(2)}) collective-permute-start(bf16[128,1408]{1,0:T(8,128)(2,1)S(1)} %get-tuple-element.120), channel_id=1, source_target_pairs={{0,16},{8,24},{16,0},{24,8},{1,17},{9,25},{17,1},{25,9},{2,18},{10... | collective-permute-start | bytes 1081352 | tf_op jit(solution)/shard_map/ppermute | solution.py:521
  7.6 17.9 %collective-permute-start.2 = (bf16[128,1408]{1,0:T(8,128)(2,1)S(1)}, bf16[128,1408]{1,0:T(8,128)(2,1)S(1)}, u32[]{:S(2)}, u32[]{:S(2)}) collective-permute-start(bf16[128,1408]{1,0:T(8,128)(2,1)S(1)} %get-tuple-element.121), channel_id=1, source_target_pairs={{0,24},{8,0},{16,8},{24,16},{1,25},{9,1},{17,9},{25,17},{2,26},{10... | collective-permute-start | bytes 1081352 | tf_op jit(solution)/shard_map/ppermute | solution.py:521
  13.8 11.6 %collective-permute-start.3 = (bf16[16,2048]{1,0:T(8,128)(2,1)S(1)}, bf16[16,2048]{1,0:T(8,128)(2,1)S(1)}, u32[]{:S(2)}, u32[]{:S(2)}) collective-permute-start(bf16[16,2048]{1,0:T(8,128)(2,1)S(1)} %get-tuple-element.126), channel_id=1, source_target_pairs={{0,8},{8,16},{16,24},{24,32},{32,40},{40,48},{48,56},{56,64},{64,7... | collective-permute-start | bytes 196616 | tf_op jit(solution)/shard_map/ppermute | solution.py:512
  16.3 9.1 %collective-permute-start.4 = (bf16[16,2048]{1,0:T(8,128)(2,1)S(1)}, bf16[16,2048]{1,0:T(8,128)(2,1)S(1)}, u32[]{:S(2)}, u32[]{:S(2)}) collective-permute-start(bf16[16,2048]{1,0:T(8,128)(2,1)S(1)} %get-tuple-element.127), channel_id=1, source_target_pairs={{8,0},{16,8},{24,16},{32,24},{40,32},{48,40},{56,48},{64,56},{72,6... | collective-permute-start | bytes 196616 | tf_op jit(solution)/shard_map/ppermute | solution.py:512
  25.4 27.0 %copy-start.2 = (bf16[1024,1024]{1,0:T(8,128)(2,1)S(1)}, bf16[1024,1024]{1,0:T(8,128)(2,1)}, u32[]{:S(2)}) copy-start(bf16[1024,1024]{1,0:T(8,128)(2,1)} %w_down.3) | copy-start | bytes 6291460
  26.8 25.7 %copy-start = (bf16[1024,2048]{1,0:T(8,128)(2,1)S(1)}, bf16[1024,2048]{1,0:T(8,128)(2,1)}, u32[]{:S(2)}) copy-start(bf16[1024,2048]{1,0:T(8,128)(2,1)} %w_up.3) | copy-start | bytes 12582916
  26.8 9.7 %collective-permute-start.5 = (bf16[4,128,256]{2,1,0:T(8,128)(2,1)S(1)}, bf16[4,128,256]{2,1,0:T(8,128)(2,1)S(1)}, u32[]{:S(2)}, u32[]{:S(2)}) collective-permute-start(bf16[4,128,256]{2,1,0:T(8,128)(2,1)S(1)} %get-tuple-element.136.kv), channel_id=1, source_target_pairs={{0,32},{8,40},{16,48},{24,56},{32,64},{40,72},{48,80},{56,88},{64,... | collective-permute-start | bytes 786440 | tf_op jit(solution)/shard_map/ppermute | solution.py:512
  30.5 10.0 %collective-permute-start.6 = (bf16[4,128,256]{2,1,0:T(8,128)(2,1)S(1)}, bf16[4,128,256]{2,1,0:T(8,128)(2,1)S(1)}, u32[]{:S(2)}, u32[]{:S(2)}) collective-permute-start(bf16[4,128,256]{2,1,0:T(8,128)(2,1)S(1)} %get-tuple-element.136.kv), channel_id=1, source_target_pairs={{32,0},{40,8},{48,16},{56,24},{64,32},{72,40},{80,48},{88,56},{96,... | collective-permute-start | bytes 786440 | tf_op jit(solution)/shard_map/ppermute | solution.py:512
  36.5 19.7 %collective-permute-start.7 = (bf16[1600,128]{1,0:T(8,128)(2,1)S(1)}, bf16[1600,128]{1,0:T(8,128)(2,1)S(1)}, u32[]{:S(2)}, u32[]{:S(2)}) collective-permute-start(bf16[1600,128]{1,0:T(8,128)(2,1)S(1)} %get-tuple-element.155), channel_id=1, source_target_pairs={{0,8},{8,16},{16,24},{24,0},{1,9},{9,17},{17,25},{25,1},{2,10},{10... | collective-permute-start | bytes 1228808 | tf_op jit(solution)/shard_map/ppermute | solution.py:521
  37.2 19.5 %collective-permute-start.8 = (bf16[1600,128]{1,0:T(8,128)(2,1)S(1)}, bf16[1600,128]{1,0:T(8,128)(2,1)S(1)}, u32[]{:S(2)}, u32[]{:S(2)}) collective-permute-start(bf16[1600,128]{1,0:T(8,128)(2,1)S(1)} %get-tuple-element.156), channel_id=1, source_target_pairs={{0,16},{8,24},{16,0},{24,8},{1,17},{9,25},{17,1},{25,9},{2,18},{10... | collective-permute-start | bytes 1228808 | tf_op jit(solution)/shard_map/ppermute | solution.py:521
  40.4 16.4 %collective-permute-start.9 = (bf16[1600,128]{1,0:T(8,128)(2,1)S(1)}, bf16[1600,128]{1,0:T(8,128)(2,1)S(1)}, u32[]{:S(2)}, u32[]{:S(2)}) collective-permute-start(bf16[1600,128]{1,0:T(8,128)(2,1)S(1)} %get-tuple-element.157), channel_id=1, source_target_pairs={{0,24},{8,0},{16,8},{24,16},{1,25},{9,1},{17,9},{25,17},{2,26},{10... | collective-permute-start | bytes 1228808 | tf_op jit(solution)/shard_map/ppermute | solution.py:521
  46.5 10.3 %collective-permute-start.10 = (bf16[4,128,256]{2,1,0:T(8,128)(2,1)S(1)}, bf16[4,128,256]{2,1,0:T(8,128)(2,1)S(1)}, u32[]{:S(2)}, u32[]{:S(2)}) collective-permute-start(bf16[4,128,256]{2,1,0:T(8,128)(2,1)S(1)} %get-tuple-element.164), channel_id=1, source_target_pairs={{0,32},{8,40},{16,48},{24,56},{32,64},{40,72},{48,80},{56,88},{64,... | collective-permute-start | bytes 786440 | tf_op jit(solution)/shard_map/ppermute | solution.py:512
  50.3 9.8 %collective-permute-start.11 = (bf16[4,128,256]{2,1,0:T(8,128)(2,1)S(1)}, bf16[4,128,256]{2,1,0:T(8,128)(2,1)S(1)}, u32[]{:S(2)}, u32[]{:S(2)}) collective-permute-start(bf16[4,128,256]{2,1,0:T(8,128)(2,1)S(1)} %get-tuple-element.165), channel_id=1, source_target_pairs={{32,0},{40,8},{48,16},{56,24},{64,32},{72,40},{80,48},{88,56},{96,... | collective-permute-start | bytes 786440 | tf_op jit(solution)/shard_map/ppermute | solution.py:512
  61.7 3.7 %collective-permute-start.15 = (bf16[8,112,512]{2,1,0:T(8,128)(2,1)S(1)}, bf16[8,112,512]{2,1,0:T(8,128)(2,1)S(1)}, u32[]{:S(2)}, u32[]{:S(2)}) collective-permute-start(bf16[8,112,512]{2,1,0:T(8,128)(2,1)S(1)} %get-tuple-element.184), channel_id=1, source_target_pairs={{0,1},{1,0},{2,3},{3,2},{4,5},{5,4},{6,7},{7,6},{8,9},{9,8},{10,11... | collective-permute-start | bytes 2752520 | tf_op jit(solution)/shard_map/ppermute | solution.py:516
  61.8 18.4 %collective-permute-start.12 = (bf16[320,512]{1,0:T(8,128)(2,1)S(1)}, bf16[320,512]{1,0:T(8,128)(2,1)S(1)}, u32[]{:S(2)}, u32[]{:S(2)}) collective-permute-start(bf16[320,512]{1,0:T(8,128)(2,1)S(1)} %get-tuple-element.180), channel_id=1, source_target_pairs={{0,8},{8,16},{16,24},{24,0},{1,9},{9,17},{17,25},{25,1},{2,10},{10... | collective-permute-start | bytes 983048 | tf_op jit(solution)/shard_map/ppermute | solution.py:521
  62.6 17.6 %collective-permute-start.13 = (bf16[320,512]{1,0:T(8,128)(2,1)S(1)}, bf16[320,512]{1,0:T(8,128)(2,1)S(1)}, u32[]{:S(2)}, u32[]{:S(2)}) collective-permute-start(bf16[320,512]{1,0:T(8,128)(2,1)S(1)} %get-tuple-element.181), channel_id=1, source_target_pairs={{0,16},{8,24},{16,0},{24,8},{1,17},{9,25},{17,1},{25,9},{2,18},{10... | collective-permute-start | bytes 983048 | tf_op jit(solution)/shard_map/ppermute | solution.py:521
  64.6 16.2 %collective-permute-start.14 = (bf16[320,512]{1,0:T(8,128)(2,1)S(1)}, bf16[320,512]{1,0:T(8,128)(2,1)S(1)}, u32[]{:S(2)}, u32[]{:S(2)}) collective-permute-start(bf16[320,512]{1,0:T(8,128)(2,1)S(1)} %get-tuple-element.182), channel_id=1, source_target_pairs={{0,24},{8,0},{16,8},{24,16},{1,25},{9,1},{17,9},{25,17},{2,26},{10... | collective-permute-start | bytes 983048 | tf_op jit(solution)/shard_map/ppermute | solution.py:521
  65.6 41.4 %copy-start.3 = (bf16[1,128,1024]{2,1,0:T(8,128)(2,1)S(1)}, bf16[1,128,1024]{2,1,0:T(8,128)(2,1)}, u32[]{:S(2)}) copy-start(bf16[1,128,1024]{2,1,0:T(8,128)(2,1)} %param.8) | copy-start | bytes 786436
  65.6 41.4 %copy-start.4 = (bf16[1,128,1024]{2,1,0:T(8,128)(2,1)S(1)}, bf16[1,128,1024]{2,1,0:T(8,128)(2,1)}, u32[]{:S(2)}) copy-start(bf16[1,128,1024]{2,1,0:T(8,128)(2,1)} %param.9) | copy-start | bytes 786436
  65.6 41.3 %copy-start.5 = (f32[128,1024]{1,0:T(8,128)S(1)}, f32[128,1024]{1,0:T(8,128)}, u32[]{:S(2)}) copy-start(f32[128,1024]{1,0:T(8,128)} %get-tuple-element.203.layer_part) | copy-start | bytes 1572868
  65.6 41.3 %copy-start.6 = (f32[128,1024]{1,0:T(8,128)S(1)}, f32[128,1024]{1,0:T(8,128)}, u32[]{:S(2)}) copy-start(f32[128,1024]{1,0:T(8,128)} %get-tuple-element.204.d_normed) | copy-start | bytes 1572868
  65.6 15.2 %collective-permute-start.16 = (bf16[2,112,512]{2,1,0:T(8,128)(2,1)S(1)}, bf16[2,112,512]{2,1,0:T(8,128)(2,1)S(1)}, u32[]{:S(2)}, u32[]{:S(2)}) collective-permute-start(bf16[2,112,512]{2,1,0:T(8,128)(2,1)S(1)} %get-tuple-element.185), channel_id=1, source_target_pairs={{0,32},{32,64},{64,96},{96,0},{1,33},{33,65},{65,97},{97,1},{2,34}... | collective-permute-start | bytes 688136 | tf_op jit(solution)/shard_map/ppermute | solution.py:527
  81.9 17.2 %collective-permute-start.19 = (bf16[8,64,512]{2,1,0:T(8,128)(2,1)S(1)}, bf16[8,64,512]{2,1,0:T(8,128)(2,1)S(1)}, u32[]{:S(2)}, u32[]{:S(2)}) collective-permute-start(bf16[8,64,512]{2,1,0:T(8,128)(2,1)S(1)} %get-tuple-element.202), channel_id=1, source_target_pairs={{0,1},{1,0},{2,3},{3,2},{4,5},{5,4},{6,7},{7,6},{8,9},{9,8},{10,11... | collective-permute-start | bytes 1572872 | tf_op jit(solution)/shard_map/ppermute | solution.py:516
  82.0 11.8 %collective-permute-start.17 = (bf16[2,112,512]{2,1,0:T(8,128)(2,1)S(1)}, bf16[2,112,512]{2,1,0:T(8,128)(2,1)S(1)}, u32[]{:S(2)}, u32[]{:S(2)}) collective-permute-start(bf16[2,112,512]{2,1,0:T(8,128)(2,1)S(1)} %get-tuple-element.193), channel_id=1, source_target_pairs={{0,64},{32,96},{64,0},{96,32},{1,65},{33,97},{65,1},{97,33},{2,66}... | collective-permute-start | bytes 688136 | tf_op jit(solution)/shard_map/ppermute | solution.py:527
  87.3 11.1 %collective-permute-start.18 = (bf16[2,112,512]{2,1,0:T(8,128)(2,1)S(1)}, bf16[2,112,512]{2,1,0:T(8,128)(2,1)S(1)}, u32[]{:S(2)}, u32[]{:S(2)}) collective-permute-start(bf16[2,112,512]{2,1,0:T(8,128)(2,1)S(1)} %get-tuple-element.194), channel_id=1, source_target_pairs={{0,96},{32,0},{64,32},{96,64},{1,97},{33,1},{65,33},{97,65},{2,98}... | collective-permute-start | bytes 688136 | tf_op jit(solution)/shard_map/ppermute | solution.py:527
  100.1 14.0 %all-to-all-start = ((bf16[8,64,512]{2,1,0:T(8,128)(2,1)}), bf16[8,64,512]{2,1,0:T(8,128)(2,1)S(1)}, u32[]{:S(2)}, u32[]{:S(2)}) async-start(bf16[8,64,512]{2,1,0:T(8,128)(2,1)} %shard_map.147), calls=%async_computation | async-start | bytes 1048576 | tf_op jit(solution)/shard_map/all_to_all | solution.py:620
  105.5 9.9 %collective-permute-start.20 = (bf16[112,512]{1,0:T(8,128)(2,1)}, bf16[112,512]{1,0:T(8,128)(2,1)}, u32[]{:S(2)}, u32[]{:S(2)}) collective-permute-start(bf16[112,512]{1,0:T(8,128)(2,1)} %get-tuple-element.210), channel_id=1, source_target_pairs={{0,128},{128,0},{1,129},{129,1},{2,130},{130,2},{3,131},{131,3},{4... | collective-permute-start | bytes 344072 | tf_op jit(solution)/shard_map/ppermute | solution.py:621
  106.9 8.5 %copy-start.8 = (bf16[112,512]{1,0:T(8,128)(2,1)S(1)}, bf16[112,512]{1,0:T(8,128)(2,1)}, u32[]{:S(2)}) copy-start(bf16[112,512]{1,0:T(8,128)(2,1)} %get-tuple-element.209.gate) | copy-start | bytes 344068
  116.4 10.5 %collective-permute-start.21 = (bf16[176,128]{1,0:T(8,128)(2,1)S(1)}, bf16[176,128]{1,0:T(8,128)(2,1)S(1)}, u32[]{:S(2)}, u32[]{:S(2)}) collective-permute-start(bf16[176,128]{1,0:T(8,128)(2,1)S(1)} %get-tuple-element.213), channel_id=1, source_target_pairs={{0,2},{2,4},{4,6},{6,0},{1,3},{3,5},{5,7},{7,1},{8,10},{10,12},{12... | collective-permute-start | bytes 135176 | tf_op jit(solution)/shard_map/ppermute | solution.py:533
  119.8 8.2 %collective-permute-start.22 = (bf16[176,128]{1,0:T(8,128)(2,1)S(1)}, bf16[176,128]{1,0:T(8,128)(2,1)S(1)}, u32[]{:S(2)}, u32[]{:S(2)}) collective-permute-start(bf16[176,128]{1,0:T(8,128)(2,1)S(1)} %get-tuple-element.214), channel_id=1, source_target_pairs={{0,4},{2,6},{4,0},{6,2},{1,5},{3,7},{5,1},{7,3},{8,12},{10,14},{12... | collective-permute-start | bytes 135176 | tf_op jit(solution)/shard_map/ppermute | solution.py:533
  124.2 5.7 %collective-permute-start.23 = (bf16[176,128]{1,0:T(8,128)(2,1)S(1)}, bf16[176,128]{1,0:T(8,128)(2,1)S(1)}, u32[]{:S(2)}, u32[]{:S(2)}) collective-permute-start(bf16[176,128]{1,0:T(8,128)(2,1)S(1)} %get-tuple-element.215), channel_id=1, source_target_pairs={{0,6},{2,0},{4,2},{6,4},{1,7},{3,1},{5,3},{7,5},{8,14},{10,8},{12,... | collective-permute-start | bytes 135176 | tf_op jit(solution)/shard_map/ppermute | solution.py:533

commit v9 on v8

--- a/solution.py
+++ b/solution.py
@@ -613,7 +613,7 @@
         [pltpu.VMEM((512, 512), BF16), pltpu.VMEM((384, 512), BF16)],
         scalars=1,
     )(lengths, normed, cot_own, *far_x)
-    attention_keep, gate_y = lax.optimization_barrier((attention_keep, gate_y))
+    send, gate_y = lax.optimization_barrier((send, gate_y))
     gate_keep, gate_send = call(gate_sum_kernel, [((112, 512), BF16, HBM)] * 2, scalars=1)(lengths, *gate_y)
     attention_keep, gate_send = lax.optimization_barrier((attention_keep, gate_send))
     (parts,) = call(add_kernel, [((8, 64, 512), BF16, HBM)])(attention_keep, other_core(send))

time: 131 us -> 120 us (0.916)
  waiting for transfers between devices: 34.5 us -> 25.3 us
  starting transfers between devices: 60.1 us -> 58.4 us
    ppermute x3, waiting for transfers between devices: 11.1 us -> 4.25 us  [turn_y(): lax.ppermute(pieces[by], 'y', [(i, (i + by) % 4) for i in range(4)])]
    ppermute x9, waiting for transfers between devices: 11.9 us -> 8.21 us  [turn_x(): lax.ppermute(pieces[by], 'x', [(i, (i + by) % 4) for i in range(4)])]
    ppermute x3, starting transfers between devices: 9.24 us -> 7.64 us  [turn_y(): lax.ppermute(pieces[by], 'y', [(i, (i + by) % 4) for i in range(4)])]
  transfers between devices with their start and end apart: 25 -> 25, of which waited for: 12 -> 12; matrix products, arithmetic and copies ran while one was open for 0% -> 0% of each run, Pallas kernels for 20% -> 22%
where the time goes in v9:
time: 120 us
  starting transfers between devices  58.4 us (49%)
  Pallas kernels  34.5 us (29%)
  waiting for transfers between devices  25.3 us (21%)
  between operations  1.57 us (1%)
    pallas_call x16, Pallas kernels, run(): pl.pallas_call(body, out_shape=[HBM(*out[:2]) if len(out) > 2 else jax.Sh...  34.5 us
    ppermute x6, starting transfers between devices, shift(): lax.ppermute(array, SEQ, [(i, i + by) for i in range(32) if 0 <= i + by <...  19.9 us
    ppermute x9, starting transfers between devices, turn_x(): lax.ppermute(pieces[by], 'x', [(i, (i + by) % 4) for i in range(4)])  13.4 us
    ppermute x3, starting transfers between devices, turn_z(): lax.ppermute(pieces[by], 'z_high', [(i, (i + by) % 4) for i in range(4)])  10.5 us
    ppermute x9, waiting for transfers between devices, turn_x(): lax.ppermute(pieces[by], 'x', [(i, (i + by) % 4) for i in range(4)])  8.21 us
    ppermute x3, starting transfers between devices, turn_y(): lax.ppermute(pieces[by], 'y', [(i, (i + by) % 4) for i in range(4)])  7.64 us
    all_to_all x1, starting transfers between devices, local(): parts = lax.all_to_all(parts, ('z_low', 'y'), 0, 0)  5.36 us
    ppermute x6, waiting for transfers between devices, shift(): lax.ppermute(array, SEQ, [(i, i + by) for i in range(32) if 0 <= i + by <...  4.55 us
  transfers between devices with their start and end apart: 25, of which 12 were waited for; matrix products, arithmetic and copies ran while one was open for 0% of the time, Pallas kernels for 22%

profile of v9, /device:TPU:8, one launch (start us, length us, event | category | flops | bytes accessed | tf_op | source)
XLA Modules:
  0.0 119.8 jit_solution(16544600373623586374)
XLA Ops:
  1.3 2.0 %shard_map.135 = (bf16[128,1408]{1,0:T(8,128)(2,1)S(1)}, bf16[128,1408]{1,0:T(8,128)(2,1)S(1)}, bf16[128,1408]{1,0:T(8,128)(2,1)S(1)}, bf16[128,1408]{1,0:T(8,128)(2,1)S(1)}) custom-call(s32[1]{0:T(128)S(6)} %copy.15.lengths, bf16[128,1024]{1,0:T(8,128)(2,1)} %bitcast.8, bf16[128,1024]{1,0:T(8,128)(2,1)} %bitcast.12, bf16[512,1024]{1,0:T(8,128)(2,1)} %w_out.3), custom_call_target="tpu_custom_call" | custom-call | tf_op jit(solution)/shard_map/pallas_call | solution.py:32
  3.3 1.6 %collective-permute-start = (bf16[128,1408]{1,0:T(8,128)(2,1)S(1)}, bf16[128,1408]{1,0:T(8,128)(2,1)S(1)}, u32[]{:S(2)}, u32[]{:S(2)}) collective-permute-start(bf16[128,1408]{1,0:T(8,128)(2,1)S(1)} %get-tuple-element.119), channel_id=1, source_target_pairs={{0,8},{8,16},{16,24},{24,0},{1,9},{9,17},{17,25},{25,1},{2,10},{10... | collective-permute-start | bytes 1081352 | tf_op jit(solution)/shard_map/ppermute | solution.py:521
  4.8 2.7 %collective-permute-start.1 = (bf16[128,1408]{1,0:T(8,128)(2,1)S(1)}, bf16[128,1408]{1,0:T(8,128)(2,1)S(1)}, u32[]{:S(2)}, u32[]{:S(2)}) collective-permute-start(bf16[128,1408]{1,0:T(8,128)(2,1)S(1)} %get-tuple-element.120), channel_id=1, source_target_pairs={{0,16},{8,24},{16,0},{24,8},{1,17},{9,25},{17,1},{25,9},{2,18},{10... | collective-permute-start | bytes 1081352 | tf_op jit(solution)/shard_map/ppermute | solution.py:521
  7.6 1.4 %collective-permute-start.2 = (bf16[128,1408]{1,0:T(8,128)(2,1)S(1)}, bf16[128,1408]{1,0:T(8,128)(2,1)S(1)}, u32[]{:S(2)}, u32[]{:S(2)}) collective-permute-start(bf16[128,1408]{1,0:T(8,128)(2,1)S(1)} %get-tuple-element.121), channel_id=1, source_target_pairs={{0,24},{8,0},{16,8},{24,16},{1,25},{9,1},{17,9},{25,17},{2,26},{10... | collective-permute-start | bytes 1081352 | tf_op jit(solution)/shard_map/ppermute | solution.py:521
  9.0 4.8 %shard_map.136 = (bf16[128,1024]{1,0:T(8,128)(2,1)S(1)}, bf16[128,1024]{1,0:T(8,128)(2,1)S(1)}, bf16[128,1024]{1,0:T(8,128)(2,1)S(1)}, bf16[128,1024]{1,0:T(8,12...) custom-call(s32[1]{0:T(128)S(6)} %copy.15.lengths, ...), custom_call_target="tpu_custom_call" | custom-call | tf_op jit(solution)/shard_map/pallas_call | solution.py:32
  13.8 2.5 %collective-permute-start.3 = (bf16[16,2048]{1,0:T(8,128)(2,1)S(1)}, bf16[16,2048]{1,0:T(8,128)(2,1)S(1)}, u32[]{:S(2)}, u32[]{:S(2)}) collective-permute-start(bf16[16,2048]{1,0:T(8,128)(2,1)S(1)} %get-tuple-element.126), channel_id=1, source_target_pairs={{0,8},{8,16},{16,24},{24,32},{32,40},{40,48},{48,56},{56,64},{64,7... | collective-permute-start | bytes 196616 | tf_op jit(solution)/shard_map/ppermute | solution.py:512
  16.3 5.4 %collective-permute-start.4 = (bf16[16,2048]{1,0:T(8,128)(2,1)S(1)}, bf16[16,2048]{1,0:T(8,128)(2,1)S(1)}, u32[]{:S(2)}, u32[]{:S(2)}) collective-permute-start(bf16[16,2048]{1,0:T(8,128)(2,1)S(1)} %get-tuple-element.127), channel_id=1, source_target_pairs={{8,0},{16,8},{24,16},{32,24},{40,32},{48,40},{56,48},{64,56},{72,6... | collective-permute-start | bytes 196616 | tf_op jit(solution)/shard_map/ppermute | solution.py:512
  21.8 3.6 %shard_map.137 = (f32[128,1024]{1,0:T(8,128)S(1)}, f32[128,1024]{1,0:T(8,128)S(1)}, f32[32,1024]{1,0:T(8,128)S(1)}) custom-call(bf16[128,1024]{1,0:T(8,128)(2,1)S(1)} %get-tuple-element.123.gating, bf16[128,1024]{1,0:T(8,128)(2,1)S(1)} %get-tuple-element.124.d_conv, f32[31,1024]{1,0:T(8,128)S(1)} %copy-done.7), custom_call_target="tpu_custom_call" | custom-call | tf_op jit(solution)/shard_map/pallas_call | solution.py:32
  25.5 1.3 %shard_map.138 = (bf16[512,1024]{1,0:T(8,128)(2,1)S(1)}, bf16[4,128,128]{2,1,0:T(8,128)(2,1)S(1)}, bf16[4,128,256]{2,1,0:T(8,128)(2,1)S(1)}) custom-call(s32[1]{0:T(128)S(6)} %copy.15.lengths, bf16[128,1408]{1,0:T(8,128)(2,1)S(1)} %get-tuple-element.128.frames_0.cot_0, bf16[128,1408]{1,0:T(8,128)(2,1)S(1)} %collective-permute-done.frames_1.cot_1, ...), custom_call_target="tpu_custom_call" | custom-call | tf_op jit(solution)/shard_map/pallas_call | solution.py:32
  26.8 3.7 %collective-permute-start.5 = (bf16[4,128,256]{2,1,0:T(8,128)(2,1)S(1)}, bf16[4,128,256]{2,1,0:T(8,128)(2,1)S(1)}, u32[]{:S(2)}, u32[]{:S(2)}) collective-permute-start(bf16[4,128,256]{2,1,0:T(8,128)(2,1)S(1)} %get-tuple-element.136.kv), channel_id=1, source_target_pairs={{0,32},{8,40},{16,48},{24,56},{32,64},{40,72},{48,80},{56,88},{64,... | collective-permute-start | bytes 786440 | tf_op jit(solution)/shard_map/ppermute | solution.py:512
  30.5 2.4 %collective-permute-start.6 = (bf16[4,128,256]{2,1,0:T(8,128)(2,1)S(1)}, bf16[4,128,256]{2,1,0:T(8,128)(2,1)S(1)}, u32[]{:S(2)}, u32[]{:S(2)}) collective-permute-start(bf16[4,128,256]{2,1,0:T(8,128)(2,1)S(1)} %get-tuple-element.136.kv), channel_id=1, source_target_pairs={{32,0},{40,8},{48,16},{56,24},{64,32},{72,40},{80,48},{88,56},{96,... | collective-permute-start | bytes 786440 | tf_op jit(solution)/shard_map/ppermute | solution.py:512
  32.9 2.2 %shard_map.139 = (bf16[128,2048]{1,0:T(8,128)(2,1)}, bf16[1600,128]{1,0:T(8,128)(2,1)S(1)}, bf16[1600,128]{1,0:T(8,128)(2,1)S(1)}, bf16[1600,128]{1,0:T(8,128)(2,1)S(1)}, bf16[1600,128]{1,0:T(8,128)(2,1)S(1)}) custom-call(s32[1]{0:T(128)S(6)} %copy.15.lengths, f32[128,1024]{1,0:T(8,128)S(1)} %get-tuple-element.137.conv_in, ...), custom_call_target="tpu_custom_call" | custom-call | tf_op jit(solution)/shard_map/pallas_call | solution.py:32
  35.1 1.4 %collective-permute-done.5.before = bf16[4,128,256]{2,1,0:T(8,128)(2,1)S(1)} collective-permute-done((bf16[4,128,256]{2,1,0:T(8,128)(2,1)S(1)}, bf16[4,128,256]{2,1,0:T(8,128)(2,1)S(1)}, u32[]{:S(2)}, u32[]{:S(2)}) %collective-permute-start.5) | collective-permute-done | bytes 262176 | tf_op jit(solution)/shard_map/ppermute | solution.py:512
  36.5 0.7 collective-permute-start.7
  37.2 3.3 %collective-permute-start.8 = (bf16[1600,128]{1,0:T(8,128)(2,1)S(1)}, bf16[1600,128]{1,0:T(8,128)(2,1)S(1)}, u32[]{:S(2)}, u32[]{:S(2)}) collective-permute-start(bf16[1600,128]{1,0:T(8,128)(2,1)S(1)} %get-tuple-element.156), channel_id=1, source_target_pairs={{0,16},{8,24},{16,0},{24,8},{1,17},{9,25},{17,1},{25,9},{2,18},{10... | collective-permute-start | bytes 1228808 | tf_op jit(solution)/shard_map/ppermute | solution.py:521
  40.6 6.0 %shard_map.140 = (bf16[4,128,128]{2,1,0:T(8,128)(2,1)S(1)}, bf16[128,512]{1,0:T(8,128)(2,1)S(1)}, bf16[4,128,256]{2,1,0:T(8,128)(2,1)S(1)}, bf16[4,128,256]{2,1,0:T(8,128)(2,1)S(1)}, f32[4,128,256]{2,1,0:T(8,128)S(1)}) custom-call(s32[1]{0:T(128)S(6)} %copy.15.lengths, bf16[4,128,128]{2,1,0:T(8,128)(2,1)S(1)} %get-tuple-element.133.queries, ...), custom_call_target="tpu_custom_call" | custom-call | tf_op jit(solution)/shard_map/pallas_call | solution.py:32
  46.5 3.7 %collective-permute-start.10 = (bf16[4,128,256]{2,1,0:T(8,128)(2,1)S(1)}, bf16[4,128,256]{2,1,0:T(8,128)(2,1)S(1)}, u32[]{:S(2)}, u32[]{:S(2)}) collective-permute-start(bf16[4,128,256]{2,1,0:T(8,128)(2,1)S(1)} %get-tuple-element.164), channel_id=1, source_target_pairs={{0,32},{8,40},{16,48},{24,56},{32,64},{40,72},{48,80},{56,88},{64,... | collective-permute-start | bytes 786440 | tf_op jit(solution)/shard_map/ppermute | solution.py:512
  50.3 2.2 %collective-permute-start.11 = (bf16[4,128,256]{2,1,0:T(8,128)(2,1)S(1)}, bf16[4,128,256]{2,1,0:T(8,128)(2,1)S(1)}, u32[]{:S(2)}, u32[]{:S(2)}) collective-permute-start(bf16[4,128,256]{2,1,0:T(8,128)(2,1)S(1)} %get-tuple-element.165), channel_id=1, source_target_pairs={{32,0},{40,8},{48,16},{56,24},{64,32},{72,40},{80,48},{88,56},{96,... | collective-permute-start | bytes 786440 | tf_op jit(solution)/shard_map/ppermute | solution.py:512
  52.4 3.7 %shard_map.141 = (f32[128,1024]{1,0:T(8,128)}, f32[128,1024]{1,0:T(8,128)}) custom-call(bf16[128,1024]{1,0:T(8,128)(2,1)} %bitcast.10, bf16[1600,128]{1,0:T(8,128)(2,1)S(1)} %get-tuple-element.174.gate.gate_0, bf16[128,2048]{1,0:T(8,128)(2,1)} %get-tuple-element.160.d_upper, bf16[1024,2048]{1,0:T(8,128)(2,1)S(1)} %copy-done, bf16[1024,1024]{1,0:T(8,128)(2,1)S(1)} %copy-done.2), custom_call_target="tpu_custom_call" | custom-call | tf_op jit(solution)/shard_map/pallas_call | solution.py:32
  56.2 0.5 collective-permute-done.8.gate_2
  56.8 3.2 %collective-permute-done.11.from_after = bf16[4,128,256]{2,1,0:T(8,128)(2,1)S(1)} collective-permute-done((bf16[4,128,256]{2,1,0:T(8,128)(2,1)S(1)}, bf16[4,128,256]{2,1,0:T(8,128)(2,1)S(1)}, u32[]{:S(2)}, u32[]{:S(2)}) %collective-permute-start.11) | collective-permute-done | bytes 262176 | tf_op jit(solution)/shard_map/ppermute | solution.py:512
  60.0 0.3 shard_map.142
  60.4 1.3 %shard_map.143 = (bf16[8,112,512]{2,1,0:T(8,128)(2,1)S(1)}, bf16[8,112,512]{2,1,0:T(8,128)(2,1)S(1)}, bf16[256,512]{1,0:T(8,128)(2,1)S(1)}) custom-call(s32[1]{0:T(128)S(6)} %copy.15.lengths, bf16[512,1024]{1,0:T(8,128)(2,1)S(1)} %get-tuple-element.132.normed, bf16[128,1408]{1,0:T(8,128)(2,1)S(1)} %get-tuple-element.128.frames_0.cot_0, ...), custom_call_target="tpu_custom_call" | custom-call | tf_op jit(solution)/shard_map/pallas_call | solution.py:32
  61.8 0.8 collective-permute-start.12
  62.6 2.0 %collective-permute-start.13 = (bf16[320,512]{1,0:T(8,128)(2,1)S(1)}, bf16[320,512]{1,0:T(8,128)(2,1)S(1)}, u32[]{:S(2)}, u32[]{:S(2)}) collective-permute-start(bf16[320,512]{1,0:T(8,128)(2,1)S(1)} %get-tuple-element.181), channel_id=1, source_target_pairs={{0,16},{8,24},{16,0},{24,8},{1,17},{9,25},{17,1},{25,9},{2,18},{10... | collective-permute-start | bytes 983048 | tf_op jit(solution)/shard_map/ppermute | solution.py:521
  64.6 0.7 collective-permute-start.14
  65.4 0.2 shard_map.144
  65.6 3.8 %collective-permute-start.16 = (bf16[2,112,512]{2,1,0:T(8,128)(2,1)S(1)}, bf16[2,112,512]{2,1,0:T(8,128)(2,1)S(1)}, u32[]{:S(2)}, u32[]{:S(2)}) collective-permute-start(bf16[2,112,512]{2,1,0:T(8,128)(2,1)S(1)} %get-tuple-element.185), channel_id=1, source_target_pairs={{0,32},{32,64},{64,96},{96,0},{1,33},{33,65},{65,97},{97,1},{2,34}... | collective-permute-start | bytes 688136 | tf_op jit(solution)/shard_map/ppermute | solution.py:527
  69.4 3.9 %collective-permute-start.17 = (bf16[2,112,512]{2,1,0:T(8,128)(2,1)S(1)}, bf16[2,112,512]{2,1,0:T(8,128)(2,1)S(1)}, u32[]{:S(2)}, u32[]{:S(2)}) collective-permute-start(bf16[2,112,512]{2,1,0:T(8,128)(2,1)S(1)} %get-tuple-element.194), channel_id=1, source_target_pairs={{0,64},{32,96},{64,0},{96,32},{1,65},{33,97},{65,1},{97,33},{2,66}... | collective-permute-start | bytes 688136 | tf_op jit(solution)/shard_map/ppermute | solution.py:527
  73.3 6.9 %collective-permute-done.12.far_1 = bf16[320,512]{1,0:T(8,128)(2,1)S(1)} collective-permute-done((bf16[320,512]{1,0:T(8,128)(2,1)S(1)}, bf16[320,512]{1,0:T(8,128)(2,1)S(1)}, u32[]{:S(2)}, u32[]{:S(2)}) %collective-permute-start.12) | collective-permute-done | bytes 327712 | tf_op jit(solution)/shard_map/ppermute | solution.py:521
  80.2 0.6 collective-permute-done.14.far_3
  80.8 1.1 shard_map.145
  81.9 4.2 %collective-permute-done.18.part_3 = bf16[2,112,512]{2,1,0:T(8,128)(2,1)S(1)} collective-permute-done((bf16[2,112,512]{2,1,0:T(8,128)(2,1)S(1)}, bf16[2,112,512]{2,1,0:T(8,128)(2,1)S(1)}, u32[]{:S(2)}, u32[]{:S(2)}) %collective-permute-start.18) | collective-permute-done | bytes 229408 | tf_op jit(solution)/shard_map/ppermute | solution.py:527
  86.2 0.8 shard_map.146
  86.9 1.1 collective-permute-done.19.far
  88.1 0.9 shard_map.147
  89.0 5.4 %all-to-all-start = ((bf16[8,64,512]{2,1,0:T(8,128)(2,1)}), bf16[8,64,512]{2,1,0:T(8,128)(2,1)S(1)}, u32[]{:S(2)}, u32[]{:S(2)}) async-start(bf16[8,64,512]{2,1,0:T(8,128)(2,1)} %shard_map.147), calls=%async_computation | async-start | bytes 1048576 | tf_op jit(solution)/shard_map/all_to_all | solution.py:620
  94.4 1.5 %collective-permute-start.20 = (bf16[112,512]{1,0:T(8,128)(2,1)}, bf16[112,512]{1,0:T(8,128)(2,1)}, u32[]{:S(2)}, u32[]{:S(2)}) collective-permute-start(bf16[112,512]{1,0:T(8,128)(2,1)} %get-tuple-element.210), channel_id=1, source_target_pairs={{0,128},{128,0},{1,129},{129,1},{2,130},{130,2},{3,131},{131,3},{4... | collective-permute-start | bytes 344072 | tf_op jit(solution)/shard_map/ppermute | solution.py:621
  95.9 4.5 %shard_map.148 = (bf16[128,1024]{1,0:T(8,128)(2,1)}, bf16[128,1024]{1,0:T(8,128)(2,1)}) custom-call(s32[1]{0:T(128)S(6)} %copy.15.lengths, bf16[128,1024]{1,0:T(8,128)(2,1)S(1)} %bitcast.11, bf16[128,1024]{1,0:T(8,128)(2,1)S(1)} %bitcast.14, bf16[320,512]{1,0:T(8,128)(2,1)S(1)} %get-tuple-element.186.far_0, ...), custom_call_target="tpu_custom_call" | custom-call | tf_op jit(solution)/shard_map/pallas_call | solution.py:32
  100.3 2.9 %all-to-all-done.parts = bf16[8,64,512]{2,1,0:T(8,128)(2,1)S(1)} async-done(((bf16[8,64,512]{2,1,0:T(8,128)(2,1)}), bf16[8,64,512]{2,1,0:T(8,128)(2,1)S(1)}, u32[]{:S(2)}, u32[]{:S(2)}) %all-to-all-start) | async-done | bytes 524320 | tf_op jit(solution)/shard_map/all_to_all | solution.py:620
  103.2 1.5 %collective-permute-done.20.gate_far = bf16[112,512]{1,0:T(8,128)(2,1)} collective-permute-done((bf16[112,512]{1,0:T(8,128)(2,1)}, bf16[112,512]{1,0:T(8,128)(2,1)}, u32[]{:S(2)}, u32[]{:S(2)}) %collective-permute-start.20) | collective-permute-done | bytes 114720 | tf_op jit(solution)/shard_map/ppermute | solution.py:621
  104.7 1.0 shard_map.149
  105.7 3.3 %collective-permute-start.21 = (bf16[176,128]{1,0:T(8,128)(2,1)S(1)}, bf16[176,128]{1,0:T(8,128)(2,1)S(1)}, u32[]{:S(2)}, u32[]{:S(2)}) collective-permute-start(bf16[176,128]{1,0:T(8,128)(2,1)S(1)} %get-tuple-element.213), channel_id=1, source_target_pairs={{0,2},{2,4},{4,6},{6,0},{1,3},{3,5},{5,7},{7,1},{8,10},{10,12},{12... | collective-permute-start | bytes 135176 | tf_op jit(solution)/shard_map/ppermute | solution.py:533
  109.1 4.5 %collective-permute-start.22 = (bf16[176,128]{1,0:T(8,128)(2,1)S(1)}, bf16[176,128]{1,0:T(8,128)(2,1)S(1)}, u32[]{:S(2)}, u32[]{:S(2)}) collective-permute-start(bf16[176,128]{1,0:T(8,128)(2,1)S(1)} %get-tuple-element.214), channel_id=1, source_target_pairs={{0,4},{2,6},{4,0},{6,2},{1,5},{3,7},{5,1},{7,3},{8,12},{10,14},{12... | collective-permute-start | bytes 135176 | tf_op jit(solution)/shard_map/ppermute | solution.py:533
  113.6 2.7 %collective-permute-start.23 = (bf16[176,128]{1,0:T(8,128)(2,1)S(1)}, bf16[176,128]{1,0:T(8,128)(2,1)S(1)}, u32[]{:S(2)}, u32[]{:S(2)}) collective-permute-start(bf16[176,128]{1,0:T(8,128)(2,1)S(1)} %get-tuple-element.215), channel_id=1, source_target_pairs={{0,6},{2,0},{4,2},{6,4},{1,7},{3,1},{5,3},{7,5},{8,14},{10,8},{12,... | collective-permute-start | bytes 135176 | tf_op jit(solution)/shard_map/ppermute | solution.py:533
  116.2 1.5 %collective-permute-done.22.part_2 = bf16[176,128]{1,0:T(8,128)(2,1)S(1)} collective-permute-done((bf16[176,128]{1,0:T(8,128)(2,1)S(1)}, bf16[176,128]{1,0:T(8,128)(2,1)S(1)}, u32[]{:S(2)}, u32[]{:S(2)}) %collective-permute-start.22) | collective-permute-done | bytes 45088 | tf_op jit(solution)/shard_map/ppermute | solution.py:533
  117.7 1.3 %collective-permute-done.23.part_3 = bf16[176,128]{1,0:T(8,128)(2,1)S(1)} collective-permute-done((bf16[176,128]{1,0:T(8,128)(2,1)S(1)}, bf16[176,128]{1,0:T(8,128)(2,1)S(1)}, u32[]{:S(2)}, u32[]{:S(2)}) %collective-permute-start.23) | collective-permute-done | bytes 45088 | tf_op jit(solution)/shard_map/ppermute | solution.py:533
  119.0 0.8 shard_map.150
  (36 shorter events, 0.5 us)
Async XLA Ops:
  3.2 18.5 %copy-start.7 = (f32[31,1024]{1,0:T(8,128)S(1)}, f32[31,1024]{1,0:T(8,128)}, u32[]{:S(2)}) copy-start(f32[31,1024]{1,0:T(8,128)} %taps.3) | copy-start | bytes 380932
  3.3 22.2 %copy-start.1 = (bf16[1024,1536]{1,0:T(8,128)(2,1)S(1)}, bf16[1024,1536]{1,0:T(8,128)(2,1)}, u32[]{:S(2)}) copy-start(bf16[1024,1536]{1,0:T(8,128)(2,1)} %w_qkv.3) | copy-start | bytes 9437188
  3.3 22.1 %collective-permute-start = (bf16[128,1408]{1,0:T(8,128)(2,1)S(1)}, bf16[128,1408]{1,0:T(8,128)(2,1)S(1)}, u32[]{:S(2)}, u32[]{:S(2)}) collective-permute-start(bf16[128,1408]{1,0:T(8,128)(2,1)S(1)} %get-tuple-element.119), channel_id=1, source_target_pairs={{0,8},{8,16},{16,24},{24,0},{1,9},{9,17},{17,25},{25,1},{2,10},{10... | collective-permute-start | bytes 1081352 | tf_op jit(solution)/shard_map/ppermute | solution.py:521
  4.8 20.6 %collective-permute-start.1 = (bf16[128,1408]{1,0:T(8,128)(2,1)S(1)}, bf16[128,1408]{1,0:T(8,128)(2,1)S(1)}, u32[]{:S(2)}, u32[]{:S(2)}) collective-permute-start(bf16[128,1408]{1,0:T(8,128)(2,1)S(1)} %get-tuple-element.120), channel_id=1, source_target_pairs={{0,16},{8,24},{16,0},{24,8},{1,17},{9,25},{17,1},{25,9},{2,18},{10... | collective-permute-start | bytes 1081352 | tf_op jit(solution)/shard_map/ppermute | solution.py:521
  7.6 17.9 %collective-permute-start.2 = (bf16[128,1408]{1,0:T(8,128)(2,1)S(1)}, bf16[128,1408]{1,0:T(8,128)(2,1)S(1)}, u32[]{:S(2)}, u32[]{:S(2)}) collective-permute-start(bf16[128,1408]{1,0:T(8,128)(2,1)S(1)} %get-tuple-element.121), channel_id=1, source_target_pairs={{0,24},{8,0},{16,8},{24,16},{1,25},{9,1},{17,9},{25,17},{2,26},{10... | collective-permute-start | bytes 1081352 | tf_op jit(solution)/shard_map/ppermute | solution.py:521
  13.8 11.6 %collective-permute-start.3 = (bf16[16,2048]{1,0:T(8,128)(2,1)S(1)}, bf16[16,2048]{1,0:T(8,128)(2,1)S(1)}, u32[]{:S(2)}, u32[]{:S(2)}) collective-permute-start(bf16[16,2048]{1,0:T(8,128)(2,1)S(1)} %get-tuple-element.126), channel_id=1, source_target_pairs={{0,8},{8,16},{16,24},{24,32},{32,40},{40,48},{48,56},{56,64},{64,7... | collective-permute-start | bytes 196616 | tf_op jit(solution)/shard_map/ppermute | solution.py:512
  16.3 9.1 %collective-permute-start.4 = (bf16[16,2048]{1,0:T(8,128)(2,1)S(1)}, bf16[16,2048]{1,0:T(8,128)(2,1)S(1)}, u32[]{:S(2)}, u32[]{:S(2)}) collective-permute-start(bf16[16,2048]{1,0:T(8,128)(2,1)S(1)} %get-tuple-element.127), channel_id=1, source_target_pairs={{8,0},{16,8},{24,16},{32,24},{40,32},{48,40},{56,48},{64,56},{72,6... | collective-permute-start | bytes 196616 | tf_op jit(solution)/shard_map/ppermute | solution.py:512
  25.4 27.0 %copy-start.2 = (bf16[1024,1024]{1,0:T(8,128)(2,1)S(1)}, bf16[1024,1024]{1,0:T(8,128)(2,1)}, u32[]{:S(2)}) copy-start(bf16[1024,1024]{1,0:T(8,128)(2,1)} %w_down.3) | copy-start | bytes 6291460
  26.8 25.7 %copy-start = (bf16[1024,2048]{1,0:T(8,128)(2,1)S(1)}, bf16[1024,2048]{1,0:T(8,128)(2,1)}, u32[]{:S(2)}) copy-start(bf16[1024,2048]{1,0:T(8,128)(2,1)} %w_up.3) | copy-start | bytes 12582916
  26.8 9.7 %collective-permute-start.5 = (bf16[4,128,256]{2,1,0:T(8,128)(2,1)S(1)}, bf16[4,128,256]{2,1,0:T(8,128)(2,1)S(1)}, u32[]{:S(2)}, u32[]{:S(2)}) collective-permute-start(bf16[4,128,256]{2,1,0:T(8,128)(2,1)S(1)} %get-tuple-element.136.kv), channel_id=1, source_target_pairs={{0,32},{8,40},{16,48},{24,56},{32,64},{40,72},{48,80},{56,88},{64,... | collective-permute-start | bytes 786440 | tf_op jit(solution)/shard_map/ppermute | solution.py:512
  30.5 10.0 %collective-permute-start.6 = (bf16[4,128,256]{2,1,0:T(8,128)(2,1)S(1)}, bf16[4,128,256]{2,1,0:T(8,128)(2,1)S(1)}, u32[]{:S(2)}, u32[]{:S(2)}) collective-permute-start(bf16[4,128,256]{2,1,0:T(8,128)(2,1)S(1)} %get-tuple-element.136.kv), channel_id=1, source_target_pairs={{32,0},{40,8},{48,16},{56,24},{64,32},{72,40},{80,48},{88,56},{96,... | collective-permute-start | bytes 786440 | tf_op jit(solution)/shard_map/ppermute | solution.py:512
  36.5 19.7 %collective-permute-start.7 = (bf16[1600,128]{1,0:T(8,128)(2,1)S(1)}, bf16[1600,128]{1,0:T(8,128)(2,1)S(1)}, u32[]{:S(2)}, u32[]{:S(2)}) collective-permute-start(bf16[1600,128]{1,0:T(8,128)(2,1)S(1)} %get-tuple-element.155), channel_id=1, source_target_pairs={{0,8},{8,16},{16,24},{24,0},{1,9},{9,17},{17,25},{25,1},{2,10},{10... | collective-permute-start | bytes 1228808 | tf_op jit(solution)/shard_map/ppermute | solution.py:521
  37.2 19.5 %collective-permute-start.8 = (bf16[1600,128]{1,0:T(8,128)(2,1)S(1)}, bf16[1600,128]{1,0:T(8,128)(2,1)S(1)}, u32[]{:S(2)}, u32[]{:S(2)}) collective-permute-start(bf16[1600,128]{1,0:T(8,128)(2,1)S(1)} %get-tuple-element.156), channel_id=1, source_target_pairs={{0,16},{8,24},{16,0},{24,8},{1,17},{9,25},{17,1},{25,9},{2,18},{10... | collective-permute-start | bytes 1228808 | tf_op jit(solution)/shard_map/ppermute | solution.py:521
  40.4 16.4 %collective-permute-start.9 = (bf16[1600,128]{1,0:T(8,128)(2,1)S(1)}, bf16[1600,128]{1,0:T(8,128)(2,1)S(1)}, u32[]{:S(2)}, u32[]{:S(2)}) collective-permute-start(bf16[1600,128]{1,0:T(8,128)(2,1)S(1)} %get-tuple-element.157), channel_id=1, source_target_pairs={{0,24},{8,0},{16,8},{24,16},{1,25},{9,1},{17,9},{25,17},{2,26},{10... | collective-permute-start | bytes 1228808 | tf_op jit(solution)/shard_map/ppermute | solution.py:521
  46.5 10.3 %collective-permute-start.10 = (bf16[4,128,256]{2,1,0:T(8,128)(2,1)S(1)}, bf16[4,128,256]{2,1,0:T(8,128)(2,1)S(1)}, u32[]{:S(2)}, u32[]{:S(2)}) collective-permute-start(bf16[4,128,256]{2,1,0:T(8,128)(2,1)S(1)} %get-tuple-element.164), channel_id=1, source_target_pairs={{0,32},{8,40},{16,48},{24,56},{32,64},{40,72},{48,80},{56,88},{64,... | collective-permute-start | bytes 786440 | tf_op jit(solution)/shard_map/ppermute | solution.py:512
  50.3 9.8 %collective-permute-start.11 = (bf16[4,128,256]{2,1,0:T(8,128)(2,1)S(1)}, bf16[4,128,256]{2,1,0:T(8,128)(2,1)S(1)}, u32[]{:S(2)}, u32[]{:S(2)}) collective-permute-start(bf16[4,128,256]{2,1,0:T(8,128)(2,1)S(1)} %get-tuple-element.165), channel_id=1, source_target_pairs={{32,0},{40,8},{48,16},{56,24},{64,32},{72,40},{80,48},{88,56},{96,... | collective-permute-start | bytes 786440 | tf_op jit(solution)/shard_map/ppermute | solution.py:512
  61.7 3.7 %collective-permute-start.15 = (bf16[8,112,512]{2,1,0:T(8,128)(2,1)S(1)}, bf16[8,112,512]{2,1,0:T(8,128)(2,1)S(1)}, u32[]{:S(2)}, u32[]{:S(2)}) collective-permute-start(bf16[8,112,512]{2,1,0:T(8,128)(2,1)S(1)} %get-tuple-element.184), channel_id=1, source_target_pairs={{0,1},{1,0},{2,3},{3,2},{4,5},{5,4},{6,7},{7,6},{8,9},{9,8},{10,11... | collective-permute-start | bytes 2752520 | tf_op jit(solution)/shard_map/ppermute | solution.py:516
  61.8 18.4 %collective-permute-start.12 = (bf16[320,512]{1,0:T(8,128)(2,1)S(1)}, bf16[320,512]{1,0:T(8,128)(2,1)S(1)}, u32[]{:S(2)}, u32[]{:S(2)}) collective-permute-start(bf16[320,512]{1,0:T(8,128)(2,1)S(1)} %get-tuple-element.180), channel_id=1, source_target_pairs={{0,8},{8,16},{16,24},{24,0},{1,9},{9,17},{17,25},{25,1},{2,10},{10... | collective-permute-start | bytes 983048 | tf_op jit(solution)/shard_map/ppermute | solution.py:521
  62.6 17.6 %collective-permute-start.13 = (bf16[320,512]{1,0:T(8,128)(2,1)S(1)}, bf16[320,512]{1,0:T(8,128)(2,1)S(1)}, u32[]{:S(2)}, u32[]{:S(2)}) collective-permute-start(bf16[320,512]{1,0:T(8,128)(2,1)S(1)} %get-tuple-element.181), channel_id=1, source_target_pairs={{0,16},{8,24},{16,0},{24,8},{1,17},{9,25},{17,1},{25,9},{2,18},{10... | collective-permute-start | bytes 983048 | tf_op jit(solution)/shard_map/ppermute | solution.py:521
  64.6 16.2 %collective-permute-start.14 = (bf16[320,512]{1,0:T(8,128)(2,1)S(1)}, bf16[320,512]{1,0:T(8,128)(2,1)S(1)}, u32[]{:S(2)}, u32[]{:S(2)}) collective-permute-start(bf16[320,512]{1,0:T(8,128)(2,1)S(1)} %get-tuple-element.182), channel_id=1, source_target_pairs={{0,24},{8,0},{16,8},{24,16},{1,25},{9,1},{17,9},{25,17},{2,26},{10... | collective-permute-start | bytes 983048 | tf_op jit(solution)/shard_map/ppermute | solution.py:521
  65.6 30.3 %copy-start.3 = (bf16[1,128,1024]{2,1,0:T(8,128)(2,1)S(1)}, bf16[1,128,1024]{2,1,0:T(8,128)(2,1)}, u32[]{:S(2)}) copy-start(bf16[1,128,1024]{2,1,0:T(8,128)(2,1)} %param.8) | copy-start | bytes 786436
  65.6 30.3 %copy-start.4 = (bf16[1,128,1024]{2,1,0:T(8,128)(2,1)S(1)}, bf16[1,128,1024]{2,1,0:T(8,128)(2,1)}, u32[]{:S(2)}) copy-start(bf16[1,128,1024]{2,1,0:T(8,128)(2,1)} %param.9) | copy-start | bytes 786436
  65.6 30.3 %copy-start.5 = (f32[128,1024]{1,0:T(8,128)S(1)}, f32[128,1024]{1,0:T(8,128)}, u32[]{:S(2)}) copy-start(f32[128,1024]{1,0:T(8,128)} %get-tuple-element.203.layer_part) | copy-start | bytes 1572868
  65.6 30.3 %copy-start.6 = (f32[128,1024]{1,0:T(8,128)S(1)}, f32[128,1024]{1,0:T(8,128)}, u32[]{:S(2)}) copy-start(f32[128,1024]{1,0:T(8,128)} %get-tuple-element.204.d_normed) | copy-start | bytes 1572868
  65.6 15.2 %collective-permute-start.16 = (bf16[2,112,512]{2,1,0:T(8,128)(2,1)S(1)}, bf16[2,112,512]{2,1,0:T(8,128)(2,1)S(1)}, u32[]{:S(2)}, u32[]{:S(2)}) collective-permute-start(bf16[2,112,512]{2,1,0:T(8,128)(2,1)S(1)} %get-tuple-element.185), channel_id=1, source_target_pairs={{0,32},{32,64},{64,96},{96,0},{1,33},{33,65},{65,97},{97,1},{2,34}... | collective-permute-start | bytes 688136 | tf_op jit(solution)/shard_map/ppermute | solution.py:527
  69.4 12.6 %collective-permute-start.17 = (bf16[2,112,512]{2,1,0:T(8,128)(2,1)S(1)}, bf16[2,112,512]{2,1,0:T(8,128)(2,1)S(1)}, u32[]{:S(2)}, u32[]{:S(2)}) collective-permute-start(bf16[2,112,512]{2,1,0:T(8,128)(2,1)S(1)} %get-tuple-element.194), channel_id=1, source_target_pairs={{0,64},{32,96},{64,0},{96,32},{1,65},{33,97},{65,1},{97,33},{2,66}... | collective-permute-start | bytes 688136 | tf_op jit(solution)/shard_map/ppermute | solution.py:527
  80.2 6.0 %collective-permute-start.18 = (bf16[2,112,512]{2,1,0:T(8,128)(2,1)S(1)}, bf16[2,112,512]{2,1,0:T(8,128)(2,1)S(1)}, u32[]{:S(2)}, u32[]{:S(2)}) collective-permute-start(bf16[2,112,512]{2,1,0:T(8,128)(2,1)S(1)} %get-tuple-element.195), channel_id=1, source_target_pairs={{0,96},{32,0},{64,32},{96,64},{1,97},{33,1},{65,33},{97,65},{2,98}... | collective-permute-start | bytes 688136 | tf_op jit(solution)/shard_map/ppermute | solution.py:527
  86.2 1.9 %collective-permute-start.19 = (bf16[8,64,512]{2,1,0:T(8,128)(2,1)S(1)}, bf16[8,64,512]{2,1,0:T(8,128)(2,1)S(1)}, u32[]{:S(2)}, u32[]{:S(2)}) collective-permute-start(bf16[8,64,512]{2,1,0:T(8,128)(2,1)S(1)} %get-tuple-element.202), channel_id=1, source_target_pairs={{0,1},{1,0},{2,3},{3,2},{4,5},{5,4},{6,7},{7,6},{8,9},{9,8},{10,11... | collective-permute-start | bytes 1572872 | tf_op jit(solution)/shard_map/ppermute | solution.py:516
  89.0 14.2 %all-to-all-start = ((bf16[8,64,512]{2,1,0:T(8,128)(2,1)}), bf16[8,64,512]{2,1,0:T(8,128)(2,1)S(1)}, u32[]{:S(2)}, u32[]{:S(2)}) async-start(bf16[8,64,512]{2,1,0:T(8,128)(2,1)} %shard_map.147), calls=%async_computation | async-start | bytes 1048576 | tf_op jit(solution)/shard_map/all_to_all | solution.py:620
  94.4 10.3 %collective-permute-start.20 = (bf16[112,512]{1,0:T(8,128)(2,1)}, bf16[112,512]{1,0:T(8,128)(2,1)}, u32[]{:S(2)}, u32[]{:S(2)}) collective-permute-start(bf16[112,512]{1,0:T(8,128)(2,1)} %get-tuple-element.210), channel_id=1, source_target_pairs={{0,128},{128,0},{1,129},{129,1},{2,130},{130,2},{3,131},{131,3},{4... | collective-permute-start | bytes 344072 | tf_op jit(solution)/shard_map/ppermute | solution.py:621
  95.9 8.8 %copy-start.8 = (bf16[112,512]{1,0:T(8,128)(2,1)S(1)}, bf16[112,512]{1,0:T(8,128)(2,1)}, u32[]{:S(2)}) copy-start(bf16[112,512]{1,0:T(8,128)(2,1)} %get-tuple-element.209.gate) | copy-start | bytes 344068
  105.7 10.5 %collective-permute-start.21 = (bf16[176,128]{1,0:T(8,128)(2,1)S(1)}, bf16[176,128]{1,0:T(8,128)(2,1)S(1)}, u32[]{:S(2)}, u32[]{:S(2)}) collective-permute-start(bf16[176,128]{1,0:T(8,128)(2,1)S(1)} %get-tuple-element.213), channel_id=1, source_target_pairs={{0,2},{2,4},{4,6},{6,0},{1,3},{3,5},{5,7},{7,1},{8,10},{10,12},{12... | collective-permute-start | bytes 135176 | tf_op jit(solution)/shard_map/ppermute | solution.py:533
  109.1 8.6 %collective-permute-start.22 = (bf16[176,128]{1,0:T(8,128)(2,1)S(1)}, bf16[176,128]{1,0:T(8,128)(2,1)S(1)}, u32[]{:S(2)}, u32[]{:S(2)}) collective-permute-start(bf16[176,128]{1,0:T(8,128)(2,1)S(1)} %get-tuple-element.214), channel_id=1, source_target_pairs={{0,4},{2,6},{4,0},{6,2},{1,5},{3,7},{5,1},{7,3},{8,12},{10,14},{12... | collective-permute-start | bytes 135176 | tf_op jit(solution)/shard_map/ppermute | solution.py:533
  113.6 5.4 %collective-permute-start.23 = (bf16[176,128]{1,0:T(8,128)(2,1)S(1)}, bf16[176,128]{1,0:T(8,128)(2,1)S(1)}, u32[]{:S(2)}, u32[]{:S(2)}) collective-permute-start(bf16[176,128]{1,0:T(8,128)(2,1)S(1)} %get-tuple-element.215), channel_id=1, source_target_pairs={{0,6},{2,0},{4,2},{6,4},{1,7},{3,1},{5,3},{7,5},{8,14},{10,8},{12,... | collective-permute-start | bytes 135176 | tf_op jit(solution)/shard_map/ppermute | solution.py:533
